TPU v7x, 256 devices: a whole 4x4x8 slice. The times are simulated.
256 devices in a mesh: gx: 4 (over z_hi), gy: 8 (over y, core), gz: 8 (over x, z_lo).
Axes of the slice: x: 4, y: 4, z: 8 (z_hi: 4, z_lo: 2; z = z_hi * 2 + z_lo), core: 2. Of those that a mesh axis runs over, the one named last changes fastest.
Arguments:
- inputs: bfloat16 [512, 12288], P(('gx', 'gy'), 'gz'), may hold values from -6 to 6
- w_in: bfloat16 [12288, 24576], P('gz', ('gx', 'gy')), may hold values from -0.0546875 to 0.0546875
- w_out: bfloat16 [24576, 12288], P(('gx', 'gy'), 'gz'), may hold values from -0.0390625 to 0.0390625
- grad_out: bfloat16 [512, 12288], P(('gx', 'gy'), 'gz'), may hold values from -6 to 6
Outputs:
- output: bfloat16 [512, 12288], P(('gx', 'gy'), 'gz')
- grad_inputs: bfloat16 [512, 12288], P(('gx', 'gy'), 'gz')
- grad_w_in: bfloat16 [12288, 24576], P('gz', ('gx', 'gy'))
- grad_w_out: bfloat16 [24576, 12288], P(('gx', 'gy'), 'gz')
All inputs are finite; a program needn't handle non-finite values.
Results may differ from a plain program's by a relative error of at most 0.005.
Values may be sent and summed in bfloat16 or wider, within the bound.
No kernel may reach another device: no remote copies, remote signals or barrier semaphores. Data moves between devices by JAX's collectives and lax.ppermute only.
A program may use at most 64 MiB of HBM per device.

v0:
```python
import jax
import jax.numpy as jnp
from jax import lax
from jax.sharding import PartitionSpec as P

gelu_scale = 0.7978845608028654
cubic_term = 0.044715


def gelu_parts(value):
    inner = gelu_scale * (value + cubic_term * value * value * value)
    tanh_part = jnp.tanh(inner)
    result = 0.5 * value * (1.0 + tanh_part)
    slope = 0.5 * (1.0 + tanh_part) + 0.5 * value * (1.0 - tanh_part * tanh_part) * gelu_scale * (
        1.0 + 3.0 * cubic_term * value * value
    )
    return (result, slope)


def row_product(left, right, transposed):

    def term(start, count):
        if transposed:
            return lax.dot_general(
                left, right, (((1,), (1,)), ((), ())), preferred_element_type=jnp.float32
            )
        return jnp.dot(left, right, preferred_element_type=jnp.float32)

    return term


def width_share(term, total_rows):
    return lax.psum_scatter(
        term(jnp.int32(0), lax.axis_size("gz") * (total_rows // lax.axis_size("gz"))),
        "gz",
        scatter_dimension=0,
        tiled=True,
    )


def units_whole(share):
    return lax.all_gather(share, "gz", axis=0, tiled=True)


def token_share(term, total_rows):
    return lax.psum_scatter(
        term(
            jnp.int32(0), lax.axis_size(("gx", "gy")) * (total_rows // lax.axis_size(("gx", "gy")))
        ),
        ("gx", "gy"),
        scatter_dimension=0,
        tiled=True,
    )


def on_device(inputs, w_in, w_out, grad_out):
    all_inputs, all_grads = (
        lax.all_gather(inputs, ("gx", "gy"), axis=0, tiled=True),
        lax.all_gather(grad_out, ("gx", "gy"), axis=0, tiled=True),
    )
    total_rows = all_inputs.shape[0]
    preact = width_share(row_product(all_inputs, w_in, False), total_rows)
    result, slope = gelu_parts(preact)
    hidden_all = units_whole(result.astype(jnp.bfloat16))
    grad_hidden = width_share(row_product(all_grads, w_out, True), total_rows)
    grad_pre_all = units_whole((grad_hidden * slope).astype(jnp.bfloat16))
    output = token_share(row_product(hidden_all, w_out, False), total_rows).astype(jnp.bfloat16)
    grad_inputs = token_share(row_product(grad_pre_all, w_in, True), total_rows).astype(
        jnp.bfloat16
    )
    grad_w_in = lax.dot_general(
        all_inputs, grad_pre_all, (((0,), (0,)), ((), ())), preferred_element_type=jnp.float32
    ).astype(jnp.bfloat16)
    grad_w_out = lax.dot_general(
        hidden_all, all_grads, (((0,), (0,)), ((), ())), preferred_element_type=jnp.float32
    ).astype(jnp.bfloat16)
    return (output, grad_inputs, grad_w_in, grad_w_out)


def solution(mesh):
    in_specs = (
        P(("gx", "gy"), "gz"),
        P("gz", ("gx", "gy")),
        P(("gx", "gy"), "gz"),
        P(("gx", "gy"), "gz"),
    )
    out_specs = (
        P(("gx", "gy"), "gz"),
        P(("gx", "gy"), "gz"),
        P("gz", ("gx", "gy")),
        P(("gx", "gy"), "gz"),
    )
    return jax.shard_map(
        on_device, mesh=mesh, in_specs=in_specs, out_specs=out_specs, check_vma=False
    )
```

profile of v0, /device:TPU:8, one launch (start us, length us, event | category | flops | bytes accessed | tf_op | source)
XLA Modules:
  0.0 449.6 jit_solution(17945589339856776361)
XLA Ops:
  7.2 0.0 copy-start
  7.2 0.0 all-gather.5.cloned.1.call-start
  7.2 0.7 all-gather.5.cloned.1.call-update
  7.9 0.0 all-gather.3.cloned.1.call-start
  8.0 0.7 all-gather.3.cloned.1.call-update
  8.7 0.0 reduce-scatter.9.cloned.1.call-start
  8.7 56.9 %all-gather.5.cloned.1.call-done = bf16[512,1536]{1,0:T(8,128)(2,1)} async-done(((bf16[16,1536]{1,0:T(8,128)(2,1)}), bf16[512,1536]{1,0:T(8,128)(2,1)}) %all-gather.5.cloned.1.call-update) | async-done | bytes 1572880 | tf_op jit(solution)/shard_map/all_gather | solution.py:59
  65.6 4.0 fusion.10
  69.6 0.0 reduce-scatter.9.cloned.1.call-update
  69.6 0.0 reduce-scatter.5.cloned.1.call-start
  69.7 48.9 %all-gather.3.cloned.1.call-done = bf16[512,1536]{1,0:T(8,128)(2,1)} async-done(((bf16[16,1536]{1,0:T(8,128)(2,1)}), bf16[512,1536]{1,0:T(8,128)(2,1)}) %all-gather.3.cloned.1.call-update) | async-done | bytes 1572880 | tf_op jit(solution)/shard_map/all_gather | solution.py:58
  118.5 4.7 %fusion.8 = f32[512,768]{1,0:T(8,128)} fusion(bf16[512,1536]{1,0:T(8,128)(2,1)} %all-gather.3.cloned.1.call-done, bf16[1536,768]{1,0:T(8,128)(2,1)} %param.5), kind=kOutput, calls=%fused_computation.13 | convolution fusion | flops 1207959552 | bytes 5505024 | tf_op jit(solution)/shard_map/dot_general | solution.py:27
  123.2 0.0 reduce-scatter.5.cloned.1.call-update
  123.2 0.0 reduce-scatter.7.cloned.1.call-start
  123.3 43.5 %reduce-scatter.9.cloned.1.call-done = f32[64,768]{1,0:T(8,128)} async-done(((f32[512,768]{1,0:T(8,128)}), f32[64,768]{1,0:T(8,128)}) %reduce-scatter.9.cloned.1.call-update) | async-done | bytes 196624 | tf_op jit(solution)/shard_map/reduce_scatter | solution.py:33
  166.8 48.4 %reduce-scatter.5.cloned.1.call-done = f32[64,768]{1,0:T(8,128)} async-done(((f32[512,768]{1,0:T(8,128)}), f32[64,768]{1,0:T(8,128)}) %reduce-scatter.5.cloned.1.call-update) | async-done | bytes 196624 | tf_op jit(solution)/shard_map/reduce_scatter | solution.py:33
  215.3 1.2 fusion.7
  216.4 31.2 %all_gather.13 = bf16[512,768]{1,0:T(8,128)(2,1)S(1)} all-gather(bf16[64,768]{1,0:T(8,128)(2,1)S(1)} %get-tuple-element.9), channel_id=1, replica_groups=mesh['gx'=4,'gy'=8,'gz'=8] {'gz'}, dimensions={0}, use_global_device_ids=true | all-gather | bytes 884736 | tf_op jit(solution)/shard_map/all_gather | solution.py:42
  247.7 3.0 fusion.9
  250.7 0.0 reduce-scatter.7.cloned.1.call-update
  250.7 0.0 reduce-scatter.11.cloned.1.call-start
  250.7 30.4 %all_gather.15 = bf16[512,768]{1,0:T(8,128)(2,1)S(1)} all-gather(bf16[64,768]{1,0:T(8,128)(2,1)S(1)} %get-tuple-element.8), channel_id=1, replica_groups=mesh['gx'=4,'gy'=8,'gz'=8] {'gz'}, dimensions={0}, use_global_device_ids=true | all-gather | bytes 884736 | tf_op jit(solution)/shard_map/all_gather | solution.py:42
  281.2 0.9 copy-done.1
  282.0 4.8 %fusion.11 = f32[512,1536]{1,0:T(8,128)} fusion(bf16[512,768]{1,0:T(8,128)(2,1)S(1)} %all_gather.15, bf16[1536,768]{1,0:T(8,128)(2,1)} %param.5), kind=kOutput, calls=%fused_computation.16 | convolution fusion | flops 1207959552 | bytes 6291456 | tf_op jit(solution)/shard_map/dot_general | solution.py:24
  286.9 0.0 reduce-scatter.11.cloned.1.call-update
  286.9 4.5 fusion
  291.4 4.3 copy.8
  295.6 4.2 convolution_convert_fusion
  299.9 44.0 %reduce-scatter.7.cloned.1.call-done = f32[16,1536]{1,0:T(8,128)} async-done(((f32[512,1536]{1,0:T(8,128)}), f32[16,1536]{1,0:T(8,128)}) %reduce-scatter.7.cloned.1.call-update) | async-done | bytes 98320 | tf_op jit(solution)/shard_map/reduce_scatter | solution.py:46
  343.8 1.5 convert_element_type.22
  345.4 95.9 %reduce-scatter.11.cloned.1.call-done = f32[16,1536]{1,0:T(8,128)} async-done(((f32[512,1536]{1,0:T(8,128)}), f32[16,1536]{1,0:T(8,128)}) %reduce-scatter.11.cloned.1.call-update) | async-done | bytes 98320 | tf_op jit(solution)/shard_map/reduce_scatter | solution.py:46
  441.3 1.5 convert_element_type.24
  (2 shorter events, 0.0 us)
Async XLA Ops:
  7.2 58.5 %copy-start = (bf16[768,1536]{1,0:T(8,128)(2,1)S(1)}, bf16[768,1536]{1,0:T(8,128)(2,1)}, u32[]{:S(2)}) copy-start(bf16[768,1536]{1,0:T(8,128)(2,1)} %param.6) | copy-start | bytes 7077892
  7.2 58.5 %all-gather.5.cloned.1.call-start = ((), (), s32[]{:S(2)}) async-start(), calls=%async_computation.7 | async-start | bytes 1622016 | tf_op jit(solution)/shard_map/all_gather | solution.py:59
  7.9 110.6 %all-gather.3.cloned.1.call-start = ((), (), s32[]{:S(2)}) async-start(), calls=%async_computation.4 | async-start | bytes 1622016 | tf_op jit(solution)/shard_map/all_gather | solution.py:58
  8.7 158.2 %reduce-scatter.9.cloned.1.call-start = ((), (), s32[]{:S(2)}) async-start(), calls=%async_computation.8 | async-start | bytes 1769472 | tf_op jit(solution)/shard_map/reduce_scatter | solution.py:33
  69.6 145.6 %reduce-scatter.5.cloned.1.call-start = ((), (), s32[]{:S(2)}) async-start(), calls=%async_computation.5 | async-start | bytes 1769472 | tf_op jit(solution)/shard_map/reduce_scatter | solution.py:33
  123.2 220.6 %reduce-scatter.7.cloned.1.call-start = ((), (), s32[]{:S(2)}) async-start(), calls=%async_computation.6 | async-start | bytes 3244032 | tf_op jit(solution)/shard_map/reduce_scatter | solution.py:46
  250.7 190.6 %reduce-scatter.11.cloned.1.call-start = ((), (), s32[]{:S(2)}) async-start(), calls=%async_computation.9 | async-start | bytes 3244032 | tf_op jit(solution)/shard_map/reduce_scatter | solution.py:46
  281.2 0.9 copy-start.1
Sparse Core Ops, SparseCore 0:
  10.6 55.0 all-gather.4
  68.2 50.3 all-gather.2
  121.7 45.0 reduce-scatter.8
  169.8 45.4 reduce-scatter.4
  250.8 92.9 reduce-scatter.6
  348.1 93.0 reduce-scatter.10
where the time goes:
time: 451 us; the launch traced here: 450 us
  waiting for transfers between devices  339 us (75%)
  blocking collectives  61.6 us (14%)
  matrix products  25.2 us (6%)
  between operations  14.1 us (3%)
  local copies, waits for them, and re-layouts  5.16 us (1%)
    reduce_scatter x2, waiting for transfers between devices, token_share(): lax.psum_scatter(term(jnp.int32(0), lax.axis_size(('gx', 'gy')) * (total_...  140 us
    reduce_scatter x2, waiting for transfers between devices, width_share(): lax.psum_scatter(term(jnp.int32(0), lax.axis_size('gz') * (total_rows //...  92 us
    all_gather x2, blocking collectives, units_whole(): return lax.all_gather(share, 'gz', axis=0, tiled=True)  61.6 us
    all_gather x1, waiting for transfers between devices, on_device(): lax.all_gather(grad_out, ('gx', 'gy'), axis=0, tiled=True)  56.9 us
    all_gather x1, waiting for transfers between devices, on_device(): lax.all_gather(inputs, ('gx', 'gy'), axis=0, tiled=True)  48.9 us
  transfers between devices with their start and end apart: 6, of which 6 were waited for; matrix products, arithmetic and copies ran while one was open for 6% of the time, Pallas kernels for 0%

commit v1 on v0

v1 whole, which is shorter than its diff:
```python
import functools

import jax
import jax.numpy as jnp
from jax import lax
from jax.experimental import pallas as pl
from jax.experimental.pallas import tpu as pltpu
from jax.sharding import PartitionSpec as P

gelu_scale = 0.7978845608028654
cubic_term = 0.044715
tile = 256
bf16 = jnp.bfloat16
f32 = jnp.float32
same_core = [[2 * y + c for y in range(4)] for c in range(2)]


def gelu_parts(value):
    inner = gelu_scale * (value + cubic_term * value * value * value)
    tanh_part = jnp.tanh(inner)
    result = 0.5 * value * (1.0 + tanh_part)
    slope = 0.5 * (1.0 + tanh_part) + 0.5 * value * (1.0 - tanh_part * tanh_part) * gelu_scale * (
        1.0 + 3.0 * cubic_term * value * value
    )
    return (result, slope)


def from_gx(value, step):
    return lax.ppermute(value, "gx", [((i + step) % 4, i) for i in range(4)])


def to_gx(value, step):
    return lax.ppermute(value, "gx", [(i, (i + step) % 4) for i in range(4)])


def other_core(value):
    return lax.ppermute(value, "gy", [(i, i ^ 1) for i in range(8)])


def over_y(value):
    return lax.all_to_all(value, "gy", 0, 0, tiled=True, axis_index_groups=same_core)


def over_gz(value):
    return lax.all_to_all(value, "gz", 0, 0, tiled=True)


def product(left, right, transposed):
    dims = (((1,), (1,)), ((), ())) if transposed else (((1,), (0,)), ((), ()))
    return lax.dot_general(left, right, dims, preferred_element_type=f32)


def columns_of(weight_ref, start, transposed):
    if transposed:
        return weight_ref[pl.ds(start, tile), :]
    return weight_ref[:, pl.ds(start, tile)]


def call(kernel, name, outs, args, scratch=(), flops=0, moved=0, scalars=1):
    vmem = pl.BlockSpec(memory_space=pltpu.VMEM)
    return pl.pallas_call(
        kernel,
        out_shape=[jax.ShapeDtypeStruct(*out) for out in outs],
        in_specs=[pl.BlockSpec(memory_space=pltpu.SMEM)] * scalars + [vmem] * (len(args) - scalars),
        out_specs=[vmem] * len(outs),
        scratch_shapes=[pltpu.VMEM(*shape) for shape in scratch],
        compiler_params=pltpu.CompilerParams(vmem_limit_bytes=16 * 2**20),
        cost_estimate=pl.CostEstimate(flops=flops, bytes_accessed=moved, transcendentals=0),
        name=name,
    )(*args)


def column_gather_kernel(inputs_ref, grads_ref, *refs):
    out_ref = refs[3]
    for y in range(4):
        out_ref[y, 0:16, :] = inputs_ref[...]
        out_ref[y, 64:80, :] = grads_ref[...]
        for step in (1, 2, 3):
            out_ref[y, 16 * step : 16 * step + 16, :] = refs[step - 1][0:16, :]
            out_ref[y, 64 + 16 * step : 80 + 16 * step, :] = refs[step - 1][16:32, :]


def width_kernel(
    index_ref, near_ref, far_ref, w_in_ref, w_out_ref,
    inputs_ref, grads_ref, own_ref, send_ref, acc,
):
    me = index_ref[0]
    for part, whole in ((0, inputs_ref), (1, grads_ref)):
        for half, source in ((0, near_ref), (1, far_ref)):
            for y in range(4):
                row = 256 * half + 64 * y
                whole[row : row + 64, :] = source[y, 64 * part : 64 * part + 64, :]

    @pl.loop(0, own_ref.shape[1] // tile)
    def _(j):
        start = pl.multiple_of(j * tile, tile)
        for part, whole, weight, transposed in (
            (0, inputs_ref, w_in_ref, False),
            (1, grads_ref, w_out_ref, True),
        ):
            rows = slice(64 * part, 64 * part + 64)
            acc[part] = product(whole[...], columns_of(weight, start, transposed), transposed)
            own_ref[rows, pl.ds(start, tile)] = acc[part, pl.ds(pl.multiple_of(me * 64, 64), 64), :]
            for peer in range(8):
                send_ref[peer, rows, pl.ds(start, tile)] = acc[
                    part, 64 * peer : 64 * peer + 64, :
                ].astype(bf16)


def activation_kernel(index_ref, parts_ref, own_ref, out_ref):
    me = index_ref[0]

    @pl.loop(0, 4)
    def _(j):
        sums = []
        for part in range(2):
            rows = pl.ds(pl.multiple_of(64 * part + j * 16, 16), 16)
            total = own_ref[rows, :]
            for peer in range(8):
                total = total + jnp.where(peer == me, 0.0, parts_ref[peer, rows, :].astype(f32))
            sums.append(total)
        result, slope = gelu_parts(sums[0])
        for part, value in ((0, result), (1, sums[1] * slope)):
            rows = pl.ds(pl.multiple_of(64 * part + j * 16, 16), 16)
            rounded = value.astype(bf16)
            for peer in range(8):
                out_ref[peer, rows, :] = rounded


def far_kernel(part, transposed, parts_ref, weight_ref, whole_ref, far_ref):
    for share in range(8):
        whole_ref[64 * share : 64 * share + 64, :] = parts_ref[share, 64 * part : 64 * part + 64, :]

    @pl.loop(0, far_ref.shape[1] // tile)
    def _(j):
        start = pl.multiple_of(j * tile, tile)
        far_ref[:, pl.ds(start, tile)] = product(
            whole_ref[256:, :], columns_of(weight_ref, start, transposed), transposed
        )


def near_kernel(
    index_ref, hidden_ref, grad_pre_ref, w_out_ref, w_in_ref, far_hidden_ref, far_grad_ref,
    own_ref, send_ref, acc,
):
    me = lax.shift_right_logical(index_ref[0], 1)

    @pl.loop(0, own_ref.shape[1] // tile)
    def _(j):
        start = pl.multiple_of(j * tile, tile)
        cols = pl.ds(start, tile)
        for part, whole, weight, far, transposed in (
            (0, hidden_ref, w_out_ref, far_hidden_ref, False),
            (1, grad_pre_ref, w_in_ref, far_grad_ref, True),
        ):
            rows = slice(64 * part, 64 * part + 64)
            acc[part] = far[:, cols] + product(
                whole[:256, :], columns_of(weight, start, transposed), transposed
            )
            own_ref[rows, cols] = acc[part, pl.ds(pl.multiple_of(me * 64, 64), 64), :]
            for peer in range(4):
                send_ref[peer, rows, cols] = acc[part, 64 * peer : 64 * peer + 64, :].astype(bf16)


def column_kernel(index_ref, parts_ref, own_ref, mine_ref, *sends):
    me = lax.shift_right_logical(index_ref[0], 1)
    for step in range(4):
        for part in range(2):
            rows = slice(64 * part + 16 * step, 64 * part + 16 * step + 16)
            total = own_ref[rows, :]
            for peer in range(4):
                total = total + jnp.where(peer == me, 0.0, parts_ref[peer, rows, :].astype(f32))
            if step == 0:
                mine_ref[16 * part : 16 * part + 16, :] = total
            else:
                sends[step - 1][16 * part : 16 * part + 16, :] = total.astype(bf16)


def on_device(inputs, w_in, w_out, grad_out):
    width, units = w_in.shape
    gz_index = jnp.reshape(lax.axis_index("gz"), (1,)).astype(jnp.int32)
    y_index = jnp.reshape(lax.axis_index("gy"), (1,)).astype(jnp.int32)
    both = jnp.concatenate([inputs, grad_out], axis=0)
    (column,) = call(
        column_gather_kernel,
        "column_gather",
        [((4, 128, width), bf16)],
        [inputs, grad_out] + [from_gx(both, step) for step in (1, 2, 3)],
        moved=2 * 2**20,
        scalars=0,
    )
    near = over_y(column)
    far = other_core(near)
    all_inputs, all_grads, own, sends = call(
        width_kernel,
        "width_product",
        [
            ((512, width), bf16),
            ((512, width), bf16),
            ((128, units), f32),
            ((8, 128, units), bf16),
        ],
        [gz_index, near, far, w_in, w_out],
        scratch=[((2, 512, tile), f32)],
        flops=4 * 512 * width * units,
        moved=12 * 2**20,
    )
    (shares,) = call(
        activation_kernel,
        "activation",
        [((8, 128, units), bf16)],
        [gz_index, over_gz(sends), own],
        moved=4 * 2**20,
    )
    gathered = over_gz(shares)
    far_flops = 2 * 256 * width * units
    hidden_all, far_hidden = call(
        functools.partial(far_kernel, 0, False),
        "far_hidden",
        [((512, units), bf16), ((256, width), f32)],
        [gathered, w_out],
        flops=far_flops,
        moved=6 * 2**20,
        scalars=0,
    )
    grad_pre_all, far_grad = call(
        functools.partial(far_kernel, 1, True),
        "far_grad",
        [((512, units), bf16), ((256, width), f32)],
        [gathered, w_in],
        flops=far_flops,
        moved=6 * 2**20,
        scalars=0,
    )
    own, sends = call(
        near_kernel,
        "near_product",
        [((128, width), f32), ((4, 128, width), bf16)],
        [y_index, hidden_all, grad_pre_all, w_out, w_in, other_core(far_hidden), other_core(far_grad)],
        scratch=[((2, 256, tile), f32)],
        flops=2 * far_flops,
        moved=12 * 2**20,
    )
    mine, *sends = call(
        column_kernel,
        "column_sum",
        [((32, width), f32)] + [((32, width), bf16)] * 3,
        [y_index, over_y(sends), own],
        moved=4 * 2**20,
    )
    ends = [to_gx(send, step) for step, send in zip((1, 2, 3), sends)]
    result = (mine + sum(end.astype(f32) for end in ends)).astype(bf16)
    grad_w_in = lax.dot_general(
        all_inputs, grad_pre_all, (((0,), (0,)), ((), ())), preferred_element_type=f32
    ).astype(bf16)
    grad_w_out = lax.dot_general(
        hidden_all, all_grads, (((0,), (0,)), ((), ())), preferred_element_type=f32
    ).astype(bf16)
    return (result[:16], result[16:], grad_w_in, grad_w_out)


def solution(mesh):
    in_specs = (
        P(("gx", "gy"), "gz"),
        P("gz", ("gx", "gy")),
        P(("gx", "gy"), "gz"),
        P(("gx", "gy"), "gz"),
    )
    out_specs = (
        P(("gx", "gy"), "gz"),
        P(("gx", "gy"), "gz"),
        P("gz", ("gx", "gy")),
        P(("gx", "gy"), "gz"),
    )
    return jax.shard_map(
        on_device, mesh=mesh, in_specs=in_specs, out_specs=out_specs, check_vma=False
    )
```

time: 451 us -> 170 us (0.38)
  waiting for transfers between devices: 339 us -> 33.8 us
  starting transfers between devices: 0.24 us -> 25.6 us
  matrix products: 25.2 us -> 7.06 us
  Pallas kernels: 0 us -> 16.2 us
  between operations: 14.1 us -> 0.73 us
  blocking collectives: 61.6 us -> 73.1 us
  local copies, waits for them, and re-layouts: 5.16 us -> 11.5 us
    reduce_scatter x4 -> x0, waiting for transfers between devices: 232 us -> none  [the longest x2 140 us: token_share(): lax.psum_scatter(term(jnp.int32(0), lax.axis_size(('gx', 'gy')) * (total_...]
    all_gather x2 -> x0, waiting for transfers between devices: 106 us -> none  [the longest x1 56.9 us: on_device(): lax.all_gather(grad_out, ('gx', 'gy'), axis=0, tiled=True)]
    all_to_all x0 -> x3, blocking collectives: none -> 73.1 us  [the longest x2 51.9 us: over_gz(): return lax.all_to_all(value, 'gz', 0, 0, tiled=True)]
    all_gather x2 -> x0, blocking collectives: 61.6 us -> none  [units_whole(): return lax.all_gather(share, 'gz', axis=0, tiled=True)]
    ppermute x0 -> x9, starting transfers between devices: none -> 20.5 us  [the longest x3 10.1 us: from_gx(): return lax.ppermute(value, 'gx', [((i + step) % 4, i) for i in range(4)])]
    ppermute x0 -> x9, waiting for transfers between devices: none -> 18 us  [the longest x3 7.71 us: from_gx(): return lax.ppermute(value, 'gx', [((i + step) % 4, i) for i in range(4)])]
    dot_general x4 -> x0, matrix products: 16.5 us -> none  [the longest x2 8.78 us: term(): lax.dot_general(left, right, (((1,), (1,)), ((), ())), preferred_element_...]
    pallas_call x0 -> x7, Pallas kernels: none -> 16.2 us  [call(): pl.pallas_call(kernel, out_shape=[jax.ShapeDtypeStruct(*out) for out in o...]
  transfers between devices with their start and end apart: 6 -> 10, of which waited for: 6 -> 8; matrix products, arithmetic and copies ran while one was open for 6% -> 4% of each run, Pallas kernels for 0% -> 2%
where the time goes in v1:
time: 170 us; the launch traced here: 168 us
  blocking collectives  73.1 us (43%)
  waiting for transfers between devices  33.8 us (20%)
  starting transfers between devices  25.6 us (15%)
  Pallas kernels  16.2 us (10%)
  local copies, waits for them, and re-layouts  11.5 us (7%)
  matrix products  7.06 us (4%)
    all_to_all x2, blocking collectives, over_gz(): return lax.all_to_all(value, 'gz', 0, 0, tiled=True)  51.9 us
    all_to_all x1, blocking collectives, over_y(): lax.all_to_all(value, 'gy', 0, 0, tiled=True, axis_index_groups=same_core)  21.1 us
    pallas_call x7, Pallas kernels, call(): pl.pallas_call(kernel, out_shape=[jax.ShapeDtypeStruct(*out) for out in o...  16.2 us
    all_to_all x1, waiting for transfers between devices, over_y(): lax.all_to_all(value, 'gy', 0, 0, tiled=True, axis_index_groups=same_core)  15.8 us
    ppermute x3, starting transfers between devices, from_gx(): return lax.ppermute(value, 'gx', [((i + step) % 4, i) for i in range(4)])  10.1 us
    unnamed x31, local copies, waits for them, and re-layouts  10.1 us
    ppermute x3, starting transfers between devices, to_gx(): return lax.ppermute(value, 'gx', [(i, (i + step) % 4) for i in range(4)])  9.83 us
    ppermute x3, waiting for transfers between devices, from_gx(): return lax.ppermute(value, 'gx', [((i + step) % 4, i) for i in range(4)])  7.71 us
  transfers between devices with their start and end apart: 10, of which 8 were waited for; matrix products, arithmetic and copies ran while one was open for 4% of the time, Pallas kernels for 2%

profile of v1, /device:TPU:8, one launch (start us, length us, event | category | flops | bytes accessed | tf_op | source)
XLA Modules:
  0.0 168.0 jit_solution(18304554886890818667)
XLA Ops:
  0.6 0.8 constant_dynamic-update-slice_fusion.1
  1.4 0.8 constant_dynamic-update-slice_fusion
  2.2 6.3 %collective-permute-start = (bf16[32,1536]{1,0:T(8,128)(2,1)S(1)}, bf16[32,1536]{1,0:T(8,128)(2,1)S(1)}, u32[]{:S(2)}, u32[]{:S(2)}) collective-permute-start(bf16[32,1536]{1,0:T(8,128)(2,1)S(1)} %constant_dynamic-update-slice_fusion), channel_id=1, source_target_pairs={{64,0},{128,64},{192,128},{0,192},{65,1},{129,65},{193,129},{1,193... | collective-permute-start | bytes 294920 | tf_op jit(solution)/shard_map/ppermute | solution.py:29
  8.5 0.9 collective-permute-start.1
  9.4 2.9 %collective-permute-start.2 = (bf16[32,1536]{1,0:T(8,128)(2,1)S(1)}, bf16[32,1536]{1,0:T(8,128)(2,1)S(1)}, u32[]{:S(2)}, u32[]{:S(2)}) collective-permute-start(bf16[32,1536]{1,0:T(8,128)(2,1)S(1)} %constant_dynamic-update-slice_fusion), channel_id=1, source_target_pairs={{192,0},{0,64},{64,128},{128,192},{193,1},{1,65},{65,129},{129,193... | collective-permute-start | bytes 294920 | tf_op jit(solution)/shard_map/ppermute | solution.py:29
  12.4 4.6 %collective-permute-done.refs_0_ = bf16[32,1536]{1,0:T(8,128)(2,1)S(1)} collective-permute-done((bf16[32,1536]{1,0:T(8,128)(2,1)S(1)}, bf16[32,1536]{1,0:T(8,128)(2,1)S(1)}, u32[]{:S(2)}, u32[]{:S(2)}) %collective-permute-start) | collective-permute-done | bytes 98336 | tf_op jit(solution)/shard_map/ppermute | solution.py:29
  16.9 3.1 %collective-permute-done.1.refs_1_ = bf16[32,1536]{1,0:T(8,128)(2,1)S(1)} collective-permute-done((bf16[32,1536]{1,0:T(8,128)(2,1)S(1)}, bf16[32,1536]{1,0:T(8,128)(2,1)S(1)}, u32[]{:S(2)}, u32[]{:S(2)}) %collective-permute-start.1) | collective-permute-done | bytes 98336 | tf_op jit(solution)/shard_map/ppermute | solution.py:29
  20.1 0.8 copy-done.10
  20.9 0.8 copy-done.11
  21.8 21.1 %all_to_all.20.near_ref = bf16[4,128,1536]{2,1,0:T(8,128)(2,1)} all-to-all(bf16[4,128,1536]{2,1,0:T(8,128)(2,1)S(1)} %column_gather.1), channel_id=1, replica_groups={{0,16,32,48},{8,24,40,56},{1,17,33,49},{9,25,41,57},{2,18,34,50},{10,26..., dimensions={0} | all-to-all | bytes 3145728 | tf_op jit(solution)/shard_map/all_to_all | solution.py:41
  42.9 3.7 %collective-permute-done.3.far_ref = bf16[4,128,1536]{2,1,0:T(8,128)(2,1)} collective-permute-done((bf16[4,128,1536]{2,1,0:T(8,128)(2,1)}, bf16[4,128,1536]{2,1,0:T(8,128)(2,1)}, u32[]{:S(2)}, u32[]{:S(2)}) %collective-permute-start.3) | collective-permute-done | bytes 1572896 | tf_op jit(solution)/shard_map/ppermute | solution.py:37
  46.7 1.7 copy-done.1
  48.3 5.1 %width_product.1 = (bf16[512,1536]{1,0:T(8,128)(2,1)S(1)}, bf16[512,1536]{1,0:T(8,128)(2,1)S(1)}, f32[128,768]{1,0:T(8,128)S(1)}, bf16[8,128,768]{2,1,0:T(8,128)(2,1)S(1)}) custom-call(s32[1]{0:T(128)} %bitcast.1.index_ref, bf16[4,128,1536]{2,1,0:T(8,128)(2,1)} %all_to_all.20.near_ref, bf16[4,128,1536]{2,1,0:T(8,128)(2,1)} %collective-permute-done.3.far_ref, ...), custom_call_target="tpu_custom_call" | custom-call | flops 2415919104 | bytes 12582912 | tf_op jit(solution)/shard_map/width_product/pallas_call | solution.py:61
  53.5 28.4 %all_to_all.21.parts_ref = bf16[8,128,768]{2,1,0:T(8,128)(2,1)S(1)} all-to-all(bf16[8,128,768]{2,1,0:T(8,128)(2,1)S(1)} %get-tuple-element.18), channel_id=1, replica_groups=mesh['gx'=4,'gy'=8,'gz'=8] {'gz'}, dimensions={0} | all-to-all | bytes 3145728 | tf_op jit(solution)/shard_map/all_to_all | solution.py:45
  82.5 23.5 %all_to_all.22.parts_ref = bf16[8,128,768]{2,1,0:T(8,128)(2,1)S(1)} all-to-all(bf16[8,128,768]{2,1,0:T(8,128)(2,1)S(1)} %activation.1), channel_id=1, replica_groups=mesh['gx'=4,'gy'=8,'gz'=8] {'gz'}, dimensions={0} | all-to-all | bytes 3145728 | tf_op jit(solution)/shard_map/all_to_all | solution.py:45
  106.0 2.8 %far_hidden.1 = (bf16[512,768]{1,0:T(8,128)(2,1)S(1)}, f32[256,1536]{1,0:T(8,128)}) custom-call(bf16[8,128,768]{2,1,0:T(8,128)(2,1)S(1)} %all_to_all.22.parts_ref, bf16[768,1536]{1,0:T(8,128)(2,1)S(1)} %copy-done.2), custom_call_target="tpu_custom_call" | custom-call | flops 603979776 | bytes 6291456 | tf_op jit(solution)/shard_map/far_hidden/pallas_call | solution.py:61
  108.8 3.0 %far_grad.1 = (bf16[512,768]{1,0:T(8,128)(2,1)S(1)}, f32[256,1536]{1,0:T(8,128)}) custom-call(bf16[8,128,768]{2,1,0:T(8,128)(2,1)S(1)} %all_to_all.22.parts_ref, bf16[1536,768]{1,0:T(8,128)(2,1)S(1)} %copy-done), custom_call_target="tpu_custom_call" | custom-call | flops 603979776 | bytes 6291456 | tf_op jit(solution)/shard_map/far_grad/pallas_call | solution.py:61
  112.6 3.1 %collective-permute-done.5.far_grad_ref = f32[256,1536]{1,0:T(8,128)} collective-permute-done((f32[256,1536]{1,0:T(8,128)}, f32[256,1536]{1,0:T(8,128)}, u32[]{:S(2)}, u32[]{:S(2)}) %collective-permute-start.5) | collective-permute-done | bytes 1572896 | tf_op jit(solution)/shard_map/ppermute | solution.py:37
  115.7 1.7 copy-done.3
  117.4 1.1 copy-done.6
  118.5 4.2 %near_product.1 = (f32[128,1536]{1,0:T(8,128)S(1)}, bf16[4,128,1536]{2,1,0:T(8,128)(2,1)S(1)}) custom-call(s32[1]{0:T(128)} %bitcast.index_ref, bf16[512,768]{1,0:T(8,128)(2,1)S(1)} %copy-done.6, bf16[512,768]{1,0:T(8,128)(2,1)S(1)} %get-tuple-element.21.grad_pre_ref, bf16[768,1536]{1,0:T(8,128)(2,1)S(1)} %copy-done.3, bf16[1536,768]{1,0:T(8,128)(2,1)S(1)} %copy-done, ...), custom_call_target="tpu_custom_call" | custom-call | flops 1207959552 | bytes 12582912 | tf_op jit(solution)/shard_map/near_product/pallas_call | solution.py:61
  122.8 1.1 copy-done.4
  123.9 0.9 copy-done.8
  124.8 5.1 %all-to-all-start.3 = ((bf16[4,128,1536]{2,1,0:T(8,128)(2,1)}), bf16[4,128,1536]{2,1,0:T(8,128)(2,1)S(1)}, u32[]{:S(2)}, u32[]{:S(2)}) async-start(bf16[4,128,1536]{2,1,0:T(8,128)(2,1)} %copy-done.4), calls=%async_computation.3 | async-start | bytes 3145728 | tf_op jit(solution)/shard_map/all_to_all | solution.py:41
  129.9 4.2 %convolution_convert_fusion = bf16[768,1536]{1,0:T(8,128)(2,1)} fusion(bf16[512,768]{1,0:T(8,128)(2,1)S(1)} %copy-done.7, bf16[512,1536]{1,0:T(8,128)(2,1)} %copy-done.14), kind=kOutput, calls=%fused_computation | convolution fusion | flops 1209139200 | bytes 4718592 | tf_op jit(solution)/shard_map/dot_general | solution.py:256
  134.2 15.8 %all-to-all-done.3.parts_ref = bf16[4,128,1536]{2,1,0:T(8,128)(2,1)S(1)} async-done(((bf16[4,128,1536]{2,1,0:T(8,128)(2,1)}), bf16[4,128,1536]{2,1,0:T(8,128)(2,1)S(1)}, u32[]{:S(2)}, u32[]{:S(2)}) %all-to-all-start.3) | async-done | bytes 1572896 | tf_op jit(solution)/shard_map/all_to_all | solution.py:41
  150.0 1.1 copy-done.9
  151.4 2.6 %collective-permute-start.6 = (bf16[32,1536]{1,0:T(8,128)(2,1)S(1)}, bf16[32,1536]{1,0:T(8,128)(2,1)S(1)}, u32[]{:S(2)}, u32[]{:S(2)}) collective-permute-start(bf16[32,1536]{1,0:T(8,128)(2,1)S(1)} %get-tuple-element.27), channel_id=1, source_target_pairs={{0,64},{64,128},{128,192},{192,0},{1,65},{65,129},{129,193},{193,1... | collective-permute-start | bytes 294920 | tf_op jit(solution)/shard_map/ppermute | solution.py:33
  154.0 3.9 %collective-permute-start.7 = (bf16[32,1536]{1,0:T(8,128)(2,1)S(1)}, bf16[32,1536]{1,0:T(8,128)(2,1)S(1)}, u32[]{:S(2)}, u32[]{:S(2)}) collective-permute-start(bf16[32,1536]{1,0:T(8,128)(2,1)S(1)} %get-tuple-element.28), channel_id=1, source_target_pairs={{0,128},{64,192},{128,0},{192,64},{1,129},{65,193},{129,1},{193,65... | collective-permute-start | bytes 294920 | tf_op jit(solution)/shard_map/ppermute | solution.py:33
  158.0 3.3 %collective-permute-start.8 = (bf16[32,1536]{1,0:T(8,128)(2,1)S(1)}, bf16[32,1536]{1,0:T(8,128)(2,1)S(1)}, u32[]{:S(2)}, u32[]{:S(2)}) collective-permute-start(bf16[32,1536]{1,0:T(8,128)(2,1)S(1)} %get-tuple-element.29), channel_id=1, source_target_pairs={{0,192},{64,0},{128,64},{192,128},{1,193},{65,1},{129,65},{193,129... | collective-permute-start | bytes 294920 | tf_op jit(solution)/shard_map/ppermute | solution.py:33
  161.3 2.8 %convolution_convert_fusion.1 = bf16[1536,768]{1,0:T(8,128)(2,1)} fusion(bf16[512,1536]{1,0:T(8,128)(2,1)S(1)} %copy-done.13, bf16[512,768]{1,0:T(8,128)(2,1)S(1)} %get-tuple-element.21.grad_pre_ref), kind=kOutput, calls=%fused_computation.1 | convolution fusion | flops 1209139200 | bytes 4718592 | tf_op jit(solution)/shard_map/dot_general | solution.py:253
  164.8 2.4 %collective-permute-done.8 = bf16[32,1536]{1,0:T(8,128)(2,1)S(1)} collective-permute-done((bf16[32,1536]{1,0:T(8,128)(2,1)S(1)}, bf16[32,1536]{1,0:T(8,128)(2,1)S(1)}, u32[]{:S(2)}, u32[]{:S(2)}) %collective-permute-start.8) | collective-permute-done | bytes 98336 | tf_op jit(solution)/shard_map/ppermute | solution.py:33
  (34 shorter events, 3.1 us)
Async XLA Ops:
  2.2 14.7 %collective-permute-start = (bf16[32,1536]{1,0:T(8,128)(2,1)S(1)}, bf16[32,1536]{1,0:T(8,128)(2,1)S(1)}, u32[]{:S(2)}, u32[]{:S(2)}) collective-permute-start(bf16[32,1536]{1,0:T(8,128)(2,1)S(1)} %constant_dynamic-update-slice_fusion), channel_id=1, source_target_pairs={{64,0},{128,64},{192,128},{0,192},{65,1},{129,65},{193,129},{1,193... | collective-permute-start | bytes 294920 | tf_op jit(solution)/shard_map/ppermute | solution.py:29
  8.5 11.5 %collective-permute-start.1 = (bf16[32,1536]{1,0:T(8,128)(2,1)S(1)}, bf16[32,1536]{1,0:T(8,128)(2,1)S(1)}, u32[]{:S(2)}, u32[]{:S(2)}) collective-permute-start(bf16[32,1536]{1,0:T(8,128)(2,1)S(1)} %constant_dynamic-update-slice_fusion), channel_id=1, source_target_pairs={{128,0},{192,64},{0,128},{64,192},{129,1},{193,65},{1,129},{65,193... | collective-permute-start | bytes 294920 | tf_op jit(solution)/shard_map/ppermute | solution.py:29
  9.4 10.6 %collective-permute-start.2 = (bf16[32,1536]{1,0:T(8,128)(2,1)S(1)}, bf16[32,1536]{1,0:T(8,128)(2,1)S(1)}, u32[]{:S(2)}, u32[]{:S(2)}) collective-permute-start(bf16[32,1536]{1,0:T(8,128)(2,1)S(1)} %constant_dynamic-update-slice_fusion), channel_id=1, source_target_pairs={{192,0},{0,64},{64,128},{128,192},{193,1},{1,65},{65,129},{129,193... | collective-permute-start | bytes 294920 | tf_op jit(solution)/shard_map/ppermute | solution.py:29
  20.1 0.8 copy-start.10
  20.9 0.8 copy-start.11
  21.8 24.9 %copy-start = (bf16[1536,768]{1,0:T(8,128)(2,1)S(1)}, bf16[1536,768]{1,0:T(8,128)(2,1)}, u32[]{:S(2)}) copy-start(bf16[1536,768]{1,0:T(8,128)(2,1)} %w_in_ref.3) | copy-start | bytes 7077892
  42.9 3.8 %collective-permute-start.3 = (bf16[4,128,1536]{2,1,0:T(8,128)(2,1)}, bf16[4,128,1536]{2,1,0:T(8,128)(2,1)}, u32[]{:S(2)}, u32[]{:S(2)}) collective-permute-start(bf16[4,128,1536]{2,1,0:T(8,128)(2,1)} %all_to_all.20.near_ref), channel_id=1, source_target_pairs={{0,8},{8,0},{16,24},{24,16},{32,40},{40,32},{48,56},{56,48},{1,9},... | collective-permute-start | bytes 4718600 | tf_op jit(solution)/shard_map/ppermute | solution.py:37
  46.7 1.7 copy-start.1
  53.5 28.5 %copy-start.12 = (bf16[512,1536]{1,0:T(8,128)(2,1)}, bf16[512,1536]{1,0:T(8,128)(2,1)S(1)}, u32[]{:S(2)}) copy-start(bf16[512,1536]{1,0:T(8,128)(2,1)S(1)} %get-tuple-element.30) | copy-start | bytes 4718596
  53.5 28.4 %copy-start.14 = (bf16[512,1536]{1,0:T(8,128)(2,1)}, bf16[512,1536]{1,0:T(8,128)(2,1)S(1)}, u32[]{:S(2)}) copy-start(bf16[512,1536]{1,0:T(8,128)(2,1)S(1)} %get-tuple-element.31) | copy-start | bytes 4718596
  82.5 23.5 %copy-start.2 = (bf16[768,1536]{1,0:T(8,128)(2,1)S(1)}, bf16[768,1536]{1,0:T(8,128)(2,1)}, u32[]{:S(2)}) copy-start(bf16[768,1536]{1,0:T(8,128)(2,1)} %w_out_ref.3) | copy-start | bytes 7077892
  108.8 3.0 %copy-start.5 = (bf16[512,768]{1,0:T(8,128)(2,1)}, bf16[512,768]{1,0:T(8,128)(2,1)S(1)}, u32[]{:S(2)}) copy-start(bf16[512,768]{1,0:T(8,128)(2,1)S(1)} %get-tuple-element.20.hidden_ref) | copy-start | bytes 2359300
  108.8 3.8 %collective-permute-start.4 = (f32[256,1536]{1,0:T(8,128)}, f32[256,1536]{1,0:T(8,128)}, u32[]{:S(2)}, u32[]{:S(2)}) collective-permute-start(f32[256,1536]{1,0:T(8,128)} %get-tuple-element.22), channel_id=1, source_target_pairs={{0,8},{8,0},{16,24},{24,16},{32,40},{40,32},{48,56},{56,48},{1,9},... | collective-permute-start | bytes 4718600 | tf_op jit(solution)/shard_map/ppermute | solution.py:37
  111.8 3.9 %collective-permute-start.5 = (f32[256,1536]{1,0:T(8,128)}, f32[256,1536]{1,0:T(8,128)}, u32[]{:S(2)}, u32[]{:S(2)}) collective-permute-start(f32[256,1536]{1,0:T(8,128)} %get-tuple-element.23), channel_id=1, source_target_pairs={{0,8},{8,0},{16,24},{24,16},{32,40},{40,32},{48,56},{56,48},{1,9},... | collective-permute-start | bytes 4718600 | tf_op jit(solution)/shard_map/ppermute | solution.py:37
  115.7 1.7 copy-start.3
  117.4 1.1 copy-start.6
  122.8 1.1 copy-start.4
  123.9 0.9 copy-start.8
  124.8 5.1 %copy-start.7 = (bf16[512,768]{1,0:T(8,128)(2,1)S(1)}, bf16[512,768]{1,0:T(8,128)(2,1)}, u32[]{:S(2)}) copy-start(bf16[512,768]{1,0:T(8,128)(2,1)} %copy-done.5) | copy-start | bytes 2359300
  124.8 25.2 %all-to-all-start.3 = ((bf16[4,128,1536]{2,1,0:T(8,128)(2,1)}), bf16[4,128,1536]{2,1,0:T(8,128)(2,1)S(1)}, u32[]{:S(2)}, u32[]{:S(2)}) async-start(bf16[4,128,1536]{2,1,0:T(8,128)(2,1)} %copy-done.4), calls=%async_computation.3 | async-start | bytes 3145728 | tf_op jit(solution)/shard_map/all_to_all | solution.py:41
  150.0 1.1 copy-start.9
  151.1 10.2 %copy-start.13 = (bf16[512,1536]{1,0:T(8,128)(2,1)S(1)}, bf16[512,1536]{1,0:T(8,128)(2,1)}, u32[]{:S(2)}) copy-start(bf16[512,1536]{1,0:T(8,128)(2,1)} %copy-done.12) | copy-start | bytes 4718596
  151.4 12.7 %collective-permute-start.6 = (bf16[32,1536]{1,0:T(8,128)(2,1)S(1)}, bf16[32,1536]{1,0:T(8,128)(2,1)S(1)}, u32[]{:S(2)}, u32[]{:S(2)}) collective-permute-start(bf16[32,1536]{1,0:T(8,128)(2,1)S(1)} %get-tuple-element.27), channel_id=1, source_target_pairs={{0,64},{64,128},{128,192},{192,0},{1,65},{65,129},{129,193},{193,1... | collective-permute-start | bytes 294920 | tf_op jit(solution)/shard_map/ppermute | solution.py:33
  154.0 10.8 %collective-permute-start.7 = (bf16[32,1536]{1,0:T(8,128)(2,1)S(1)}, bf16[32,1536]{1,0:T(8,128)(2,1)S(1)}, u32[]{:S(2)}, u32[]{:S(2)}) collective-permute-start(bf16[32,1536]{1,0:T(8,128)(2,1)S(1)} %get-tuple-element.28), channel_id=1, source_target_pairs={{0,128},{64,192},{128,0},{192,64},{1,129},{65,193},{129,1},{193,65... | collective-permute-start | bytes 294920 | tf_op jit(solution)/shard_map/ppermute | solution.py:33
  158.0 9.3 %collective-permute-start.8 = (bf16[32,1536]{1,0:T(8,128)(2,1)S(1)}, bf16[32,1536]{1,0:T(8,128)(2,1)S(1)}, u32[]{:S(2)}, u32[]{:S(2)}) collective-permute-start(bf16[32,1536]{1,0:T(8,128)(2,1)S(1)} %get-tuple-element.29), channel_id=1, source_target_pairs={{0,192},{64,0},{128,64},{192,128},{1,193},{65,1},{129,65},{193,129... | collective-permute-start | bytes 294920 | tf_op jit(solution)/shard_map/ppermute | solution.py:33

commit v2 on v0

v2 whole, which is shorter than its diff:
```python
import functools

import jax
import jax.numpy as jnp
from jax import lax
from jax.experimental import pallas as pl
from jax.experimental.pallas import tpu as pltpu
from jax.sharding import PartitionSpec as P

gelu_scale = 0.7978845608028654
cubic_term = 0.044715
tile = 256
bf16 = jnp.bfloat16
f32 = jnp.float32


def gelu_parts(value):
    inner = gelu_scale * (value + cubic_term * value * value * value)
    tanh_part = jnp.tanh(inner)
    result = 0.5 * value * (1.0 + tanh_part)
    slope = 0.5 * (1.0 + tanh_part) + 0.5 * value * (1.0 - tanh_part * tanh_part) * gelu_scale * (
        1.0 + 3.0 * cubic_term * value * value
    )
    return (result, slope)


def from_gx(value, step):
    return lax.ppermute(value, "gx", [((i + step) % 4, i) for i in range(4)])


def to_gx(value, step):
    return lax.ppermute(value, "gx", [(i, (i + step) % 4) for i in range(4)])


def other_core(value):
    return lax.ppermute(value, "gy", [(i, i ^ 1) for i in range(8)])


def from_y(value, step):
    return lax.ppermute(value, "gy", [((i + 2 * step) % 8, i) for i in range(8)])


def to_y(value, step):
    return lax.ppermute(value, "gy", [(i, (i + 2 * step) % 8) for i in range(8)])


def over_gz(value):
    return lax.all_to_all(value, "gz", 0, 0, tiled=True)


def product(left, right, transposed):
    dims = (((1,), (1,)), ((), ())) if transposed else (((1,), (0,)), ((), ()))
    return lax.dot_general(left, right, dims, preferred_element_type=f32)


def columns_of(weight_ref, start, transposed):
    if transposed:
        return weight_ref[pl.ds(start, tile), :]
    return weight_ref[:, pl.ds(start, tile)]


def call(kernel, name, outs, args, scratch=(), flops=0, moved=0, scalars=0, aliases=None):
    vmem = pl.BlockSpec(memory_space=pltpu.VMEM)
    return pl.pallas_call(
        kernel,
        out_shape=[jax.ShapeDtypeStruct(*out) for out in outs],
        in_specs=[pl.BlockSpec(memory_space=pltpu.SMEM)] * scalars + [vmem] * (len(args) - scalars),
        out_specs=[vmem] * len(outs),
        scratch_shapes=[pltpu.VMEM(*shape) for shape in scratch],
        input_output_aliases=aliases or {},
        compiler_params=pltpu.CompilerParams(vmem_limit_bytes=8 * 2**20),
        cost_estimate=pl.CostEstimate(flops=flops, bytes_accessed=moved, transcendentals=0),
        name=name,
    )(*args)


def stack_kernel(*refs):
    rows = refs[0].shape[0]
    for i, piece in enumerate(refs[:4]):
        refs[4][rows * i : rows * (i + 1), :] = piece[...]


def stack(pieces, name):
    rows, width = pieces[0].shape
    return call(stack_kernel, name, [((4 * rows, width), bf16)], pieces, moved=2**20)[0]


def width_kernel(part, transposed, index_ref, near_ref, far_ref, weight_ref, *refs):
    whole_ref, own_ref, send_ref, acc = refs[-4:]
    me = index_ref[0]
    rows = slice(64 * part, 64 * part + 64)
    whole_ref[:256, :] = near_ref[...]
    whole_ref[256:, :] = far_ref[...]

    @pl.loop(0, own_ref.shape[1] // tile)
    def _(j):
        start = pl.multiple_of(j * tile, tile)
        cols = pl.ds(start, tile)
        acc[...] = product(whole_ref[...], columns_of(weight_ref, start, transposed), transposed)
        own_ref[:, cols] = acc[pl.ds(pl.multiple_of(me * 64, 64), 64), :]
        for peer in range(8):
            send_ref[peer, rows, cols] = acc[64 * peer : 64 * peer + 64, :].astype(bf16)


def width_product(part, index, near, far, weight, sends):
    width = near.shape[1]
    units = weight.shape[0] if part else weight.shape[1]
    return call(
        functools.partial(width_kernel, part, bool(part)),
        "width_grad" if part else "width_inputs",
        [((512, width), bf16), ((64, units), f32), ((8, 128, units), bf16)],
        [index, near, far, weight] + sends,
        scratch=[((512, tile), f32)],
        flops=2 * 512 * width * units,
        moved=6 * 2**20,
        scalars=1,
        aliases={4: 2} if sends else None,
    )


def activation_kernel(index_ref, parts_ref, preact_ref, grad_ref, out_ref):
    me = index_ref[0]

    @pl.loop(0, 4)
    def _(j):
        sums = []
        for part, own_ref in ((0, preact_ref), (1, grad_ref)):
            total = own_ref[pl.ds(pl.multiple_of(j * 16, 16), 16), :]
            rows = pl.ds(pl.multiple_of(64 * part + j * 16, 16), 16)
            for peer in range(8):
                total = total + jnp.where(peer == me, 0.0, parts_ref[peer, rows, :].astype(f32))
            sums.append(total)
        result, slope = gelu_parts(sums[0])
        for part, value in ((0, result), (1, sums[1] * slope)):
            rows = pl.ds(pl.multiple_of(64 * part + j * 16, 16), 16)
            rounded = value.astype(bf16)
            for peer in range(8):
                out_ref[peer, rows, :] = rounded


def far_kernel(part, transposed, parts_ref, weight_ref, whole_ref, far_ref):
    for share in range(8):
        whole_ref[64 * share : 64 * share + 64, :] = parts_ref[share, 64 * part : 64 * part + 64, :]

    @pl.loop(0, far_ref.shape[1] // tile)
    def _(j):
        start = pl.multiple_of(j * tile, tile)
        far_ref[:, pl.ds(start, tile)] = product(
            whole_ref[256:, :], columns_of(weight_ref, start, transposed), transposed
        )


def near_kernel(transposed, whole_ref, weight_ref, far_ref, mine_ref, *refs):
    sends, acc = refs[:3], refs[3]

    @pl.loop(0, mine_ref.shape[1] // tile)
    def _(j):
        start = pl.multiple_of(j * tile, tile)
        cols = pl.ds(start, tile)
        acc[...] = far_ref[:, cols] + product(
            whole_ref[:256, :], columns_of(weight_ref, start, transposed), transposed
        )
        mine_ref[:, cols] = acc[:64, :]
        for step in (1, 2, 3):
            sends[step - 1][:, cols] = acc[64 * step : 64 * step + 64, :].astype(bf16)


def column_kernel(own_ref, first_ref, second_ref, third_ref, mine_ref, *sends):
    for step in range(4):
        rows = slice(16 * step, 16 * step + 16)
        total = own_ref[rows, :]
        for part in (first_ref, second_ref, third_ref):
            total = total + part[rows, :].astype(f32)
        if step == 0:
            mine_ref[...] = total
        else:
            sends[step - 1][...] = total.astype(bf16)


def last_kernel(own_ref, first_ref, second_ref, third_ref, out_ref):
    total = own_ref[...]
    for part in (first_ref, second_ref, third_ref):
        total = total + part[...].astype(f32)
    out_ref[...] = total.astype(bf16)


def units_far(part, gathered, weight):
    units = gathered.shape[2]
    width = weight.shape[0] if part else weight.shape[1]
    whole, far = call(
        functools.partial(far_kernel, part, bool(part)),
        "far_grad" if part else "far_hidden",
        [((512, units), bf16), ((256, width), f32)],
        [gathered, weight],
        flops=2 * 256 * width * units,
        moved=6 * 2**20,
    )
    return whole, other_core(far)


def units_near(part, whole, weight, far):
    units, width = whole.shape[1], far.shape[1]
    mine, *sends = call(
        functools.partial(near_kernel, bool(part)),
        "near_grad" if part else "near_hidden",
        [((64, width), f32)] + [((64, width), bf16)] * 3,
        [whole, weight, far],
        scratch=[((256, tile), f32)],
        flops=2 * 256 * width * units,
        moved=6 * 2**20,
    )
    return mine, [to_y(send, step) for step, send in zip((1, 2, 3), sends)]


def column_sum(mine, parts):
    width = mine.shape[1]
    mine, *sends = call(
        column_kernel,
        "column_sum",
        [((16, width), f32)] + [((16, width), bf16)] * 3,
        [mine] + parts,
        moved=2**20,
    )
    return mine, [to_gx(send, step) for step, send in zip((1, 2, 3), sends)]


def last_sum(mine, parts):
    return call(last_kernel, "last_sum", [(mine.shape, bf16)], [mine] + parts, moved=2**18)[0]


def on_device(inputs, w_in, w_out, grad_out):
    width, units = w_in.shape
    index = jnp.reshape(lax.axis_index("gz"), (1,)).astype(jnp.int32)
    steps = (1, 2, 3)
    columns = [[shard] + [from_gx(shard, step) for step in steps] for shard in (inputs, grad_out)]
    columns = [stack(column, "column") for column in columns]
    planes = [[column] + [from_y(column, step) for step in steps] for column in columns]
    near = stack(planes[0], "plane")
    all_inputs, preact, sends = width_product(0, index, near, other_core(near), w_in, [])
    plane, sends = lax.optimization_barrier((planes[1], sends))
    near = stack(plane, "plane")
    all_grads, grad_hidden, sends = width_product(
        1, index, near, other_core(near), w_out, [sends]
    )
    (shares,) = call(
        activation_kernel,
        "activation",
        [((8, 128, units), bf16)],
        [index, over_gz(sends), preact, grad_hidden],
        moved=4 * 2**20,
        scalars=1,
    )
    gathered = over_gz(shares)
    hidden_all, far_hidden = units_far(0, gathered, w_out)
    grad_pre_all, far_grad = units_far(1, gathered, w_in)
    mine_hidden, parts_hidden = units_near(0, hidden_all, w_out, far_hidden)
    mine_grad, parts_grad = units_near(1, grad_pre_all, w_in, far_grad)
    mine_hidden, parts_hidden = column_sum(mine_hidden, parts_hidden)
    mine_grad, parts_grad = column_sum(mine_grad, parts_grad)
    output = last_sum(mine_hidden, parts_hidden)
    grad_inputs = last_sum(mine_grad, parts_grad)
    grad_w_out = lax.dot_general(
        hidden_all, all_grads, (((0,), (0,)), ((), ())), preferred_element_type=f32
    ).astype(bf16)
    grad_w_in = lax.dot_general(
        all_inputs, grad_pre_all, (((0,), (0,)), ((), ())), preferred_element_type=f32
    ).astype(bf16)
    return (output, grad_inputs, grad_w_in, grad_w_out)


def solution(mesh):
    in_specs = (
        P(("gx", "gy"), "gz"),
        P("gz", ("gx", "gy")),
        P(("gx", "gy"), "gz"),
        P(("gx", "gy"), "gz"),
    )
    out_specs = (
        P(("gx", "gy"), "gz"),
        P(("gx", "gy"), "gz"),
        P("gz", ("gx", "gy")),
        P(("gx", "gy"), "gz"),
    )
    return jax.shard_map(
        on_device, mesh=mesh, in_specs=in_specs, out_specs=out_specs, check_vma=False
    )
```

time: 451 us -> 155 us (0.34)
  waiting for transfers between devices: 339 us -> 23.9 us
  starting transfers between devices: 0.24 us -> 57.1 us
  matrix products: 25.2 us -> 5.65 us
  Pallas kernels: 0 us -> 15.3 us
  between operations: 14.1 us -> 0.79 us
  blocking collectives: 61.6 us -> 50.4 us
    reduce_scatter x4 -> x0, waiting for transfers between devices: 232 us -> none  [the longest x2 140 us: token_share(): lax.psum_scatter(term(jnp.int32(0), lax.axis_size(('gx', 'gy')) * (total_...]
    all_gather x2 -> x0, waiting for transfers between devices: 106 us -> none  [the longest x1 56.9 us: on_device(): lax.all_gather(grad_out, ('gx', 'gy'), axis=0, tiled=True)]
    all_gather x2 -> x0, blocking collectives: 61.6 us -> none  [units_whole(): return lax.all_gather(share, 'gz', axis=0, tiled=True)]
    ppermute x0 -> x28, starting transfers between devices: none -> 57.1 us  [the longest x6 17.9 us: from_gx(): return lax.ppermute(value, 'gx', [((i + step) % 4, i) for i in range(4)])]
    all_to_all x0 -> x2, blocking collectives: none -> 50.4 us  [over_gz(): return lax.all_to_all(value, 'gz', 0, 0, tiled=True)]
    ppermute x0 -> x28, waiting for transfers between devices: none -> 23.9 us  [the longest x6 9.77 us: from_y(): lax.ppermute(value, 'gy', [((i + 2 * step) % 8, i) for i in range(8)])]
    dot_general x4 -> x0, matrix products: 16.5 us -> none  [the longest x2 8.78 us: term(): lax.dot_general(left, right, (((1,), (1,)), ((), ())), preferred_element_...]
    pallas_call x0 -> x15, Pallas kernels: none -> 15.3 us  [call(): pl.pallas_call(kernel, out_shape=[jax.ShapeDtypeStruct(*out) for out in o...]
  transfers between devices with their start and end apart: 6 -> 28, of which waited for: 6 -> 12; matrix products, arithmetic and copies ran while one was open for 6% -> 4% of each run, Pallas kernels for 0% -> 6%
where the time goes in v2:
time: 155 us
  starting transfers between devices  57.1 us (37%)
  blocking collectives  50.4 us (33%)
  waiting for transfers between devices  23.9 us (15%)
  Pallas kernels  15.3 us (10%)
  matrix products  5.65 us (4%)
  local copies, waits for them, and re-layouts  1.61 us (1%)
    all_to_all x2, blocking collectives, over_gz(): return lax.all_to_all(value, 'gz', 0, 0, tiled=True)  50.4 us
    ppermute x6, starting transfers between devices, from_gx(): return lax.ppermute(value, 'gx', [((i + step) % 4, i) for i in range(4)])  17.9 us
    pallas_call x15, Pallas kernels, call(): pl.pallas_call(kernel, out_shape=[jax.ShapeDtypeStruct(*out) for out in o...  15.3 us
    ppermute x6, starting transfers between devices, to_gx(): return lax.ppermute(value, 'gx', [(i, (i + step) % 4) for i in range(4)])  14.4 us
    ppermute x6, starting transfers between devices, to_y(): lax.ppermute(value, 'gy', [(i, (i + 2 * step) % 8) for i in range(8)])  13.7 us
    ppermute x6, starting transfers between devices, from_y(): lax.ppermute(value, 'gy', [((i + 2 * step) % 8, i) for i in range(8)])  10 us
    ppermute x6, waiting for transfers between devices, from_y(): lax.ppermute(value, 'gy', [((i + 2 * step) % 8, i) for i in range(8)])  9.77 us
    ppermute x6, waiting for transfers between devices, from_gx(): return lax.ppermute(value, 'gx', [((i + step) % 4, i) for i in range(4)])  9.39 us
  transfers between devices with their start and end apart: 28, of which 12 were waited for; matrix products, arithmetic and copies ran while one was open for 4% of the time, Pallas kernels for 6%

profile of v2, /device:TPU:8, one launch (start us, length us, event | category | flops | bytes accessed | tf_op | source)
XLA Modules:
  0.0 154.7 jit_solution(5498726365534201066)
XLA Ops:
  0.6 6.4 %collective-permute-start.6 = (bf16[16,1536]{1,0:T(8,128)(2,1)}, bf16[16,1536]{1,0:T(8,128)(2,1)S(1)}, u32[]{:S(2)}, u32[]{:S(2)}) collective-permute-start(bf16[16,1536]{1,0:T(8,128)(2,1)} %refs_0_.3), channel_id=1, source_target_pairs={{64,0},{128,64},{192,128},{0,192},{65,1},{129,65},{193,129},{1,193... | collective-permute-start | bytes 147464 | tf_op jit(solution)/shard_map/ppermute | solution.py:28
  8.0 2.8 %collective-permute-start.8 = (bf16[16,1536]{1,0:T(8,128)(2,1)}, bf16[16,1536]{1,0:T(8,128)(2,1)S(1)}, u32[]{:S(2)}, u32[]{:S(2)}) collective-permute-start(bf16[16,1536]{1,0:T(8,128)(2,1)} %refs_0_.3), channel_id=1, source_target_pairs={{192,0},{0,64},{64,128},{128,192},{193,1},{1,65},{65,129},{129,193... | collective-permute-start | bytes 147464 | tf_op jit(solution)/shard_map/ppermute | solution.py:28
  10.8 4.7 %collective-permute-done.7.refs_2_ = bf16[16,1536]{1,0:T(8,128)(2,1)S(1)} collective-permute-done((bf16[16,1536]{1,0:T(8,128)(2,1)}, bf16[16,1536]{1,0:T(8,128)(2,1)S(1)}, u32[]{:S(2)}, u32[]{:S(2)}) %collective-permute-start.7) | collective-permute-done | bytes 49184 | tf_op jit(solution)/shard_map/ppermute | solution.py:28
  16.8 2.7 %collective-permute-start.10 = (bf16[64,1536]{1,0:T(8,128)(2,1)S(1)}, bf16[64,1536]{1,0:T(8,128)(2,1)S(1)}, u32[]{:S(2)}, u32[]{:S(2)}) collective-permute-start(bf16[64,1536]{1,0:T(8,128)(2,1)S(1)} %column.3.refs_0_), channel_id=1, source_target_pairs={{32,0},{40,8},{48,16},{56,24},{0,32},{8,40},{16,48},{24,56},{33,1}... | collective-permute-start | bytes 589832 | tf_op jit(solution)/shard_map/ppermute | solution.py:40
  19.5 1.9 %collective-permute-start.11 = (bf16[64,1536]{1,0:T(8,128)(2,1)S(1)}, bf16[64,1536]{1,0:T(8,128)(2,1)S(1)}, u32[]{:S(2)}, u32[]{:S(2)}) collective-permute-start(bf16[64,1536]{1,0:T(8,128)(2,1)S(1)} %column.3.refs_0_), channel_id=1, source_target_pairs={{48,0},{56,8},{0,16},{8,24},{16,32},{24,40},{32,48},{40,56},{49,1}... | collective-permute-start | bytes 589832 | tf_op jit(solution)/shard_map/ppermute | solution.py:40
  21.4 2.8 %collective-permute-done.9.refs_1_ = bf16[64,1536]{1,0:T(8,128)(2,1)S(1)} collective-permute-done((bf16[64,1536]{1,0:T(8,128)(2,1)S(1)}, bf16[64,1536]{1,0:T(8,128)(2,1)S(1)}, u32[]{:S(2)}, u32[]{:S(2)}) %collective-permute-start.9) | collective-permute-done | bytes 196640 | tf_op jit(solution)/shard_map/ppermute | solution.py:40
  24.2 2.6 %collective-permute-done.10.refs_2_ = bf16[64,1536]{1,0:T(8,128)(2,1)S(1)} collective-permute-done((bf16[64,1536]{1,0:T(8,128)(2,1)S(1)}, bf16[64,1536]{1,0:T(8,128)(2,1)S(1)}, u32[]{:S(2)}, u32[]{:S(2)}) %collective-permute-start.10) | collective-permute-done | bytes 196640 | tf_op jit(solution)/shard_map/ppermute | solution.py:40
  27.7 2.0 %collective-permute-start = (bf16[16,1536]{1,0:T(8,128)(2,1)}, bf16[16,1536]{1,0:T(8,128)(2,1)S(1)}, u32[]{:S(2)}, u32[]{:S(2)}) collective-permute-start(bf16[16,1536]{1,0:T(8,128)(2,1)} %refs_0_.2), channel_id=1, source_target_pairs={{64,0},{128,64},{192,128},{0,192},{65,1},{129,65},{193,129},{1,193... | collective-permute-start | bytes 147464 | tf_op jit(solution)/shard_map/ppermute | solution.py:28
  29.7 2.9 %collective-permute-start.1 = (bf16[16,1536]{1,0:T(8,128)(2,1)}, bf16[16,1536]{1,0:T(8,128)(2,1)S(1)}, u32[]{:S(2)}, u32[]{:S(2)}) collective-permute-start(bf16[16,1536]{1,0:T(8,128)(2,1)} %refs_0_.2), channel_id=1, source_target_pairs={{128,0},{192,64},{0,128},{64,192},{129,1},{193,65},{1,129},{65,193... | collective-permute-start | bytes 147464 | tf_op jit(solution)/shard_map/ppermute | solution.py:28
  32.6 2.8 %collective-permute-start.2 = (bf16[16,1536]{1,0:T(8,128)(2,1)}, bf16[16,1536]{1,0:T(8,128)(2,1)S(1)}, u32[]{:S(2)}, u32[]{:S(2)}) collective-permute-start(bf16[16,1536]{1,0:T(8,128)(2,1)} %refs_0_.2), channel_id=1, source_target_pairs={{192,0},{0,64},{64,128},{128,192},{193,1},{1,65},{65,129},{129,193... | collective-permute-start | bytes 147464 | tf_op jit(solution)/shard_map/ppermute | solution.py:28
  35.4 3.0 %collective-permute-done.1.refs_2_ = bf16[16,1536]{1,0:T(8,128)(2,1)S(1)} collective-permute-done((bf16[16,1536]{1,0:T(8,128)(2,1)}, bf16[16,1536]{1,0:T(8,128)(2,1)S(1)}, u32[]{:S(2)}, u32[]{:S(2)}) %collective-permute-start.1) | collective-permute-done | bytes 49184 | tf_op jit(solution)/shard_map/ppermute | solution.py:28
  38.5 1.6 %collective-permute-done.2.refs_3_ = bf16[16,1536]{1,0:T(8,128)(2,1)S(1)} collective-permute-done((bf16[16,1536]{1,0:T(8,128)(2,1)}, bf16[16,1536]{1,0:T(8,128)(2,1)S(1)}, u32[]{:S(2)}, u32[]{:S(2)}) %collective-permute-start.2) | collective-permute-done | bytes 49184 | tf_op jit(solution)/shard_map/ppermute | solution.py:28
  40.9 3.0 %collective-permute-start.3 = (bf16[64,1536]{1,0:T(8,128)(2,1)S(1)}, bf16[64,1536]{1,0:T(8,128)(2,1)S(1)}, u32[]{:S(2)}, u32[]{:S(2)}) collective-permute-start(bf16[64,1536]{1,0:T(8,128)(2,1)S(1)} %column.2.refs_0_), channel_id=1, source_target_pairs={{16,0},{24,8},{32,16},{40,24},{48,32},{56,40},{0,48},{8,56},{17,1}... | collective-permute-start | bytes 589832 | tf_op jit(solution)/shard_map/ppermute | solution.py:40
  43.9 2.1 %collective-permute-start.5 = (bf16[64,1536]{1,0:T(8,128)(2,1)S(1)}, bf16[64,1536]{1,0:T(8,128)(2,1)}, u32[]{:S(2)}, u32[]{:S(2)}) collective-permute-start(bf16[64,1536]{1,0:T(8,128)(2,1)S(1)} %column.2.refs_0_), channel_id=1, source_target_pairs={{48,0},{56,8},{0,16},{8,24},{16,32},{24,40},{32,48},{40,56},{49,1}... | collective-permute-start | bytes 589832 | tf_op jit(solution)/shard_map/ppermute | solution.py:40
  46.0 3.1 %width_inputs.1 = (bf16[512,1536]{1,0:T(8,128)(2,1)S(1)}, f32[64,768]{1,0:T(8,128)S(1)}, bf16[8,128,768]{2,1,0:T(8,128)(2,1)S(1)}) custom-call(s32[1]{0:T(128)} %bitcast.index_ref, bf16[256,1536]{1,0:T(8,128)(2,1)S(1)} %plane.2.near_ref, bf16[256,1536]{1,0:T(8,128)(2,1)} %collective-permute-done.12.far_ref, bf16[1536,768]{1,0:T(8,128)(2,1)S(1)} %copy-done.1), custom_call_target="tpu_custom_call" | custom-call | flops 1207959552 | bytes 6291456 | tf_op jit(solution)/shard_map/width_inputs/pallas_call | solution.py:64
  49.1 2.7 %collective-permute-done.4.refs_2_ = bf16[64,1536]{1,0:T(8,128)(2,1)} collective-permute-done((bf16[64,1536]{1,0:T(8,128)(2,1)S(1)}, bf16[64,1536]{1,0:T(8,128)(2,1)}, u32[]{:S(2)}, u32[]{:S(2)}) %collective-permute-start.4) | collective-permute-done | bytes 196640 | tf_op jit(solution)/shard_map/ppermute | solution.py:40
  53.9 2.3 %collective-permute-done.13.far_ref = bf16[256,1536]{1,0:T(8,128)(2,1)S(1)} collective-permute-done((bf16[256,1536]{1,0:T(8,128)(2,1)S(1)}, bf16[256,1536]{1,0:T(8,128)(2,1)S(1)}, u32[]{:S(2)}, u32[]{:S(2)}) %collective-permute-start.13) | collective-permute-done | bytes 786464 | tf_op jit(solution)/shard_map/ppermute | solution.py:36
  56.2 1.9 %width_grad.1 = (bf16[512,1536]{1,0:T(8,128)(2,1)S(1)}, f32[64,768]{1,0:T(8,128)S(1)}, bf16[8,128,768]{2,1,0:T(8,128)(2,1)S(1)}) custom-call(s32[1]{0:T(128)} %bitcast.index_ref, bf16[256,1536]{1,0:T(8,128)(2,1)S(1)} %plane.3.near_ref, bf16[256,1536]{1,0:T(8,128)(2,1)S(1)} %collective-permute-done.13.far_ref, ...), custom_call_target="tpu_custom_call", output_to_operand_aliasing={{2}: (4, {})} | custom-call | flops 1207959552 | bytes 6291456 | tf_op jit(solution)/shard_map/width_grad/pallas_call | solution.py:64
  58.1 27.1 %all_to_all.10.parts_ref = bf16[8,128,768]{2,1,0:T(8,128)(2,1)S(1)} all-to-all(bf16[8,128,768]{2,1,0:T(8,128)(2,1)S(1)} %get-tuple-element.41), channel_id=1, replica_groups=mesh['gx'=4,'gy'=8,'gz'=8] {'gz'}, dimensions={0} | all-to-all | bytes 3145728 | tf_op jit(solution)/shard_map/all_to_all | solution.py:48
  85.7 23.3 %all_to_all.11.parts_ref = bf16[8,128,768]{2,1,0:T(8,128)(2,1)S(1)} all-to-all(bf16[8,128,768]{2,1,0:T(8,128)(2,1)S(1)} %activation.1), channel_id=1, replica_groups=mesh['gx'=4,'gy'=8,'gz'=8] {'gz'}, dimensions={0} | all-to-all | bytes 3145728 | tf_op jit(solution)/shard_map/all_to_all | solution.py:48
  109.1 1.7 %far_hidden.1 = (bf16[512,768]{1,0:T(8,128)(2,1)S(1)}, f32[256,1536]{1,0:T(8,128)S(1)}) custom-call(bf16[8,128,768]{2,1,0:T(8,128)(2,1)S(1)} %all_to_all.11.parts_ref, bf16[768,1536]{1,0:T(8,128)(2,1)S(1)} %copy-done), custom_call_target="tpu_custom_call" | custom-call | flops 603979776 | bytes 6291456 | tf_op jit(solution)/shard_map/far_hidden/pallas_call | solution.py:64
  110.9 1.9 %far_grad.1 = (bf16[512,768]{1,0:T(8,128)(2,1)S(1)}, f32[256,1536]{1,0:T(8,128)S(1)}) custom-call(bf16[8,128,768]{2,1,0:T(8,128)(2,1)S(1)} %all_to_all.11.parts_ref, bf16[1536,768]{1,0:T(8,128)(2,1)S(1)} %copy-done.1), custom_call_target="tpu_custom_call" | custom-call | flops 603979776 | bytes 6291456 | tf_op jit(solution)/shard_map/far_grad/pallas_call | solution.py:64
  117.5 3.3 %collective-permute-start.16 = (bf16[64,1536]{1,0:T(8,128)(2,1)S(1)}, bf16[64,1536]{1,0:T(8,128)(2,1)S(1)}, u32[]{:S(2)}, u32[]{:S(2)}) collective-permute-start(bf16[64,1536]{1,0:T(8,128)(2,1)S(1)} %get-tuple-element.48), channel_id=1, source_target_pairs={{0,32},{8,40},{16,48},{24,56},{32,0},{40,8},{48,16},{56,24},{1,33}... | collective-permute-start | bytes 589832 | tf_op jit(solution)/shard_map/ppermute | solution.py:44
  121.3 1.8 %near_grad.1 = (f32[64,1536]{1,0:T(8,128)S(1)}, bf16[64,1536]{1,0:T(8,128)(2,1)S(1)}, bf16[64,1536]{1,0:T(8,128)(2,1)S(1)}, bf16[64,1536]{1,0:T(8,128)(2,1)S(1)}) custom-call(bf16[512,768]{1,0:T(8,128)(2,1)S(1)} %get-tuple-element.54.whole_ref, bf16[1536,768]{1,0:T(8,128)(2,1)S(1)} %copy-done.1, f32[256,1536]{1,0:T(8,128)S(1)} %collective-permute-done.21.far_ref), custom_call_target="tpu_custom_call" | custom-call | flops 603979776 | bytes 6291456 | tf_op jit(solution)/shard_map/near_grad/pallas_call | solution.py:64
  126.2 5.3 %collective-permute-start.24 = (bf16[64,1536]{1,0:T(8,128)(2,1)S(1)}, bf16[64,1536]{1,0:T(8,128)(2,1)S(1)}, u32[]{:S(2)}, u32[]{:S(2)}) collective-permute-start(bf16[64,1536]{1,0:T(8,128)(2,1)S(1)} %get-tuple-element.59), channel_id=1, source_target_pairs={{0,48},{8,56},{16,0},{24,8},{32,16},{40,24},{48,32},{56,40},{1,49}... | collective-permute-start | bytes 589832 | tf_op jit(solution)/shard_map/ppermute | solution.py:44
  131.6 1.7 %collective-permute-start.18 = (bf16[16,1536]{1,0:T(8,128)(2,1)S(1)}, bf16[16,1536]{1,0:T(8,128)(2,1)S(1)}, u32[]{:S(2)}, u32[]{:S(2)}) collective-permute-start(bf16[16,1536]{1,0:T(8,128)(2,1)S(1)} %get-tuple-element.51), channel_id=1, source_target_pairs={{0,64},{64,128},{128,192},{192,0},{1,65},{65,129},{129,193},{193,1... | collective-permute-start | bytes 147464 | tf_op jit(solution)/shard_map/ppermute | solution.py:32
  133.3 2.8 %convolution_convert_fusion.1 = bf16[1536,768]{1,0:T(8,128)(2,1)} fusion(bf16[512,1536]{1,0:T(8,128)(2,1)S(1)} %get-tuple-element.64, bf16[512,768]{1,0:T(8,128)(2,1)S(1)} %get-tuple-element.54.whole_ref), kind=kOutput, calls=%fused_computation.1 | convolution fusion | flops 1209139200 | bytes 4718592 | tf_op jit(solution)/shard_map/dot_general | solution.py:265
  136.1 3.5 %collective-permute-start.19 = (bf16[16,1536]{1,0:T(8,128)(2,1)S(1)}, bf16[16,1536]{1,0:T(8,128)(2,1)S(1)}, u32[]{:S(2)}, u32[]{:S(2)}) collective-permute-start(bf16[16,1536]{1,0:T(8,128)(2,1)S(1)} %get-tuple-element.52), channel_id=1, source_target_pairs={{0,128},{64,192},{128,0},{192,64},{1,129},{65,193},{129,1},{193,65... | collective-permute-start | bytes 147464 | tf_op jit(solution)/shard_map/ppermute | solution.py:32
  139.6 4.1 %collective-permute-start.20 = (bf16[16,1536]{1,0:T(8,128)(2,1)S(1)}, bf16[16,1536]{1,0:T(8,128)(2,1)S(1)}, u32[]{:S(2)}, u32[]{:S(2)}) collective-permute-start(bf16[16,1536]{1,0:T(8,128)(2,1)S(1)} %get-tuple-element.53), channel_id=1, source_target_pairs={{0,192},{64,0},{128,64},{192,128},{1,193},{65,1},{129,65},{193,129... | collective-permute-start | bytes 147464 | tf_op jit(solution)/shard_map/ppermute | solution.py:32
  143.9 2.4 %collective-permute-start.26 = (bf16[16,1536]{1,0:T(8,128)(2,1)S(1)}, bf16[16,1536]{1,0:T(8,128)(2,1)S(1)}, u32[]{:S(2)}, u32[]{:S(2)}) collective-permute-start(bf16[16,1536]{1,0:T(8,128)(2,1)S(1)} %get-tuple-element.62), channel_id=1, source_target_pairs={{0,128},{64,192},{128,0},{192,64},{1,129},{65,193},{129,1},{193,65... | collective-permute-start | bytes 147464 | tf_op jit(solution)/shard_map/ppermute | solution.py:32
  146.3 2.6 %collective-permute-start.27 = (bf16[16,1536]{1,0:T(8,128)(2,1)S(1)}, bf16[16,1536]{1,0:T(8,128)(2,1)S(1)}, u32[]{:S(2)}, u32[]{:S(2)}) collective-permute-start(bf16[16,1536]{1,0:T(8,128)(2,1)S(1)} %get-tuple-element.63), channel_id=1, source_target_pairs={{0,192},{64,0},{128,64},{192,128},{1,193},{65,1},{129,65},{193,129... | collective-permute-start | bytes 147464 | tf_op jit(solution)/shard_map/ppermute | solution.py:32
  148.9 2.8 %convolution_convert_fusion = bf16[768,1536]{1,0:T(8,128)(2,1)} fusion(bf16[512,768]{1,0:T(8,128)(2,1)S(1)} %get-tuple-element.44.whole_ref, bf16[512,1536]{1,0:T(8,128)(2,1)S(1)} %get-tuple-element.65), kind=kOutput, calls=%fused_computation | convolution fusion | flops 1209139200 | bytes 4718592 | tf_op jit(solution)/shard_map/dot_general | solution.py:262
  (51 shorter events, 18.2 us)
Async XLA Ops:
  0.6 45.3 %copy-start.1 = (bf16[1536,768]{1,0:T(8,128)(2,1)S(1)}, bf16[1536,768]{1,0:T(8,128)(2,1)}, u32[]{:S(2)}) copy-start(bf16[1536,768]{1,0:T(8,128)(2,1)} %weight_ref.11) | copy-start | bytes 7077892
  0.6 10.2 %collective-permute-start.6 = (bf16[16,1536]{1,0:T(8,128)(2,1)}, bf16[16,1536]{1,0:T(8,128)(2,1)S(1)}, u32[]{:S(2)}, u32[]{:S(2)}) collective-permute-start(bf16[16,1536]{1,0:T(8,128)(2,1)} %refs_0_.3), channel_id=1, source_target_pairs={{64,0},{128,64},{192,128},{0,192},{65,1},{129,65},{193,129},{1,193... | collective-permute-start | bytes 147464 | tf_op jit(solution)/shard_map/ppermute | solution.py:28
  7.0 8.5 %collective-permute-start.7 = (bf16[16,1536]{1,0:T(8,128)(2,1)}, bf16[16,1536]{1,0:T(8,128)(2,1)S(1)}, u32[]{:S(2)}, u32[]{:S(2)}) collective-permute-start(bf16[16,1536]{1,0:T(8,128)(2,1)} %refs_0_.3), channel_id=1, source_target_pairs={{128,0},{192,64},{0,128},{64,192},{129,1},{193,65},{1,129},{65,193... | collective-permute-start | bytes 147464 | tf_op jit(solution)/shard_map/ppermute | solution.py:28
  8.0 7.5 %collective-permute-start.8 = (bf16[16,1536]{1,0:T(8,128)(2,1)}, bf16[16,1536]{1,0:T(8,128)(2,1)S(1)}, u32[]{:S(2)}, u32[]{:S(2)}) collective-permute-start(bf16[16,1536]{1,0:T(8,128)(2,1)} %refs_0_.3), channel_id=1, source_target_pairs={{192,0},{0,64},{64,128},{128,192},{193,1},{1,65},{65,129},{129,193... | collective-permute-start | bytes 147464 | tf_op jit(solution)/shard_map/ppermute | solution.py:28
  15.5 0.8 copy-start.2
  16.4 7.9 %collective-permute-start.9 = (bf16[64,1536]{1,0:T(8,128)(2,1)S(1)}, bf16[64,1536]{1,0:T(8,128)(2,1)S(1)}, u32[]{:S(2)}, u32[]{:S(2)}) collective-permute-start(bf16[64,1536]{1,0:T(8,128)(2,1)S(1)} %column.3.refs_0_), channel_id=1, source_target_pairs={{16,0},{24,8},{32,16},{40,24},{48,32},{56,40},{0,48},{8,56},{17,1}... | collective-permute-start | bytes 589832 | tf_op jit(solution)/shard_map/ppermute | solution.py:40
  16.8 10.0 %collective-permute-start.10 = (bf16[64,1536]{1,0:T(8,128)(2,1)S(1)}, bf16[64,1536]{1,0:T(8,128)(2,1)S(1)}, u32[]{:S(2)}, u32[]{:S(2)}) collective-permute-start(bf16[64,1536]{1,0:T(8,128)(2,1)S(1)} %column.3.refs_0_), channel_id=1, source_target_pairs={{32,0},{40,8},{48,16},{56,24},{0,32},{8,40},{16,48},{24,56},{33,1}... | collective-permute-start | bytes 589832 | tf_op jit(solution)/shard_map/ppermute | solution.py:40
  19.5 8.1 %collective-permute-start.11 = (bf16[64,1536]{1,0:T(8,128)(2,1)S(1)}, bf16[64,1536]{1,0:T(8,128)(2,1)S(1)}, u32[]{:S(2)}, u32[]{:S(2)}) collective-permute-start(bf16[64,1536]{1,0:T(8,128)(2,1)S(1)} %column.3.refs_0_), channel_id=1, source_target_pairs={{48,0},{56,8},{0,16},{8,24},{16,32},{24,40},{32,48},{40,56},{49,1}... | collective-permute-start | bytes 589832 | tf_op jit(solution)/shard_map/ppermute | solution.py:40
  27.6 18.4 %collective-permute-start.12 = (bf16[256,1536]{1,0:T(8,128)(2,1)S(1)}, bf16[256,1536]{1,0:T(8,128)(2,1)}, u32[]{:S(2)}, u32[]{:S(2)}) collective-permute-start(bf16[256,1536]{1,0:T(8,128)(2,1)S(1)} %plane.2.near_ref), channel_id=1, source_target_pairs={{0,8},{8,0},{16,24},{24,16},{32,40},{40,32},{48,56},{56,48},{1,9},... | collective-permute-start | bytes 2359304 | tf_op jit(solution)/shard_map/ppermute | solution.py:36
  27.7 7.7 %collective-permute-start = (bf16[16,1536]{1,0:T(8,128)(2,1)}, bf16[16,1536]{1,0:T(8,128)(2,1)S(1)}, u32[]{:S(2)}, u32[]{:S(2)}) collective-permute-start(bf16[16,1536]{1,0:T(8,128)(2,1)} %refs_0_.2), channel_id=1, source_target_pairs={{64,0},{128,64},{192,128},{0,192},{65,1},{129,65},{193,129},{1,193... | collective-permute-start | bytes 147464 | tf_op jit(solution)/shard_map/ppermute | solution.py:28
  29.7 8.7 %collective-permute-start.1 = (bf16[16,1536]{1,0:T(8,128)(2,1)}, bf16[16,1536]{1,0:T(8,128)(2,1)S(1)}, u32[]{:S(2)}, u32[]{:S(2)}) collective-permute-start(bf16[16,1536]{1,0:T(8,128)(2,1)} %refs_0_.2), channel_id=1, source_target_pairs={{128,0},{192,64},{0,128},{64,192},{129,1},{193,65},{1,129},{65,193... | collective-permute-start | bytes 147464 | tf_op jit(solution)/shard_map/ppermute | solution.py:28
  32.6 7.5 %collective-permute-start.2 = (bf16[16,1536]{1,0:T(8,128)(2,1)}, bf16[16,1536]{1,0:T(8,128)(2,1)S(1)}, u32[]{:S(2)}, u32[]{:S(2)}) collective-permute-start(bf16[16,1536]{1,0:T(8,128)(2,1)} %refs_0_.2), channel_id=1, source_target_pairs={{192,0},{0,64},{64,128},{128,192},{193,1},{1,65},{65,129},{129,193... | collective-permute-start | bytes 147464 | tf_op jit(solution)/shard_map/ppermute | solution.py:28
  40.1 0.8 copy-start.3
  40.9 8.2 %collective-permute-start.3 = (bf16[64,1536]{1,0:T(8,128)(2,1)S(1)}, bf16[64,1536]{1,0:T(8,128)(2,1)S(1)}, u32[]{:S(2)}, u32[]{:S(2)}) collective-permute-start(bf16[64,1536]{1,0:T(8,128)(2,1)S(1)} %column.2.refs_0_), channel_id=1, source_target_pairs={{16,0},{24,8},{32,16},{40,24},{48,32},{56,40},{0,48},{8,56},{17,1}... | collective-permute-start | bytes 589832 | tf_op jit(solution)/shard_map/ppermute | solution.py:40
  43.9 8.0 %collective-permute-start.4 = (bf16[64,1536]{1,0:T(8,128)(2,1)S(1)}, bf16[64,1536]{1,0:T(8,128)(2,1)}, u32[]{:S(2)}, u32[]{:S(2)}) collective-permute-start(bf16[64,1536]{1,0:T(8,128)(2,1)S(1)} %column.2.refs_0_), channel_id=1, source_target_pairs={{32,0},{40,8},{48,16},{56,24},{0,32},{8,40},{16,48},{24,56},{33,1}... | collective-permute-start | bytes 589832 | tf_op jit(solution)/shard_map/ppermute | solution.py:40
  43.9 8.8 %collective-permute-start.5 = (bf16[64,1536]{1,0:T(8,128)(2,1)S(1)}, bf16[64,1536]{1,0:T(8,128)(2,1)}, u32[]{:S(2)}, u32[]{:S(2)}) collective-permute-start(bf16[64,1536]{1,0:T(8,128)(2,1)S(1)} %column.2.refs_0_), channel_id=1, source_target_pairs={{48,0},{56,8},{0,16},{8,24},{16,32},{24,40},{32,48},{40,56},{49,1}... | collective-permute-start | bytes 589832 | tf_op jit(solution)/shard_map/ppermute | solution.py:40
  46.0 10.2 %copy-start = (bf16[768,1536]{1,0:T(8,128)(2,1)S(1)}, bf16[768,1536]{1,0:T(8,128)(2,1)}, u32[]{:S(2)}) copy-start(bf16[768,1536]{1,0:T(8,128)(2,1)} %weight_ref.9) | copy-start | bytes 7077892
  53.8 2.4 %collective-permute-start.13 = (bf16[256,1536]{1,0:T(8,128)(2,1)S(1)}, bf16[256,1536]{1,0:T(8,128)(2,1)S(1)}, u32[]{:S(2)}, u32[]{:S(2)}) collective-permute-start(bf16[256,1536]{1,0:T(8,128)(2,1)S(1)} %plane.3.near_ref), channel_id=1, source_target_pairs={{0,8},{8,0},{16,24},{24,16},{32,40},{40,32},{48,56},{56,48},{1,9},... | collective-permute-start | bytes 2359304 | tf_op jit(solution)/shard_map/ppermute | solution.py:36
  110.8 3.5 %collective-permute-start.14 = (f32[256,1536]{1,0:T(8,128)S(1)}, f32[256,1536]{1,0:T(8,128)S(1)}, u32[]{:S(2)}, u32[]{:S(2)}) collective-permute-start(f32[256,1536]{1,0:T(8,128)S(1)} %get-tuple-element.45), channel_id=1, source_target_pairs={{0,8},{8,0},{16,24},{24,16},{32,40},{40,32},{48,56},{56,48},{1,9},... | collective-permute-start | bytes 4718600 | tf_op jit(solution)/shard_map/ppermute | solution.py:36
  112.7 8.5 %collective-permute-start.21 = (f32[256,1536]{1,0:T(8,128)S(1)}, f32[256,1536]{1,0:T(8,128)S(1)}, u32[]{:S(2)}, u32[]{:S(2)}) collective-permute-start(f32[256,1536]{1,0:T(8,128)S(1)} %get-tuple-element.55), channel_id=1, source_target_pairs={{0,8},{8,0},{16,24},{24,16},{32,40},{40,32},{48,56},{56,48},{1,9},... | collective-permute-start | bytes 4718600 | tf_op jit(solution)/shard_map/ppermute | solution.py:36
  115.9 10.3 %collective-permute-start.15 = (bf16[64,1536]{1,0:T(8,128)(2,1)S(1)}, bf16[64,1536]{1,0:T(8,128)(2,1)S(1)}, u32[]{:S(2)}, u32[]{:S(2)}) collective-permute-start(bf16[64,1536]{1,0:T(8,128)(2,1)S(1)} %get-tuple-element.47), channel_id=1, source_target_pairs={{0,16},{8,24},{16,32},{24,40},{32,48},{40,56},{48,0},{56,8},{1,17}... | collective-permute-start | bytes 589832 | tf_op jit(solution)/shard_map/ppermute | solution.py:44
  117.5 14.0 %collective-permute-start.16 = (bf16[64,1536]{1,0:T(8,128)(2,1)S(1)}, bf16[64,1536]{1,0:T(8,128)(2,1)S(1)}, u32[]{:S(2)}, u32[]{:S(2)}) collective-permute-start(bf16[64,1536]{1,0:T(8,128)(2,1)S(1)} %get-tuple-element.48), channel_id=1, source_target_pairs={{0,32},{8,40},{16,48},{24,56},{32,0},{40,8},{48,16},{56,24},{1,33}... | collective-permute-start | bytes 589832 | tf_op jit(solution)/shard_map/ppermute | solution.py:44
  120.7 10.8 %collective-permute-start.17 = (bf16[64,1536]{1,0:T(8,128)(2,1)S(1)}, bf16[64,1536]{1,0:T(8,128)(2,1)S(1)}, u32[]{:S(2)}, u32[]{:S(2)}) collective-permute-start(bf16[64,1536]{1,0:T(8,128)(2,1)S(1)} %get-tuple-element.49), channel_id=1, source_target_pairs={{0,48},{8,56},{16,0},{24,8},{32,16},{40,24},{48,32},{56,40},{1,49}... | collective-permute-start | bytes 589832 | tf_op jit(solution)/shard_map/ppermute | solution.py:44
  123.1 16.5 %collective-permute-start.22 = (bf16[64,1536]{1,0:T(8,128)(2,1)S(1)}, bf16[64,1536]{1,0:T(8,128)(2,1)S(1)}, u32[]{:S(2)}, u32[]{:S(2)}) collective-permute-start(bf16[64,1536]{1,0:T(8,128)(2,1)S(1)} %get-tuple-element.57), channel_id=1, source_target_pairs={{0,16},{8,24},{16,32},{24,40},{32,48},{40,56},{48,0},{56,8},{1,17}... | collective-permute-start | bytes 589832 | tf_op jit(solution)/shard_map/ppermute | solution.py:44
  124.7 19.0 %collective-permute-start.23 = (bf16[64,1536]{1,0:T(8,128)(2,1)S(1)}, bf16[64,1536]{1,0:T(8,128)(2,1)S(1)}, u32[]{:S(2)}, u32[]{:S(2)}) collective-permute-start(bf16[64,1536]{1,0:T(8,128)(2,1)S(1)} %get-tuple-element.58), channel_id=1, source_target_pairs={{0,32},{8,40},{16,48},{24,56},{32,0},{40,8},{48,16},{56,24},{1,33}... | collective-permute-start | bytes 589832 | tf_op jit(solution)/shard_map/ppermute | solution.py:44
  126.2 17.6 %collective-permute-start.24 = (bf16[64,1536]{1,0:T(8,128)(2,1)S(1)}, bf16[64,1536]{1,0:T(8,128)(2,1)S(1)}, u32[]{:S(2)}, u32[]{:S(2)}) collective-permute-start(bf16[64,1536]{1,0:T(8,128)(2,1)S(1)} %get-tuple-element.59), channel_id=1, source_target_pairs={{0,48},{8,56},{16,0},{24,8},{32,16},{40,24},{48,32},{56,40},{1,49}... | collective-permute-start | bytes 589832 | tf_op jit(solution)/shard_map/ppermute | solution.py:44
  131.6 14.7 %collective-permute-start.18 = (bf16[16,1536]{1,0:T(8,128)(2,1)S(1)}, bf16[16,1536]{1,0:T(8,128)(2,1)S(1)}, u32[]{:S(2)}, u32[]{:S(2)}) collective-permute-start(bf16[16,1536]{1,0:T(8,128)(2,1)S(1)} %get-tuple-element.51), channel_id=1, source_target_pairs={{0,64},{64,128},{128,192},{192,0},{1,65},{65,129},{129,193},{193,1... | collective-permute-start | bytes 147464 | tf_op jit(solution)/shard_map/ppermute | solution.py:32
  136.1 15.6 %collective-permute-start.19 = (bf16[16,1536]{1,0:T(8,128)(2,1)S(1)}, bf16[16,1536]{1,0:T(8,128)(2,1)S(1)}, u32[]{:S(2)}, u32[]{:S(2)}) collective-permute-start(bf16[16,1536]{1,0:T(8,128)(2,1)S(1)} %get-tuple-element.52), channel_id=1, source_target_pairs={{0,128},{64,192},{128,0},{192,64},{1,129},{65,193},{129,1},{193,65... | collective-permute-start | bytes 147464 | tf_op jit(solution)/shard_map/ppermute | solution.py:32
  139.6 12.1 %collective-permute-start.20 = (bf16[16,1536]{1,0:T(8,128)(2,1)S(1)}, bf16[16,1536]{1,0:T(8,128)(2,1)S(1)}, u32[]{:S(2)}, u32[]{:S(2)}) collective-permute-start(bf16[16,1536]{1,0:T(8,128)(2,1)S(1)} %get-tuple-element.53), channel_id=1, source_target_pairs={{0,192},{64,0},{128,64},{192,128},{1,193},{65,1},{129,65},{193,129... | collective-permute-start | bytes 147464 | tf_op jit(solution)/shard_map/ppermute | solution.py:32
  143.8 8.6 %collective-permute-start.25 = (bf16[16,1536]{1,0:T(8,128)(2,1)S(1)}, bf16[16,1536]{1,0:T(8,128)(2,1)S(1)}, u32[]{:S(2)}, u32[]{:S(2)}) collective-permute-start(bf16[16,1536]{1,0:T(8,128)(2,1)S(1)} %get-tuple-element.61), channel_id=1, source_target_pairs={{0,64},{64,128},{128,192},{192,0},{1,65},{65,129},{129,193},{193,1... | collective-permute-start | bytes 147464 | tf_op jit(solution)/shard_map/ppermute | solution.py:32
  143.9 8.6 %collective-permute-start.26 = (bf16[16,1536]{1,0:T(8,128)(2,1)S(1)}, bf16[16,1536]{1,0:T(8,128)(2,1)S(1)}, u32[]{:S(2)}, u32[]{:S(2)}) collective-permute-start(bf16[16,1536]{1,0:T(8,128)(2,1)S(1)} %get-tuple-element.62), channel_id=1, source_target_pairs={{0,128},{64,192},{128,0},{192,64},{1,129},{65,193},{129,1},{193,65... | collective-permute-start | bytes 147464 | tf_op jit(solution)/shard_map/ppermute | solution.py:32
  146.3 7.8 %collective-permute-start.27 = (bf16[16,1536]{1,0:T(8,128)(2,1)S(1)}, bf16[16,1536]{1,0:T(8,128)(2,1)S(1)}, u32[]{:S(2)}, u32[]{:S(2)}) collective-permute-start(bf16[16,1536]{1,0:T(8,128)(2,1)S(1)} %get-tuple-element.63), channel_id=1, source_target_pairs={{0,192},{64,0},{128,64},{192,128},{1,193},{65,1},{129,65},{193,129... | collective-permute-start | bytes 147464 | tf_op jit(solution)/shard_map/ppermute | solution.py:32

commit v3 on v2

--- a/solution.py
+++ b/solution.py
@@ -72,6 +72,17 @@
         cost_estimate=pl.CostEstimate(flops=flops, bytes_accessed=moved, transcendentals=0),
         name=name,
     )(*args)
+
+
+def pair_kernel(inputs_ref, grads_ref, both_ref):
+    both_ref[:16, :] = inputs_ref[...]
+    both_ref[16:, :] = grads_ref[...]
+
+
+def columns_kernel(both_ref, first_ref, second_ref, third_ref, inputs_ref, grads_ref):
+    for i, source in enumerate((both_ref, first_ref, second_ref, third_ref)):
+        inputs_ref[16 * i : 16 * i + 16, :] = source[:16, :]
+        grads_ref[16 * i : 16 * i + 16, :] = source[16:, :]
 
 
 def stack_kernel(*refs):
@@ -165,23 +176,27 @@
             sends[step - 1][:, cols] = acc[64 * step : 64 * step + 64, :].astype(bf16)
 
 
-def column_kernel(own_ref, first_ref, second_ref, third_ref, mine_ref, *sends):
+def column_kernel(*refs):
+    mine_ref, sends = refs[8], refs[9:12]
     for step in range(4):
         rows = slice(16 * step, 16 * step + 16)
-        total = own_ref[rows, :]
-        for part in (first_ref, second_ref, third_ref):
-            total = total + part[rows, :].astype(f32)
-        if step == 0:
-            mine_ref[...] = total
-        else:
-            sends[step - 1][...] = total.astype(bf16)
-
-
-def last_kernel(own_ref, first_ref, second_ref, third_ref, out_ref):
-    total = own_ref[...]
-    for part in (first_ref, second_ref, third_ref):
-        total = total + part[...].astype(f32)
-    out_ref[...] = total.astype(bf16)
+        for part in range(2):
+            total = refs[4 * part][rows, :]
+            for piece in refs[4 * part + 1 : 4 * part + 4]:
+                total = total + piece[rows, :].astype(f32)
+            if step == 0:
+                mine_ref[16 * part : 16 * part + 16, :] = total
+            else:
+                sends[step - 1][16 * part : 16 * part + 16, :] = total.astype(bf16)
+
+
+def last_kernel(mine_ref, first_ref, second_ref, third_ref, *outs):
+    for part, out in enumerate(outs):
+        rows = slice(16 * part, 16 * part + 16)
+        total = mine_ref[rows, :]
+        for piece in (first_ref, second_ref, third_ref):
+            total = total + piece[rows, :].astype(f32)
+        out[...] = total.astype(bf16)
 
 
 def units_far(part, gathered, weight):
@@ -212,33 +227,22 @@
     return mine, [to_y(send, step) for step, send in zip((1, 2, 3), sends)]
 
 
-def column_sum(mine, parts):
-    width = mine.shape[1]
-    mine, *sends = call(
-        column_kernel,
-        "column_sum",
-        [((16, width), f32)] + [((16, width), bf16)] * 3,
-        [mine] + parts,
-        moved=2**20,
-    )
-    return mine, [to_gx(send, step) for step, send in zip((1, 2, 3), sends)]
-
-
-def last_sum(mine, parts):
-    return call(last_kernel, "last_sum", [(mine.shape, bf16)], [mine] + parts, moved=2**18)[0]
-
-
 def on_device(inputs, w_in, w_out, grad_out):
     width, units = w_in.shape
     index = jnp.reshape(lax.axis_index("gz"), (1,)).astype(jnp.int32)
     steps = (1, 2, 3)
-    columns = [[shard] + [from_gx(shard, step) for step in steps] for shard in (inputs, grad_out)]
-    columns = [stack(column, "column") for column in columns]
+    (both,) = call(pair_kernel, "pair", [((32, width), bf16)], [inputs, grad_out], moved=2**18)
+    columns = call(
+        columns_kernel,
+        "columns",
+        [((64, width), bf16)] * 2,
+        [both] + [from_gx(both, step) for step in steps],
+        moved=2**20,
+    )
     planes = [[column] + [from_y(column, step) for step in steps] for column in columns]
     near = stack(planes[0], "plane")
     all_inputs, preact, sends = width_product(0, index, near, other_core(near), w_in, [])
-    plane, sends = lax.optimization_barrier((planes[1], sends))
-    near = stack(plane, "plane")
+    near = stack(planes[1], "plane")
     all_grads, grad_hidden, sends = width_product(
         1, index, near, other_core(near), w_out, [sends]
     )
@@ -255,10 +259,20 @@
     grad_pre_all, far_grad = units_far(1, gathered, w_in)
     mine_hidden, parts_hidden = units_near(0, hidden_all, w_out, far_hidden)
     mine_grad, parts_grad = units_near(1, grad_pre_all, w_in, far_grad)
-    mine_hidden, parts_hidden = column_sum(mine_hidden, parts_hidden)
-    mine_grad, parts_grad = column_sum(mine_grad, parts_grad)
-    output = last_sum(mine_hidden, parts_hidden)
-    grad_inputs = last_sum(mine_grad, parts_grad)
+    mine, *sends = call(
+        column_kernel,
+        "column_sums",
+        [((32, width), f32)] + [((32, width), bf16)] * 3,
+        [mine_hidden] + parts_hidden + [mine_grad] + parts_grad,
+        moved=2 * 2**20,
+    )
+    output, grad_inputs = call(
+        last_kernel,
+        "last_sums",
+        [((16, width), bf16)] * 2,
+        [mine] + [to_gx(send, step) for step, send in zip(steps, sends)],
+        moved=2**19,
+    )
     grad_w_out = lax.dot_general(
         hidden_all, all_grads, (((0,), (0,)), ((), ())), preferred_element_type=f32
     ).astype(bf16)

time: 155 us -> 146 us (0.942); the launches traced: 155 us -> 144 us
  starting transfers between devices: 57.1 us -> 41.8 us
  waiting for transfers between devices: 23.9 us -> 26.6 us
    ppermute x6 -> x3, starting transfers between devices: 17.9 us -> 10.2 us  [from_gx(): return lax.ppermute(value, 'gx', [((i + step) % 4, i) for i in range(4)])]
    ppermute x6 -> x3, starting transfers between devices: 14.4 us -> 9.93 us  [to_gx(): return lax.ppermute(value, 'gx', [(i, (i + step) % 4) for i in range(4)])]
    ppermute x6, waiting for transfers between devices: 0.02 us -> 3.63 us  [to_y(): lax.ppermute(value, 'gy', [(i, (i + 2 * step) % 8) for i in range(8)])]
    ppermute x6, starting transfers between devices: 10 us -> 6.64 us  [from_y(): lax.ppermute(value, 'gy', [((i + 2 * step) % 8, i) for i in range(8)])]
    ppermute x4, waiting for transfers between devices: 3.04 us -> 0.94 us  [other_core(): return lax.ppermute(value, 'gy', [(i, i ^ 1) for i in range(8)])]
    ppermute x6 -> x3, waiting for transfers between devices: 1.64 us -> 3.33 us  [to_gx(): return lax.ppermute(value, 'gx', [(i, (i + step) % 4) for i in range(4)])]
    ppermute x6 -> x3, waiting for transfers between devices: 9.39 us -> 7.8 us  [from_gx(): return lax.ppermute(value, 'gx', [((i + step) % 4, i) for i in range(4)])]
    pallas_call x15 -> x13, Pallas kernels: 15.3 us -> 15.8 us  [call(): pl.pallas_call(kernel, out_shape=[jax.ShapeDtypeStruct(*out) for out in o...]
  transfers between devices with their start and end apart: 28 -> 22, of which waited for: 12 -> 13; matrix products, arithmetic and copies ran while one was open for 4% -> 4% of each run, Pallas kernels for 6% -> 7%
where the time goes in v3:
time: 146 us; the launch traced here: 144 us
  blocking collectives  51.7 us (35%)
  starting transfers between devices  41.8 us (29%)
  waiting for transfers between devices  26.6 us (18%)
  Pallas kernels  15.8 us (11%)
  matrix products  5.65 us (4%)
  local copies, waits for them, and re-layouts  1.6 us (1%)
    all_to_all x2, blocking collectives, over_gz(): return lax.all_to_all(value, 'gz', 0, 0, tiled=True)  51.7 us
    pallas_call x13, Pallas kernels, call(): pl.pallas_call(kernel, out_shape=[jax.ShapeDtypeStruct(*out) for out in o...  15.8 us
    ppermute x6, starting transfers between devices, to_y(): lax.ppermute(value, 'gy', [(i, (i + 2 * step) % 8) for i in range(8)])  14.3 us
    ppermute x6, waiting for transfers between devices, from_y(): lax.ppermute(value, 'gy', [((i + 2 * step) % 8, i) for i in range(8)])  10.8 us
    ppermute x3, starting transfers between devices, from_gx(): return lax.ppermute(value, 'gx', [((i + step) % 4, i) for i in range(4)])  10.2 us
    ppermute x3, starting transfers between devices, to_gx(): return lax.ppermute(value, 'gx', [(i, (i + step) % 4) for i in range(4)])  9.93 us
    ppermute x3, waiting for transfers between devices, from_gx(): return lax.ppermute(value, 'gx', [((i + step) % 4, i) for i in range(4)])  7.8 us
    ppermute x6, starting transfers between devices, from_y(): lax.ppermute(value, 'gy', [((i + 2 * step) % 8, i) for i in range(8)])  6.64 us
  transfers between devices with their start and end apart: 22, of which 13 were waited for; matrix products, arithmetic and copies ran while one was open for 4% of the time, Pallas kernels for 7%

profile of v3, /device:TPU:8, one launch (start us, length us, event | category | flops | bytes accessed | tf_op | source)
XLA Modules:
  0.0 144.0 jit_solution(864970273187024252)
XLA Ops:
  2.2 6.4 %collective-permute-start = (bf16[32,1536]{1,0:T(8,128)(2,1)S(1)}, bf16[32,1536]{1,0:T(8,128)(2,1)S(1)}, u32[]{:S(2)}, u32[]{:S(2)}) collective-permute-start(bf16[32,1536]{1,0:T(8,128)(2,1)S(1)} %pair.1.both_ref), channel_id=1, source_target_pairs={{64,0},{128,64},{192,128},{0,192},{65,1},{129,65},{193,129},{1,193... | collective-permute-start | bytes 294920 | tf_op jit(solution)/shard_map/ppermute | solution.py:28
  8.6 1.0 collective-permute-start.1
  9.6 2.8 %collective-permute-start.2 = (bf16[32,1536]{1,0:T(8,128)(2,1)S(1)}, bf16[32,1536]{1,0:T(8,128)(2,1)S(1)}, u32[]{:S(2)}, u32[]{:S(2)}) collective-permute-start(bf16[32,1536]{1,0:T(8,128)(2,1)S(1)} %pair.1.both_ref), channel_id=1, source_target_pairs={{192,0},{0,64},{64,128},{128,192},{193,1},{1,65},{65,129},{129,193... | collective-permute-start | bytes 294920 | tf_op jit(solution)/shard_map/ppermute | solution.py:28
  12.4 4.6 %collective-permute-done.first_ref = bf16[32,1536]{1,0:T(8,128)(2,1)S(1)} collective-permute-done((bf16[32,1536]{1,0:T(8,128)(2,1)S(1)}, bf16[32,1536]{1,0:T(8,128)(2,1)S(1)}, u32[]{:S(2)}, u32[]{:S(2)}) %collective-permute-start) | collective-permute-done | bytes 98336 | tf_op jit(solution)/shard_map/ppermute | solution.py:28
  17.0 3.2 %collective-permute-done.1.second_ref = bf16[32,1536]{1,0:T(8,128)(2,1)S(1)} collective-permute-done((bf16[32,1536]{1,0:T(8,128)(2,1)S(1)}, bf16[32,1536]{1,0:T(8,128)(2,1)S(1)}, u32[]{:S(2)}, u32[]{:S(2)}) %collective-permute-start.1) | collective-permute-done | bytes 98336 | tf_op jit(solution)/shard_map/ppermute | solution.py:28
  21.0 2.4 %collective-permute-start.8 = (bf16[64,1536]{1,0:T(8,128)(2,1)S(1)}, bf16[64,1536]{1,0:T(8,128)(2,1)S(1)}, u32[]{:S(2)}, u32[]{:S(2)}) collective-permute-start(bf16[64,1536]{1,0:T(8,128)(2,1)S(1)} %get-tuple-element.31.refs_0_), channel_id=1, source_target_pairs={{32,0},{40,8},{48,16},{56,24},{0,32},{8,40},{16,48},{24,56},{33,1}... | collective-permute-start | bytes 589832 | tf_op jit(solution)/shard_map/ppermute | solution.py:40
  23.4 1.9 %collective-permute-start.9 = (bf16[64,1536]{1,0:T(8,128)(2,1)S(1)}, bf16[64,1536]{1,0:T(8,128)(2,1)S(1)}, u32[]{:S(2)}, u32[]{:S(2)}) collective-permute-start(bf16[64,1536]{1,0:T(8,128)(2,1)S(1)} %get-tuple-element.31.refs_0_), channel_id=1, source_target_pairs={{48,0},{56,8},{0,16},{8,24},{16,32},{24,40},{32,48},{40,56},{49,1}... | collective-permute-start | bytes 589832 | tf_op jit(solution)/shard_map/ppermute | solution.py:40
  25.4 1.3 collective-permute-start.4
  26.7 2.8 %collective-permute-done.7.refs_1_ = bf16[64,1536]{1,0:T(8,128)(2,1)S(1)} collective-permute-done((bf16[64,1536]{1,0:T(8,128)(2,1)S(1)}, bf16[64,1536]{1,0:T(8,128)(2,1)S(1)}, u32[]{:S(2)}, u32[]{:S(2)}) %collective-permute-start.7) | collective-permute-done | bytes 196640 | tf_op jit(solution)/shard_map/ppermute | solution.py:40
  29.8 3.7 %collective-permute-done.8.refs_2_ = bf16[64,1536]{1,0:T(8,128)(2,1)S(1)} collective-permute-done((bf16[64,1536]{1,0:T(8,128)(2,1)S(1)}, bf16[64,1536]{1,0:T(8,128)(2,1)S(1)}, u32[]{:S(2)}, u32[]{:S(2)}) %collective-permute-start.8) | collective-permute-done | bytes 196640 | tf_op jit(solution)/shard_map/ppermute | solution.py:40
  35.7 2.1 %collective-permute-done.4.refs_2_ = bf16[64,1536]{1,0:T(8,128)(2,1)S(1)} collective-permute-done((bf16[64,1536]{1,0:T(8,128)(2,1)S(1)}, bf16[64,1536]{1,0:T(8,128)(2,1)S(1)}, u32[]{:S(2)}, u32[]{:S(2)}) %collective-permute-start.4) | collective-permute-done | bytes 196640 | tf_op jit(solution)/shard_map/ppermute | solution.py:40
  38.9 3.4 %width_inputs.1 = (bf16[512,1536]{1,0:T(8,128)(2,1)S(1)}, f32[64,768]{1,0:T(8,128)S(1)}, bf16[8,128,768]{2,1,0:T(8,128)(2,1)S(1)}) custom-call(s32[1]{0:T(128)} %bitcast.index_ref, bf16[256,1536]{1,0:T(8,128)(2,1)} %plane.3.near_ref, bf16[256,1536]{1,0:T(8,128)(2,1)} %collective-permute-done.10.far_ref, bf16[1536,768]{1,0:T(8,128)(2,1)S(1)} %copy-done.1), custom_call_target="tpu_custom_call" | custom-call | flops 1207959552 | bytes 6291456 | tf_op jit(solution)/shard_map/width_inputs/pallas_call | solution.py:64
  42.3 3.1 %width_grad.1 = (bf16[512,1536]{1,0:T(8,128)(2,1)S(1)}, f32[64,768]{1,0:T(8,128)S(1)}, bf16[8,128,768]{2,1,0:T(8,128)(2,1)S(1)}) custom-call(s32[1]{0:T(128)} %bitcast.index_ref, bf16[256,1536]{1,0:T(8,128)(2,1)S(1)} %plane.2.near_ref, bf16[256,1536]{1,0:T(8,128)(2,1)} %collective-permute-done.6.far_ref, ...), custom_call_target="tpu_custom_call", output_to_operand_aliasing={{2}: (4, {})} | custom-call | flops 1207959552 | bytes 6291456 | tf_op jit(solution)/shard_map/width_grad/pallas_call | solution.py:64
  45.4 28.1 %all_to_all.10.parts_ref = bf16[8,128,768]{2,1,0:T(8,128)(2,1)S(1)} all-to-all(bf16[8,128,768]{2,1,0:T(8,128)(2,1)S(1)} %get-tuple-element.33), channel_id=1, replica_groups=mesh['gx'=4,'gy'=8,'gz'=8] {'gz'}, dimensions={0} | all-to-all | bytes 3145728 | tf_op jit(solution)/shard_map/all_to_all | solution.py:48
  74.0 23.6 %all_to_all.11.parts_ref = bf16[8,128,768]{2,1,0:T(8,128)(2,1)S(1)} all-to-all(bf16[8,128,768]{2,1,0:T(8,128)(2,1)S(1)} %activation.1), channel_id=1, replica_groups=mesh['gx'=4,'gy'=8,'gz'=8] {'gz'}, dimensions={0} | all-to-all | bytes 3145728 | tf_op jit(solution)/shard_map/all_to_all | solution.py:48
  97.6 1.7 %far_hidden.1 = (bf16[512,768]{1,0:T(8,128)(2,1)S(1)}, f32[256,1536]{1,0:T(8,128)S(1)}) custom-call(bf16[8,128,768]{2,1,0:T(8,128)(2,1)S(1)} %all_to_all.11.parts_ref, bf16[768,1536]{1,0:T(8,128)(2,1)S(1)} %copy-done), custom_call_target="tpu_custom_call" | custom-call | flops 603979776 | bytes 6291456 | tf_op jit(solution)/shard_map/far_hidden/pallas_call | solution.py:64
  99.4 1.9 %far_grad.1 = (bf16[512,768]{1,0:T(8,128)(2,1)S(1)}, f32[256,1536]{1,0:T(8,128)S(1)}) custom-call(bf16[8,128,768]{2,1,0:T(8,128)(2,1)S(1)} %all_to_all.11.parts_ref, bf16[1536,768]{1,0:T(8,128)(2,1)S(1)} %copy-done.1), custom_call_target="tpu_custom_call" | custom-call | flops 603979776 | bytes 6291456 | tf_op jit(solution)/shard_map/far_grad/pallas_call | solution.py:64
  101.9 0.9 collective-permute-done.11.far_ref
  102.8 1.6 %near_hidden.1 = (f32[64,1536]{1,0:T(8,128)S(1)}, bf16[64,1536]{1,0:T(8,128)(2,1)S(1)}, bf16[64,1536]{1,0:T(8,128)(2,1)S(1)}, bf16[64,1536]{1,0:T(8,128)(2,1)S(1)}) custom-call(bf16[512,768]{1,0:T(8,128)(2,1)S(1)} %get-tuple-element.36.whole_ref, bf16[768,1536]{1,0:T(8,128)(2,1)S(1)} %copy-done, f32[256,1536]{1,0:T(8,128)S(1)} %collective-permute-done.11.far_ref), custom_call_target="tpu_custom_call" | custom-call | flops 603979776 | bytes 6291456 | tf_op jit(solution)/shard_map/near_hidden/pallas_call | solution.py:64
  104.4 1.5 %collective-permute-start.12 = (bf16[64,1536]{1,0:T(8,128)(2,1)S(1)}, bf16[64,1536]{1,0:T(8,128)(2,1)S(1)}, u32[]{:S(2)}, u32[]{:S(2)}) collective-permute-start(bf16[64,1536]{1,0:T(8,128)(2,1)S(1)} %get-tuple-element.39), channel_id=1, source_target_pairs={{0,16},{8,24},{16,32},{24,40},{32,48},{40,56},{48,0},{56,8},{1,17}... | collective-permute-start | bytes 589832 | tf_op jit(solution)/shard_map/ppermute | solution.py:44
  105.9 3.6 %collective-permute-start.13 = (bf16[64,1536]{1,0:T(8,128)(2,1)S(1)}, bf16[64,1536]{1,0:T(8,128)(2,1)S(1)}, u32[]{:S(2)}, u32[]{:S(2)}) collective-permute-start(bf16[64,1536]{1,0:T(8,128)(2,1)S(1)} %get-tuple-element.40), channel_id=1, source_target_pairs={{0,32},{8,40},{16,48},{24,56},{32,0},{40,8},{48,16},{56,24},{1,33}... | collective-permute-start | bytes 589832 | tf_op jit(solution)/shard_map/ppermute | solution.py:44
  109.5 1.8 %near_grad.1 = (f32[64,1536]{1,0:T(8,128)S(1)}, bf16[64,1536]{1,0:T(8,128)(2,1)S(1)}, bf16[64,1536]{1,0:T(8,128)(2,1)S(1)}, bf16[64,1536]{1,0:T(8,128)(2,1)S(1)}) custom-call(bf16[512,768]{1,0:T(8,128)(2,1)S(1)} %get-tuple-element.42.whole_ref, bf16[1536,768]{1,0:T(8,128)(2,1)S(1)} %copy-done.1, f32[256,1536]{1,0:T(8,128)S(1)} %collective-permute-done.15.far_ref), custom_call_target="tpu_custom_call" | custom-call | flops 603979776 | bytes 6291456 | tf_op jit(solution)/shard_map/near_grad/pallas_call | solution.py:64
  111.4 2.1 %collective-permute-start.16 = (bf16[64,1536]{1,0:T(8,128)(2,1)S(1)}, bf16[64,1536]{1,0:T(8,128)(2,1)S(1)}, u32[]{:S(2)}, u32[]{:S(2)}) collective-permute-start(bf16[64,1536]{1,0:T(8,128)(2,1)S(1)} %get-tuple-element.45), channel_id=1, source_target_pairs={{0,16},{8,24},{16,32},{24,40},{32,48},{40,56},{48,0},{56,8},{1,17}... | collective-permute-start | bytes 589832 | tf_op jit(solution)/shard_map/ppermute | solution.py:44
  113.4 1.2 collective-permute-start.17
  114.7 5.9 %collective-permute-start.18 = (bf16[64,1536]{1,0:T(8,128)(2,1)S(1)}, bf16[64,1536]{1,0:T(8,128)(2,1)S(1)}, u32[]{:S(2)}, u32[]{:S(2)}) collective-permute-start(bf16[64,1536]{1,0:T(8,128)(2,1)S(1)} %get-tuple-element.47), channel_id=1, source_target_pairs={{0,48},{8,56},{16,0},{24,8},{32,16},{40,24},{48,32},{56,40},{1,49}... | collective-permute-start | bytes 589832 | tf_op jit(solution)/shard_map/ppermute | solution.py:44
  120.6 2.8 %convolution_convert_fusion.1 = bf16[1536,768]{1,0:T(8,128)(2,1)} fusion(bf16[512,1536]{1,0:T(8,128)(2,1)S(1)} %get-tuple-element.54, bf16[512,768]{1,0:T(8,128)(2,1)S(1)} %get-tuple-element.42.whole_ref), kind=kOutput, calls=%fused_computation.1 | convolution fusion | flops 1209139200 | bytes 4718592 | tf_op jit(solution)/shard_map/dot_general | solution.py:279
  123.7 3.3 %collective-permute-done.18.refs_7_ = bf16[64,1536]{1,0:T(8,128)(2,1)S(1)} collective-permute-done((bf16[64,1536]{1,0:T(8,128)(2,1)S(1)}, bf16[64,1536]{1,0:T(8,128)(2,1)S(1)}, u32[]{:S(2)}, u32[]{:S(2)}) %collective-permute-start.18) | collective-permute-done | bytes 196640 | tf_op jit(solution)/shard_map/ppermute | solution.py:44
  127.2 2.6 %collective-permute-start.19 = (bf16[32,1536]{1,0:T(8,128)(2,1)S(1)}, bf16[32,1536]{1,0:T(8,128)(2,1)S(1)}, u32[]{:S(2)}, u32[]{:S(2)}) collective-permute-start(bf16[32,1536]{1,0:T(8,128)(2,1)S(1)} %get-tuple-element.49), channel_id=1, source_target_pairs={{0,64},{64,128},{128,192},{192,0},{1,65},{65,129},{129,193},{193,1... | collective-permute-start | bytes 294920 | tf_op jit(solution)/shard_map/ppermute | solution.py:32
  129.8 4.0 %collective-permute-start.20 = (bf16[32,1536]{1,0:T(8,128)(2,1)S(1)}, bf16[32,1536]{1,0:T(8,128)(2,1)S(1)}, u32[]{:S(2)}, u32[]{:S(2)}) collective-permute-start(bf16[32,1536]{1,0:T(8,128)(2,1)S(1)} %get-tuple-element.50), channel_id=1, source_target_pairs={{0,128},{64,192},{128,0},{192,64},{1,129},{65,193},{129,1},{193,65... | collective-permute-start | bytes 294920 | tf_op jit(solution)/shard_map/ppermute | solution.py:32
  133.9 3.3 %collective-permute-start.21 = (bf16[32,1536]{1,0:T(8,128)(2,1)S(1)}, bf16[32,1536]{1,0:T(8,128)(2,1)S(1)}, u32[]{:S(2)}, u32[]{:S(2)}) collective-permute-start(bf16[32,1536]{1,0:T(8,128)(2,1)S(1)} %get-tuple-element.51), channel_id=1, source_target_pairs={{0,192},{64,0},{128,64},{192,128},{1,193},{65,1},{129,65},{193,129... | collective-permute-start | bytes 294920 | tf_op jit(solution)/shard_map/ppermute | solution.py:32
  137.1 2.8 %convolution_convert_fusion = bf16[768,1536]{1,0:T(8,128)(2,1)} fusion(bf16[512,768]{1,0:T(8,128)(2,1)S(1)} %get-tuple-element.36.whole_ref, bf16[512,1536]{1,0:T(8,128)(2,1)S(1)} %get-tuple-element.55), kind=kOutput, calls=%fused_computation | convolution fusion | flops 1209139200 | bytes 4718592 | tf_op jit(solution)/shard_map/dot_general | solution.py:276
  140.6 2.7 %collective-permute-done.21.third_ref = bf16[32,1536]{1,0:T(8,128)(2,1)S(1)} collective-permute-done((bf16[32,1536]{1,0:T(8,128)(2,1)S(1)}, bf16[32,1536]{1,0:T(8,128)(2,1)S(1)}, u32[]{:S(2)}, u32[]{:S(2)}) %collective-permute-start.21) | collective-permute-done | bytes 98336 | tf_op jit(solution)/shard_map/ppermute | solution.py:32
  (37 shorter events, 8.9 us)
Async XLA Ops:
  0.6 0.8 copy-start.2
  1.4 0.8 copy-start.3
  2.2 14.8 %collective-permute-start = (bf16[32,1536]{1,0:T(8,128)(2,1)S(1)}, bf16[32,1536]{1,0:T(8,128)(2,1)S(1)}, u32[]{:S(2)}, u32[]{:S(2)}) collective-permute-start(bf16[32,1536]{1,0:T(8,128)(2,1)S(1)} %pair.1.both_ref), channel_id=1, source_target_pairs={{64,0},{128,64},{192,128},{0,192},{65,1},{129,65},{193,129},{1,193... | collective-permute-start | bytes 294920 | tf_op jit(solution)/shard_map/ppermute | solution.py:28
  8.6 11.6 %collective-permute-start.1 = (bf16[32,1536]{1,0:T(8,128)(2,1)S(1)}, bf16[32,1536]{1,0:T(8,128)(2,1)S(1)}, u32[]{:S(2)}, u32[]{:S(2)}) collective-permute-start(bf16[32,1536]{1,0:T(8,128)(2,1)S(1)} %pair.1.both_ref), channel_id=1, source_target_pairs={{128,0},{192,64},{0,128},{64,192},{129,1},{193,65},{1,129},{65,193... | collective-permute-start | bytes 294920 | tf_op jit(solution)/shard_map/ppermute | solution.py:28
  9.6 10.6 %collective-permute-start.2 = (bf16[32,1536]{1,0:T(8,128)(2,1)S(1)}, bf16[32,1536]{1,0:T(8,128)(2,1)S(1)}, u32[]{:S(2)}, u32[]{:S(2)}) collective-permute-start(bf16[32,1536]{1,0:T(8,128)(2,1)S(1)} %pair.1.both_ref), channel_id=1, source_target_pairs={{192,0},{0,64},{64,128},{128,192},{193,1},{1,65},{65,129},{129,193... | collective-permute-start | bytes 294920 | tf_op jit(solution)/shard_map/ppermute | solution.py:28
  20.3 9.3 %collective-permute-start.7 = (bf16[64,1536]{1,0:T(8,128)(2,1)S(1)}, bf16[64,1536]{1,0:T(8,128)(2,1)S(1)}, u32[]{:S(2)}, u32[]{:S(2)}) collective-permute-start(bf16[64,1536]{1,0:T(8,128)(2,1)S(1)} %get-tuple-element.31.refs_0_), channel_id=1, source_target_pairs={{16,0},{24,8},{32,16},{40,24},{48,32},{56,40},{0,48},{8,56},{17,1}... | collective-permute-start | bytes 589832 | tf_op jit(solution)/shard_map/ppermute | solution.py:40
  21.0 12.5 %collective-permute-start.8 = (bf16[64,1536]{1,0:T(8,128)(2,1)S(1)}, bf16[64,1536]{1,0:T(8,128)(2,1)S(1)}, u32[]{:S(2)}, u32[]{:S(2)}) collective-permute-start(bf16[64,1536]{1,0:T(8,128)(2,1)S(1)} %get-tuple-element.31.refs_0_), channel_id=1, source_target_pairs={{32,0},{40,8},{48,16},{56,24},{0,32},{8,40},{16,48},{24,56},{33,1}... | collective-permute-start | bytes 589832 | tf_op jit(solution)/shard_map/ppermute | solution.py:40
  23.4 11.1 %collective-permute-start.9 = (bf16[64,1536]{1,0:T(8,128)(2,1)S(1)}, bf16[64,1536]{1,0:T(8,128)(2,1)S(1)}, u32[]{:S(2)}, u32[]{:S(2)}) collective-permute-start(bf16[64,1536]{1,0:T(8,128)(2,1)S(1)} %get-tuple-element.31.refs_0_), channel_id=1, source_target_pairs={{48,0},{56,8},{0,16},{8,24},{16,32},{24,40},{32,48},{40,56},{49,1}... | collective-permute-start | bytes 589832 | tf_op jit(solution)/shard_map/ppermute | solution.py:40
  25.3 13.6 %copy-start.1 = (bf16[1536,768]{1,0:T(8,128)(2,1)S(1)}, bf16[1536,768]{1,0:T(8,128)(2,1)}, u32[]{:S(2)}) copy-start(bf16[1536,768]{1,0:T(8,128)(2,1)} %weight_ref.11) | copy-start | bytes 7077892
  25.3 10.5 %collective-permute-start.3 = (bf16[64,1536]{1,0:T(8,128)(2,1)S(1)}, bf16[64,1536]{1,0:T(8,128)(2,1)S(1)}, u32[]{:S(2)}, u32[]{:S(2)}) collective-permute-start(bf16[64,1536]{1,0:T(8,128)(2,1)S(1)} %get-tuple-element.30.refs_0_), channel_id=1, source_target_pairs={{16,0},{24,8},{32,16},{40,24},{48,32},{56,40},{0,48},{8,56},{17,1}... | collective-permute-start | bytes 589832 | tf_op jit(solution)/shard_map/ppermute | solution.py:40
  25.4 12.5 %collective-permute-start.4 = (bf16[64,1536]{1,0:T(8,128)(2,1)S(1)}, bf16[64,1536]{1,0:T(8,128)(2,1)S(1)}, u32[]{:S(2)}, u32[]{:S(2)}) collective-permute-start(bf16[64,1536]{1,0:T(8,128)(2,1)S(1)} %get-tuple-element.30.refs_0_), channel_id=1, source_target_pairs={{32,0},{40,8},{48,16},{56,24},{0,32},{8,40},{16,48},{24,56},{33,1}... | collective-permute-start | bytes 589832 | tf_op jit(solution)/shard_map/ppermute | solution.py:40
  29.6 9.1 %collective-permute-start.5 = (bf16[64,1536]{1,0:T(8,128)(2,1)S(1)}, bf16[64,1536]{1,0:T(8,128)(2,1)S(1)}, u32[]{:S(2)}, u32[]{:S(2)}) collective-permute-start(bf16[64,1536]{1,0:T(8,128)(2,1)S(1)} %get-tuple-element.30.refs_0_), channel_id=1, source_target_pairs={{48,0},{56,8},{0,16},{8,24},{16,32},{24,40},{32,48},{40,56},{49,1}... | collective-permute-start | bytes 589832 | tf_op jit(solution)/shard_map/ppermute | solution.py:40
  35.4 3.5 %collective-permute-start.10 = (bf16[256,1536]{1,0:T(8,128)(2,1)}, bf16[256,1536]{1,0:T(8,128)(2,1)}, u32[]{:S(2)}, u32[]{:S(2)}) collective-permute-start(bf16[256,1536]{1,0:T(8,128)(2,1)} %plane.3.near_ref), channel_id=1, source_target_pairs={{0,8},{8,0},{16,24},{24,16},{32,40},{40,32},{48,56},{56,48},{1,9},... | collective-permute-start | bytes 2359304 | tf_op jit(solution)/shard_map/ppermute | solution.py:36
  38.7 3.5 %collective-permute-start.6 = (bf16[256,1536]{1,0:T(8,128)(2,1)S(1)}, bf16[256,1536]{1,0:T(8,128)(2,1)}, u32[]{:S(2)}, u32[]{:S(2)}) collective-permute-start(bf16[256,1536]{1,0:T(8,128)(2,1)S(1)} %plane.2.near_ref), channel_id=1, source_target_pairs={{0,8},{8,0},{16,24},{24,16},{32,40},{40,32},{48,56},{56,48},{1,9},... | collective-permute-start | bytes 2359304 | tf_op jit(solution)/shard_map/ppermute | solution.py:36
  38.9 3.4 %copy-start = (bf16[768,1536]{1,0:T(8,128)(2,1)S(1)}, bf16[768,1536]{1,0:T(8,128)(2,1)}, u32[]{:S(2)}) copy-start(bf16[768,1536]{1,0:T(8,128)(2,1)} %weight_ref.9) | copy-start | bytes 7077892
  99.3 3.5 %collective-permute-start.11 = (f32[256,1536]{1,0:T(8,128)S(1)}, f32[256,1536]{1,0:T(8,128)S(1)}, u32[]{:S(2)}, u32[]{:S(2)}) collective-permute-start(f32[256,1536]{1,0:T(8,128)S(1)} %get-tuple-element.37), channel_id=1, source_target_pairs={{0,8},{8,0},{16,24},{24,16},{32,40},{40,32},{48,56},{56,48},{1,9},... | collective-permute-start | bytes 4718600 | tf_op jit(solution)/shard_map/ppermute | solution.py:36
  101.3 8.2 %collective-permute-start.15 = (f32[256,1536]{1,0:T(8,128)S(1)}, f32[256,1536]{1,0:T(8,128)S(1)}, u32[]{:S(2)}, u32[]{:S(2)}) collective-permute-start(f32[256,1536]{1,0:T(8,128)S(1)} %get-tuple-element.43), channel_id=1, source_target_pairs={{0,8},{8,0},{16,24},{24,16},{32,40},{40,32},{48,56},{56,48},{1,9},... | collective-permute-start | bytes 4718600 | tf_op jit(solution)/shard_map/ppermute | solution.py:36
  104.4 10.2 %collective-permute-start.12 = (bf16[64,1536]{1,0:T(8,128)(2,1)S(1)}, bf16[64,1536]{1,0:T(8,128)(2,1)S(1)}, u32[]{:S(2)}, u32[]{:S(2)}) collective-permute-start(bf16[64,1536]{1,0:T(8,128)(2,1)S(1)} %get-tuple-element.39), channel_id=1, source_target_pairs={{0,16},{8,24},{16,32},{24,40},{32,48},{40,56},{48,0},{56,8},{1,17}... | collective-permute-start | bytes 589832 | tf_op jit(solution)/shard_map/ppermute | solution.py:44
  105.9 17.5 %collective-permute-start.13 = (bf16[64,1536]{1,0:T(8,128)(2,1)S(1)}, bf16[64,1536]{1,0:T(8,128)(2,1)S(1)}, u32[]{:S(2)}, u32[]{:S(2)}) collective-permute-start(bf16[64,1536]{1,0:T(8,128)(2,1)S(1)} %get-tuple-element.40), channel_id=1, source_target_pairs={{0,32},{8,40},{16,48},{24,56},{32,0},{40,8},{48,16},{56,24},{1,33}... | collective-permute-start | bytes 589832 | tf_op jit(solution)/shard_map/ppermute | solution.py:44
  109.5 13.9 %collective-permute-start.14 = (bf16[64,1536]{1,0:T(8,128)(2,1)S(1)}, bf16[64,1536]{1,0:T(8,128)(2,1)S(1)}, u32[]{:S(2)}, u32[]{:S(2)}) collective-permute-start(bf16[64,1536]{1,0:T(8,128)(2,1)S(1)} %get-tuple-element.41), channel_id=1, source_target_pairs={{0,48},{8,56},{16,0},{24,8},{32,16},{40,24},{48,32},{56,40},{1,49}... | collective-permute-start | bytes 589832 | tf_op jit(solution)/shard_map/ppermute | solution.py:44
  111.4 12.1 %collective-permute-start.16 = (bf16[64,1536]{1,0:T(8,128)(2,1)S(1)}, bf16[64,1536]{1,0:T(8,128)(2,1)S(1)}, u32[]{:S(2)}, u32[]{:S(2)}) collective-permute-start(bf16[64,1536]{1,0:T(8,128)(2,1)S(1)} %get-tuple-element.45), channel_id=1, source_target_pairs={{0,16},{8,24},{16,32},{24,40},{32,48},{40,56},{48,0},{56,8},{1,17}... | collective-permute-start | bytes 589832 | tf_op jit(solution)/shard_map/ppermute | solution.py:44
  113.4 10.3 %collective-permute-start.17 = (bf16[64,1536]{1,0:T(8,128)(2,1)S(1)}, bf16[64,1536]{1,0:T(8,128)(2,1)S(1)}, u32[]{:S(2)}, u32[]{:S(2)}) collective-permute-start(bf16[64,1536]{1,0:T(8,128)(2,1)S(1)} %get-tuple-element.46), channel_id=1, source_target_pairs={{0,32},{8,40},{16,48},{24,56},{32,0},{40,8},{48,16},{56,24},{1,33}... | collective-permute-start | bytes 589832 | tf_op jit(solution)/shard_map/ppermute | solution.py:44
  114.7 12.4 %collective-permute-start.18 = (bf16[64,1536]{1,0:T(8,128)(2,1)S(1)}, bf16[64,1536]{1,0:T(8,128)(2,1)S(1)}, u32[]{:S(2)}, u32[]{:S(2)}) collective-permute-start(bf16[64,1536]{1,0:T(8,128)(2,1)S(1)} %get-tuple-element.47), channel_id=1, source_target_pairs={{0,48},{8,56},{16,0},{24,8},{32,16},{40,24},{48,32},{56,40},{1,49}... | collective-permute-start | bytes 589832 | tf_op jit(solution)/shard_map/ppermute | solution.py:44
  127.2 12.8 %collective-permute-start.19 = (bf16[32,1536]{1,0:T(8,128)(2,1)S(1)}, bf16[32,1536]{1,0:T(8,128)(2,1)S(1)}, u32[]{:S(2)}, u32[]{:S(2)}) collective-permute-start(bf16[32,1536]{1,0:T(8,128)(2,1)S(1)} %get-tuple-element.49), channel_id=1, source_target_pairs={{0,64},{64,128},{128,192},{192,0},{1,65},{65,129},{129,193},{193,1... | collective-permute-start | bytes 294920 | tf_op jit(solution)/shard_map/ppermute | solution.py:32
  129.8 10.7 %collective-permute-start.20 = (bf16[32,1536]{1,0:T(8,128)(2,1)S(1)}, bf16[32,1536]{1,0:T(8,128)(2,1)S(1)}, u32[]{:S(2)}, u32[]{:S(2)}) collective-permute-start(bf16[32,1536]{1,0:T(8,128)(2,1)S(1)} %get-tuple-element.50), channel_id=1, source_target_pairs={{0,128},{64,192},{128,0},{192,64},{1,129},{65,193},{129,1},{193,65... | collective-permute-start | bytes 294920 | tf_op jit(solution)/shard_map/ppermute | solution.py:32
  133.9 9.4 %collective-permute-start.21 = (bf16[32,1536]{1,0:T(8,128)(2,1)S(1)}, bf16[32,1536]{1,0:T(8,128)(2,1)S(1)}, u32[]{:S(2)}, u32[]{:S(2)}) collective-permute-start(bf16[32,1536]{1,0:T(8,128)(2,1)S(1)} %get-tuple-element.51), channel_id=1, source_target_pairs={{0,192},{64,0},{128,64},{192,128},{1,193},{65,1},{129,65},{193,129... | collective-permute-start | bytes 294920 | tf_op jit(solution)/shard_map/ppermute | solution.py:32

commit v4 on v3

--- a/solution.py
+++ b/solution.py
@@ -44,8 +44,16 @@
     return lax.ppermute(value, "gy", [(i, (i + 2 * step) % 8) for i in range(8)])
 
 
-def over_gz(value):
-    return lax.all_to_all(value, "gz", 0, 0, tiled=True)
+def from_x(value, step):
+    return lax.ppermute(value, "gz", [((i + 2 * step) % 8, i) for i in range(8)])
+
+
+def to_x(value, step):
+    return lax.ppermute(value, "gz", [(i, (i + 2 * step) % 8) for i in range(8)])
+
+
+def other_z(value):
+    return lax.ppermute(value, "gz", [(i, i ^ 1) for i in range(8)])
 
 
 def product(left, right, transposed):
@@ -96,10 +104,18 @@
     return call(stack_kernel, name, [((4 * rows, width), bf16)], pieces, moved=2**20)[0]
 
 
-def width_kernel(part, transposed, index_ref, near_ref, far_ref, weight_ref, *refs):
-    whole_ref, own_ref, send_ref, acc = refs[-4:]
+def place(index_ref):
     me = index_ref[0]
-    rows = slice(64 * part, 64 * part + 64)
+    return lax.shift_right_logical(me, 1), lax.bitwise_and(me, 1)
+
+
+def block(x, step, size, offset=0):
+    return pl.ds(pl.multiple_of(lax.bitwise_and(x + step, 3) * 128 + offset, 64), size)
+
+
+def width_inputs_kernel(index_ref, near_ref, far_ref, weight_ref, *refs):
+    whole_ref, own_ref, sends, acc = refs[0], refs[1], refs[2:5], refs[5]
+    x, z = place(index_ref)
     whole_ref[:256, :] = near_ref[...]
     whole_ref[256:, :] = far_ref[...]
 
@@ -107,58 +123,105 @@
     def _(j):
         start = pl.multiple_of(j * tile, tile)
         cols = pl.ds(start, tile)
-        acc[...] = product(whole_ref[...], columns_of(weight_ref, start, transposed), transposed)
-        own_ref[:, cols] = acc[pl.ds(pl.multiple_of(me * 64, 64), 64), :]
-        for peer in range(8):
-            send_ref[peer, rows, cols] = acc[64 * peer : 64 * peer + 64, :].astype(bf16)
-
-
-def width_product(part, index, near, far, weight, sends):
-    width = near.shape[1]
-    units = weight.shape[0] if part else weight.shape[1]
-    return call(
-        functools.partial(width_kernel, part, bool(part)),
-        "width_grad" if part else "width_inputs",
-        [((512, width), bf16), ((64, units), f32), ((8, 128, units), bf16)],
-        [index, near, far, weight] + sends,
-        scratch=[((512, tile), f32)],
-        flops=2 * 512 * width * units,
-        moved=6 * 2**20,
-        scalars=1,
-        aliases={4: 2} if sends else None,
-    )
-
-
-def activation_kernel(index_ref, parts_ref, preact_ref, grad_ref, out_ref):
-    me = index_ref[0]
-
+        acc[...] = product(whole_ref[...], columns_of(weight_ref, start, False), False)
+        own_ref[:, cols] = acc[block(x, 0, 128), :]
+        for step in (1, 2, 3):
+            sends[step - 1][:, cols] = acc[block(x, step, 128), :].astype(bf16)
+
+
+def width_grad_kernel(index_ref, near_ref, far_ref, weight_ref, *refs):
+    whole_ref, own_ref, send_ref, acc = refs
+    x, z = place(index_ref)
+    whole_ref[:256, :] = near_ref[...]
+    whole_ref[256:, :] = far_ref[...]
+
+    @pl.loop(0, own_ref.shape[1] // tile)
+    def _(j):
+        start = pl.multiple_of(j * tile, tile)
+        cols = pl.ds(start, tile)
+        acc[...] = product(whole_ref[...], columns_of(weight_ref, start, True), True)
+        for step in range(4):
+            rows = slice(64 * step, 64 * step + 64)
+            own_ref[rows, cols] = acc[block(x, step, 64, 64 * z), :]
+            send_ref[rows, cols] = acc[block(x, step, 64, 64 * (1 - z)), :].astype(bf16)
+
+
+def sum_x_kernel(index_ref, own_ref, first_ref, second_ref, third_ref, mine_ref, send_ref):
+    x, z = place(index_ref)
+    for target, half in ((mine_ref, z), (send_ref, 1 - z)):
+
+        @pl.loop(0, 4)
+        def _(j):
+            rows = pl.ds(pl.multiple_of(64 * half + 16 * j, 16), 16)
+            total = own_ref[rows, :]
+            for piece in (first_ref, second_ref, third_ref):
+                total = total + piece[rows, :].astype(f32)
+            target[pl.ds(pl.multiple_of(16 * j, 16), 16), :] = total
+
+
+def activation_kernel(mine_ref, part_ref, hidden_ref, slope_ref):
     @pl.loop(0, 4)
     def _(j):
-        sums = []
-        for part, own_ref in ((0, preact_ref), (1, grad_ref)):
-            total = own_ref[pl.ds(pl.multiple_of(j * 16, 16), 16), :]
-            rows = pl.ds(pl.multiple_of(64 * part + j * 16, 16), 16)
-            for peer in range(8):
-                total = total + jnp.where(peer == me, 0.0, parts_ref[peer, rows, :].astype(f32))
-            sums.append(total)
-        result, slope = gelu_parts(sums[0])
-        for part, value in ((0, result), (1, sums[1] * slope)):
-            rows = pl.ds(pl.multiple_of(64 * part + j * 16, 16), 16)
-            rounded = value.astype(bf16)
-            for peer in range(8):
-                out_ref[peer, rows, :] = rounded
-
-
-def far_kernel(part, transposed, parts_ref, weight_ref, whole_ref, far_ref):
-    for share in range(8):
-        whole_ref[64 * share : 64 * share + 64, :] = parts_ref[share, 64 * part : 64 * part + 64, :]
-
+        rows = pl.ds(pl.multiple_of(16 * j, 16), 16)
+        result, slope = gelu_parts(mine_ref[rows, :] + part_ref[rows, :])
+        hidden_ref[rows, :] = result.astype(bf16)
+        slope_ref[rows, :] = slope
+
+
+def sum_z_kernel(own_ref, part_ref, mine_ref, *sends):
+    for step in range(4):
+
+        @pl.loop(0, 4)
+        def _(j):
+            rows = pl.ds(pl.multiple_of(64 * step + 16 * j, 16), 16)
+            local = pl.ds(pl.multiple_of(16 * j, 16), 16)
+            total = own_ref[rows, :] + part_ref[rows, :].astype(f32)
+            if step == 0:
+                mine_ref[local, :] = total
+            else:
+                sends[step - 1][local, :] = total.astype(bf16)
+
+
+def grad_pre_kernel(mine_ref, first_ref, second_ref, third_ref, slope_ref, out_ref):
+    @pl.loop(0, 4)
+    def _(j):
+        rows = pl.ds(pl.multiple_of(16 * j, 16), 16)
+        total = mine_ref[rows, :]
+        for piece in (first_ref, second_ref, third_ref):
+            total = total + piece[rows, :].astype(f32)
+        out_ref[rows, :] = (total * slope_ref[rows, :]).astype(bf16)
+
+
+def pair_z_kernel(index_ref, own_ref, part_ref, out_ref):
+    x, z = place(index_ref)
+    out_ref[pl.ds(pl.multiple_of(64 * z, 64), 64), :] = own_ref[...]
+    out_ref[pl.ds(pl.multiple_of(64 * (1 - z), 64), 64), :] = part_ref[...]
+
+
+def far_columns(whole_ref, weight_ref, far_ref, transposed):
     @pl.loop(0, far_ref.shape[1] // tile)
     def _(j):
         start = pl.multiple_of(j * tile, tile)
         far_ref[:, pl.ds(start, tile)] = product(
             whole_ref[256:, :], columns_of(weight_ref, start, transposed), transposed
         )
+
+
+def far_hidden_kernel(index_ref, *refs):
+    pieces, weight_ref, whole_ref, far_ref = refs[:4], refs[4], refs[5], refs[6]
+    x, z = place(index_ref)
+    for step in range(4):
+        whole_ref[block(x, step, 128), :] = pieces[step][...]
+    far_columns(whole_ref, weight_ref, far_ref, False)
+
+
+def far_grad_kernel(index_ref, own_ref, part_ref, weight_ref, whole_ref, far_ref):
+    x, z = place(index_ref)
+    for step in range(4):
+        rows = slice(64 * step, 64 * step + 64)
+        whole_ref[block(x, step, 64, 64 * z), :] = own_ref[rows, :]
+        whole_ref[block(x, step, 64, 64 * (1 - z)), :] = part_ref[rows, :]
+    far_columns(whole_ref, weight_ref, far_ref, True)
 
 
 def near_kernel(transposed, whole_ref, weight_ref, far_ref, mine_ref, *refs):
@@ -199,16 +262,17 @@
         out[...] = total.astype(bf16)
 
 
-def units_far(part, gathered, weight):
-    units = gathered.shape[2]
-    width = weight.shape[0] if part else weight.shape[1]
+def units_far(kernel, name, index, pieces, weight, transposed):
+    units = pieces[0].shape[1]
+    width = weight.shape[0] if transposed else weight.shape[1]
     whole, far = call(
-        functools.partial(far_kernel, part, bool(part)),
-        "far_grad" if part else "far_hidden",
+        kernel,
+        name,
         [((512, units), bf16), ((256, width), f32)],
-        [gathered, weight],
+        [index] + pieces + [weight],
         flops=2 * 256 * width * units,
         moved=6 * 2**20,
+        scalars=1,
     )
     return whole, other_core(far)
 
@@ -241,22 +305,73 @@
     )
     planes = [[column] + [from_y(column, step) for step in steps] for column in columns]
     near = stack(planes[0], "plane")
-    all_inputs, preact, sends = width_product(0, index, near, other_core(near), w_in, [])
-    near = stack(planes[1], "plane")
-    all_grads, grad_hidden, sends = width_product(
-        1, index, near, other_core(near), w_out, [sends]
-    )
-    (shares,) = call(
+    width_flops = 2 * 512 * width * units
+    all_inputs, own, *sends = call(
+        width_inputs_kernel,
+        "width_inputs",
+        [((512, width), bf16), ((128, units), f32)] + [((128, units), bf16)] * 3,
+        [index, near, other_core(near), w_in],
+        scratch=[((512, tile), f32)],
+        flops=width_flops,
+        moved=6 * 2**20,
+        scalars=1,
+    )
+    mine, send = call(
+        sum_x_kernel,
+        "sum_x",
+        [((64, units), f32)] * 2,
+        [index, own] + [to_x(send, step) for step, send in zip(steps, sends)],
+        moved=2**20,
+        scalars=1,
+    )
+    hidden, slope = call(
         activation_kernel,
         "activation",
-        [((8, 128, units), bf16)],
-        [index, over_gz(sends), preact, grad_hidden],
-        moved=4 * 2**20,
+        [((64, units), bf16), ((64, units), f32)],
+        [mine, other_z(send)],
+        moved=2**20,
+    )
+    near = stack(planes[1], "plane")
+    all_grads, own, send = call(
+        width_grad_kernel,
+        "width_grad",
+        [((512, width), bf16), ((256, units), f32), ((256, units), bf16)],
+        [index, near, other_core(near), w_out],
+        scratch=[((512, tile), f32)],
+        flops=width_flops,
+        moved=6 * 2**20,
         scalars=1,
     )
-    gathered = over_gz(shares)
-    hidden_all, far_hidden = units_far(0, gathered, w_out)
-    grad_pre_all, far_grad = units_far(1, gathered, w_in)
+    mine, *sends = call(
+        sum_z_kernel,
+        "sum_z",
+        [((64, units), f32)] + [((64, units), bf16)] * 3,
+        [own, other_z(send)],
+        moved=2**20,
+    )
+    (pair,) = call(
+        pair_z_kernel,
+        "pair_z",
+        [((128, units), bf16)],
+        [index, hidden, other_z(hidden)],
+        moved=2**19,
+        scalars=1,
+    )
+    (grad_pre,) = call(
+        grad_pre_kernel,
+        "grad_pre",
+        [((64, units), bf16)],
+        [mine] + [to_x(send, step) for step, send in zip(steps, sends)] + [slope],
+        moved=2**20,
+    )
+    hidden_pieces = [pair] + [from_x(pair, step) for step in steps]
+    grad_stack = stack([grad_pre] + [from_x(grad_pre, step) for step in steps], "grad_stack")
+    hidden_all, far_hidden = units_far(
+        far_hidden_kernel, "far_hidden", index, hidden_pieces, w_out, False
+    )
+    grad_pre_all, far_grad = units_far(
+        far_grad_kernel, "far_grad", index, [grad_stack, other_z(grad_stack)], w_in, True
+    )
     mine_hidden, parts_hidden = units_near(0, hidden_all, w_out, far_hidden)
     mine_grad, parts_grad = units_near(1, grad_pre_all, w_in, far_grad)
     mine, *sends = call(

time: 146 us -> 142 us (0.973)
  blocking collectives: 51.7 us -> 0 us
  starting transfers between devices: 41.8 us -> 65.7 us
  waiting for transfers between devices: 26.6 us -> 49.8 us
    all_to_all x2 -> x0, blocking collectives: 51.7 us -> none  [over_gz(): return lax.all_to_all(value, 'gz', 0, 0, tiled=True)]
    ppermute x0 -> x16, starting transfers between devices: none -> 23.9 us  [the longest x6 11.3 us: to_x(): lax.ppermute(value, 'gz', [(i, (i + 2 * step) % 8) for i in range(8)])]
    ppermute x0 -> x16, waiting for transfers between devices: none -> 23 us  [the longest x6 13.6 us: from_x(): lax.ppermute(value, 'gz', [((i + 2 * step) % 8, i) for i in range(8)])]
    pallas_call x13 -> x18, Pallas kernels: 15.8 us -> 16.2 us  [call(): pl.pallas_call(kernel, out_shape=[jax.ShapeDtypeStruct(*out) for out in o...]
  transfers between devices with their start and end apart: 22 -> 38, of which waited for: 13 -> 24; matrix products, arithmetic and copies ran while one was open for 4% -> 4% of each run, Pallas kernels for 7% -> 11%
where the time goes in v4:
time: 142 us; the launch traced here: 140 us
  starting transfers between devices  65.7 us (46%)
  waiting for transfers between devices  49.8 us (35%)
  Pallas kernels  16.2 us (11%)
  matrix products  5.65 us (4%)
  local copies, waits for them, and re-layouts  1.6 us (1%)
    pallas_call x18, Pallas kernels, call(): pl.pallas_call(kernel, out_shape=[jax.ShapeDtypeStruct(*out) for out in o...  16.2 us
    ppermute x6, starting transfers between devices, to_y(): lax.ppermute(value, 'gy', [(i, (i + 2 * step) % 8) for i in range(8)])  14.3 us
    ppermute x6, waiting for transfers between devices, from_x(): lax.ppermute(value, 'gz', [((i + 2 * step) % 8, i) for i in range(8)])  13.6 us
    ppermute x6, waiting for transfers between devices, from_y(): lax.ppermute(value, 'gy', [((i + 2 * step) % 8, i) for i in range(8)])  11.6 us
    ppermute x6, starting transfers between devices, to_x(): lax.ppermute(value, 'gz', [(i, (i + 2 * step) % 8) for i in range(8)])  11.3 us
    ppermute x3, starting transfers between devices, from_gx(): return lax.ppermute(value, 'gx', [((i + step) % 4, i) for i in range(4)])  10.2 us
    ppermute x3, starting transfers between devices, to_gx(): return lax.ppermute(value, 'gx', [(i, (i + step) % 4) for i in range(4)])  9.94 us
    ppermute x6, waiting for transfers between devices, to_x(): lax.ppermute(value, 'gz', [(i, (i + 2 * step) % 8) for i in range(8)])  9.18 us
  transfers between devices with their start and end apart: 38, of which 24 were waited for; matrix products, arithmetic and copies ran while one was open for 4% of the time, Pallas kernels for 11%

profile of v4, /device:TPU:8, one launch (start us, length us, event | category | flops | bytes accessed | tf_op | source)
XLA Modules:
  0.0 139.7 jit_solution(573182144133533169)
XLA Ops:
  2.2 6.4 %collective-permute-start = (bf16[32,1536]{1,0:T(8,128)(2,1)S(1)}, bf16[32,1536]{1,0:T(8,128)(2,1)S(1)}, u32[]{:S(2)}, u32[]{:S(2)}) collective-permute-start(bf16[32,1536]{1,0:T(8,128)(2,1)S(1)} %pair.1.both_ref), channel_id=1, source_target_pairs={{64,0},{128,64},{192,128},{0,192},{65,1},{129,65},{193,129},{1,193... | collective-permute-start | bytes 294920 | tf_op jit(solution)/shard_map/ppermute | solution.py:28
  9.6 2.8 %collective-permute-start.2 = (bf16[32,1536]{1,0:T(8,128)(2,1)S(1)}, bf16[32,1536]{1,0:T(8,128)(2,1)S(1)}, u32[]{:S(2)}, u32[]{:S(2)}) collective-permute-start(bf16[32,1536]{1,0:T(8,128)(2,1)S(1)} %pair.1.both_ref), channel_id=1, source_target_pairs={{192,0},{0,64},{64,128},{128,192},{193,1},{1,65},{65,129},{129,193... | collective-permute-start | bytes 294920 | tf_op jit(solution)/shard_map/ppermute | solution.py:28
  12.4 4.6 %collective-permute-done.first_ref = bf16[32,1536]{1,0:T(8,128)(2,1)S(1)} collective-permute-done((bf16[32,1536]{1,0:T(8,128)(2,1)S(1)}, bf16[32,1536]{1,0:T(8,128)(2,1)S(1)}, u32[]{:S(2)}, u32[]{:S(2)}) %collective-permute-start) | collective-permute-done | bytes 98336 | tf_op jit(solution)/shard_map/ppermute | solution.py:28
  17.0 3.2 %collective-permute-done.1.second_ref = bf16[32,1536]{1,0:T(8,128)(2,1)S(1)} collective-permute-done((bf16[32,1536]{1,0:T(8,128)(2,1)S(1)}, bf16[32,1536]{1,0:T(8,128)(2,1)S(1)}, u32[]{:S(2)}, u32[]{:S(2)}) %collective-permute-start.1) | collective-permute-done | bytes 98336 | tf_op jit(solution)/shard_map/ppermute | solution.py:28
  21.0 2.4 %collective-permute-start.20 = (bf16[64,1536]{1,0:T(8,128)(2,1)S(1)}, bf16[64,1536]{1,0:T(8,128)(2,1)S(1)}, u32[]{:S(2)}, u32[]{:S(2)}) collective-permute-start(bf16[64,1536]{1,0:T(8,128)(2,1)S(1)} %get-tuple-element.54.refs_0_), channel_id=1, source_target_pairs={{32,0},{40,8},{48,16},{56,24},{0,32},{8,40},{16,48},{24,56},{33,1}... | collective-permute-start | bytes 589832 | tf_op jit(solution)/shard_map/ppermute | solution.py:40
  23.4 1.9 %collective-permute-start.21 = (bf16[64,1536]{1,0:T(8,128)(2,1)S(1)}, bf16[64,1536]{1,0:T(8,128)(2,1)S(1)}, u32[]{:S(2)}, u32[]{:S(2)}) collective-permute-start(bf16[64,1536]{1,0:T(8,128)(2,1)S(1)} %get-tuple-element.54.refs_0_), channel_id=1, source_target_pairs={{48,0},{56,8},{0,16},{8,24},{16,32},{24,40},{32,48},{40,56},{49,1}... | collective-permute-start | bytes 589832 | tf_op jit(solution)/shard_map/ppermute | solution.py:40
  26.7 2.8 %collective-permute-done.19.refs_1_ = bf16[64,1536]{1,0:T(8,128)(2,1)S(1)} collective-permute-done((bf16[64,1536]{1,0:T(8,128)(2,1)S(1)}, bf16[64,1536]{1,0:T(8,128)(2,1)S(1)}, u32[]{:S(2)}, u32[]{:S(2)}) %collective-permute-start.19) | collective-permute-done | bytes 196640 | tf_op jit(solution)/shard_map/ppermute | solution.py:40
  29.8 3.7 %collective-permute-done.20.refs_2_ = bf16[64,1536]{1,0:T(8,128)(2,1)S(1)} collective-permute-done((bf16[64,1536]{1,0:T(8,128)(2,1)S(1)}, bf16[64,1536]{1,0:T(8,128)(2,1)S(1)}, u32[]{:S(2)}, u32[]{:S(2)}) %collective-permute-start.20) | collective-permute-done | bytes 196640 | tf_op jit(solution)/shard_map/ppermute | solution.py:40
  35.7 2.1 %collective-permute-done.4.refs_2_ = bf16[64,1536]{1,0:T(8,128)(2,1)S(1)} collective-permute-done((bf16[64,1536]{1,0:T(8,128)(2,1)S(1)}, bf16[64,1536]{1,0:T(8,128)(2,1)S(1)}, u32[]{:S(2)}, u32[]{:S(2)}) %collective-permute-start.4) | collective-permute-done | bytes 196640 | tf_op jit(solution)/shard_map/ppermute | solution.py:40
  39.6 3.3 %width_grad.1 = (bf16[512,1536]{1,0:T(8,128)(2,1)S(1)}, f32[256,768]{1,0:T(8,128)S(1)}, bf16[256,768]{1,0:T(8,128)(2,1)S(1)}) custom-call(s32[1]{0:T(128)} %bitcast.index_ref, bf16[256,1536]{1,0:T(8,128)(2,1)S(1)} %plane.3.near_ref, bf16[256,1536]{1,0:T(8,128)(2,1)} %collective-permute-done.22.far_ref, bf16[768,1536]{1,0:T(8,128)(2,1)S(1)} %copy-done), custom_call_target="tpu_custom_call" | custom-call | flops 1207959552 | bytes 6291456 | tf_op jit(solution)/shard_map/width_grad/pallas_call | solution.py:72
  43.0 2.7 %collective-permute-start.23 = (bf16[256,768]{1,0:T(8,128)(2,1)S(1)}, bf16[256,768]{1,0:T(8,128)(2,1)S(1)}, u32[]{:S(2)}, u32[]{:S(2)}) collective-permute-start(bf16[256,768]{1,0:T(8,128)(2,1)S(1)} %get-tuple-element.56), channel_id=1, source_target_pairs={{0,1},{1,0},{2,3},{3,2},{4,5},{5,4},{6,7},{7,6},{8,9},{9,8},{10,11... | collective-permute-start | bytes 1179656 | tf_op jit(solution)/shard_map/ppermute | solution.py:56
  45.7 3.4 %width_inputs.1 = (bf16[512,1536]{1,0:T(8,128)(2,1)S(1)}, f32[128,768]{1,0:T(8,128)S(1)}, bf16[128,768]{1,0:T(8,128)(2,1)S(1)}, bf16[128,768]{1,0:T(8,128)(2,1)S(1)}, bf16[128,768]{1,0:T(8,128)(2,1)S(1)}) custom-call(s32[1]{0:T(128)} %bitcast.index_ref, bf16[256,1536]{1,0:T(8,128)(2,1)} %plane.2.near_ref, bf16[256,1536]{1,0:T(8,128)(2,1)} %collective-permute-done.6.far_ref, ...), custom_call_target="tpu_custom_call" | custom-call | flops 1207959552 | bytes 6291456 | tf_op jit(solution)/shard_map/width_inputs/pallas_call | solution.py:72
  50.7 2.7 %collective-permute-start.8 = (bf16[128,768]{1,0:T(8,128)(2,1)S(1)}, bf16[128,768]{1,0:T(8,128)(2,1)S(1)}, u32[]{:S(2)}, u32[]{:S(2)}) collective-permute-start(bf16[128,768]{1,0:T(8,128)(2,1)S(1)} %get-tuple-element.43), channel_id=1, source_target_pairs={{0,4},{1,5},{2,6},{3,7},{4,0},{5,1},{6,2},{7,3},{8,12},{9,13},{10,... | collective-permute-start | bytes 589832 | tf_op jit(solution)/shard_map/ppermute | solution.py:52
  54.8 2.6 %collective-permute-done.7.first_ref = bf16[128,768]{1,0:T(8,128)(2,1)S(1)} collective-permute-done((bf16[128,768]{1,0:T(8,128)(2,1)S(1)}, bf16[128,768]{1,0:T(8,128)(2,1)S(1)}, u32[]{:S(2)}, u32[]{:S(2)}) %collective-permute-start.7) | collective-permute-done | bytes 196640 | tf_op jit(solution)/shard_map/ppermute | solution.py:52
  57.4 5.2 %collective-permute-done.8.second_ref = bf16[128,768]{1,0:T(8,128)(2,1)S(1)} collective-permute-done((bf16[128,768]{1,0:T(8,128)(2,1)S(1)}, bf16[128,768]{1,0:T(8,128)(2,1)S(1)}, u32[]{:S(2)}, u32[]{:S(2)}) %collective-permute-start.8) | collective-permute-done | bytes 196640 | tf_op jit(solution)/shard_map/ppermute | solution.py:52
  64.9 2.4 %collective-permute-start.25 = (bf16[64,768]{1,0:T(8,128)(2,1)S(1)}, bf16[64,768]{1,0:T(8,128)(2,1)S(1)}, u32[]{:S(2)}, u32[]{:S(2)}) collective-permute-start(bf16[64,768]{1,0:T(8,128)(2,1)S(1)} %get-tuple-element.59), channel_id=1, source_target_pairs={{0,4},{1,5},{2,6},{3,7},{4,0},{5,1},{6,2},{7,3},{8,12},{9,13},{10,... | collective-permute-start | bytes 294920 | tf_op jit(solution)/shard_map/ppermute | solution.py:52
  72.3 2.7 %collective-permute-start.27 = (bf16[64,768]{1,0:T(8,128)(2,1)S(1)}, bf16[64,768]{1,0:T(8,128)(2,1)S(1)}, u32[]{:S(2)}, u32[]{:S(2)}) collective-permute-start(bf16[64,768]{1,0:T(8,128)(2,1)S(1)} %grad_pre.1.refs_0_), channel_id=1, source_target_pairs={{2,0},{3,1},{4,2},{5,3},{6,4},{7,5},{0,6},{1,7},{10,8},{11,9},{12,... | collective-permute-start | bytes 294920 | tf_op jit(solution)/shard_map/ppermute | solution.py:48
  76.0 2.2 %collective-permute-done.27.refs_1_ = bf16[64,768]{1,0:T(8,128)(2,1)S(1)} collective-permute-done((bf16[64,768]{1,0:T(8,128)(2,1)S(1)}, bf16[64,768]{1,0:T(8,128)(2,1)S(1)}, u32[]{:S(2)}, u32[]{:S(2)}) %collective-permute-start.27) | collective-permute-done | bytes 98336 | tf_op jit(solution)/shard_map/ppermute | solution.py:48
  78.3 3.0 %collective-permute-done.28.refs_2_ = bf16[64,768]{1,0:T(8,128)(2,1)S(1)} collective-permute-done((bf16[64,768]{1,0:T(8,128)(2,1)S(1)}, bf16[64,768]{1,0:T(8,128)(2,1)S(1)}, u32[]{:S(2)}, u32[]{:S(2)}) %collective-permute-start.28) | collective-permute-done | bytes 98336 | tf_op jit(solution)/shard_map/ppermute | solution.py:48
  86.4 3.3 %collective-permute-done.12.refs_1_ = bf16[128,768]{1,0:T(8,128)(2,1)S(1)} collective-permute-done((bf16[128,768]{1,0:T(8,128)(2,1)S(1)}, bf16[128,768]{1,0:T(8,128)(2,1)S(1)}, u32[]{:S(2)}, u32[]{:S(2)}) %collective-permute-start.12) | collective-permute-done | bytes 196640 | tf_op jit(solution)/shard_map/ppermute | solution.py:48
  89.7 2.2 %collective-permute-done.13.refs_2_ = bf16[128,768]{1,0:T(8,128)(2,1)S(1)} collective-permute-done((bf16[128,768]{1,0:T(8,128)(2,1)S(1)}, bf16[128,768]{1,0:T(8,128)(2,1)S(1)}, u32[]{:S(2)}, u32[]{:S(2)}) %collective-permute-start.13) | collective-permute-done | bytes 196640 | tf_op jit(solution)/shard_map/ppermute | solution.py:48
  91.9 2.0 %collective-permute-done.14.refs_3_ = bf16[128,768]{1,0:T(8,128)(2,1)S(1)} collective-permute-done((bf16[128,768]{1,0:T(8,128)(2,1)S(1)}, bf16[128,768]{1,0:T(8,128)(2,1)S(1)}, u32[]{:S(2)}, u32[]{:S(2)}) %collective-permute-start.14) | collective-permute-done | bytes 196640 | tf_op jit(solution)/shard_map/ppermute | solution.py:48
  102.3 3.5 %collective-permute-start.17 = (bf16[64,1536]{1,0:T(8,128)(2,1)S(1)}, bf16[64,1536]{1,0:T(8,128)(2,1)S(1)}, u32[]{:S(2)}, u32[]{:S(2)}) collective-permute-start(bf16[64,1536]{1,0:T(8,128)(2,1)S(1)} %get-tuple-element.52), channel_id=1, source_target_pairs={{0,32},{8,40},{16,48},{24,56},{32,0},{40,8},{48,16},{56,24},{1,33}... | collective-permute-start | bytes 589832 | tf_op jit(solution)/shard_map/ppermute | solution.py:44
  107.6 2.1 %collective-permute-start.32 = (bf16[64,1536]{1,0:T(8,128)(2,1)S(1)}, bf16[64,1536]{1,0:T(8,128)(2,1)S(1)}, u32[]{:S(2)}, u32[]{:S(2)}) collective-permute-start(bf16[64,1536]{1,0:T(8,128)(2,1)S(1)} %get-tuple-element.65), channel_id=1, source_target_pairs={{0,16},{8,24},{16,32},{24,40},{32,48},{40,56},{48,0},{56,8},{1,17}... | collective-permute-start | bytes 589832 | tf_op jit(solution)/shard_map/ppermute | solution.py:44
  111.0 5.9 %collective-permute-start.34 = (bf16[64,1536]{1,0:T(8,128)(2,1)S(1)}, bf16[64,1536]{1,0:T(8,128)(2,1)S(1)}, u32[]{:S(2)}, u32[]{:S(2)}) collective-permute-start(bf16[64,1536]{1,0:T(8,128)(2,1)S(1)} %get-tuple-element.67), channel_id=1, source_target_pairs={{0,48},{8,56},{16,0},{24,8},{32,16},{40,24},{48,32},{56,40},{1,49}... | collective-permute-start | bytes 589832 | tf_op jit(solution)/shard_map/ppermute | solution.py:44
  116.9 2.8 %convolution_convert_fusion = bf16[768,1536]{1,0:T(8,128)(2,1)} fusion(bf16[512,768]{1,0:T(8,128)(2,1)S(1)} %get-tuple-element.48.whole_ref, bf16[512,1536]{1,0:T(8,128)(2,1)S(1)} %get-tuple-element.75), kind=kOutput, calls=%fused_computation | convolution fusion | flops 1209139200 | bytes 4718592 | tf_op jit(solution)/shard_map/dot_general | solution.py:391
  120.0 3.3 %collective-permute-done.34.refs_7_ = bf16[64,1536]{1,0:T(8,128)(2,1)S(1)} collective-permute-done((bf16[64,1536]{1,0:T(8,128)(2,1)S(1)}, bf16[64,1536]{1,0:T(8,128)(2,1)S(1)}, u32[]{:S(2)}, u32[]{:S(2)}) %collective-permute-start.34) | collective-permute-done | bytes 196640 | tf_op jit(solution)/shard_map/ppermute | solution.py:44
  123.5 2.7 %collective-permute-start.35 = (bf16[32,1536]{1,0:T(8,128)(2,1)S(1)}, bf16[32,1536]{1,0:T(8,128)(2,1)S(1)}, u32[]{:S(2)}, u32[]{:S(2)}) collective-permute-start(bf16[32,1536]{1,0:T(8,128)(2,1)S(1)} %get-tuple-element.69), channel_id=1, source_target_pairs={{0,64},{64,128},{128,192},{192,0},{1,65},{65,129},{129,193},{193,1... | collective-permute-start | bytes 294920 | tf_op jit(solution)/shard_map/ppermute | solution.py:32
  126.2 4.0 %collective-permute-start.36 = (bf16[32,1536]{1,0:T(8,128)(2,1)S(1)}, bf16[32,1536]{1,0:T(8,128)(2,1)S(1)}, u32[]{:S(2)}, u32[]{:S(2)}) collective-permute-start(bf16[32,1536]{1,0:T(8,128)(2,1)S(1)} %get-tuple-element.70), channel_id=1, source_target_pairs={{0,128},{64,192},{128,0},{192,64},{1,129},{65,193},{129,1},{193,65... | collective-permute-start | bytes 294920 | tf_op jit(solution)/shard_map/ppermute | solution.py:32
  130.2 3.2 %collective-permute-start.37 = (bf16[32,1536]{1,0:T(8,128)(2,1)S(1)}, bf16[32,1536]{1,0:T(8,128)(2,1)S(1)}, u32[]{:S(2)}, u32[]{:S(2)}) collective-permute-start(bf16[32,1536]{1,0:T(8,128)(2,1)S(1)} %get-tuple-element.71), channel_id=1, source_target_pairs={{0,192},{64,0},{128,64},{192,128},{1,193},{65,1},{129,65},{193,129... | collective-permute-start | bytes 294920 | tf_op jit(solution)/shard_map/ppermute | solution.py:32
  133.4 2.8 %convolution_convert_fusion.1 = bf16[1536,768]{1,0:T(8,128)(2,1)} fusion(bf16[512,1536]{1,0:T(8,128)(2,1)S(1)} %get-tuple-element.74, bf16[512,768]{1,0:T(8,128)(2,1)S(1)} %get-tuple-element.62.whole_ref), kind=kOutput, calls=%fused_computation.1 | convolution fusion | flops 1209139200 | bytes 4718592 | tf_op jit(solution)/shard_map/dot_general | solution.py:394
  137.2 1.9 %collective-permute-done.37.third_ref = bf16[32,1536]{1,0:T(8,128)(2,1)S(1)} collective-permute-done((bf16[32,1536]{1,0:T(8,128)(2,1)S(1)}, bf16[32,1536]{1,0:T(8,128)(2,1)S(1)}, u32[]{:S(2)}, u32[]{:S(2)}) %collective-permute-start.37) | collective-permute-done | bytes 98336 | tf_op jit(solution)/shard_map/ppermute | solution.py:32
  (72 shorter events, 38.9 us)
Async XLA Ops:
  2.2 14.8 %collective-permute-start = (bf16[32,1536]{1,0:T(8,128)(2,1)S(1)}, bf16[32,1536]{1,0:T(8,128)(2,1)S(1)}, u32[]{:S(2)}, u32[]{:S(2)}) collective-permute-start(bf16[32,1536]{1,0:T(8,128)(2,1)S(1)} %pair.1.both_ref), channel_id=1, source_target_pairs={{64,0},{128,64},{192,128},{0,192},{65,1},{129,65},{193,129},{1,193... | collective-permute-start | bytes 294920 | tf_op jit(solution)/shard_map/ppermute | solution.py:28
  8.6 11.6 %collective-permute-start.1 = (bf16[32,1536]{1,0:T(8,128)(2,1)S(1)}, bf16[32,1536]{1,0:T(8,128)(2,1)S(1)}, u32[]{:S(2)}, u32[]{:S(2)}) collective-permute-start(bf16[32,1536]{1,0:T(8,128)(2,1)S(1)} %pair.1.both_ref), channel_id=1, source_target_pairs={{128,0},{192,64},{0,128},{64,192},{129,1},{193,65},{1,129},{65,193... | collective-permute-start | bytes 294920 | tf_op jit(solution)/shard_map/ppermute | solution.py:28
  9.6 10.6 %collective-permute-start.2 = (bf16[32,1536]{1,0:T(8,128)(2,1)S(1)}, bf16[32,1536]{1,0:T(8,128)(2,1)S(1)}, u32[]{:S(2)}, u32[]{:S(2)}) collective-permute-start(bf16[32,1536]{1,0:T(8,128)(2,1)S(1)} %pair.1.both_ref), channel_id=1, source_target_pairs={{192,0},{0,64},{64,128},{128,192},{193,1},{1,65},{65,129},{129,193... | collective-permute-start | bytes 294920 | tf_op jit(solution)/shard_map/ppermute | solution.py:28
  20.3 9.3 %collective-permute-start.19 = (bf16[64,1536]{1,0:T(8,128)(2,1)S(1)}, bf16[64,1536]{1,0:T(8,128)(2,1)S(1)}, u32[]{:S(2)}, u32[]{:S(2)}) collective-permute-start(bf16[64,1536]{1,0:T(8,128)(2,1)S(1)} %get-tuple-element.54.refs_0_), channel_id=1, source_target_pairs={{16,0},{24,8},{32,16},{40,24},{48,32},{56,40},{0,48},{8,56},{17,1}... | collective-permute-start | bytes 589832 | tf_op jit(solution)/shard_map/ppermute | solution.py:40
  21.0 12.5 %collective-permute-start.20 = (bf16[64,1536]{1,0:T(8,128)(2,1)S(1)}, bf16[64,1536]{1,0:T(8,128)(2,1)S(1)}, u32[]{:S(2)}, u32[]{:S(2)}) collective-permute-start(bf16[64,1536]{1,0:T(8,128)(2,1)S(1)} %get-tuple-element.54.refs_0_), channel_id=1, source_target_pairs={{32,0},{40,8},{48,16},{56,24},{0,32},{8,40},{16,48},{24,56},{33,1}... | collective-permute-start | bytes 589832 | tf_op jit(solution)/shard_map/ppermute | solution.py:40
  23.4 11.1 %collective-permute-start.21 = (bf16[64,1536]{1,0:T(8,128)(2,1)S(1)}, bf16[64,1536]{1,0:T(8,128)(2,1)S(1)}, u32[]{:S(2)}, u32[]{:S(2)}) collective-permute-start(bf16[64,1536]{1,0:T(8,128)(2,1)S(1)} %get-tuple-element.54.refs_0_), channel_id=1, source_target_pairs={{48,0},{56,8},{0,16},{8,24},{16,32},{24,40},{32,48},{40,56},{49,1}... | collective-permute-start | bytes 589832 | tf_op jit(solution)/shard_map/ppermute | solution.py:40
  25.3 10.5 %collective-permute-start.3 = (bf16[64,1536]{1,0:T(8,128)(2,1)S(1)}, bf16[64,1536]{1,0:T(8,128)(2,1)S(1)}, u32[]{:S(2)}, u32[]{:S(2)}) collective-permute-start(bf16[64,1536]{1,0:T(8,128)(2,1)S(1)} %get-tuple-element.40.refs_0_), channel_id=1, source_target_pairs={{16,0},{24,8},{32,16},{40,24},{48,32},{56,40},{0,48},{8,56},{17,1}... | collective-permute-start | bytes 589832 | tf_op jit(solution)/shard_map/ppermute | solution.py:40
  25.4 12.5 %collective-permute-start.4 = (bf16[64,1536]{1,0:T(8,128)(2,1)S(1)}, bf16[64,1536]{1,0:T(8,128)(2,1)S(1)}, u32[]{:S(2)}, u32[]{:S(2)}) collective-permute-start(bf16[64,1536]{1,0:T(8,128)(2,1)S(1)} %get-tuple-element.40.refs_0_), channel_id=1, source_target_pairs={{32,0},{40,8},{48,16},{56,24},{0,32},{8,40},{16,48},{24,56},{33,1}... | collective-permute-start | bytes 589832 | tf_op jit(solution)/shard_map/ppermute | solution.py:40
  29.6 9.1 %collective-permute-start.5 = (bf16[64,1536]{1,0:T(8,128)(2,1)S(1)}, bf16[64,1536]{1,0:T(8,128)(2,1)S(1)}, u32[]{:S(2)}, u32[]{:S(2)}) collective-permute-start(bf16[64,1536]{1,0:T(8,128)(2,1)S(1)} %get-tuple-element.40.refs_0_), channel_id=1, source_target_pairs={{48,0},{56,8},{0,16},{8,24},{16,32},{24,40},{32,48},{40,56},{49,1}... | collective-permute-start | bytes 589832 | tf_op jit(solution)/shard_map/ppermute | solution.py:40
  43.0 20.1 %collective-permute-start.23 = (bf16[256,768]{1,0:T(8,128)(2,1)S(1)}, bf16[256,768]{1,0:T(8,128)(2,1)S(1)}, u32[]{:S(2)}, u32[]{:S(2)}) collective-permute-start(bf16[256,768]{1,0:T(8,128)(2,1)S(1)} %get-tuple-element.56), channel_id=1, source_target_pairs={{0,1},{1,0},{2,3},{3,2},{4,5},{5,4},{6,7},{7,6},{8,9},{9,8},{10,11... | collective-permute-start | bytes 1179656 | tf_op jit(solution)/shard_map/ppermute | solution.py:56
  49.1 8.3 %collective-permute-start.7 = (bf16[128,768]{1,0:T(8,128)(2,1)S(1)}, bf16[128,768]{1,0:T(8,128)(2,1)S(1)}, u32[]{:S(2)}, u32[]{:S(2)}) collective-permute-start(bf16[128,768]{1,0:T(8,128)(2,1)S(1)} %get-tuple-element.42), channel_id=1, source_target_pairs={{0,2},{1,3},{2,4},{3,5},{4,6},{5,7},{6,0},{7,1},{8,10},{9,11},{10,... | collective-permute-start | bytes 589832 | tf_op jit(solution)/shard_map/ppermute | solution.py:52
  50.7 11.9 %collective-permute-start.8 = (bf16[128,768]{1,0:T(8,128)(2,1)S(1)}, bf16[128,768]{1,0:T(8,128)(2,1)S(1)}, u32[]{:S(2)}, u32[]{:S(2)}) collective-permute-start(bf16[128,768]{1,0:T(8,128)(2,1)S(1)} %get-tuple-element.43), channel_id=1, source_target_pairs={{0,4},{1,5},{2,6},{3,7},{4,0},{5,1},{6,2},{7,3},{8,12},{9,13},{10,... | collective-permute-start | bytes 589832 | tf_op jit(solution)/shard_map/ppermute | solution.py:52
  53.4 9.2 %collective-permute-start.9 = (bf16[128,768]{1,0:T(8,128)(2,1)S(1)}, bf16[128,768]{1,0:T(8,128)(2,1)S(1)}, u32[]{:S(2)}, u32[]{:S(2)}) collective-permute-start(bf16[128,768]{1,0:T(8,128)(2,1)S(1)} %get-tuple-element.44), channel_id=1, source_target_pairs={{0,6},{1,7},{2,0},{3,1},{4,2},{5,3},{6,4},{7,5},{8,14},{9,15},{10,... | collective-permute-start | bytes 589832 | tf_op jit(solution)/shard_map/ppermute | solution.py:52
  62.7 6.3 %collective-permute-start.10 = (f32[64,768]{1,0:T(8,128)S(1)}, f32[64,768]{1,0:T(8,128)S(1)}, u32[]{:S(2)}, u32[]{:S(2)}) collective-permute-start(f32[64,768]{1,0:T(8,128)S(1)} %get-tuple-element.46), channel_id=1, source_target_pairs={{0,1},{1,0},{2,3},{3,2},{4,5},{5,4},{6,7},{7,6},{8,9},{9,8},{10,11... | collective-permute-start | bytes 589832 | tf_op jit(solution)/shard_map/ppermute | solution.py:56
  63.3 7.5 %collective-permute-start.24 = (bf16[64,768]{1,0:T(8,128)(2,1)S(1)}, bf16[64,768]{1,0:T(8,128)(2,1)S(1)}, u32[]{:S(2)}, u32[]{:S(2)}) collective-permute-start(bf16[64,768]{1,0:T(8,128)(2,1)S(1)} %get-tuple-element.58), channel_id=1, source_target_pairs={{0,2},{1,3},{2,4},{3,5},{4,6},{5,7},{6,0},{7,1},{8,10},{9,11},{10,... | collective-permute-start | bytes 294920 | tf_op jit(solution)/shard_map/ppermute | solution.py:52
  64.9 6.9 %collective-permute-start.25 = (bf16[64,768]{1,0:T(8,128)(2,1)S(1)}, bf16[64,768]{1,0:T(8,128)(2,1)S(1)}, u32[]{:S(2)}, u32[]{:S(2)}) collective-permute-start(bf16[64,768]{1,0:T(8,128)(2,1)S(1)} %get-tuple-element.59), channel_id=1, source_target_pairs={{0,4},{1,5},{2,6},{3,7},{4,0},{5,1},{6,2},{7,3},{8,12},{9,13},{10,... | collective-permute-start | bytes 294920 | tf_op jit(solution)/shard_map/ppermute | solution.py:52
  69.2 6.8 %collective-permute-start.11 = (bf16[64,768]{1,0:T(8,128)(2,1)S(1)}, bf16[64,768]{1,0:T(8,128)(2,1)S(1)}, u32[]{:S(2)}, u32[]{:S(2)}) collective-permute-start(bf16[64,768]{1,0:T(8,128)(2,1)S(1)} %get-tuple-element.47.own_ref), channel_id=1, source_target_pairs={{0,1},{1,0},{2,3},{3,2},{4,5},{5,4},{6,7},{7,6},{8,9},{9,8},{10,11... | collective-permute-start | bytes 294920 | tf_op jit(solution)/shard_map/ppermute | solution.py:56
  75.0 6.2 %collective-permute-start.28 = (bf16[64,768]{1,0:T(8,128)(2,1)S(1)}, bf16[64,768]{1,0:T(8,128)(2,1)S(1)}, u32[]{:S(2)}, u32[]{:S(2)}) collective-permute-start(bf16[64,768]{1,0:T(8,128)(2,1)S(1)} %grad_pre.1.refs_0_), channel_id=1, source_target_pairs={{4,0},{5,1},{6,2},{7,3},{0,4},{1,5},{2,6},{3,7},{12,8},{13,9},{14,... | collective-permute-start | bytes 294920 | tf_op jit(solution)/shard_map/ppermute | solution.py:48
  75.6 6.6 %collective-permute-start.29 = (bf16[64,768]{1,0:T(8,128)(2,1)S(1)}, bf16[64,768]{1,0:T(8,128)(2,1)S(1)}, u32[]{:S(2)}, u32[]{:S(2)}) collective-permute-start(bf16[64,768]{1,0:T(8,128)(2,1)S(1)} %grad_pre.1.refs_0_), channel_id=1, source_target_pairs={{6,0},{7,1},{0,2},{1,3},{2,4},{3,5},{4,6},{5,7},{14,8},{15,9},{8,1... | collective-permute-start | bytes 294920 | tf_op jit(solution)/shard_map/ppermute | solution.py:48
  82.2 13.4 %collective-permute-start.30 = (bf16[256,768]{1,0:T(8,128)(2,1)S(1)}, bf16[256,768]{1,0:T(8,128)(2,1)S(1)}, u32[]{:S(2)}, u32[]{:S(2)}) collective-permute-start(bf16[256,768]{1,0:T(8,128)(2,1)S(1)} %grad_stack.1.own_ref), channel_id=1, source_target_pairs={{0,1},{1,0},{2,3},{3,2},{4,5},{5,4},{6,7},{7,6},{8,9},{9,8},{10,11... | collective-permute-start | bytes 1179656 | tf_op jit(solution)/shard_map/ppermute | solution.py:56
  84.6 7.3 %collective-permute-start.13 = (bf16[128,768]{1,0:T(8,128)(2,1)S(1)}, bf16[128,768]{1,0:T(8,128)(2,1)S(1)}, u32[]{:S(2)}, u32[]{:S(2)}) collective-permute-start(bf16[128,768]{1,0:T(8,128)(2,1)S(1)} %pair_z.1.refs_0_), channel_id=1, source_target_pairs={{4,0},{5,1},{6,2},{7,3},{0,4},{1,5},{2,6},{3,7},{12,8},{13,9},{14,... | collective-permute-start | bytes 589832 | tf_op jit(solution)/shard_map/ppermute | solution.py:48
  85.1 8.7 %collective-permute-start.14 = (bf16[128,768]{1,0:T(8,128)(2,1)S(1)}, bf16[128,768]{1,0:T(8,128)(2,1)S(1)}, u32[]{:S(2)}, u32[]{:S(2)}) collective-permute-start(bf16[128,768]{1,0:T(8,128)(2,1)S(1)} %pair_z.1.refs_0_), channel_id=1, source_target_pairs={{6,0},{7,1},{0,2},{1,3},{2,4},{3,5},{4,6},{5,7},{14,8},{15,9},{8,1... | collective-permute-start | bytes 589832 | tf_op jit(solution)/shard_map/ppermute | solution.py:48
  97.6 8.2 %collective-permute-start.31 = (f32[256,1536]{1,0:T(8,128)S(1)}, f32[256,1536]{1,0:T(8,128)S(1)}, u32[]{:S(2)}, u32[]{:S(2)}) collective-permute-start(f32[256,1536]{1,0:T(8,128)S(1)} %get-tuple-element.63), channel_id=1, source_target_pairs={{0,8},{8,0},{16,24},{24,16},{32,40},{40,32},{48,56},{56,48},{1,9},... | collective-permute-start | bytes 4718600 | tf_op jit(solution)/shard_map/ppermute | solution.py:36
  100.7 10.2 %collective-permute-start.16 = (bf16[64,1536]{1,0:T(8,128)(2,1)S(1)}, bf16[64,1536]{1,0:T(8,128)(2,1)S(1)}, u32[]{:S(2)}, u32[]{:S(2)}) collective-permute-start(bf16[64,1536]{1,0:T(8,128)(2,1)S(1)} %get-tuple-element.51), channel_id=1, source_target_pairs={{0,16},{8,24},{16,32},{24,40},{32,48},{40,56},{48,0},{56,8},{1,17}... | collective-permute-start | bytes 589832 | tf_op jit(solution)/shard_map/ppermute | solution.py:44
  102.3 17.4 %collective-permute-start.17 = (bf16[64,1536]{1,0:T(8,128)(2,1)S(1)}, bf16[64,1536]{1,0:T(8,128)(2,1)S(1)}, u32[]{:S(2)}, u32[]{:S(2)}) collective-permute-start(bf16[64,1536]{1,0:T(8,128)(2,1)S(1)} %get-tuple-element.52), channel_id=1, source_target_pairs={{0,32},{8,40},{16,48},{24,56},{32,0},{40,8},{48,16},{56,24},{1,33}... | collective-permute-start | bytes 589832 | tf_op jit(solution)/shard_map/ppermute | solution.py:44
  105.8 13.9 %collective-permute-start.18 = (bf16[64,1536]{1,0:T(8,128)(2,1)S(1)}, bf16[64,1536]{1,0:T(8,128)(2,1)S(1)}, u32[]{:S(2)}, u32[]{:S(2)}) collective-permute-start(bf16[64,1536]{1,0:T(8,128)(2,1)S(1)} %get-tuple-element.53), channel_id=1, source_target_pairs={{0,48},{8,56},{16,0},{24,8},{32,16},{40,24},{48,32},{56,40},{1,49}... | collective-permute-start | bytes 589832 | tf_op jit(solution)/shard_map/ppermute | solution.py:44
  107.6 12.1 %collective-permute-start.32 = (bf16[64,1536]{1,0:T(8,128)(2,1)S(1)}, bf16[64,1536]{1,0:T(8,128)(2,1)S(1)}, u32[]{:S(2)}, u32[]{:S(2)}) collective-permute-start(bf16[64,1536]{1,0:T(8,128)(2,1)S(1)} %get-tuple-element.65), channel_id=1, source_target_pairs={{0,16},{8,24},{16,32},{24,40},{32,48},{40,56},{48,0},{56,8},{1,17}... | collective-permute-start | bytes 589832 | tf_op jit(solution)/shard_map/ppermute | solution.py:44
  109.7 10.3 %collective-permute-start.33 = (bf16[64,1536]{1,0:T(8,128)(2,1)S(1)}, bf16[64,1536]{1,0:T(8,128)(2,1)S(1)}, u32[]{:S(2)}, u32[]{:S(2)}) collective-permute-start(bf16[64,1536]{1,0:T(8,128)(2,1)S(1)} %get-tuple-element.66), channel_id=1, source_target_pairs={{0,32},{8,40},{16,48},{24,56},{32,0},{40,8},{48,16},{56,24},{1,33}... | collective-permute-start | bytes 589832 | tf_op jit(solution)/shard_map/ppermute | solution.py:44
  111.0 12.4 %collective-permute-start.34 = (bf16[64,1536]{1,0:T(8,128)(2,1)S(1)}, bf16[64,1536]{1,0:T(8,128)(2,1)S(1)}, u32[]{:S(2)}, u32[]{:S(2)}) collective-permute-start(bf16[64,1536]{1,0:T(8,128)(2,1)S(1)} %get-tuple-element.67), channel_id=1, source_target_pairs={{0,48},{8,56},{16,0},{24,8},{32,16},{40,24},{48,32},{56,40},{1,49}... | collective-permute-start | bytes 589832 | tf_op jit(solution)/shard_map/ppermute | solution.py:44
  123.5 12.8 %collective-permute-start.35 = (bf16[32,1536]{1,0:T(8,128)(2,1)S(1)}, bf16[32,1536]{1,0:T(8,128)(2,1)S(1)}, u32[]{:S(2)}, u32[]{:S(2)}) collective-permute-start(bf16[32,1536]{1,0:T(8,128)(2,1)S(1)} %get-tuple-element.69), channel_id=1, source_target_pairs={{0,64},{64,128},{128,192},{192,0},{1,65},{65,129},{129,193},{193,1... | collective-permute-start | bytes 294920 | tf_op jit(solution)/shard_map/ppermute | solution.py:32
  126.2 11.0 %collective-permute-start.36 = (bf16[32,1536]{1,0:T(8,128)(2,1)S(1)}, bf16[32,1536]{1,0:T(8,128)(2,1)S(1)}, u32[]{:S(2)}, u32[]{:S(2)}) collective-permute-start(bf16[32,1536]{1,0:T(8,128)(2,1)S(1)} %get-tuple-element.70), channel_id=1, source_target_pairs={{0,128},{64,192},{128,0},{192,64},{1,129},{65,193},{129,1},{193,65... | collective-permute-start | bytes 294920 | tf_op jit(solution)/shard_map/ppermute | solution.py:32
  130.2 8.9 %collective-permute-start.37 = (bf16[32,1536]{1,0:T(8,128)(2,1)S(1)}, bf16[32,1536]{1,0:T(8,128)(2,1)S(1)}, u32[]{:S(2)}, u32[]{:S(2)}) collective-permute-start(bf16[32,1536]{1,0:T(8,128)(2,1)S(1)} %get-tuple-element.71), channel_id=1, source_target_pairs={{0,192},{64,0},{128,64},{192,128},{1,193},{65,1},{129,65},{193,129... | collective-permute-start | bytes 294920 | tf_op jit(solution)/shard_map/ppermute | solution.py:32
  (10 other events, 53.3 us)

commit v5 on v4

--- a/solution.py
+++ b/solution.py
@@ -24,6 +24,9 @@
     return (result, slope)
 
 
+barrier = lax.optimization_barrier
+
+
 def from_gx(value, step):
     return lax.ppermute(value, "gx", [((i + step) % 4, i) for i in range(4)])
 
@@ -67,7 +70,7 @@
     return weight_ref[:, pl.ds(start, tile)]
 
 
-def call(kernel, name, outs, args, scratch=(), flops=0, moved=0, scalars=0, aliases=None):
+def call(kernel, name, outs, args, scratch=(), moved=0, scalars=0, aliases=None):
     vmem = pl.BlockSpec(memory_space=pltpu.VMEM)
     return pl.pallas_call(
         kernel,
@@ -77,7 +80,7 @@
         scratch_shapes=[pltpu.VMEM(*shape) for shape in scratch],
         input_output_aliases=aliases or {},
         compiler_params=pltpu.CompilerParams(vmem_limit_bytes=8 * 2**20),
-        cost_estimate=pl.CostEstimate(flops=flops, bytes_accessed=moved, transcendentals=0),
+        cost_estimate=pl.CostEstimate(flops=0, bytes_accessed=moved, transcendentals=0),
         name=name,
     )(*args)
 
@@ -97,6 +100,11 @@
     rows = refs[0].shape[0]
     for i, piece in enumerate(refs[:4]):
         refs[4][rows * i : rows * (i + 1), :] = piece[...]
+
+
+def stack_two_kernel(*refs):
+    for i, piece in enumerate(refs[:4]):
+        refs[4 + i // 2][64 * (i % 2) : 64 * (i % 2) + 64, :] = piece[...]
 
 
 def stack(pieces, name):
@@ -215,12 +223,13 @@
     far_columns(whole_ref, weight_ref, far_ref, False)
 
 
-def far_grad_kernel(index_ref, own_ref, part_ref, weight_ref, whole_ref, far_ref):
+def far_grad_kernel(index_ref, *refs):
+    own, parts, weight_ref, whole_ref, far_ref = refs[:2], refs[2:4], refs[4], refs[5], refs[6]
     x, z = place(index_ref)
     for step in range(4):
-        rows = slice(64 * step, 64 * step + 64)
-        whole_ref[block(x, step, 64, 64 * z), :] = own_ref[rows, :]
-        whole_ref[block(x, step, 64, 64 * (1 - z)), :] = part_ref[rows, :]
+        rows = slice(64 * (step % 2), 64 * (step % 2) + 64)
+        whole_ref[block(x, step, 64, 64 * z), :] = own[step // 2][rows, :]
+        whole_ref[block(x, step, 64, 64 * (1 - z)), :] = parts[step // 2][rows, :]
     far_columns(whole_ref, weight_ref, far_ref, True)
 
 
@@ -270,7 +279,6 @@
         name,
         [((512, units), bf16), ((256, width), f32)],
         [index] + pieces + [weight],
-        flops=2 * 256 * width * units,
         moved=6 * 2**20,
         scalars=1,
     )
@@ -285,7 +293,6 @@
         [((64, width), f32)] + [((64, width), bf16)] * 3,
         [whole, weight, far],
         scratch=[((256, tile), f32)],
-        flops=2 * 256 * width * units,
         moved=6 * 2**20,
     )
     return mine, [to_y(send, step) for step, send in zip((1, 2, 3), sends)]
@@ -305,32 +312,16 @@
     )
     planes = [[column] + [from_y(column, step) for step in steps] for column in columns]
     near = stack(planes[0], "plane")
-    width_flops = 2 * 512 * width * units
     all_inputs, own, *sends = call(
         width_inputs_kernel,
         "width_inputs",
         [((512, width), bf16), ((128, units), f32)] + [((128, units), bf16)] * 3,
         [index, near, other_core(near), w_in],
         scratch=[((512, tile), f32)],
-        flops=width_flops,
         moved=6 * 2**20,
         scalars=1,
     )
-    mine, send = call(
-        sum_x_kernel,
-        "sum_x",
-        [((64, units), f32)] * 2,
-        [index, own] + [to_x(send, step) for step, send in zip(steps, sends)],
-        moved=2**20,
-        scalars=1,
-    )
-    hidden, slope = call(
-        activation_kernel,
-        "activation",
-        [((64, units), bf16), ((64, units), f32)],
-        [mine, other_z(send)],
-        moved=2**20,
-    )
+    parts_inputs, own_inputs = [to_x(send, step) for step, send in zip(steps, sends)], own
     near = stack(planes[1], "plane")
     all_grads, own, send = call(
         width_grad_kernel,
@@ -338,39 +329,69 @@
         [((512, width), bf16), ((256, units), f32), ((256, units), bf16)],
         [index, near, other_core(near), w_out],
         scratch=[((512, tile), f32)],
-        flops=width_flops,
         moved=6 * 2**20,
         scalars=1,
     )
-    mine, *sends = call(
+    mine_grads, *sends = call(
         sum_z_kernel,
         "sum_z",
         [((64, units), f32)] + [((64, units), bf16)] * 3,
         [own, other_z(send)],
         moved=2**20,
     )
+    parts_grads = [to_x(send, step) for step, send in zip(steps, sends)]
+    parts_inputs, mine_grads = barrier((parts_inputs, mine_grads))
+    mine, send = call(
+        sum_x_kernel,
+        "sum_x",
+        [((64, units), f32)] * 2,
+        [index, own_inputs] + list(parts_inputs),
+        moved=2**20,
+        scalars=1,
+    )
+    hidden, slope = call(
+        activation_kernel,
+        "activation",
+        [((64, units), bf16), ((64, units), f32)],
+        [mine, other_z(send)],
+        moved=2**20,
+    )
+    (grad_pre,) = call(
+        grad_pre_kernel,
+        "grad_pre",
+        [((64, units), bf16)],
+        [mine_grads] + parts_grads + [slope],
+        moved=2**20,
+    )
+    grad_parts = [from_x(grad_pre, step) for step in steps]
+    part_hidden, grad_pre = barrier((other_z(hidden), grad_pre))
     (pair,) = call(
         pair_z_kernel,
         "pair_z",
         [((128, units), bf16)],
-        [index, hidden, other_z(hidden)],
+        [index, hidden, part_hidden],
         moved=2**19,
         scalars=1,
     )
-    (grad_pre,) = call(
-        grad_pre_kernel,
-        "grad_pre",
-        [((64, units), bf16)],
-        [mine] + [to_x(send, step) for step, send in zip(steps, sends)] + [slope],
-        moved=2**20,
-    )
     hidden_pieces = [pair] + [from_x(pair, step) for step in steps]
-    grad_stack = stack([grad_pre] + [from_x(grad_pre, step) for step in steps], "grad_stack")
+    grad_parts, pair = barrier((grad_parts, pair))
+    stacks = call(
+        stack_two_kernel,
+        "grad_stack",
+        [((128, units), bf16)] * 2,
+        [grad_pre] + list(grad_parts),
+        moved=2**20,
+    )
     hidden_all, far_hidden = units_far(
         far_hidden_kernel, "far_hidden", index, hidden_pieces, w_out, False
     )
     grad_pre_all, far_grad = units_far(
-        far_grad_kernel, "far_grad", index, [grad_stack, other_z(grad_stack)], w_in, True
+        far_grad_kernel,
+        "far_grad",
+        index,
+        list(stacks) + [other_z(half) for half in stacks],
+        w_in,
+        True,
     )
     mine_hidden, parts_hidden = units_near(0, hidden_all, w_out, far_hidden)
     mine_grad, parts_grad = units_near(1, grad_pre_all, w_in, far_grad)

time: 142 us -> 145 us (1.021)
  starting transfers between devices: 65.7 us -> 68.1 us
  waiting for transfers between devices: 49.8 us -> 51.4 us
    ppermute x4 -> x5, waiting for transfers between devices: 0.17 us -> 5.93 us  [other_z(): return lax.ppermute(value, 'gz', [(i, i ^ 1) for i in range(8)])]
    ppermute x6, waiting for transfers between devices: 13.6 us -> 9.67 us  [from_x(): lax.ppermute(value, 'gz', [((i + 2 * step) % 8, i) for i in range(8)])]
    ppermute x6, starting transfers between devices: 6.05 us -> 9.38 us  [from_x(): lax.ppermute(value, 'gz', [((i + 2 * step) % 8, i) for i in range(8)])]
    ppermute x4 -> x5, starting transfers between devices: 6.57 us -> 6.44 us  [other_z(): return lax.ppermute(value, 'gz', [(i, i ^ 1) for i in range(8)])]
  transfers between devices with their start and end apart: 38 -> 39, of which waited for: 24 -> 22; matrix products, arithmetic and copies ran while one was open for 4% -> 4% of each run, Pallas kernels for 11% -> 11%
where the time goes in v5:
time: 145 us; the launch traced here: 144 us
  starting transfers between devices  68.1 us (47%)
  waiting for transfers between devices  51.4 us (35%)
  Pallas kernels  16.2 us (11%)
  matrix products  5.65 us (4%)
  local copies, waits for them, and re-layouts  1.6 us (1%)
    pallas_call x18, Pallas kernels, call(): pl.pallas_call(kernel, out_shape=[jax.ShapeDtypeStruct(*out) for out in o...  16.2 us
    ppermute x6, starting transfers between devices, to_y(): lax.ppermute(value, 'gy', [(i, (i + 2 * step) % 8) for i in range(8)])  14.3 us
    ppermute x6, waiting for transfers between devices, from_y(): lax.ppermute(value, 'gy', [((i + 2 * step) % 8, i) for i in range(8)])  11.6 us
    ppermute x6, starting transfers between devices, to_x(): lax.ppermute(value, 'gz', [(i, (i + 2 * step) % 8) for i in range(8)])  11 us
    ppermute x3, starting transfers between devices, from_gx(): return lax.ppermute(value, 'gx', [((i + step) % 4, i) for i in range(4)])  10.2 us
    ppermute x3, starting transfers between devices, to_gx(): return lax.ppermute(value, 'gx', [(i, (i + step) % 4) for i in range(4)])  9.93 us
    ppermute x6, waiting for transfers between devices, from_x(): lax.ppermute(value, 'gz', [((i + 2 * step) % 8, i) for i in range(8)])  9.67 us
    ppermute x6, starting transfers between devices, from_x(): lax.ppermute(value, 'gz', [((i + 2 * step) % 8, i) for i in range(8)])  9.38 us
  transfers between devices with their start and end apart: 39, of which 22 were waited for; matrix products, arithmetic and copies ran while one was open for 4% of the time, Pallas kernels for 11%

profile of v5, /device:TPU:8, one launch (start us, length us, event | category | flops | bytes accessed | tf_op | source)
XLA Modules:
  0.0 143.7 jit_solution(12653817409072336036)
XLA Ops:
  2.2 6.4 %collective-permute-start = (bf16[32,1536]{1,0:T(8,128)(2,1)S(1)}, bf16[32,1536]{1,0:T(8,128)(2,1)S(1)}, u32[]{:S(2)}, u32[]{:S(2)}) collective-permute-start(bf16[32,1536]{1,0:T(8,128)(2,1)S(1)} %pair.1.both_ref), channel_id=1, source_target_pairs={{64,0},{128,64},{192,128},{0,192},{65,1},{129,65},{193,129},{1,193... | collective-permute-start | bytes 294920 | tf_op jit(solution)/shard_map/ppermute | solution.py:31
  9.6 2.8 %collective-permute-start.2 = (bf16[32,1536]{1,0:T(8,128)(2,1)S(1)}, bf16[32,1536]{1,0:T(8,128)(2,1)S(1)}, u32[]{:S(2)}, u32[]{:S(2)}) collective-permute-start(bf16[32,1536]{1,0:T(8,128)(2,1)S(1)} %pair.1.both_ref), channel_id=1, source_target_pairs={{192,0},{0,64},{64,128},{128,192},{193,1},{1,65},{65,129},{129,193... | collective-permute-start | bytes 294920 | tf_op jit(solution)/shard_map/ppermute | solution.py:31
  12.4 4.6 %collective-permute-done.first_ref = bf16[32,1536]{1,0:T(8,128)(2,1)S(1)} collective-permute-done((bf16[32,1536]{1,0:T(8,128)(2,1)S(1)}, bf16[32,1536]{1,0:T(8,128)(2,1)S(1)}, u32[]{:S(2)}, u32[]{:S(2)}) %collective-permute-start) | collective-permute-done | bytes 98336 | tf_op jit(solution)/shard_map/ppermute | solution.py:31
  17.0 3.2 %collective-permute-done.1.second_ref = bf16[32,1536]{1,0:T(8,128)(2,1)S(1)} collective-permute-done((bf16[32,1536]{1,0:T(8,128)(2,1)S(1)}, bf16[32,1536]{1,0:T(8,128)(2,1)S(1)}, u32[]{:S(2)}, u32[]{:S(2)}) %collective-permute-start.1) | collective-permute-done | bytes 98336 | tf_op jit(solution)/shard_map/ppermute | solution.py:31
  21.0 2.4 %collective-permute-start.11 = (bf16[64,1536]{1,0:T(8,128)(2,1)S(1)}, bf16[64,1536]{1,0:T(8,128)(2,1)S(1)}, u32[]{:S(2)}, u32[]{:S(2)}) collective-permute-start(bf16[64,1536]{1,0:T(8,128)(2,1)S(1)} %get-tuple-element.56.refs_0_), channel_id=1, source_target_pairs={{32,0},{40,8},{48,16},{56,24},{0,32},{8,40},{16,48},{24,56},{33,1}... | collective-permute-start | bytes 589832 | tf_op jit(solution)/shard_map/ppermute | solution.py:43
  23.4 1.9 %collective-permute-start.12 = (bf16[64,1536]{1,0:T(8,128)(2,1)S(1)}, bf16[64,1536]{1,0:T(8,128)(2,1)S(1)}, u32[]{:S(2)}, u32[]{:S(2)}) collective-permute-start(bf16[64,1536]{1,0:T(8,128)(2,1)S(1)} %get-tuple-element.56.refs_0_), channel_id=1, source_target_pairs={{48,0},{56,8},{0,16},{8,24},{16,32},{24,40},{32,48},{40,56},{49,1}... | collective-permute-start | bytes 589832 | tf_op jit(solution)/shard_map/ppermute | solution.py:43
  26.7 2.8 %collective-permute-done.10.refs_1_ = bf16[64,1536]{1,0:T(8,128)(2,1)S(1)} collective-permute-done((bf16[64,1536]{1,0:T(8,128)(2,1)S(1)}, bf16[64,1536]{1,0:T(8,128)(2,1)S(1)}, u32[]{:S(2)}, u32[]{:S(2)}) %collective-permute-start.10) | collective-permute-done | bytes 196640 | tf_op jit(solution)/shard_map/ppermute | solution.py:43
  29.8 3.7 %collective-permute-done.11.refs_2_ = bf16[64,1536]{1,0:T(8,128)(2,1)S(1)} collective-permute-done((bf16[64,1536]{1,0:T(8,128)(2,1)S(1)}, bf16[64,1536]{1,0:T(8,128)(2,1)S(1)}, u32[]{:S(2)}, u32[]{:S(2)}) %collective-permute-start.11) | collective-permute-done | bytes 196640 | tf_op jit(solution)/shard_map/ppermute | solution.py:43
  35.7 2.1 %collective-permute-done.4.refs_2_ = bf16[64,1536]{1,0:T(8,128)(2,1)S(1)} collective-permute-done((bf16[64,1536]{1,0:T(8,128)(2,1)S(1)}, bf16[64,1536]{1,0:T(8,128)(2,1)S(1)}, u32[]{:S(2)}, u32[]{:S(2)}) %collective-permute-start.4) | collective-permute-done | bytes 196640 | tf_op jit(solution)/shard_map/ppermute | solution.py:43
  39.6 3.3 %width_grad.1 = (bf16[512,1536]{1,0:T(8,128)(2,1)S(1)}, f32[256,768]{1,0:T(8,128)S(1)}, bf16[256,768]{1,0:T(8,128)(2,1)S(1)}) custom-call(s32[1]{0:T(128)} %bitcast.index_ref, bf16[256,1536]{1,0:T(8,128)(2,1)S(1)} %plane.3.near_ref, bf16[256,1536]{1,0:T(8,128)(2,1)} %collective-permute-done.13.far_ref, bf16[768,1536]{1,0:T(8,128)(2,1)S(1)} %copy-done), custom_call_target="tpu_custom_call" | custom-call | bytes 6291456 | tf_op jit(solution)/shard_map/width_grad/pallas_call | solution.py:75
  43.0 2.7 %collective-permute-start.14 = (bf16[256,768]{1,0:T(8,128)(2,1)S(1)}, bf16[256,768]{1,0:T(8,128)(2,1)S(1)}, u32[]{:S(2)}, u32[]{:S(2)}) collective-permute-start(bf16[256,768]{1,0:T(8,128)(2,1)S(1)} %get-tuple-element.58), channel_id=1, source_target_pairs={{0,1},{1,0},{2,3},{3,2},{4,5},{5,4},{6,7},{7,6},{8,9},{9,8},{10,11... | collective-permute-start | bytes 1179656 | tf_op jit(solution)/shard_map/ppermute | solution.py:59
  45.7 3.4 %width_inputs.1 = (bf16[512,1536]{1,0:T(8,128)(2,1)S(1)}, f32[128,768]{1,0:T(8,128)S(1)}, bf16[128,768]{1,0:T(8,128)(2,1)S(1)}, bf16[128,768]{1,0:T(8,128)(2,1)S(1)}, bf16[128,768]{1,0:T(8,128)(2,1)S(1)}) custom-call(s32[1]{0:T(128)} %bitcast.index_ref, bf16[256,1536]{1,0:T(8,128)(2,1)} %plane.2.near_ref, bf16[256,1536]{1,0:T(8,128)(2,1)} %collective-permute-done.6.far_ref, ...), custom_call_target="tpu_custom_call" | custom-call | bytes 6291456 | tf_op jit(solution)/shard_map/width_inputs/pallas_call | solution.py:75
  50.7 2.7 %collective-permute-start.8 = (bf16[128,768]{1,0:T(8,128)(2,1)S(1)}, bf16[128,768]{1,0:T(8,128)(2,1)S(1)}, u32[]{:S(2)}, u32[]{:S(2)}) collective-permute-start(bf16[128,768]{1,0:T(8,128)(2,1)S(1)} %get-tuple-element.54), channel_id=1, source_target_pairs={{0,4},{1,5},{2,6},{3,7},{4,0},{5,1},{6,2},{7,3},{8,12},{9,13},{10,... | collective-permute-start | bytes 589832 | tf_op jit(solution)/shard_map/ppermute | solution.py:55
  57.4 5.2 %collective-permute-done.8.second_ref = bf16[128,768]{1,0:T(8,128)(2,1)S(1)} collective-permute-done((bf16[128,768]{1,0:T(8,128)(2,1)S(1)}, bf16[128,768]{1,0:T(8,128)(2,1)S(1)}, u32[]{:S(2)}, u32[]{:S(2)}) %collective-permute-start.8) | collective-permute-done | bytes 196640 | tf_op jit(solution)/shard_map/ppermute | solution.py:55
  64.5 2.4 %collective-permute-start.18 = (bf16[64,768]{1,0:T(8,128)(2,1)S(1)}, bf16[64,768]{1,0:T(8,128)(2,1)S(1)}, u32[]{:S(2)}, u32[]{:S(2)}) collective-permute-start(bf16[64,768]{1,0:T(8,128)(2,1)S(1)} %get-tuple-element.68), channel_id=1, source_target_pairs={{0,4},{1,5},{2,6},{3,7},{4,0},{5,1},{6,2},{7,3},{8,12},{9,13},{10,... | collective-permute-start | bytes 294920 | tf_op jit(solution)/shard_map/ppermute | solution.py:55
  72.0 2.5 %collective-permute-start.27 = (bf16[64,768]{1,0:T(8,128)(2,1)S(1)}, bf16[64,768]{1,0:T(8,128)(2,1)S(1)}, u32[]{:S(2)}, u32[]{:S(2)}) collective-permute-start(bf16[64,768]{1,0:T(8,128)(2,1)S(1)} %grad_pre.1.refs_0_), channel_id=1, source_target_pairs={{2,0},{3,1},{4,2},{5,3},{6,4},{7,5},{0,6},{1,7},{10,8},{11,9},{12,... | collective-permute-start | bytes 294920 | tf_op jit(solution)/shard_map/ppermute | solution.py:51
  74.6 2.3 %collective-permute-start.20 = (bf16[128,768]{1,0:T(8,128)(2,1)S(1)}, bf16[128,768]{1,0:T(8,128)(2,1)S(1)}, u32[]{:S(2)}, u32[]{:S(2)}) collective-permute-start(bf16[128,768]{1,0:T(8,128)(2,1)S(1)} %pair_z.1.refs_0_), channel_id=1, source_target_pairs={{2,0},{3,1},{4,2},{5,3},{6,4},{7,5},{0,6},{1,7},{10,8},{11,9},{12,... | collective-permute-start | bytes 589832 | tf_op jit(solution)/shard_map/ppermute | solution.py:51
  77.9 3.0 %collective-permute-start.28 = (bf16[64,768]{1,0:T(8,128)(2,1)S(1)}, bf16[64,768]{1,0:T(8,128)(2,1)S(1)}, u32[]{:S(2)}, u32[]{:S(2)}) collective-permute-start(bf16[64,768]{1,0:T(8,128)(2,1)S(1)} %grad_pre.1.refs_0_), channel_id=1, source_target_pairs={{4,0},{5,1},{6,2},{7,3},{0,4},{1,5},{2,6},{3,7},{12,8},{13,9},{14,... | collective-permute-start | bytes 294920 | tf_op jit(solution)/shard_map/ppermute | solution.py:51
  81.4 9.1 %collective-permute-done.28.refs_2_ = bf16[64,768]{1,0:T(8,128)(2,1)S(1)} collective-permute-done((bf16[64,768]{1,0:T(8,128)(2,1)S(1)}, bf16[64,768]{1,0:T(8,128)(2,1)S(1)}, u32[]{:S(2)}, u32[]{:S(2)}) %collective-permute-start.28) | collective-permute-done | bytes 98336 | tf_op jit(solution)/shard_map/ppermute | solution.py:51
  95.0 2.6 %collective-permute-done.30.refs_2_ = bf16[128,768]{1,0:T(8,128)(2,1)S(1)} collective-permute-done((bf16[128,768]{1,0:T(8,128)(2,1)S(1)}, bf16[128,768]{1,0:T(8,128)(2,1)S(1)}, u32[]{:S(2)}, u32[]{:S(2)}) %collective-permute-start.30) | collective-permute-done | bytes 196640 | tf_op jit(solution)/shard_map/ppermute | solution.py:59
  97.6 2.1 %collective-permute-done.31.refs_3_ = bf16[128,768]{1,0:T(8,128)(2,1)S(1)} collective-permute-done((bf16[128,768]{1,0:T(8,128)(2,1)S(1)}, bf16[128,768]{1,0:T(8,128)(2,1)S(1)}, u32[]{:S(2)}, u32[]{:S(2)}) %collective-permute-start.31) | collective-permute-done | bytes 196640 | tf_op jit(solution)/shard_map/ppermute | solution.py:59
  99.7 1.9 %far_grad.1 = (bf16[512,768]{1,0:T(8,128)(2,1)S(1)}, f32[256,1536]{1,0:T(8,128)S(1)}) custom-call(s32[1]{0:T(128)} %bitcast.index_ref, bf16[128,768]{1,0:T(8,128)(2,1)S(1)} %get-tuple-element.82.refs_0_, bf16[128,768]{1,0:T(8,128)(2,1)S(1)} %get-tuple-element.83.refs_1_, bf16[128,768]{1,0:T(8,128)(2,1)S(1)} %collective-permute-done.30.refs_2_, ...), custom_call_target="tpu_custom_call" | custom-call | bytes 6291456 | tf_op jit(solution)/shard_map/far_grad/pallas_call | solution.py:75
  104.9 3.5 %collective-permute-start.25 = (bf16[64,1536]{1,0:T(8,128)(2,1)S(1)}, bf16[64,1536]{1,0:T(8,128)(2,1)S(1)}, u32[]{:S(2)}, u32[]{:S(2)}) collective-permute-start(bf16[64,1536]{1,0:T(8,128)(2,1)S(1)} %get-tuple-element.76), channel_id=1, source_target_pairs={{0,32},{8,40},{16,48},{24,56},{32,0},{40,8},{48,16},{56,24},{1,33}... | collective-permute-start | bytes 589832 | tf_op jit(solution)/shard_map/ppermute | solution.py:47
  110.3 2.3 %collective-permute-start.33 = (bf16[64,1536]{1,0:T(8,128)(2,1)S(1)}, bf16[64,1536]{1,0:T(8,128)(2,1)S(1)}, u32[]{:S(2)}, u32[]{:S(2)}) collective-permute-start(bf16[64,1536]{1,0:T(8,128)(2,1)S(1)} %get-tuple-element.87), channel_id=1, source_target_pairs={{0,16},{8,24},{16,32},{24,40},{32,48},{40,56},{48,0},{56,8},{1,17}... | collective-permute-start | bytes 589832 | tf_op jit(solution)/shard_map/ppermute | solution.py:47
  113.8 5.6 %collective-permute-start.35 = (bf16[64,1536]{1,0:T(8,128)(2,1)S(1)}, bf16[64,1536]{1,0:T(8,128)(2,1)S(1)}, u32[]{:S(2)}, u32[]{:S(2)}) collective-permute-start(bf16[64,1536]{1,0:T(8,128)(2,1)S(1)} %get-tuple-element.89), channel_id=1, source_target_pairs={{0,48},{8,56},{16,0},{24,8},{32,16},{40,24},{48,32},{56,40},{1,49}... | collective-permute-start | bytes 589832 | tf_op jit(solution)/shard_map/ppermute | solution.py:47
  119.5 2.8 %convolution_convert_fusion.1 = bf16[1536,768]{1,0:T(8,128)(2,1)} fusion(bf16[512,1536]{1,0:T(8,128)(2,1)S(1)} %get-tuple-element.96, bf16[512,768]{1,0:T(8,128)(2,1)S(1)} %get-tuple-element.84.whole_ref), kind=kOutput, calls=%fused_computation.1 | convolution fusion | flops 1209139200 | bytes 4718592 | tf_op jit(solution)/shard_map/dot_general | solution.py:415
  122.6 3.7 %collective-permute-done.35.refs_7_ = bf16[64,1536]{1,0:T(8,128)(2,1)S(1)} collective-permute-done((bf16[64,1536]{1,0:T(8,128)(2,1)S(1)}, bf16[64,1536]{1,0:T(8,128)(2,1)S(1)}, u32[]{:S(2)}, u32[]{:S(2)}) %collective-permute-start.35) | collective-permute-done | bytes 196640 | tf_op jit(solution)/shard_map/ppermute | solution.py:47
  126.5 2.7 %collective-permute-start.36 = (bf16[32,1536]{1,0:T(8,128)(2,1)S(1)}, bf16[32,1536]{1,0:T(8,128)(2,1)S(1)}, u32[]{:S(2)}, u32[]{:S(2)}) collective-permute-start(bf16[32,1536]{1,0:T(8,128)(2,1)S(1)} %get-tuple-element.91), channel_id=1, source_target_pairs={{0,64},{64,128},{128,192},{192,0},{1,65},{65,129},{129,193},{193,1... | collective-permute-start | bytes 294920 | tf_op jit(solution)/shard_map/ppermute | solution.py:35
  129.2 4.0 %collective-permute-start.37 = (bf16[32,1536]{1,0:T(8,128)(2,1)S(1)}, bf16[32,1536]{1,0:T(8,128)(2,1)S(1)}, u32[]{:S(2)}, u32[]{:S(2)}) collective-permute-start(bf16[32,1536]{1,0:T(8,128)(2,1)S(1)} %get-tuple-element.92), channel_id=1, source_target_pairs={{0,128},{64,192},{128,0},{192,64},{1,129},{65,193},{129,1},{193,65... | collective-permute-start | bytes 294920 | tf_op jit(solution)/shard_map/ppermute | solution.py:35
  133.2 3.2 %collective-permute-start.38 = (bf16[32,1536]{1,0:T(8,128)(2,1)S(1)}, bf16[32,1536]{1,0:T(8,128)(2,1)S(1)}, u32[]{:S(2)}, u32[]{:S(2)}) collective-permute-start(bf16[32,1536]{1,0:T(8,128)(2,1)S(1)} %get-tuple-element.93), channel_id=1, source_target_pairs={{0,192},{64,0},{128,64},{192,128},{1,193},{65,1},{129,65},{193,129... | collective-permute-start | bytes 294920 | tf_op jit(solution)/shard_map/ppermute | solution.py:35
  136.4 2.8 %convolution_convert_fusion = bf16[768,1536]{1,0:T(8,128)(2,1)} fusion(bf16[512,768]{1,0:T(8,128)(2,1)S(1)} %get-tuple-element.72.whole_ref, bf16[512,1536]{1,0:T(8,128)(2,1)S(1)} %get-tuple-element.97), kind=kOutput, calls=%fused_computation | convolution fusion | flops 1209139200 | bytes 4718592 | tf_op jit(solution)/shard_map/dot_general | solution.py:412
  140.2 2.8 %collective-permute-done.38.third_ref = bf16[32,1536]{1,0:T(8,128)(2,1)S(1)} collective-permute-done((bf16[32,1536]{1,0:T(8,128)(2,1)S(1)}, bf16[32,1536]{1,0:T(8,128)(2,1)S(1)}, u32[]{:S(2)}, u32[]{:S(2)}) %collective-permute-start.38) | collective-permute-done | bytes 98336 | tf_op jit(solution)/shard_map/ppermute | solution.py:35
  (74 shorter events, 36.2 us)
Async XLA Ops:
  2.2 14.8 %collective-permute-start = (bf16[32,1536]{1,0:T(8,128)(2,1)S(1)}, bf16[32,1536]{1,0:T(8,128)(2,1)S(1)}, u32[]{:S(2)}, u32[]{:S(2)}) collective-permute-start(bf16[32,1536]{1,0:T(8,128)(2,1)S(1)} %pair.1.both_ref), channel_id=1, source_target_pairs={{64,0},{128,64},{192,128},{0,192},{65,1},{129,65},{193,129},{1,193... | collective-permute-start | bytes 294920 | tf_op jit(solution)/shard_map/ppermute | solution.py:31
  8.6 11.6 %collective-permute-start.1 = (bf16[32,1536]{1,0:T(8,128)(2,1)S(1)}, bf16[32,1536]{1,0:T(8,128)(2,1)S(1)}, u32[]{:S(2)}, u32[]{:S(2)}) collective-permute-start(bf16[32,1536]{1,0:T(8,128)(2,1)S(1)} %pair.1.both_ref), channel_id=1, source_target_pairs={{128,0},{192,64},{0,128},{64,192},{129,1},{193,65},{1,129},{65,193... | collective-permute-start | bytes 294920 | tf_op jit(solution)/shard_map/ppermute | solution.py:31
  9.6 10.6 %collective-permute-start.2 = (bf16[32,1536]{1,0:T(8,128)(2,1)S(1)}, bf16[32,1536]{1,0:T(8,128)(2,1)S(1)}, u32[]{:S(2)}, u32[]{:S(2)}) collective-permute-start(bf16[32,1536]{1,0:T(8,128)(2,1)S(1)} %pair.1.both_ref), channel_id=1, source_target_pairs={{192,0},{0,64},{64,128},{128,192},{193,1},{1,65},{65,129},{129,193... | collective-permute-start | bytes 294920 | tf_op jit(solution)/shard_map/ppermute | solution.py:31
  20.3 9.3 %collective-permute-start.10 = (bf16[64,1536]{1,0:T(8,128)(2,1)S(1)}, bf16[64,1536]{1,0:T(8,128)(2,1)S(1)}, u32[]{:S(2)}, u32[]{:S(2)}) collective-permute-start(bf16[64,1536]{1,0:T(8,128)(2,1)S(1)} %get-tuple-element.56.refs_0_), channel_id=1, source_target_pairs={{16,0},{24,8},{32,16},{40,24},{48,32},{56,40},{0,48},{8,56},{17,1}... | collective-permute-start | bytes 589832 | tf_op jit(solution)/shard_map/ppermute | solution.py:43
  21.0 12.5 %collective-permute-start.11 = (bf16[64,1536]{1,0:T(8,128)(2,1)S(1)}, bf16[64,1536]{1,0:T(8,128)(2,1)S(1)}, u32[]{:S(2)}, u32[]{:S(2)}) collective-permute-start(bf16[64,1536]{1,0:T(8,128)(2,1)S(1)} %get-tuple-element.56.refs_0_), channel_id=1, source_target_pairs={{32,0},{40,8},{48,16},{56,24},{0,32},{8,40},{16,48},{24,56},{33,1}... | collective-permute-start | bytes 589832 | tf_op jit(solution)/shard_map/ppermute | solution.py:43
  23.4 11.1 %collective-permute-start.12 = (bf16[64,1536]{1,0:T(8,128)(2,1)S(1)}, bf16[64,1536]{1,0:T(8,128)(2,1)S(1)}, u32[]{:S(2)}, u32[]{:S(2)}) collective-permute-start(bf16[64,1536]{1,0:T(8,128)(2,1)S(1)} %get-tuple-element.56.refs_0_), channel_id=1, source_target_pairs={{48,0},{56,8},{0,16},{8,24},{16,32},{24,40},{32,48},{40,56},{49,1}... | collective-permute-start | bytes 589832 | tf_op jit(solution)/shard_map/ppermute | solution.py:43
  25.3 10.5 %collective-permute-start.3 = (bf16[64,1536]{1,0:T(8,128)(2,1)S(1)}, bf16[64,1536]{1,0:T(8,128)(2,1)S(1)}, u32[]{:S(2)}, u32[]{:S(2)}) collective-permute-start(bf16[64,1536]{1,0:T(8,128)(2,1)S(1)} %get-tuple-element.51.refs_0_), channel_id=1, source_target_pairs={{16,0},{24,8},{32,16},{40,24},{48,32},{56,40},{0,48},{8,56},{17,1}... | collective-permute-start | bytes 589832 | tf_op jit(solution)/shard_map/ppermute | solution.py:43
  25.4 12.5 %collective-permute-start.4 = (bf16[64,1536]{1,0:T(8,128)(2,1)S(1)}, bf16[64,1536]{1,0:T(8,128)(2,1)S(1)}, u32[]{:S(2)}, u32[]{:S(2)}) collective-permute-start(bf16[64,1536]{1,0:T(8,128)(2,1)S(1)} %get-tuple-element.51.refs_0_), channel_id=1, source_target_pairs={{32,0},{40,8},{48,16},{56,24},{0,32},{8,40},{16,48},{24,56},{33,1}... | collective-permute-start | bytes 589832 | tf_op jit(solution)/shard_map/ppermute | solution.py:43
  29.6 9.1 %collective-permute-start.5 = (bf16[64,1536]{1,0:T(8,128)(2,1)S(1)}, bf16[64,1536]{1,0:T(8,128)(2,1)S(1)}, u32[]{:S(2)}, u32[]{:S(2)}) collective-permute-start(bf16[64,1536]{1,0:T(8,128)(2,1)S(1)} %get-tuple-element.51.refs_0_), channel_id=1, source_target_pairs={{48,0},{56,8},{0,16},{8,24},{16,32},{24,40},{32,48},{40,56},{49,1}... | collective-permute-start | bytes 589832 | tf_op jit(solution)/shard_map/ppermute | solution.py:43
  43.0 12.5 %collective-permute-start.14 = (bf16[256,768]{1,0:T(8,128)(2,1)S(1)}, bf16[256,768]{1,0:T(8,128)(2,1)S(1)}, u32[]{:S(2)}, u32[]{:S(2)}) collective-permute-start(bf16[256,768]{1,0:T(8,128)(2,1)S(1)} %get-tuple-element.58), channel_id=1, source_target_pairs={{0,1},{1,0},{2,3},{3,2},{4,5},{5,4},{6,7},{7,6},{8,9},{9,8},{10,11... | collective-permute-start | bytes 1179656 | tf_op jit(solution)/shard_map/ppermute | solution.py:59
  49.1 8.3 %collective-permute-start.7 = (bf16[128,768]{1,0:T(8,128)(2,1)S(1)}, bf16[128,768]{1,0:T(8,128)(2,1)S(1)}, u32[]{:S(2)}, u32[]{:S(2)}) collective-permute-start(bf16[128,768]{1,0:T(8,128)(2,1)S(1)} %get-tuple-element.53), channel_id=1, source_target_pairs={{0,2},{1,3},{2,4},{3,5},{4,6},{5,7},{6,0},{7,1},{8,10},{9,11},{10,... | collective-permute-start | bytes 589832 | tf_op jit(solution)/shard_map/ppermute | solution.py:55
  50.7 11.9 %collective-permute-start.8 = (bf16[128,768]{1,0:T(8,128)(2,1)S(1)}, bf16[128,768]{1,0:T(8,128)(2,1)S(1)}, u32[]{:S(2)}, u32[]{:S(2)}) collective-permute-start(bf16[128,768]{1,0:T(8,128)(2,1)S(1)} %get-tuple-element.54), channel_id=1, source_target_pairs={{0,4},{1,5},{2,6},{3,7},{4,0},{5,1},{6,2},{7,3},{8,12},{9,13},{10,... | collective-permute-start | bytes 589832 | tf_op jit(solution)/shard_map/ppermute | solution.py:55
  53.4 9.2 %collective-permute-start.9 = (bf16[128,768]{1,0:T(8,128)(2,1)S(1)}, bf16[128,768]{1,0:T(8,128)(2,1)S(1)}, u32[]{:S(2)}, u32[]{:S(2)}) collective-permute-start(bf16[128,768]{1,0:T(8,128)(2,1)S(1)} %get-tuple-element.55), channel_id=1, source_target_pairs={{0,6},{1,7},{2,0},{3,1},{4,2},{5,3},{6,4},{7,5},{8,14},{9,15},{10,... | collective-permute-start | bytes 589832 | tf_op jit(solution)/shard_map/ppermute | solution.py:55
  63.1 7.3 %collective-permute-start.17 = (bf16[64,768]{1,0:T(8,128)(2,1)S(1)}, bf16[64,768]{1,0:T(8,128)(2,1)S(1)}, u32[]{:S(2)}, u32[]{:S(2)}) collective-permute-start(bf16[64,768]{1,0:T(8,128)(2,1)S(1)} %get-tuple-element.67), channel_id=1, source_target_pairs={{0,2},{1,3},{2,4},{3,5},{4,6},{5,7},{6,0},{7,1},{8,10},{9,11},{10,... | collective-permute-start | bytes 294920 | tf_op jit(solution)/shard_map/ppermute | solution.py:55
  64.5 7.1 %collective-permute-start.18 = (bf16[64,768]{1,0:T(8,128)(2,1)S(1)}, bf16[64,768]{1,0:T(8,128)(2,1)S(1)}, u32[]{:S(2)}, u32[]{:S(2)}) collective-permute-start(bf16[64,768]{1,0:T(8,128)(2,1)S(1)} %get-tuple-element.68), channel_id=1, source_target_pairs={{0,4},{1,5},{2,6},{3,7},{4,0},{5,1},{6,2},{7,3},{8,12},{9,13},{10,... | collective-permute-start | bytes 294920 | tf_op jit(solution)/shard_map/ppermute | solution.py:55
  72.0 8.8 %collective-permute-start.27 = (bf16[64,768]{1,0:T(8,128)(2,1)S(1)}, bf16[64,768]{1,0:T(8,128)(2,1)S(1)}, u32[]{:S(2)}, u32[]{:S(2)}) collective-permute-start(bf16[64,768]{1,0:T(8,128)(2,1)S(1)} %grad_pre.1.refs_0_), channel_id=1, source_target_pairs={{2,0},{3,1},{4,2},{5,3},{6,4},{7,5},{0,6},{1,7},{10,8},{11,9},{12,... | collective-permute-start | bytes 294920 | tf_op jit(solution)/shard_map/ppermute | solution.py:51
  74.6 18.7 %collective-permute-start.20 = (bf16[128,768]{1,0:T(8,128)(2,1)S(1)}, bf16[128,768]{1,0:T(8,128)(2,1)S(1)}, u32[]{:S(2)}, u32[]{:S(2)}) collective-permute-start(bf16[128,768]{1,0:T(8,128)(2,1)S(1)} %pair_z.1.refs_0_), channel_id=1, source_target_pairs={{2,0},{3,1},{4,2},{5,3},{6,4},{7,5},{0,6},{1,7},{10,8},{11,9},{12,... | collective-permute-start | bytes 589832 | tf_op jit(solution)/shard_map/ppermute | solution.py:51
  76.9 16.3 %collective-permute-start.21 = (bf16[128,768]{1,0:T(8,128)(2,1)S(1)}, bf16[128,768]{1,0:T(8,128)(2,1)S(1)}, u32[]{:S(2)}, u32[]{:S(2)}) collective-permute-start(bf16[128,768]{1,0:T(8,128)(2,1)S(1)} %pair_z.1.refs_0_), channel_id=1, source_target_pairs={{4,0},{5,1},{6,2},{7,3},{0,4},{1,5},{2,6},{3,7},{12,8},{13,9},{14,... | collective-permute-start | bytes 589832 | tf_op jit(solution)/shard_map/ppermute | solution.py:51
  77.3 15.9 %collective-permute-start.22 = (bf16[128,768]{1,0:T(8,128)(2,1)S(1)}, bf16[128,768]{1,0:T(8,128)(2,1)S(1)}, u32[]{:S(2)}, u32[]{:S(2)}) collective-permute-start(bf16[128,768]{1,0:T(8,128)(2,1)S(1)} %pair_z.1.refs_0_), channel_id=1, source_target_pairs={{6,0},{7,1},{0,2},{1,3},{2,4},{3,5},{4,6},{5,7},{14,8},{15,9},{8,1... | collective-permute-start | bytes 589832 | tf_op jit(solution)/shard_map/ppermute | solution.py:51
  77.9 12.7 %collective-permute-start.28 = (bf16[64,768]{1,0:T(8,128)(2,1)S(1)}, bf16[64,768]{1,0:T(8,128)(2,1)S(1)}, u32[]{:S(2)}, u32[]{:S(2)}) collective-permute-start(bf16[64,768]{1,0:T(8,128)(2,1)S(1)} %grad_pre.1.refs_0_), channel_id=1, source_target_pairs={{4,0},{5,1},{6,2},{7,3},{0,4},{1,5},{2,6},{3,7},{12,8},{13,9},{14,... | collective-permute-start | bytes 294920 | tf_op jit(solution)/shard_map/ppermute | solution.py:51
  80.8 10.3 %collective-permute-start.29 = (bf16[64,768]{1,0:T(8,128)(2,1)S(1)}, bf16[64,768]{1,0:T(8,128)(2,1)S(1)}, u32[]{:S(2)}, u32[]{:S(2)}) collective-permute-start(bf16[64,768]{1,0:T(8,128)(2,1)S(1)} %grad_pre.1.refs_0_), channel_id=1, source_target_pairs={{6,0},{7,1},{0,2},{1,3},{2,4},{3,5},{4,6},{5,7},{14,8},{15,9},{8,1... | collective-permute-start | bytes 294920 | tf_op jit(solution)/shard_map/ppermute | solution.py:51
  92.1 7.6 %collective-permute-start.31 = (bf16[128,768]{1,0:T(8,128)(2,1)S(1)}, bf16[128,768]{1,0:T(8,128)(2,1)S(1)}, u32[]{:S(2)}, u32[]{:S(2)}) collective-permute-start(bf16[128,768]{1,0:T(8,128)(2,1)S(1)} %get-tuple-element.83.refs_1_), channel_id=1, source_target_pairs={{0,1},{1,0},{2,3},{3,2},{4,5},{5,4},{6,7},{7,6},{8,9},{9,8},{10,11... | collective-permute-start | bytes 589832 | tf_op jit(solution)/shard_map/ppermute | solution.py:59
  101.6 6.8 %collective-permute-start.32 = (f32[256,1536]{1,0:T(8,128)S(1)}, f32[256,1536]{1,0:T(8,128)S(1)}, u32[]{:S(2)}, u32[]{:S(2)}) collective-permute-start(f32[256,1536]{1,0:T(8,128)S(1)} %get-tuple-element.85), channel_id=1, source_target_pairs={{0,8},{8,0},{16,24},{24,16},{32,40},{40,32},{48,56},{56,48},{1,9},... | collective-permute-start | bytes 4718600 | tf_op jit(solution)/shard_map/ppermute | solution.py:39
  103.4 10.5 %collective-permute-start.24 = (bf16[64,1536]{1,0:T(8,128)(2,1)S(1)}, bf16[64,1536]{1,0:T(8,128)(2,1)S(1)}, u32[]{:S(2)}, u32[]{:S(2)}) collective-permute-start(bf16[64,1536]{1,0:T(8,128)(2,1)S(1)} %get-tuple-element.75), channel_id=1, source_target_pairs={{0,16},{8,24},{16,32},{24,40},{32,48},{40,56},{48,0},{56,8},{1,17}... | collective-permute-start | bytes 589832 | tf_op jit(solution)/shard_map/ppermute | solution.py:47
  104.9 17.4 %collective-permute-start.25 = (bf16[64,1536]{1,0:T(8,128)(2,1)S(1)}, bf16[64,1536]{1,0:T(8,128)(2,1)S(1)}, u32[]{:S(2)}, u32[]{:S(2)}) collective-permute-start(bf16[64,1536]{1,0:T(8,128)(2,1)S(1)} %get-tuple-element.76), channel_id=1, source_target_pairs={{0,32},{8,40},{16,48},{24,56},{32,0},{40,8},{48,16},{56,24},{1,33}... | collective-permute-start | bytes 589832 | tf_op jit(solution)/shard_map/ppermute | solution.py:47
  108.4 13.9 %collective-permute-start.26 = (bf16[64,1536]{1,0:T(8,128)(2,1)S(1)}, bf16[64,1536]{1,0:T(8,128)(2,1)S(1)}, u32[]{:S(2)}, u32[]{:S(2)}) collective-permute-start(bf16[64,1536]{1,0:T(8,128)(2,1)S(1)} %get-tuple-element.77), channel_id=1, source_target_pairs={{0,48},{8,56},{16,0},{24,8},{32,16},{40,24},{48,32},{56,40},{1,49}... | collective-permute-start | bytes 589832 | tf_op jit(solution)/shard_map/ppermute | solution.py:47
  110.3 12.0 %collective-permute-start.33 = (bf16[64,1536]{1,0:T(8,128)(2,1)S(1)}, bf16[64,1536]{1,0:T(8,128)(2,1)S(1)}, u32[]{:S(2)}, u32[]{:S(2)}) collective-permute-start(bf16[64,1536]{1,0:T(8,128)(2,1)S(1)} %get-tuple-element.87), channel_id=1, source_target_pairs={{0,16},{8,24},{16,32},{24,40},{32,48},{40,56},{48,0},{56,8},{1,17}... | collective-permute-start | bytes 589832 | tf_op jit(solution)/shard_map/ppermute | solution.py:47
  112.6 10.0 %collective-permute-start.34 = (bf16[64,1536]{1,0:T(8,128)(2,1)S(1)}, bf16[64,1536]{1,0:T(8,128)(2,1)S(1)}, u32[]{:S(2)}, u32[]{:S(2)}) collective-permute-start(bf16[64,1536]{1,0:T(8,128)(2,1)S(1)} %get-tuple-element.88), channel_id=1, source_target_pairs={{0,32},{8,40},{16,48},{24,56},{32,0},{40,8},{48,16},{56,24},{1,33}... | collective-permute-start | bytes 589832 | tf_op jit(solution)/shard_map/ppermute | solution.py:47
  113.8 12.5 %collective-permute-start.35 = (bf16[64,1536]{1,0:T(8,128)(2,1)S(1)}, bf16[64,1536]{1,0:T(8,128)(2,1)S(1)}, u32[]{:S(2)}, u32[]{:S(2)}) collective-permute-start(bf16[64,1536]{1,0:T(8,128)(2,1)S(1)} %get-tuple-element.89), channel_id=1, source_target_pairs={{0,48},{8,56},{16,0},{24,8},{32,16},{40,24},{48,32},{56,40},{1,49}... | collective-permute-start | bytes 589832 | tf_op jit(solution)/shard_map/ppermute | solution.py:47
  126.5 12.8 %collective-permute-start.36 = (bf16[32,1536]{1,0:T(8,128)(2,1)S(1)}, bf16[32,1536]{1,0:T(8,128)(2,1)S(1)}, u32[]{:S(2)}, u32[]{:S(2)}) collective-permute-start(bf16[32,1536]{1,0:T(8,128)(2,1)S(1)} %get-tuple-element.91), channel_id=1, source_target_pairs={{0,64},{64,128},{128,192},{192,0},{1,65},{65,129},{129,193},{193,1... | collective-permute-start | bytes 294920 | tf_op jit(solution)/shard_map/ppermute | solution.py:35
  129.2 11.1 %collective-permute-start.37 = (bf16[32,1536]{1,0:T(8,128)(2,1)S(1)}, bf16[32,1536]{1,0:T(8,128)(2,1)S(1)}, u32[]{:S(2)}, u32[]{:S(2)}) collective-permute-start(bf16[32,1536]{1,0:T(8,128)(2,1)S(1)} %get-tuple-element.92), channel_id=1, source_target_pairs={{0,128},{64,192},{128,0},{192,64},{1,129},{65,193},{129,1},{193,65... | collective-permute-start | bytes 294920 | tf_op jit(solution)/shard_map/ppermute | solution.py:35
  133.2 9.9 %collective-permute-start.38 = (bf16[32,1536]{1,0:T(8,128)(2,1)S(1)}, bf16[32,1536]{1,0:T(8,128)(2,1)S(1)}, u32[]{:S(2)}, u32[]{:S(2)}) collective-permute-start(bf16[32,1536]{1,0:T(8,128)(2,1)S(1)} %get-tuple-element.93), channel_id=1, source_target_pairs={{0,192},{64,0},{128,64},{192,128},{1,193},{65,1},{129,65},{193,129... | collective-permute-start | bytes 294920 | tf_op jit(solution)/shard_map/ppermute | solution.py:35
  (11 other events, 63.3 us)

commit v6 on v4

--- a/solution.py
+++ b/solution.py
@@ -24,6 +24,9 @@
     return (result, slope)
 
 
+barrier = lax.optimization_barrier
+
+
 def from_gx(value, step):
     return lax.ppermute(value, "gx", [((i + step) % 4, i) for i in range(4)])
 
@@ -67,7 +70,7 @@
     return weight_ref[:, pl.ds(start, tile)]
 
 
-def call(kernel, name, outs, args, scratch=(), flops=0, moved=0, scalars=0, aliases=None):
+def call(kernel, name, outs, args, scratch=(), moved=0, scalars=0, aliases=None):
     vmem = pl.BlockSpec(memory_space=pltpu.VMEM)
     return pl.pallas_call(
         kernel,
@@ -77,7 +80,7 @@
         scratch_shapes=[pltpu.VMEM(*shape) for shape in scratch],
         input_output_aliases=aliases or {},
         compiler_params=pltpu.CompilerParams(vmem_limit_bytes=8 * 2**20),
-        cost_estimate=pl.CostEstimate(flops=flops, bytes_accessed=moved, transcendentals=0),
+        cost_estimate=pl.CostEstimate(flops=0, bytes_accessed=moved, transcendentals=0),
         name=name,
     )(*args)
 
@@ -130,7 +133,7 @@
 
 
 def width_grad_kernel(index_ref, near_ref, far_ref, weight_ref, *refs):
-    whole_ref, own_ref, send_ref, acc = refs
+    whole_ref, own_ref, acc = refs[0], refs[1], refs[4]
     x, z = place(index_ref)
     whole_ref[:256, :] = near_ref[...]
     whole_ref[256:, :] = far_ref[...]
@@ -142,8 +145,9 @@
         acc[...] = product(whole_ref[...], columns_of(weight_ref, start, True), True)
         for step in range(4):
             rows = slice(64 * step, 64 * step + 64)
+            half = slice(64 * (step % 2), 64 * (step % 2) + 64)
             own_ref[rows, cols] = acc[block(x, step, 64, 64 * z), :]
-            send_ref[rows, cols] = acc[block(x, step, 64, 64 * (1 - z)), :].astype(bf16)
+            refs[2 + step // 2][half, cols] = acc[block(x, step, 64, 64 * (1 - z)), :].astype(bf16)
 
 
 def sum_x_kernel(index_ref, own_ref, first_ref, second_ref, third_ref, mine_ref, send_ref):
@@ -168,14 +172,16 @@
         slope_ref[rows, :] = slope
 
 
-def sum_z_kernel(own_ref, part_ref, mine_ref, *sends):
+def sum_z_kernel(own_ref, first_ref, second_ref, mine_ref, *sends):
     for step in range(4):
 
         @pl.loop(0, 4)
         def _(j):
             rows = pl.ds(pl.multiple_of(64 * step + 16 * j, 16), 16)
             local = pl.ds(pl.multiple_of(16 * j, 16), 16)
-            total = own_ref[rows, :] + part_ref[rows, :].astype(f32)
+            part = (first_ref, second_ref)[step // 2]
+            half = pl.ds(pl.multiple_of(64 * (step % 2) + 16 * j, 16), 16)
+            total = own_ref[rows, :] + part[half, :].astype(f32)
             if step == 0:
                 mine_ref[local, :] = total
             else:
@@ -270,7 +276,6 @@
         name,
         [((512, units), bf16), ((256, width), f32)],
         [index] + pieces + [weight],
-        flops=2 * 256 * width * units,
         moved=6 * 2**20,
         scalars=1,
     )
@@ -285,7 +290,6 @@
         [((64, width), f32)] + [((64, width), bf16)] * 3,
         [whole, weight, far],
         scratch=[((256, tile), f32)],
-        flops=2 * 256 * width * units,
         moved=6 * 2**20,
     )
     return mine, [to_y(send, step) for step, send in zip((1, 2, 3), sends)]
@@ -305,22 +309,32 @@
     )
     planes = [[column] + [from_y(column, step) for step in steps] for column in columns]
     near = stack(planes[0], "plane")
-    width_flops = 2 * 512 * width * units
     all_inputs, own, *sends = call(
         width_inputs_kernel,
         "width_inputs",
         [((512, width), bf16), ((128, units), f32)] + [((128, units), bf16)] * 3,
         [index, near, other_core(near), w_in],
         scratch=[((512, tile), f32)],
-        flops=width_flops,
         moved=6 * 2**20,
         scalars=1,
     )
-    mine, send = call(
+    own_inputs, parts_inputs = own, [to_x(send, step) for step, send in zip(steps, sends)]
+    plane, own_inputs = barrier((planes[1], own_inputs))
+    near = stack(plane, "plane")
+    all_grads, own, *halves = call(
+        width_grad_kernel,
+        "width_grad",
+        [((512, width), bf16), ((256, units), f32)] + [((128, units), bf16)] * 2,
+        [index, near, other_core(near), w_out],
+        scratch=[((512, tile), f32)],
+        moved=6 * 2**20,
+        scalars=1,
+    )
+    mine_inputs, send_inputs = call(
         sum_x_kernel,
         "sum_x",
         [((64, units), f32)] * 2,
-        [index, own] + [to_x(send, step) for step, send in zip(steps, sends)],
+        [index, own_inputs] + parts_inputs,
         moved=2**20,
         scalars=1,
     )
@@ -328,25 +342,14 @@
         activation_kernel,
         "activation",
         [((64, units), bf16), ((64, units), f32)],
-        [mine, other_z(send)],
+        [mine_inputs, other_z(send_inputs)],
         moved=2**20,
-    )
-    near = stack(planes[1], "plane")
-    all_grads, own, send = call(
-        width_grad_kernel,
-        "width_grad",
-        [((512, width), bf16), ((256, units), f32), ((256, units), bf16)],
-        [index, near, other_core(near), w_out],
-        scratch=[((512, tile), f32)],
-        flops=width_flops,
-        moved=6 * 2**20,
-        scalars=1,
     )
     mine, *sends = call(
         sum_z_kernel,
         "sum_z",
         [((64, units), f32)] + [((64, units), bf16)] * 3,
-        [own, other_z(send)],
+        [own] + [other_z(half) for half in halves],
         moved=2**20,
     )
     (pair,) = call(

time: 142 us -> 144 us (1.014)
  starting transfers between devices: 65.7 us -> 73.4 us
  Pallas kernels: 16.2 us -> 12.6 us
  waiting for transfers between devices: 49.8 us -> 46.6 us
  local copies, waits for them, and re-layouts: 1.6 us -> 3.27 us
    ppermute x4 -> x5, starting transfers between devices: 6.57 us -> 13.1 us  [other_z(): return lax.ppermute(value, 'gz', [(i, i ^ 1) for i in range(8)])]
    ppermute x4 -> x5, waiting for transfers between devices: 0.17 us -> 3.75 us  [other_z(): return lax.ppermute(value, 'gz', [(i, i ^ 1) for i in range(8)])]
    pallas_call x18, Pallas kernels: 16.2 us -> 12.6 us  [call(): pl.pallas_call(kernel, out_shape=[jax.ShapeDtypeStruct(*out) for out in o...]
    ppermute x6, starting transfers between devices: 6.64 us -> 10.1 us  [from_y(): lax.ppermute(value, 'gy', [((i + 2 * step) % 8, i) for i in range(8)])]
    ppermute x6, waiting for transfers between devices: 9.18 us -> 5.84 us  [to_x(): lax.ppermute(value, 'gz', [(i, (i + 2 * step) % 8) for i in range(8)])]
    ppermute x6, starting transfers between devices: 11.3 us -> 9.16 us  [to_x(): lax.ppermute(value, 'gz', [(i, (i + 2 * step) % 8) for i in range(8)])]
    ppermute x6, waiting for transfers between devices: 11.6 us -> 9.51 us  [from_y(): lax.ppermute(value, 'gy', [((i + 2 * step) % 8, i) for i in range(8)])]
    unnamed x8 -> x10, local copies, waits for them, and re-layouts: 1.6 us -> 3.27 us
  transfers between devices with their start and end apart: 38 -> 39, of which waited for: 24 -> 22; matrix products, arithmetic and copies ran while one was open for 4% -> 4% of each run, Pallas kernels for 11% -> 8%
where the time goes in v6:
time: 144 us; the launch traced here: 142 us
  starting transfers between devices  73.4 us (51%)
  waiting for transfers between devices  46.6 us (32%)
  Pallas kernels  12.6 us (9%)
  matrix products  5.67 us (4%)
  local copies, waits for them, and re-layouts  3.27 us (2%)
    ppermute x6, starting transfers between devices, to_y(): lax.ppermute(value, 'gy', [(i, (i + 2 * step) % 8) for i in range(8)])  14.3 us
    ppermute x5, starting transfers between devices, other_z(): return lax.ppermute(value, 'gz', [(i, i ^ 1) for i in range(8)])  13.1 us
    pallas_call x18, Pallas kernels, call(): pl.pallas_call(kernel, out_shape=[jax.ShapeDtypeStruct(*out) for out in o...  12.6 us
    ppermute x6, waiting for transfers between devices, from_x(): lax.ppermute(value, 'gz', [((i + 2 * step) % 8, i) for i in range(8)])  12.4 us
    ppermute x3, starting transfers between devices, from_gx(): return lax.ppermute(value, 'gx', [((i + step) % 4, i) for i in range(4)])  10.2 us
    ppermute x6, starting transfers between devices, from_y(): lax.ppermute(value, 'gy', [((i + 2 * step) % 8, i) for i in range(8)])  10.1 us
    ppermute x3, starting transfers between devices, to_gx(): return lax.ppermute(value, 'gx', [(i, (i + step) % 4) for i in range(4)])  9.94 us
    ppermute x6, waiting for transfers between devices, from_y(): lax.ppermute(value, 'gy', [((i + 2 * step) % 8, i) for i in range(8)])  9.51 us
  transfers between devices with their start and end apart: 39, of which 22 were waited for; matrix products, arithmetic and copies ran while one was open for 4% of the time, Pallas kernels for 8%

profile of v6, /device:TPU:8, one launch (start us, length us, event | category | flops | bytes accessed | tf_op | source)
XLA Modules:
  0.0 142.4 jit_solution(3287123150727494184)
XLA Ops:
  2.2 6.4 %collective-permute-start = (bf16[32,1536]{1,0:T(8,128)(2,1)S(1)}, bf16[32,1536]{1,0:T(8,128)(2,1)S(1)}, u32[]{:S(2)}, u32[]{:S(2)}) collective-permute-start(bf16[32,1536]{1,0:T(8,128)(2,1)S(1)} %pair.1.both_ref), channel_id=1, source_target_pairs={{64,0},{128,64},{192,128},{0,192},{65,1},{129,65},{193,129},{1,193... | collective-permute-start | bytes 294920 | tf_op jit(solution)/shard_map/ppermute | solution.py:31
  9.6 2.8 %collective-permute-start.2 = (bf16[32,1536]{1,0:T(8,128)(2,1)S(1)}, bf16[32,1536]{1,0:T(8,128)(2,1)S(1)}, u32[]{:S(2)}, u32[]{:S(2)}) collective-permute-start(bf16[32,1536]{1,0:T(8,128)(2,1)S(1)} %pair.1.both_ref), channel_id=1, source_target_pairs={{192,0},{0,64},{64,128},{128,192},{193,1},{1,65},{65,129},{129,193... | collective-permute-start | bytes 294920 | tf_op jit(solution)/shard_map/ppermute | solution.py:31
  12.4 4.6 %collective-permute-done.first_ref = bf16[32,1536]{1,0:T(8,128)(2,1)S(1)} collective-permute-done((bf16[32,1536]{1,0:T(8,128)(2,1)S(1)}, bf16[32,1536]{1,0:T(8,128)(2,1)S(1)}, u32[]{:S(2)}, u32[]{:S(2)}) %collective-permute-start) | collective-permute-done | bytes 98336 | tf_op jit(solution)/shard_map/ppermute | solution.py:31
  17.0 3.2 %collective-permute-done.1.second_ref = bf16[32,1536]{1,0:T(8,128)(2,1)S(1)} collective-permute-done((bf16[32,1536]{1,0:T(8,128)(2,1)S(1)}, bf16[32,1536]{1,0:T(8,128)(2,1)S(1)}, u32[]{:S(2)}, u32[]{:S(2)}) %collective-permute-start.1) | collective-permute-done | bytes 98336 | tf_op jit(solution)/shard_map/ppermute | solution.py:31
  21.0 2.4 %collective-permute-start.7 = (bf16[64,1536]{1,0:T(8,128)(2,1)S(1)}, bf16[64,1536]{1,0:T(8,128)(2,1)S(1)}, u32[]{:S(2)}, u32[]{:S(2)}) collective-permute-start(bf16[64,1536]{1,0:T(8,128)(2,1)S(1)} %get-tuple-element.47.refs_0_), channel_id=1, source_target_pairs={{32,0},{40,8},{48,16},{56,24},{0,32},{8,40},{16,48},{24,56},{33,1}... | collective-permute-start | bytes 589832 | tf_op jit(solution)/shard_map/ppermute | solution.py:43
  25.3 2.0 %collective-permute-done.6.refs_1_ = bf16[64,1536]{1,0:T(8,128)(2,1)S(1)} collective-permute-done((bf16[64,1536]{1,0:T(8,128)(2,1)S(1)}, bf16[64,1536]{1,0:T(8,128)(2,1)S(1)}, u32[]{:S(2)}, u32[]{:S(2)}) %collective-permute-start.6) | collective-permute-done | bytes 196640 | tf_op jit(solution)/shard_map/ppermute | solution.py:43
  27.3 2.1 %collective-permute-done.7.refs_2_ = bf16[64,1536]{1,0:T(8,128)(2,1)S(1)} collective-permute-done((bf16[64,1536]{1,0:T(8,128)(2,1)S(1)}, bf16[64,1536]{1,0:T(8,128)(2,1)S(1)}, u32[]{:S(2)}, u32[]{:S(2)}) %collective-permute-start.7) | collective-permute-done | bytes 196640 | tf_op jit(solution)/shard_map/ppermute | solution.py:43
  30.3 3.0 %collective-permute-start.3 = (bf16[64,1536]{1,0:T(8,128)(2,1)S(1)}, bf16[64,1536]{1,0:T(8,128)(2,1)S(1)}, u32[]{:S(2)}, u32[]{:S(2)}) collective-permute-start(bf16[64,1536]{1,0:T(8,128)(2,1)S(1)} %get-tuple-element.62.refs_0_), channel_id=1, source_target_pairs={{16,0},{24,8},{32,16},{40,24},{48,32},{56,40},{0,48},{8,56},{17,1}... | collective-permute-start | bytes 589832 | tf_op jit(solution)/shard_map/ppermute | solution.py:43
  33.4 2.1 %collective-permute-start.5 = (bf16[64,1536]{1,0:T(8,128)(2,1)S(1)}, bf16[64,1536]{1,0:T(8,128)(2,1)S(1)}, u32[]{:S(2)}, u32[]{:S(2)}) collective-permute-start(bf16[64,1536]{1,0:T(8,128)(2,1)S(1)} %get-tuple-element.62.refs_0_), channel_id=1, source_target_pairs={{48,0},{56,8},{0,16},{8,24},{16,32},{24,40},{32,48},{40,56},{49,1}... | collective-permute-start | bytes 589832 | tf_op jit(solution)/shard_map/ppermute | solution.py:43
  37.1 2.0 %width_inputs.1 = (bf16[512,1536]{1,0:T(8,128)(2,1)S(1)}, f32[128,768]{1,0:T(8,128)S(1)}, bf16[128,768]{1,0:T(8,128)(2,1)S(1)}, bf16[128,768]{1,0:T(8,128)(2,1)S(1)}, bf16[128,768]{1,0:T(8,128)(2,1)S(1)}) custom-call(s32[1]{0:T(128)} %bitcast.index_ref, bf16[256,1536]{1,0:T(8,128)(2,1)S(1)} %plane.2.near_ref, ...), custom_call_target="tpu_custom_call" | custom-call | bytes 6291456 | tf_op jit(solution)/shard_map/width_inputs/pallas_call | solution.py:75
  39.1 3.7 %collective-permute-done.4.refs_2_ = bf16[64,1536]{1,0:T(8,128)(2,1)S(1)} collective-permute-done((bf16[64,1536]{1,0:T(8,128)(2,1)S(1)}, bf16[64,1536]{1,0:T(8,128)(2,1)S(1)}, u32[]{:S(2)}, u32[]{:S(2)}) %collective-permute-start.4) | collective-permute-done | bytes 196640 | tf_op jit(solution)/shard_map/ppermute | solution.py:43
  45.4 2.7 %collective-permute-start.11 = (bf16[128,768]{1,0:T(8,128)(2,1)S(1)}, bf16[128,768]{1,0:T(8,128)(2,1)S(1)}, u32[]{:S(2)}, u32[]{:S(2)}) collective-permute-start(bf16[128,768]{1,0:T(8,128)(2,1)S(1)} %get-tuple-element.51), channel_id=1, source_target_pairs={{0,4},{1,5},{2,6},{3,7},{4,0},{5,1},{6,2},{7,3},{8,12},{9,13},{10,... | collective-permute-start | bytes 589832 | tf_op jit(solution)/shard_map/ppermute | solution.py:55
  49.6 2.0 %width_grad.1 = (bf16[512,1536]{1,0:T(8,128)(2,1)S(1)}, f32[256,768]{1,0:T(8,128)S(1)}, bf16[128,768]{1,0:T(8,128)(2,1)S(1)}, bf16[128,768]{1,0:T(8,128)(2,1)S(1)}) custom-call(s32[1]{0:T(128)} %bitcast.index_ref, bf16[256,1536]{1,0:T(8,128)(2,1)S(1)} %plane.3.near_ref, bf16[256,1536]{1,0:T(8,128)(2,1)S(1)} %collective-permute-done.22.far_ref, ...), custom_call_target="tpu_custom_call" | custom-call | bytes 6291456 | tf_op jit(solution)/shard_map/width_grad/pallas_call | solution.py:75
  51.7 2.8 %collective-permute-start.23 = (bf16[128,768]{1,0:T(8,128)(2,1)S(1)}, bf16[128,768]{1,0:T(8,128)(2,1)S(1)}, u32[]{:S(2)}, u32[]{:S(2)}) collective-permute-start(bf16[128,768]{1,0:T(8,128)(2,1)S(1)} %get-tuple-element.67), channel_id=1, source_target_pairs={{0,1},{1,0},{2,3},{3,2},{4,5},{5,4},{6,7},{7,6},{8,9},{9,8},{10,11... | collective-permute-start | bytes 589832 | tf_op jit(solution)/shard_map/ppermute | solution.py:59
  54.6 3.0 %collective-permute-done.11.second_ref = bf16[128,768]{1,0:T(8,128)(2,1)S(1)} collective-permute-done((bf16[128,768]{1,0:T(8,128)(2,1)S(1)}, bf16[128,768]{1,0:T(8,128)(2,1)S(1)}, u32[]{:S(2)}, u32[]{:S(2)}) %collective-permute-start.11) | collective-permute-done | bytes 196640 | tf_op jit(solution)/shard_map/ppermute | solution.py:55
  57.7 3.0 %collective-permute-start.13 = (f32[64,768]{1,0:T(8,128)S(1)}, f32[64,768]{1,0:T(8,128)S(1)}, u32[]{:S(2)}, u32[]{:S(2)}) collective-permute-start(f32[64,768]{1,0:T(8,128)S(1)} %get-tuple-element.54), channel_id=1, source_target_pairs={{0,1},{1,0},{2,3},{3,2},{4,5},{5,4},{6,7},{7,6},{8,9},{9,8},{10,11... | collective-permute-start | bytes 589832 | tf_op jit(solution)/shard_map/ppermute | solution.py:59
  60.7 3.7 %collective-permute-done.24.second_ref = bf16[128,768]{1,0:T(8,128)(2,1)S(1)} collective-permute-done((bf16[128,768]{1,0:T(8,128)(2,1)S(1)}, bf16[128,768]{1,0:T(8,128)(2,1)S(1)}, u32[]{:S(2)}, u32[]{:S(2)}) %collective-permute-start.24) | collective-permute-done | bytes 196640 | tf_op jit(solution)/shard_map/ppermute | solution.py:59
  65.3 2.7 %collective-permute-start.27 = (bf16[64,768]{1,0:T(8,128)(2,1)S(1)}, bf16[64,768]{1,0:T(8,128)(2,1)S(1)}, u32[]{:S(2)}, u32[]{:S(2)}) collective-permute-start(bf16[64,768]{1,0:T(8,128)(2,1)S(1)} %get-tuple-element.72), channel_id=1, source_target_pairs={{0,6},{1,7},{2,0},{3,1},{4,2},{5,3},{6,4},{7,5},{8,14},{9,15},{10,... | collective-permute-start | bytes 294920 | tf_op jit(solution)/shard_map/ppermute | solution.py:55
  68.2 2.2 %collective-permute-start.14 = (bf16[64,768]{1,0:T(8,128)(2,1)S(1)}, bf16[64,768]{1,0:T(8,128)(2,1)S(1)}, u32[]{:S(2)}, u32[]{:S(2)}) collective-permute-start(bf16[64,768]{1,0:T(8,128)(2,1)S(1)} %get-tuple-element.55.own_ref), channel_id=1, source_target_pairs={{0,1},{1,0},{2,3},{3,2},{4,5},{5,4},{6,7},{7,6},{8,9},{9,8},{10,11... | collective-permute-start | bytes 294920 | tf_op jit(solution)/shard_map/ppermute | solution.py:59
  78.0 3.2 %collective-permute-done.29.refs_2_ = bf16[64,768]{1,0:T(8,128)(2,1)S(1)} collective-permute-done((bf16[64,768]{1,0:T(8,128)(2,1)S(1)}, bf16[64,768]{1,0:T(8,128)(2,1)S(1)}, u32[]{:S(2)}, u32[]{:S(2)}) %collective-permute-start.29) | collective-permute-done | bytes 98336 | tf_op jit(solution)/shard_map/ppermute | solution.py:51
  82.3 5.0 %collective-permute-start.31 = (bf16[256,768]{1,0:T(8,128)(2,1)S(1)}, bf16[256,768]{1,0:T(8,128)(2,1)S(1)}, u32[]{:S(2)}, u32[]{:S(2)}) collective-permute-start(bf16[256,768]{1,0:T(8,128)(2,1)S(1)} %grad_stack.1.own_ref), channel_id=1, source_target_pairs={{0,1},{1,0},{2,3},{3,2},{4,5},{5,4},{6,7},{7,6},{8,9},{9,8},{10,11... | collective-permute-start | bytes 1179656 | tf_op jit(solution)/shard_map/ppermute | solution.py:59
  90.0 3.0 %collective-permute-done.15.refs_1_ = bf16[128,768]{1,0:T(8,128)(2,1)S(1)} collective-permute-done((bf16[128,768]{1,0:T(8,128)(2,1)S(1)}, bf16[128,768]{1,0:T(8,128)(2,1)S(1)}, u32[]{:S(2)}, u32[]{:S(2)}) %collective-permute-start.15) | collective-permute-done | bytes 196640 | tf_op jit(solution)/shard_map/ppermute | solution.py:51
  94.6 2.0 %collective-permute-done.17.refs_3_ = bf16[128,768]{1,0:T(8,128)(2,1)S(1)} collective-permute-done((bf16[128,768]{1,0:T(8,128)(2,1)S(1)}, bf16[128,768]{1,0:T(8,128)(2,1)S(1)}, u32[]{:S(2)}, u32[]{:S(2)}) %collective-permute-start.17) | collective-permute-done | bytes 196640 | tf_op jit(solution)/shard_map/ppermute | solution.py:51
  105.0 3.5 %collective-permute-start.20 = (bf16[64,1536]{1,0:T(8,128)(2,1)S(1)}, bf16[64,1536]{1,0:T(8,128)(2,1)S(1)}, u32[]{:S(2)}, u32[]{:S(2)}) collective-permute-start(bf16[64,1536]{1,0:T(8,128)(2,1)S(1)} %get-tuple-element.60), channel_id=1, source_target_pairs={{0,32},{8,40},{16,48},{24,56},{32,0},{40,8},{48,16},{56,24},{1,33}... | collective-permute-start | bytes 589832 | tf_op jit(solution)/shard_map/ppermute | solution.py:47
  110.5 2.1 %collective-permute-start.33 = (bf16[64,1536]{1,0:T(8,128)(2,1)S(1)}, bf16[64,1536]{1,0:T(8,128)(2,1)S(1)}, u32[]{:S(2)}, u32[]{:S(2)}) collective-permute-start(bf16[64,1536]{1,0:T(8,128)(2,1)S(1)} %get-tuple-element.77), channel_id=1, source_target_pairs={{0,16},{8,24},{16,32},{24,40},{32,48},{40,56},{48,0},{56,8},{1,17}... | collective-permute-start | bytes 589832 | tf_op jit(solution)/shard_map/ppermute | solution.py:47
  113.9 5.7 %collective-permute-start.35 = (bf16[64,1536]{1,0:T(8,128)(2,1)S(1)}, bf16[64,1536]{1,0:T(8,128)(2,1)S(1)}, u32[]{:S(2)}, u32[]{:S(2)}) collective-permute-start(bf16[64,1536]{1,0:T(8,128)(2,1)S(1)} %get-tuple-element.79), channel_id=1, source_target_pairs={{0,48},{8,56},{16,0},{24,8},{32,16},{40,24},{48,32},{56,40},{1,49}... | collective-permute-start | bytes 589832 | tf_op jit(solution)/shard_map/ppermute | solution.py:47
  119.6 2.8 %convolution_convert_fusion = bf16[768,1536]{1,0:T(8,128)(2,1)} fusion(bf16[512,768]{1,0:T(8,128)(2,1)S(1)} %get-tuple-element.56.whole_ref, bf16[512,1536]{1,0:T(8,128)(2,1)S(1)} %get-tuple-element.87), kind=kOutput, calls=%fused_computation | convolution fusion | flops 1209139200 | bytes 4718592 | tf_op jit(solution)/shard_map/dot_general | solution.py:394
  122.8 3.2 %collective-permute-done.35.refs_7_ = bf16[64,1536]{1,0:T(8,128)(2,1)S(1)} collective-permute-done((bf16[64,1536]{1,0:T(8,128)(2,1)S(1)}, bf16[64,1536]{1,0:T(8,128)(2,1)S(1)}, u32[]{:S(2)}, u32[]{:S(2)}) %collective-permute-start.35) | collective-permute-done | bytes 196640 | tf_op jit(solution)/shard_map/ppermute | solution.py:47
  126.2 2.7 %collective-permute-start.36 = (bf16[32,1536]{1,0:T(8,128)(2,1)S(1)}, bf16[32,1536]{1,0:T(8,128)(2,1)S(1)}, u32[]{:S(2)}, u32[]{:S(2)}) collective-permute-start(bf16[32,1536]{1,0:T(8,128)(2,1)S(1)} %get-tuple-element.81), channel_id=1, source_target_pairs={{0,64},{64,128},{128,192},{192,0},{1,65},{65,129},{129,193},{193,1... | collective-permute-start | bytes 294920 | tf_op jit(solution)/shard_map/ppermute | solution.py:35
  128.9 4.0 %collective-permute-start.37 = (bf16[32,1536]{1,0:T(8,128)(2,1)S(1)}, bf16[32,1536]{1,0:T(8,128)(2,1)S(1)}, u32[]{:S(2)}, u32[]{:S(2)}) collective-permute-start(bf16[32,1536]{1,0:T(8,128)(2,1)S(1)} %get-tuple-element.82), channel_id=1, source_target_pairs={{0,128},{64,192},{128,0},{192,64},{1,129},{65,193},{129,1},{193,65... | collective-permute-start | bytes 294920 | tf_op jit(solution)/shard_map/ppermute | solution.py:35
  132.9 3.2 %collective-permute-start.38 = (bf16[32,1536]{1,0:T(8,128)(2,1)S(1)}, bf16[32,1536]{1,0:T(8,128)(2,1)S(1)}, u32[]{:S(2)}, u32[]{:S(2)}) collective-permute-start(bf16[32,1536]{1,0:T(8,128)(2,1)S(1)} %get-tuple-element.83), channel_id=1, source_target_pairs={{0,192},{64,0},{128,64},{192,128},{1,193},{65,1},{129,65},{193,129... | collective-permute-start | bytes 294920 | tf_op jit(solution)/shard_map/ppermute | solution.py:35
  136.2 2.8 %convolution_convert_fusion.1 = bf16[1536,768]{1,0:T(8,128)(2,1)} fusion(bf16[512,1536]{1,0:T(8,128)(2,1)S(1)} %get-tuple-element.86, bf16[512,768]{1,0:T(8,128)(2,1)S(1)} %get-tuple-element.74.whole_ref), kind=kOutput, calls=%fused_computation.1 | convolution fusion | flops 1209139200 | bytes 4718592 | tf_op jit(solution)/shard_map/dot_general | solution.py:397
  (76 shorter events, 41.8 us)
Async XLA Ops:
  2.2 14.8 %collective-permute-start = (bf16[32,1536]{1,0:T(8,128)(2,1)S(1)}, bf16[32,1536]{1,0:T(8,128)(2,1)S(1)}, u32[]{:S(2)}, u32[]{:S(2)}) collective-permute-start(bf16[32,1536]{1,0:T(8,128)(2,1)S(1)} %pair.1.both_ref), channel_id=1, source_target_pairs={{64,0},{128,64},{192,128},{0,192},{65,1},{129,65},{193,129},{1,193... | collective-permute-start | bytes 294920 | tf_op jit(solution)/shard_map/ppermute | solution.py:31
  8.6 11.6 %collective-permute-start.1 = (bf16[32,1536]{1,0:T(8,128)(2,1)S(1)}, bf16[32,1536]{1,0:T(8,128)(2,1)S(1)}, u32[]{:S(2)}, u32[]{:S(2)}) collective-permute-start(bf16[32,1536]{1,0:T(8,128)(2,1)S(1)} %pair.1.both_ref), channel_id=1, source_target_pairs={{128,0},{192,64},{0,128},{64,192},{129,1},{193,65},{1,129},{65,193... | collective-permute-start | bytes 294920 | tf_op jit(solution)/shard_map/ppermute | solution.py:31
  9.6 10.6 %collective-permute-start.2 = (bf16[32,1536]{1,0:T(8,128)(2,1)S(1)}, bf16[32,1536]{1,0:T(8,128)(2,1)S(1)}, u32[]{:S(2)}, u32[]{:S(2)}) collective-permute-start(bf16[32,1536]{1,0:T(8,128)(2,1)S(1)} %pair.1.both_ref), channel_id=1, source_target_pairs={{192,0},{0,64},{64,128},{128,192},{193,1},{1,65},{65,129},{129,193... | collective-permute-start | bytes 294920 | tf_op jit(solution)/shard_map/ppermute | solution.py:31
  20.3 7.0 %collective-permute-start.6 = (bf16[64,1536]{1,0:T(8,128)(2,1)S(1)}, bf16[64,1536]{1,0:T(8,128)(2,1)S(1)}, u32[]{:S(2)}, u32[]{:S(2)}) collective-permute-start(bf16[64,1536]{1,0:T(8,128)(2,1)S(1)} %get-tuple-element.47.refs_0_), channel_id=1, source_target_pairs={{16,0},{24,8},{32,16},{40,24},{48,32},{56,40},{0,48},{8,56},{17,1}... | collective-permute-start | bytes 589832 | tf_op jit(solution)/shard_map/ppermute | solution.py:43
  21.0 8.4 %collective-permute-start.7 = (bf16[64,1536]{1,0:T(8,128)(2,1)S(1)}, bf16[64,1536]{1,0:T(8,128)(2,1)S(1)}, u32[]{:S(2)}, u32[]{:S(2)}) collective-permute-start(bf16[64,1536]{1,0:T(8,128)(2,1)S(1)} %get-tuple-element.47.refs_0_), channel_id=1, source_target_pairs={{32,0},{40,8},{48,16},{56,24},{0,32},{8,40},{16,48},{24,56},{33,1}... | collective-permute-start | bytes 589832 | tf_op jit(solution)/shard_map/ppermute | solution.py:43
  23.4 6.8 %collective-permute-start.8 = (bf16[64,1536]{1,0:T(8,128)(2,1)S(1)}, bf16[64,1536]{1,0:T(8,128)(2,1)S(1)}, u32[]{:S(2)}, u32[]{:S(2)}) collective-permute-start(bf16[64,1536]{1,0:T(8,128)(2,1)S(1)} %get-tuple-element.47.refs_0_), channel_id=1, source_target_pairs={{48,0},{56,8},{0,16},{8,24},{16,32},{24,40},{32,48},{40,56},{49,1}... | collective-permute-start | bytes 589832 | tf_op jit(solution)/shard_map/ppermute | solution.py:43
  30.3 8.8 %collective-permute-start.3 = (bf16[64,1536]{1,0:T(8,128)(2,1)S(1)}, bf16[64,1536]{1,0:T(8,128)(2,1)S(1)}, u32[]{:S(2)}, u32[]{:S(2)}) collective-permute-start(bf16[64,1536]{1,0:T(8,128)(2,1)S(1)} %get-tuple-element.62.refs_0_), channel_id=1, source_target_pairs={{16,0},{24,8},{32,16},{40,24},{48,32},{56,40},{0,48},{8,56},{17,1}... | collective-permute-start | bytes 589832 | tf_op jit(solution)/shard_map/ppermute | solution.py:43
  33.4 9.4 %collective-permute-start.4 = (bf16[64,1536]{1,0:T(8,128)(2,1)S(1)}, bf16[64,1536]{1,0:T(8,128)(2,1)S(1)}, u32[]{:S(2)}, u32[]{:S(2)}) collective-permute-start(bf16[64,1536]{1,0:T(8,128)(2,1)S(1)} %get-tuple-element.62.refs_0_), channel_id=1, source_target_pairs={{32,0},{40,8},{48,16},{56,24},{0,32},{8,40},{16,48},{24,56},{33,1}... | collective-permute-start | bytes 589832 | tf_op jit(solution)/shard_map/ppermute | solution.py:43
  33.4 10.3 %collective-permute-start.5 = (bf16[64,1536]{1,0:T(8,128)(2,1)S(1)}, bf16[64,1536]{1,0:T(8,128)(2,1)S(1)}, u32[]{:S(2)}, u32[]{:S(2)}) collective-permute-start(bf16[64,1536]{1,0:T(8,128)(2,1)S(1)} %get-tuple-element.62.refs_0_), channel_id=1, source_target_pairs={{48,0},{56,8},{0,16},{8,24},{16,32},{24,40},{32,48},{40,56},{49,1}... | collective-permute-start | bytes 589832 | tf_op jit(solution)/shard_map/ppermute | solution.py:43
  43.9 10.7 %collective-permute-start.10 = (bf16[128,768]{1,0:T(8,128)(2,1)S(1)}, bf16[128,768]{1,0:T(8,128)(2,1)S(1)}, u32[]{:S(2)}, u32[]{:S(2)}) collective-permute-start(bf16[128,768]{1,0:T(8,128)(2,1)S(1)} %get-tuple-element.50), channel_id=1, source_target_pairs={{0,2},{1,3},{2,4},{3,5},{4,6},{5,7},{6,0},{7,1},{8,10},{9,11},{10,... | collective-permute-start | bytes 589832 | tf_op jit(solution)/shard_map/ppermute | solution.py:55
  45.4 12.2 %collective-permute-start.11 = (bf16[128,768]{1,0:T(8,128)(2,1)S(1)}, bf16[128,768]{1,0:T(8,128)(2,1)S(1)}, u32[]{:S(2)}, u32[]{:S(2)}) collective-permute-start(bf16[128,768]{1,0:T(8,128)(2,1)S(1)} %get-tuple-element.51), channel_id=1, source_target_pairs={{0,4},{1,5},{2,6},{3,7},{4,0},{5,1},{6,2},{7,3},{8,12},{9,13},{10,... | collective-permute-start | bytes 589832 | tf_op jit(solution)/shard_map/ppermute | solution.py:55
  48.2 9.4 %collective-permute-start.12 = (bf16[128,768]{1,0:T(8,128)(2,1)S(1)}, bf16[128,768]{1,0:T(8,128)(2,1)S(1)}, u32[]{:S(2)}, u32[]{:S(2)}) collective-permute-start(bf16[128,768]{1,0:T(8,128)(2,1)S(1)} %get-tuple-element.52), channel_id=1, source_target_pairs={{0,6},{1,7},{2,0},{3,1},{4,2},{5,3},{6,4},{7,5},{8,14},{9,15},{10,... | collective-permute-start | bytes 589832 | tf_op jit(solution)/shard_map/ppermute | solution.py:55
  51.7 9.1 %collective-permute-start.23 = (bf16[128,768]{1,0:T(8,128)(2,1)S(1)}, bf16[128,768]{1,0:T(8,128)(2,1)S(1)}, u32[]{:S(2)}, u32[]{:S(2)}) collective-permute-start(bf16[128,768]{1,0:T(8,128)(2,1)S(1)} %get-tuple-element.67), channel_id=1, source_target_pairs={{0,1},{1,0},{2,3},{3,2},{4,5},{5,4},{6,7},{7,6},{8,9},{9,8},{10,11... | collective-permute-start | bytes 589832 | tf_op jit(solution)/shard_map/ppermute | solution.py:59
  54.5 10.0 %collective-permute-start.24 = (bf16[128,768]{1,0:T(8,128)(2,1)S(1)}, bf16[128,768]{1,0:T(8,128)(2,1)S(1)}, u32[]{:S(2)}, u32[]{:S(2)}) collective-permute-start(bf16[128,768]{1,0:T(8,128)(2,1)S(1)} %get-tuple-element.68), channel_id=1, source_target_pairs={{0,1},{1,0},{2,3},{3,2},{4,5},{5,4},{6,7},{7,6},{8,9},{9,8},{10,11... | collective-permute-start | bytes 589832 | tf_op jit(solution)/shard_map/ppermute | solution.py:59
  57.7 10.3 %collective-permute-start.13 = (f32[64,768]{1,0:T(8,128)S(1)}, f32[64,768]{1,0:T(8,128)S(1)}, u32[]{:S(2)}, u32[]{:S(2)}) collective-permute-start(f32[64,768]{1,0:T(8,128)S(1)} %get-tuple-element.54), channel_id=1, source_target_pairs={{0,1},{1,0},{2,3},{3,2},{4,5},{5,4},{6,7},{7,6},{8,9},{9,8},{10,11... | collective-permute-start | bytes 589832 | tf_op jit(solution)/shard_map/ppermute | solution.py:59
  64.6 7.0 %collective-permute-start.25 = (bf16[64,768]{1,0:T(8,128)(2,1)S(1)}, bf16[64,768]{1,0:T(8,128)(2,1)S(1)}, u32[]{:S(2)}, u32[]{:S(2)}) collective-permute-start(bf16[64,768]{1,0:T(8,128)(2,1)S(1)} %get-tuple-element.70), channel_id=1, source_target_pairs={{0,2},{1,3},{2,4},{3,5},{4,6},{5,7},{6,0},{7,1},{8,10},{9,11},{10,... | collective-permute-start | bytes 294920 | tf_op jit(solution)/shard_map/ppermute | solution.py:55
  65.3 6.3 %collective-permute-start.26 = (bf16[64,768]{1,0:T(8,128)(2,1)S(1)}, bf16[64,768]{1,0:T(8,128)(2,1)S(1)}, u32[]{:S(2)}, u32[]{:S(2)}) collective-permute-start(bf16[64,768]{1,0:T(8,128)(2,1)S(1)} %get-tuple-element.71), channel_id=1, source_target_pairs={{0,4},{1,5},{2,6},{3,7},{4,0},{5,1},{6,2},{7,3},{8,12},{9,13},{10,... | collective-permute-start | bytes 294920 | tf_op jit(solution)/shard_map/ppermute | solution.py:55
  65.3 7.9 %collective-permute-start.27 = (bf16[64,768]{1,0:T(8,128)(2,1)S(1)}, bf16[64,768]{1,0:T(8,128)(2,1)S(1)}, u32[]{:S(2)}, u32[]{:S(2)}) collective-permute-start(bf16[64,768]{1,0:T(8,128)(2,1)S(1)} %get-tuple-element.72), channel_id=1, source_target_pairs={{0,6},{1,7},{2,0},{3,1},{4,2},{5,3},{6,4},{7,5},{8,14},{9,15},{10,... | collective-permute-start | bytes 294920 | tf_op jit(solution)/shard_map/ppermute | solution.py:55
  68.2 8.2 %collective-permute-start.14 = (bf16[64,768]{1,0:T(8,128)(2,1)S(1)}, bf16[64,768]{1,0:T(8,128)(2,1)S(1)}, u32[]{:S(2)}, u32[]{:S(2)}) collective-permute-start(bf16[64,768]{1,0:T(8,128)(2,1)S(1)} %get-tuple-element.55.own_ref), channel_id=1, source_target_pairs={{0,1},{1,0},{2,3},{3,2},{4,5},{5,4},{6,7},{7,6},{8,9},{9,8},{10,11... | collective-permute-start | bytes 294920 | tf_op jit(solution)/shard_map/ppermute | solution.py:59
  82.3 16.1 %collective-permute-start.31 = (bf16[256,768]{1,0:T(8,128)(2,1)S(1)}, bf16[256,768]{1,0:T(8,128)(2,1)S(1)}, u32[]{:S(2)}, u32[]{:S(2)}) collective-permute-start(bf16[256,768]{1,0:T(8,128)(2,1)S(1)} %grad_stack.1.own_ref), channel_id=1, source_target_pairs={{0,1},{1,0},{2,3},{3,2},{4,5},{5,4},{6,7},{7,6},{8,9},{9,8},{10,11... | collective-permute-start | bytes 1179656 | tf_op jit(solution)/shard_map/ppermute | solution.py:59
  87.3 7.3 %collective-permute-start.16 = (bf16[128,768]{1,0:T(8,128)(2,1)S(1)}, bf16[128,768]{1,0:T(8,128)(2,1)S(1)}, u32[]{:S(2)}, u32[]{:S(2)}) collective-permute-start(bf16[128,768]{1,0:T(8,128)(2,1)S(1)} %pair_z.1.refs_0_), channel_id=1, source_target_pairs={{4,0},{5,1},{6,2},{7,3},{0,4},{1,5},{2,6},{3,7},{12,8},{13,9},{14,... | collective-permute-start | bytes 589832 | tf_op jit(solution)/shard_map/ppermute | solution.py:51
  88.6 8.0 %collective-permute-start.17 = (bf16[128,768]{1,0:T(8,128)(2,1)S(1)}, bf16[128,768]{1,0:T(8,128)(2,1)S(1)}, u32[]{:S(2)}, u32[]{:S(2)}) collective-permute-start(bf16[128,768]{1,0:T(8,128)(2,1)S(1)} %pair_z.1.refs_0_), channel_id=1, source_target_pairs={{6,0},{7,1},{0,2},{1,3},{2,4},{3,5},{4,6},{5,7},{14,8},{15,9},{8,1... | collective-permute-start | bytes 589832 | tf_op jit(solution)/shard_map/ppermute | solution.py:51
  100.3 8.4 %collective-permute-start.32 = (f32[256,1536]{1,0:T(8,128)S(1)}, f32[256,1536]{1,0:T(8,128)S(1)}, u32[]{:S(2)}, u32[]{:S(2)}) collective-permute-start(f32[256,1536]{1,0:T(8,128)S(1)} %get-tuple-element.75), channel_id=1, source_target_pairs={{0,8},{8,0},{16,24},{24,16},{32,40},{40,32},{48,56},{56,48},{1,9},... | collective-permute-start | bytes 4718600 | tf_op jit(solution)/shard_map/ppermute | solution.py:39
  103.4 10.5 %collective-permute-start.19 = (bf16[64,1536]{1,0:T(8,128)(2,1)S(1)}, bf16[64,1536]{1,0:T(8,128)(2,1)S(1)}, u32[]{:S(2)}, u32[]{:S(2)}) collective-permute-start(bf16[64,1536]{1,0:T(8,128)(2,1)S(1)} %get-tuple-element.59), channel_id=1, source_target_pairs={{0,16},{8,24},{16,32},{24,40},{32,48},{40,56},{48,0},{56,8},{1,17}... | collective-permute-start | bytes 589832 | tf_op jit(solution)/shard_map/ppermute | solution.py:47
  105.0 17.4 %collective-permute-start.20 = (bf16[64,1536]{1,0:T(8,128)(2,1)S(1)}, bf16[64,1536]{1,0:T(8,128)(2,1)S(1)}, u32[]{:S(2)}, u32[]{:S(2)}) collective-permute-start(bf16[64,1536]{1,0:T(8,128)(2,1)S(1)} %get-tuple-element.60), channel_id=1, source_target_pairs={{0,32},{8,40},{16,48},{24,56},{32,0},{40,8},{48,16},{56,24},{1,33}... | collective-permute-start | bytes 589832 | tf_op jit(solution)/shard_map/ppermute | solution.py:47
  108.5 13.9 %collective-permute-start.21 = (bf16[64,1536]{1,0:T(8,128)(2,1)S(1)}, bf16[64,1536]{1,0:T(8,128)(2,1)S(1)}, u32[]{:S(2)}, u32[]{:S(2)}) collective-permute-start(bf16[64,1536]{1,0:T(8,128)(2,1)S(1)} %get-tuple-element.61), channel_id=1, source_target_pairs={{0,48},{8,56},{16,0},{24,8},{32,16},{40,24},{48,32},{56,40},{1,49}... | collective-permute-start | bytes 589832 | tf_op jit(solution)/shard_map/ppermute | solution.py:47
  110.5 11.9 %collective-permute-start.33 = (bf16[64,1536]{1,0:T(8,128)(2,1)S(1)}, bf16[64,1536]{1,0:T(8,128)(2,1)S(1)}, u32[]{:S(2)}, u32[]{:S(2)}) collective-permute-start(bf16[64,1536]{1,0:T(8,128)(2,1)S(1)} %get-tuple-element.77), channel_id=1, source_target_pairs={{0,16},{8,24},{16,32},{24,40},{32,48},{40,56},{48,0},{56,8},{1,17}... | collective-permute-start | bytes 589832 | tf_op jit(solution)/shard_map/ppermute | solution.py:47
  112.6 10.2 %collective-permute-start.34 = (bf16[64,1536]{1,0:T(8,128)(2,1)S(1)}, bf16[64,1536]{1,0:T(8,128)(2,1)S(1)}, u32[]{:S(2)}, u32[]{:S(2)}) collective-permute-start(bf16[64,1536]{1,0:T(8,128)(2,1)S(1)} %get-tuple-element.78), channel_id=1, source_target_pairs={{0,32},{8,40},{16,48},{24,56},{32,0},{40,8},{48,16},{56,24},{1,33}... | collective-permute-start | bytes 589832 | tf_op jit(solution)/shard_map/ppermute | solution.py:47
  113.9 12.1 %collective-permute-start.35 = (bf16[64,1536]{1,0:T(8,128)(2,1)S(1)}, bf16[64,1536]{1,0:T(8,128)(2,1)S(1)}, u32[]{:S(2)}, u32[]{:S(2)}) collective-permute-start(bf16[64,1536]{1,0:T(8,128)(2,1)S(1)} %get-tuple-element.79), channel_id=1, source_target_pairs={{0,48},{8,56},{16,0},{24,8},{32,16},{40,24},{48,32},{56,40},{1,49}... | collective-permute-start | bytes 589832 | tf_op jit(solution)/shard_map/ppermute | solution.py:47
  126.2 12.8 %collective-permute-start.36 = (bf16[32,1536]{1,0:T(8,128)(2,1)S(1)}, bf16[32,1536]{1,0:T(8,128)(2,1)S(1)}, u32[]{:S(2)}, u32[]{:S(2)}) collective-permute-start(bf16[32,1536]{1,0:T(8,128)(2,1)S(1)} %get-tuple-element.81), channel_id=1, source_target_pairs={{0,64},{64,128},{128,192},{192,0},{1,65},{65,129},{129,193},{193,1... | collective-permute-start | bytes 294920 | tf_op jit(solution)/shard_map/ppermute | solution.py:35
  128.9 11.1 %collective-permute-start.37 = (bf16[32,1536]{1,0:T(8,128)(2,1)S(1)}, bf16[32,1536]{1,0:T(8,128)(2,1)S(1)}, u32[]{:S(2)}, u32[]{:S(2)}) collective-permute-start(bf16[32,1536]{1,0:T(8,128)(2,1)S(1)} %get-tuple-element.82), channel_id=1, source_target_pairs={{0,128},{64,192},{128,0},{192,64},{1,129},{65,193},{129,1},{193,65... | collective-permute-start | bytes 294920 | tf_op jit(solution)/shard_map/ppermute | solution.py:35
  132.9 8.8 %collective-permute-start.38 = (bf16[32,1536]{1,0:T(8,128)(2,1)S(1)}, bf16[32,1536]{1,0:T(8,128)(2,1)S(1)}, u32[]{:S(2)}, u32[]{:S(2)}) collective-permute-start(bf16[32,1536]{1,0:T(8,128)(2,1)S(1)} %get-tuple-element.83), channel_id=1, source_target_pairs={{0,192},{64,0},{128,64},{192,128},{1,193},{65,1},{129,65},{193,129... | collective-permute-start | bytes 294920 | tf_op jit(solution)/shard_map/ppermute | solution.py:35
  (12 other events, 68.8 us)

commit v7 on v4

--- a/solution.py
+++ b/solution.py
@@ -22,6 +22,9 @@
         1.0 + 3.0 * cubic_term * value * value
     )
     return (result, slope)
+
+
+barrier = lax.optimization_barrier
 
 
 def from_gx(value, step):
@@ -82,9 +85,26 @@
     )(*args)
 
 
-def pair_kernel(inputs_ref, grads_ref, both_ref):
-    both_ref[:16, :] = inputs_ref[...]
-    both_ref[16:, :] = grads_ref[...]
+def pair_kernel(inputs_ref, grads_ref, both_ref, sems):
+    copies = [
+        pltpu.make_async_copy(source, both_ref.at[pl.ds(16 * i, 16), :], sems.at[i])
+        for i, source in enumerate((inputs_ref, grads_ref))
+    ]
+    for copy in copies:
+        copy.start()
+    for copy in copies:
+        copy.wait()
+
+
+def pair(inputs, grads):
+    return pl.pallas_call(
+        pair_kernel,
+        out_shape=jax.ShapeDtypeStruct((32, inputs.shape[1]), bf16),
+        in_specs=[pl.BlockSpec(memory_space=pl.ANY)] * 2,
+        out_specs=pl.BlockSpec(memory_space=pltpu.VMEM),
+        scratch_shapes=[pltpu.SemaphoreType.DMA((2,))],
+        name="pair",
+    )(inputs, grads)
 
 
 def columns_kernel(both_ref, first_ref, second_ref, third_ref, inputs_ref, grads_ref):
@@ -240,26 +260,39 @@
 
 
 def column_kernel(*refs):
-    mine_ref, sends = refs[8], refs[9:12]
+    mine_ref, sends = refs[4], refs[5:8]
     for step in range(4):
         rows = slice(16 * step, 16 * step + 16)
-        for part in range(2):
-            total = refs[4 * part][rows, :]
-            for piece in refs[4 * part + 1 : 4 * part + 4]:
-                total = total + piece[rows, :].astype(f32)
-            if step == 0:
-                mine_ref[16 * part : 16 * part + 16, :] = total
-            else:
-                sends[step - 1][16 * part : 16 * part + 16, :] = total.astype(bf16)
-
-
-def last_kernel(mine_ref, first_ref, second_ref, third_ref, *outs):
-    for part, out in enumerate(outs):
-        rows = slice(16 * part, 16 * part + 16)
-        total = mine_ref[rows, :]
-        for piece in (first_ref, second_ref, third_ref):
+        total = refs[0][rows, :]
+        for piece in refs[1:4]:
             total = total + piece[rows, :].astype(f32)
-        out[...] = total.astype(bf16)
+        if step == 0:
+            mine_ref[...] = total
+        else:
+            sends[step - 1][...] = total.astype(bf16)
+
+
+def last_kernel(mine_ref, first_ref, second_ref, third_ref, out_ref):
+    total = mine_ref[...]
+    for piece in (first_ref, second_ref, third_ref):
+        total = total + piece[...].astype(f32)
+    out_ref[...] = total.astype(bf16)
+
+
+def column_sum(mine, parts):
+    width = mine.shape[1]
+    mine, *sends = call(
+        column_kernel,
+        "column_sum",
+        [((16, width), f32)] + [((16, width), bf16)] * 3,
+        [mine] + list(parts),
+        moved=2**20,
+    )
+    return mine, [to_gx(send, step) for step, send in zip((1, 2, 3), sends)]
+
+
+def last_sum(mine, parts):
+    return call(last_kernel, "last_sum", [(mine.shape, bf16)], [mine] + list(parts), moved=2**18)[0]
 
 
 def units_far(kernel, name, index, pieces, weight, transposed):
@@ -295,7 +328,7 @@
     width, units = w_in.shape
     index = jnp.reshape(lax.axis_index("gz"), (1,)).astype(jnp.int32)
     steps = (1, 2, 3)
-    (both,) = call(pair_kernel, "pair", [((32, width), bf16)], [inputs, grad_out], moved=2**18)
+    both = pair(inputs, grad_out)
     columns = call(
         columns_kernel,
         "columns",
@@ -349,7 +382,7 @@
         [own, other_z(send)],
         moved=2**20,
     )
-    (pair,) = call(
+    (both_z,) = call(
         pair_z_kernel,
         "pair_z",
         [((128, units), bf16)],
@@ -364,7 +397,7 @@
         [mine] + [to_x(send, step) for step, send in zip(steps, sends)] + [slope],
         moved=2**20,
     )
-    hidden_pieces = [pair] + [from_x(pair, step) for step in steps]
+    hidden_pieces = [both_z] + [from_x(both_z, step) for step in steps]
     grad_stack = stack([grad_pre] + [from_x(grad_pre, step) for step in steps], "grad_stack")
     hidden_all, far_hidden = units_far(
         far_hidden_kernel, "far_hidden", index, hidden_pieces, w_out, False
@@ -374,26 +407,18 @@
     )
     mine_hidden, parts_hidden = units_near(0, hidden_all, w_out, far_hidden)
     mine_grad, parts_grad = units_near(1, grad_pre_all, w_in, far_grad)
-    mine, *sends = call(
-        column_kernel,
-        "column_sums",
-        [((32, width), f32)] + [((32, width), bf16)] * 3,
-        [mine_hidden] + parts_hidden + [mine_grad] + parts_grad,
-        moved=2 * 2**20,
-    )
-    output, grad_inputs = call(
-        last_kernel,
-        "last_sums",
-        [((16, width), bf16)] * 2,
-        [mine] + [to_gx(send, step) for step, send in zip(steps, sends)],
-        moved=2**19,
-    )
     grad_w_out = lax.dot_general(
         hidden_all, all_grads, (((0,), (0,)), ((), ())), preferred_element_type=f32
     ).astype(bf16)
     grad_w_in = lax.dot_general(
         all_inputs, grad_pre_all, (((0,), (0,)), ((), ())), preferred_element_type=f32
     ).astype(bf16)
+    parts_hidden, grad_w_out = barrier((parts_hidden, grad_w_out))
+    mine_hidden, ends_hidden = column_sum(mine_hidden, parts_hidden)
+    mine_grad, ends_grad = column_sum(mine_grad, parts_grad)
+    ends_hidden, mine_grad = barrier((ends_hidden, mine_grad))
+    output = last_sum(mine_hidden, ends_hidden)
+    grad_inputs = last_sum(mine_grad, ends_grad)
     return (output, grad_inputs, grad_w_in, grad_w_out)
 
 

time: 142 us -> 142 us (level); the launches traced: 140 us -> 141 us
  starting transfers between devices: 65.7 us -> 70.7 us
  waiting for transfers between devices: 49.8 us -> 45 us
  Pallas kernels: 16.2 us -> 18.3 us
    ppermute x3 -> x6, starting transfers between devices: 9.94 us -> 14.6 us  [to_gx(): return lax.ppermute(value, 'gx', [(i, (i + step) % 4) for i in range(4)])]
    ppermute x6, waiting for transfers between devices: 3.63 us -> 0.02 us  [to_y(): lax.ppermute(value, 'gy', [(i, (i + 2 * step) % 8) for i in range(8)])]
    pallas_call x0 -> x1, Pallas kernels: none -> 1.48 us  [pair(): pl.pallas_call(pair_kernel, out_shape=jax.ShapeDtypeStruct((32, inputs.sh...]
    pallas_call x18 -> x19, Pallas kernels: 16.2 us -> 16.8 us  [call(): pl.pallas_call(kernel, out_shape=[jax.ShapeDtypeStruct(*out) for out in o...]
  transfers between devices with their start and end apart: 38 -> 41, of which waited for: 24 -> 21; matrix products, arithmetic and copies ran while one was open for 4% -> 4% of each run, Pallas kernels for 11% -> 11%
where the time goes in v7:
time: 142 us; the launch traced here: 141 us
  starting transfers between devices  70.7 us (50%)
  waiting for transfers between devices  45 us (32%)
  Pallas kernels  18.3 us (13%)
  matrix products  5.65 us (4%)
    pallas_call x19, Pallas kernels, call(): pl.pallas_call(kernel, out_shape=[jax.ShapeDtypeStruct(*out) for out in o...  16.8 us
    ppermute x6, starting transfers between devices, to_gx(): return lax.ppermute(value, 'gx', [(i, (i + step) % 4) for i in range(4)])  14.6 us
    ppermute x6, starting transfers between devices, to_y(): lax.ppermute(value, 'gy', [(i, (i + 2 * step) % 8) for i in range(8)])  14.3 us
    ppermute x6, waiting for transfers between devices, from_x(): lax.ppermute(value, 'gz', [((i + 2 * step) % 8, i) for i in range(8)])  13.6 us
    ppermute x6, waiting for transfers between devices, from_y(): lax.ppermute(value, 'gy', [((i + 2 * step) % 8, i) for i in range(8)])  11.3 us
    ppermute x6, starting transfers between devices, to_x(): lax.ppermute(value, 'gz', [(i, (i + 2 * step) % 8) for i in range(8)])  11.3 us
    ppermute x3, starting transfers between devices, from_gx(): return lax.ppermute(value, 'gx', [((i + step) % 4, i) for i in range(4)])  10.2 us
    ppermute x6, waiting for transfers between devices, to_x(): lax.ppermute(value, 'gz', [(i, (i + 2 * step) % 8) for i in range(8)])  9.19 us
  transfers between devices with their start and end apart: 41, of which 21 were waited for; matrix products, arithmetic and copies ran while one was open for 4% of the time, Pallas kernels for 11%

profile of v7, /device:TPU:8, one launch (start us, length us, event | category | flops | bytes accessed | tf_op | source)
XLA Modules:
  0.0 141.3 jit_solution(8508476381665785546)
XLA Ops:
  2.1 6.4 %collective-permute-start = (bf16[32,1536]{1,0:T(8,128)(2,1)}, bf16[32,1536]{1,0:T(8,128)(2,1)S(1)}, u32[]{:S(2)}, u32[]{:S(2)}) collective-permute-start(bf16[32,1536]{1,0:T(8,128)(2,1)} %pair.1.both_ref), channel_id=1, source_target_pairs={{64,0},{128,64},{192,128},{0,192},{65,1},{129,65},{193,129},{1,193... | collective-permute-start | bytes 294920 | tf_op jit(solution)/shard_map/ppermute | solution.py:31
  9.5 2.8 %collective-permute-start.2 = (bf16[32,1536]{1,0:T(8,128)(2,1)}, bf16[32,1536]{1,0:T(8,128)(2,1)S(1)}, u32[]{:S(2)}, u32[]{:S(2)}) collective-permute-start(bf16[32,1536]{1,0:T(8,128)(2,1)} %pair.1.both_ref), channel_id=1, source_target_pairs={{192,0},{0,64},{64,128},{128,192},{193,1},{1,65},{65,129},{129,193... | collective-permute-start | bytes 294920 | tf_op jit(solution)/shard_map/ppermute | solution.py:31
  12.3 4.9 %collective-permute-done.first_ref = bf16[32,1536]{1,0:T(8,128)(2,1)S(1)} collective-permute-done((bf16[32,1536]{1,0:T(8,128)(2,1)}, bf16[32,1536]{1,0:T(8,128)(2,1)S(1)}, u32[]{:S(2)}, u32[]{:S(2)}) %collective-permute-start) | collective-permute-done | bytes 98336 | tf_op jit(solution)/shard_map/ppermute | solution.py:31
  17.2 3.1 %collective-permute-done.1.second_ref = bf16[32,1536]{1,0:T(8,128)(2,1)S(1)} collective-permute-done((bf16[32,1536]{1,0:T(8,128)(2,1)}, bf16[32,1536]{1,0:T(8,128)(2,1)S(1)}, u32[]{:S(2)}, u32[]{:S(2)}) %collective-permute-start.1) | collective-permute-done | bytes 98336 | tf_op jit(solution)/shard_map/ppermute | solution.py:31
  22.1 2.3 %collective-permute-start.20 = (bf16[64,1536]{1,0:T(8,128)(2,1)S(1)}, bf16[64,1536]{1,0:T(8,128)(2,1)S(1)}, u32[]{:S(2)}, u32[]{:S(2)}) collective-permute-start(bf16[64,1536]{1,0:T(8,128)(2,1)S(1)} %get-tuple-element.64.refs_0_), channel_id=1, source_target_pairs={{32,0},{40,8},{48,16},{56,24},{0,32},{8,40},{16,48},{24,56},{33,1}... | collective-permute-start | bytes 589832 | tf_op jit(solution)/shard_map/ppermute | solution.py:43
  27.7 2.6 %collective-permute-done.19.refs_1_ = bf16[64,1536]{1,0:T(8,128)(2,1)S(1)} collective-permute-done((bf16[64,1536]{1,0:T(8,128)(2,1)S(1)}, bf16[64,1536]{1,0:T(8,128)(2,1)S(1)}, u32[]{:S(2)}, u32[]{:S(2)}) %collective-permute-start.19) | collective-permute-done | bytes 196640 | tf_op jit(solution)/shard_map/ppermute | solution.py:43
  30.7 3.7 %collective-permute-done.20.refs_2_ = bf16[64,1536]{1,0:T(8,128)(2,1)S(1)} collective-permute-done((bf16[64,1536]{1,0:T(8,128)(2,1)S(1)}, bf16[64,1536]{1,0:T(8,128)(2,1)S(1)}, u32[]{:S(2)}, u32[]{:S(2)}) %collective-permute-start.20) | collective-permute-done | bytes 196640 | tf_op jit(solution)/shard_map/ppermute | solution.py:43
  36.6 2.1 %collective-permute-done.4.refs_2_ = bf16[64,1536]{1,0:T(8,128)(2,1)S(1)} collective-permute-done((bf16[64,1536]{1,0:T(8,128)(2,1)S(1)}, bf16[64,1536]{1,0:T(8,128)(2,1)S(1)}, u32[]{:S(2)}, u32[]{:S(2)}) %collective-permute-start.4) | collective-permute-done | bytes 196640 | tf_op jit(solution)/shard_map/ppermute | solution.py:43
  40.5 3.3 %width_grad.1 = (bf16[512,1536]{1,0:T(8,128)(2,1)S(1)}, f32[256,768]{1,0:T(8,128)S(1)}, bf16[256,768]{1,0:T(8,128)(2,1)S(1)}) custom-call(s32[1]{0:T(128)} %bitcast.index_ref, bf16[256,1536]{1,0:T(8,128)(2,1)S(1)} %plane.3.near_ref, bf16[256,1536]{1,0:T(8,128)(2,1)} %collective-permute-done.22.far_ref, bf16[768,1536]{1,0:T(8,128)(2,1)S(1)} %copy-done), custom_call_target="tpu_custom_call" | custom-call | flops 1207959552 | bytes 6291456 | tf_op jit(solution)/shard_map/width_grad/pallas_call | solution.py:75
  43.9 2.9 %collective-permute-start.26 = (bf16[256,768]{1,0:T(8,128)(2,1)S(1)}, bf16[256,768]{1,0:T(8,128)(2,1)S(1)}, u32[]{:S(2)}, u32[]{:S(2)}) collective-permute-start(bf16[256,768]{1,0:T(8,128)(2,1)S(1)} %get-tuple-element.74), channel_id=1, source_target_pairs={{0,1},{1,0},{2,3},{3,2},{4,5},{5,4},{6,7},{7,6},{8,9},{9,8},{10,11... | collective-permute-start | bytes 1179656 | tf_op jit(solution)/shard_map/ppermute | solution.py:59
  46.8 3.4 %width_inputs.1 = (bf16[512,1536]{1,0:T(8,128)(2,1)S(1)}, f32[128,768]{1,0:T(8,128)S(1)}, bf16[128,768]{1,0:T(8,128)(2,1)S(1)}, bf16[128,768]{1,0:T(8,128)(2,1)S(1)}, bf16[128,768]{1,0:T(8,128)(2,1)S(1)}) custom-call(s32[1]{0:T(128)} %bitcast.index_ref, bf16[256,1536]{1,0:T(8,128)(2,1)} %plane.2.near_ref, bf16[256,1536]{1,0:T(8,128)(2,1)} %collective-permute-done.6.far_ref, ...), custom_call_target="tpu_custom_call" | custom-call | flops 1207959552 | bytes 6291456 | tf_op jit(solution)/shard_map/width_inputs/pallas_call | solution.py:75
  51.7 2.7 %collective-permute-start.8 = (bf16[128,768]{1,0:T(8,128)(2,1)S(1)}, bf16[128,768]{1,0:T(8,128)(2,1)S(1)}, u32[]{:S(2)}, u32[]{:S(2)}) collective-permute-start(bf16[128,768]{1,0:T(8,128)(2,1)S(1)} %get-tuple-element.53), channel_id=1, source_target_pairs={{0,4},{1,5},{2,6},{3,7},{4,0},{5,1},{6,2},{7,3},{8,12},{9,13},{10,... | collective-permute-start | bytes 589832 | tf_op jit(solution)/shard_map/ppermute | solution.py:55
  55.9 2.6 %collective-permute-done.7.first_ref = bf16[128,768]{1,0:T(8,128)(2,1)S(1)} collective-permute-done((bf16[128,768]{1,0:T(8,128)(2,1)S(1)}, bf16[128,768]{1,0:T(8,128)(2,1)S(1)}, u32[]{:S(2)}, u32[]{:S(2)}) %collective-permute-start.7) | collective-permute-done | bytes 196640 | tf_op jit(solution)/shard_map/ppermute | solution.py:55
  58.4 5.2 %collective-permute-done.8.second_ref = bf16[128,768]{1,0:T(8,128)(2,1)S(1)} collective-permute-done((bf16[128,768]{1,0:T(8,128)(2,1)S(1)}, bf16[128,768]{1,0:T(8,128)(2,1)S(1)}, u32[]{:S(2)}, u32[]{:S(2)}) %collective-permute-start.8) | collective-permute-done | bytes 196640 | tf_op jit(solution)/shard_map/ppermute | solution.py:55
  65.9 2.4 %collective-permute-start.28 = (bf16[64,768]{1,0:T(8,128)(2,1)S(1)}, bf16[64,768]{1,0:T(8,128)(2,1)S(1)}, u32[]{:S(2)}, u32[]{:S(2)}) collective-permute-start(bf16[64,768]{1,0:T(8,128)(2,1)S(1)} %get-tuple-element.77), channel_id=1, source_target_pairs={{0,4},{1,5},{2,6},{3,7},{4,0},{5,1},{6,2},{7,3},{8,12},{9,13},{10,... | collective-permute-start | bytes 294920 | tf_op jit(solution)/shard_map/ppermute | solution.py:55
  73.3 2.7 %collective-permute-start.30 = (bf16[64,768]{1,0:T(8,128)(2,1)S(1)}, bf16[64,768]{1,0:T(8,128)(2,1)S(1)}, u32[]{:S(2)}, u32[]{:S(2)}) collective-permute-start(bf16[64,768]{1,0:T(8,128)(2,1)S(1)} %grad_pre.1.refs_0_), channel_id=1, source_target_pairs={{2,0},{3,1},{4,2},{5,3},{6,4},{7,5},{0,6},{1,7},{10,8},{11,9},{12,... | collective-permute-start | bytes 294920 | tf_op jit(solution)/shard_map/ppermute | solution.py:51
  77.0 2.2 %collective-permute-done.30.refs_1_ = bf16[64,768]{1,0:T(8,128)(2,1)S(1)} collective-permute-done((bf16[64,768]{1,0:T(8,128)(2,1)S(1)}, bf16[64,768]{1,0:T(8,128)(2,1)S(1)}, u32[]{:S(2)}, u32[]{:S(2)}) %collective-permute-start.30) | collective-permute-done | bytes 98336 | tf_op jit(solution)/shard_map/ppermute | solution.py:51
  79.3 3.0 %collective-permute-done.31.refs_2_ = bf16[64,768]{1,0:T(8,128)(2,1)S(1)} collective-permute-done((bf16[64,768]{1,0:T(8,128)(2,1)S(1)}, bf16[64,768]{1,0:T(8,128)(2,1)S(1)}, u32[]{:S(2)}, u32[]{:S(2)}) %collective-permute-start.31) | collective-permute-done | bytes 98336 | tf_op jit(solution)/shard_map/ppermute | solution.py:51
  87.5 3.3 %collective-permute-done.12.refs_1_ = bf16[128,768]{1,0:T(8,128)(2,1)S(1)} collective-permute-done((bf16[128,768]{1,0:T(8,128)(2,1)S(1)}, bf16[128,768]{1,0:T(8,128)(2,1)S(1)}, u32[]{:S(2)}, u32[]{:S(2)}) %collective-permute-start.12) | collective-permute-done | bytes 196640 | tf_op jit(solution)/shard_map/ppermute | solution.py:51
  90.7 2.2 %collective-permute-done.13.refs_2_ = bf16[128,768]{1,0:T(8,128)(2,1)S(1)} collective-permute-done((bf16[128,768]{1,0:T(8,128)(2,1)S(1)}, bf16[128,768]{1,0:T(8,128)(2,1)S(1)}, u32[]{:S(2)}, u32[]{:S(2)}) %collective-permute-start.13) | collective-permute-done | bytes 196640 | tf_op jit(solution)/shard_map/ppermute | solution.py:51
  92.9 2.0 %collective-permute-done.14.refs_3_ = bf16[128,768]{1,0:T(8,128)(2,1)S(1)} collective-permute-done((bf16[128,768]{1,0:T(8,128)(2,1)S(1)}, bf16[128,768]{1,0:T(8,128)(2,1)S(1)}, u32[]{:S(2)}, u32[]{:S(2)}) %collective-permute-start.14) | collective-permute-done | bytes 196640 | tf_op jit(solution)/shard_map/ppermute | solution.py:51
  96.7 1.9 %far_grad.1 = (bf16[512,768]{1,0:T(8,128)(2,1)S(1)}, f32[256,1536]{1,0:T(8,128)S(1)}) custom-call(s32[1]{0:T(128)} %bitcast.index_ref, bf16[256,768]{1,0:T(8,128)(2,1)S(1)} %grad_stack.1.own_ref, bf16[256,768]{1,0:T(8,128)(2,1)S(1)} %collective-permute-done.33.part_ref, bf16[1536,768]{1,0:T(8,128)(2,1)S(1)} %copy-done.1), custom_call_target="tpu_custom_call" | custom-call | flops 603979776 | bytes 6291456 | tf_op jit(solution)/shard_map/far_grad/pallas_call | solution.py:75
  103.3 3.5 %collective-permute-start.17 = (bf16[64,1536]{1,0:T(8,128)(2,1)S(1)}, bf16[64,1536]{1,0:T(8,128)(2,1)S(1)}, u32[]{:S(2)}, u32[]{:S(2)}) collective-permute-start(bf16[64,1536]{1,0:T(8,128)(2,1)S(1)} %get-tuple-element.62), channel_id=1, source_target_pairs={{0,32},{8,40},{16,48},{24,56},{32,0},{40,8},{48,16},{56,24},{1,33}... | collective-permute-start | bytes 589832 | tf_op jit(solution)/shard_map/ppermute | solution.py:47
  108.6 2.1 %collective-permute-start.35 = (bf16[64,1536]{1,0:T(8,128)(2,1)S(1)}, bf16[64,1536]{1,0:T(8,128)(2,1)S(1)}, u32[]{:S(2)}, u32[]{:S(2)}) collective-permute-start(bf16[64,1536]{1,0:T(8,128)(2,1)S(1)} %get-tuple-element.83), channel_id=1, source_target_pairs={{0,16},{8,24},{16,32},{24,40},{32,48},{40,56},{48,0},{56,8},{1,17}... | collective-permute-start | bytes 589832 | tf_op jit(solution)/shard_map/ppermute | solution.py:47
  112.0 5.9 %collective-permute-start.37 = (bf16[64,1536]{1,0:T(8,128)(2,1)S(1)}, bf16[64,1536]{1,0:T(8,128)(2,1)S(1)}, u32[]{:S(2)}, u32[]{:S(2)}) collective-permute-start(bf16[64,1536]{1,0:T(8,128)(2,1)S(1)} %get-tuple-element.85), channel_id=1, source_target_pairs={{0,48},{8,56},{16,0},{24,8},{32,16},{40,24},{48,32},{56,40},{1,49}... | collective-permute-start | bytes 589832 | tf_op jit(solution)/shard_map/ppermute | solution.py:47
  117.9 2.8 %convolution_convert_fusion.1 = bf16[768,1536]{1,0:T(8,128)(2,1)} fusion(bf16[512,768]{1,0:T(8,128)(2,1)S(1)} %get-tuple-element.58.whole_ref, bf16[512,1536]{1,0:T(8,128)(2,1)S(1)} %get-tuple-element.65), kind=kOutput, calls=%fused_computation.1 | convolution fusion | flops 1209139200 | bytes 4718592 | tf_op jit(solution)/shard_map/dot_general | solution.py:410
  120.8 2.7 %collective-permute-start.23 = (bf16[16,1536]{1,0:T(8,128)(2,1)S(1)}, bf16[16,1536]{1,0:T(8,128)(2,1)S(1)}, u32[]{:S(2)}, u32[]{:S(2)}) collective-permute-start(bf16[16,1536]{1,0:T(8,128)(2,1)S(1)} %get-tuple-element.70), channel_id=1, source_target_pairs={{0,64},{64,128},{128,192},{192,0},{1,65},{65,129},{129,193},{193,1... | collective-permute-start | bytes 147464 | tf_op jit(solution)/shard_map/ppermute | solution.py:35
  123.5 4.0 %collective-permute-start.24 = (bf16[16,1536]{1,0:T(8,128)(2,1)S(1)}, bf16[16,1536]{1,0:T(8,128)(2,1)S(1)}, u32[]{:S(2)}, u32[]{:S(2)}) collective-permute-start(bf16[16,1536]{1,0:T(8,128)(2,1)S(1)} %get-tuple-element.71), channel_id=1, source_target_pairs={{0,128},{64,192},{128,0},{192,64},{1,129},{65,193},{129,1},{193,65... | collective-permute-start | bytes 147464 | tf_op jit(solution)/shard_map/ppermute | solution.py:35
  127.5 3.2 %collective-permute-start.25 = (bf16[16,1536]{1,0:T(8,128)(2,1)S(1)}, bf16[16,1536]{1,0:T(8,128)(2,1)S(1)}, u32[]{:S(2)}, u32[]{:S(2)}) collective-permute-start(bf16[16,1536]{1,0:T(8,128)(2,1)S(1)} %get-tuple-element.72), channel_id=1, source_target_pairs={{0,192},{64,0},{128,64},{192,128},{1,193},{65,1},{129,65},{193,129... | collective-permute-start | bytes 147464 | tf_op jit(solution)/shard_map/ppermute | solution.py:35
  130.9 2.4 %collective-permute-start.39 = (bf16[16,1536]{1,0:T(8,128)(2,1)S(1)}, bf16[16,1536]{1,0:T(8,128)(2,1)S(1)}, u32[]{:S(2)}, u32[]{:S(2)}) collective-permute-start(bf16[16,1536]{1,0:T(8,128)(2,1)S(1)} %get-tuple-element.92), channel_id=1, source_target_pairs={{0,128},{64,192},{128,0},{192,64},{1,129},{65,193},{129,1},{193,65... | collective-permute-start | bytes 147464 | tf_op jit(solution)/shard_map/ppermute | solution.py:35
  133.3 2.2 %collective-permute-start.40 = (bf16[16,1536]{1,0:T(8,128)(2,1)S(1)}, bf16[16,1536]{1,0:T(8,128)(2,1)S(1)}, u32[]{:S(2)}, u32[]{:S(2)}) collective-permute-start(bf16[16,1536]{1,0:T(8,128)(2,1)S(1)} %get-tuple-element.93), channel_id=1, source_target_pairs={{0,192},{64,0},{128,64},{192,128},{1,193},{65,1},{129,65},{193,129... | collective-permute-start | bytes 147464 | tf_op jit(solution)/shard_map/ppermute | solution.py:35
  135.5 2.8 %convolution_convert_fusion = bf16[1536,768]{1,0:T(8,128)(2,1)} fusion(bf16[512,1536]{1,0:T(8,128)(2,1)S(1)} %get-tuple-element.94, bf16[512,768]{1,0:T(8,128)(2,1)S(1)} %get-tuple-element.80.whole_ref), kind=kOutput, calls=%fused_computation | convolution fusion | flops 1209139200 | bytes 4718592 | tf_op jit(solution)/shard_map/dot_general | solution.py:413
  (78 shorter events, 41.0 us)
Async XLA Ops:
  2.1 15.1 %collective-permute-start = (bf16[32,1536]{1,0:T(8,128)(2,1)}, bf16[32,1536]{1,0:T(8,128)(2,1)S(1)}, u32[]{:S(2)}, u32[]{:S(2)}) collective-permute-start(bf16[32,1536]{1,0:T(8,128)(2,1)} %pair.1.both_ref), channel_id=1, source_target_pairs={{64,0},{128,64},{192,128},{0,192},{65,1},{129,65},{193,129},{1,193... | collective-permute-start | bytes 294920 | tf_op jit(solution)/shard_map/ppermute | solution.py:31
  8.5 11.8 %collective-permute-start.1 = (bf16[32,1536]{1,0:T(8,128)(2,1)}, bf16[32,1536]{1,0:T(8,128)(2,1)S(1)}, u32[]{:S(2)}, u32[]{:S(2)}) collective-permute-start(bf16[32,1536]{1,0:T(8,128)(2,1)} %pair.1.both_ref), channel_id=1, source_target_pairs={{128,0},{192,64},{0,128},{64,192},{129,1},{193,65},{1,129},{65,193... | collective-permute-start | bytes 294920 | tf_op jit(solution)/shard_map/ppermute | solution.py:31
  9.5 10.8 %collective-permute-start.2 = (bf16[32,1536]{1,0:T(8,128)(2,1)}, bf16[32,1536]{1,0:T(8,128)(2,1)S(1)}, u32[]{:S(2)}, u32[]{:S(2)}) collective-permute-start(bf16[32,1536]{1,0:T(8,128)(2,1)} %pair.1.both_ref), channel_id=1, source_target_pairs={{192,0},{0,64},{64,128},{128,192},{193,1},{1,65},{65,129},{129,193... | collective-permute-start | bytes 294920 | tf_op jit(solution)/shard_map/ppermute | solution.py:31
  21.2 9.1 %collective-permute-start.19 = (bf16[64,1536]{1,0:T(8,128)(2,1)S(1)}, bf16[64,1536]{1,0:T(8,128)(2,1)S(1)}, u32[]{:S(2)}, u32[]{:S(2)}) collective-permute-start(bf16[64,1536]{1,0:T(8,128)(2,1)S(1)} %get-tuple-element.64.refs_0_), channel_id=1, source_target_pairs={{16,0},{24,8},{32,16},{40,24},{48,32},{56,40},{0,48},{8,56},{17,1}... | collective-permute-start | bytes 589832 | tf_op jit(solution)/shard_map/ppermute | solution.py:43
  22.1 12.4 %collective-permute-start.20 = (bf16[64,1536]{1,0:T(8,128)(2,1)S(1)}, bf16[64,1536]{1,0:T(8,128)(2,1)S(1)}, u32[]{:S(2)}, u32[]{:S(2)}) collective-permute-start(bf16[64,1536]{1,0:T(8,128)(2,1)S(1)} %get-tuple-element.64.refs_0_), channel_id=1, source_target_pairs={{32,0},{40,8},{48,16},{56,24},{0,32},{8,40},{16,48},{24,56},{33,1}... | collective-permute-start | bytes 589832 | tf_op jit(solution)/shard_map/ppermute | solution.py:43
  24.4 10.9 %collective-permute-start.21 = (bf16[64,1536]{1,0:T(8,128)(2,1)S(1)}, bf16[64,1536]{1,0:T(8,128)(2,1)S(1)}, u32[]{:S(2)}, u32[]{:S(2)}) collective-permute-start(bf16[64,1536]{1,0:T(8,128)(2,1)S(1)} %get-tuple-element.64.refs_0_), channel_id=1, source_target_pairs={{48,0},{56,8},{0,16},{8,24},{16,32},{24,40},{32,48},{40,56},{49,1}... | collective-permute-start | bytes 589832 | tf_op jit(solution)/shard_map/ppermute | solution.py:43
  26.3 10.3 %collective-permute-start.3 = (bf16[64,1536]{1,0:T(8,128)(2,1)S(1)}, bf16[64,1536]{1,0:T(8,128)(2,1)S(1)}, u32[]{:S(2)}, u32[]{:S(2)}) collective-permute-start(bf16[64,1536]{1,0:T(8,128)(2,1)S(1)} %get-tuple-element.50.refs_0_), channel_id=1, source_target_pairs={{16,0},{24,8},{32,16},{40,24},{48,32},{56,40},{0,48},{8,56},{17,1}... | collective-permute-start | bytes 589832 | tf_op jit(solution)/shard_map/ppermute | solution.py:43
  26.4 12.4 %collective-permute-start.4 = (bf16[64,1536]{1,0:T(8,128)(2,1)S(1)}, bf16[64,1536]{1,0:T(8,128)(2,1)S(1)}, u32[]{:S(2)}, u32[]{:S(2)}) collective-permute-start(bf16[64,1536]{1,0:T(8,128)(2,1)S(1)} %get-tuple-element.50.refs_0_), channel_id=1, source_target_pairs={{32,0},{40,8},{48,16},{56,24},{0,32},{8,40},{16,48},{24,56},{33,1}... | collective-permute-start | bytes 589832 | tf_op jit(solution)/shard_map/ppermute | solution.py:43
  30.4 9.2 %collective-permute-start.5 = (bf16[64,1536]{1,0:T(8,128)(2,1)S(1)}, bf16[64,1536]{1,0:T(8,128)(2,1)S(1)}, u32[]{:S(2)}, u32[]{:S(2)}) collective-permute-start(bf16[64,1536]{1,0:T(8,128)(2,1)S(1)} %get-tuple-element.50.refs_0_), channel_id=1, source_target_pairs={{48,0},{56,8},{0,16},{8,24},{16,32},{24,40},{32,48},{40,56},{49,1}... | collective-permute-start | bytes 589832 | tf_op jit(solution)/shard_map/ppermute | solution.py:43
  43.9 20.3 %collective-permute-start.26 = (bf16[256,768]{1,0:T(8,128)(2,1)S(1)}, bf16[256,768]{1,0:T(8,128)(2,1)S(1)}, u32[]{:S(2)}, u32[]{:S(2)}) collective-permute-start(bf16[256,768]{1,0:T(8,128)(2,1)S(1)} %get-tuple-element.74), channel_id=1, source_target_pairs={{0,1},{1,0},{2,3},{3,2},{4,5},{5,4},{6,7},{7,6},{8,9},{9,8},{10,11... | collective-permute-start | bytes 1179656 | tf_op jit(solution)/shard_map/ppermute | solution.py:59
  50.1 8.3 %collective-permute-start.7 = (bf16[128,768]{1,0:T(8,128)(2,1)S(1)}, bf16[128,768]{1,0:T(8,128)(2,1)S(1)}, u32[]{:S(2)}, u32[]{:S(2)}) collective-permute-start(bf16[128,768]{1,0:T(8,128)(2,1)S(1)} %get-tuple-element.52), channel_id=1, source_target_pairs={{0,2},{1,3},{2,4},{3,5},{4,6},{5,7},{6,0},{7,1},{8,10},{9,11},{10,... | collective-permute-start | bytes 589832 | tf_op jit(solution)/shard_map/ppermute | solution.py:55
  51.7 11.9 %collective-permute-start.8 = (bf16[128,768]{1,0:T(8,128)(2,1)S(1)}, bf16[128,768]{1,0:T(8,128)(2,1)S(1)}, u32[]{:S(2)}, u32[]{:S(2)}) collective-permute-start(bf16[128,768]{1,0:T(8,128)(2,1)S(1)} %get-tuple-element.53), channel_id=1, source_target_pairs={{0,4},{1,5},{2,6},{3,7},{4,0},{5,1},{6,2},{7,3},{8,12},{9,13},{10,... | collective-permute-start | bytes 589832 | tf_op jit(solution)/shard_map/ppermute | solution.py:55
  54.4 9.2 %collective-permute-start.9 = (bf16[128,768]{1,0:T(8,128)(2,1)S(1)}, bf16[128,768]{1,0:T(8,128)(2,1)S(1)}, u32[]{:S(2)}, u32[]{:S(2)}) collective-permute-start(bf16[128,768]{1,0:T(8,128)(2,1)S(1)} %get-tuple-element.54), channel_id=1, source_target_pairs={{0,6},{1,7},{2,0},{3,1},{4,2},{5,3},{6,4},{7,5},{8,14},{9,15},{10,... | collective-permute-start | bytes 589832 | tf_op jit(solution)/shard_map/ppermute | solution.py:55
  64.4 7.5 %collective-permute-start.27 = (bf16[64,768]{1,0:T(8,128)(2,1)S(1)}, bf16[64,768]{1,0:T(8,128)(2,1)S(1)}, u32[]{:S(2)}, u32[]{:S(2)}) collective-permute-start(bf16[64,768]{1,0:T(8,128)(2,1)S(1)} %get-tuple-element.76), channel_id=1, source_target_pairs={{0,2},{1,3},{2,4},{3,5},{4,6},{5,7},{6,0},{7,1},{8,10},{9,11},{10,... | collective-permute-start | bytes 294920 | tf_op jit(solution)/shard_map/ppermute | solution.py:55
  65.9 6.9 %collective-permute-start.28 = (bf16[64,768]{1,0:T(8,128)(2,1)S(1)}, bf16[64,768]{1,0:T(8,128)(2,1)S(1)}, u32[]{:S(2)}, u32[]{:S(2)}) collective-permute-start(bf16[64,768]{1,0:T(8,128)(2,1)S(1)} %get-tuple-element.77), channel_id=1, source_target_pairs={{0,4},{1,5},{2,6},{3,7},{4,0},{5,1},{6,2},{7,3},{8,12},{9,13},{10,... | collective-permute-start | bytes 294920 | tf_op jit(solution)/shard_map/ppermute | solution.py:55
  70.2 6.8 %collective-permute-start.11 = (bf16[64,768]{1,0:T(8,128)(2,1)S(1)}, bf16[64,768]{1,0:T(8,128)(2,1)S(1)}, u32[]{:S(2)}, u32[]{:S(2)}) collective-permute-start(bf16[64,768]{1,0:T(8,128)(2,1)S(1)} %get-tuple-element.57.own_ref), channel_id=1, source_target_pairs={{0,1},{1,0},{2,3},{3,2},{4,5},{5,4},{6,7},{7,6},{8,9},{9,8},{10,11... | collective-permute-start | bytes 294920 | tf_op jit(solution)/shard_map/ppermute | solution.py:59
  83.3 13.4 %collective-permute-start.33 = (bf16[256,768]{1,0:T(8,128)(2,1)S(1)}, bf16[256,768]{1,0:T(8,128)(2,1)S(1)}, u32[]{:S(2)}, u32[]{:S(2)}) collective-permute-start(bf16[256,768]{1,0:T(8,128)(2,1)S(1)} %grad_stack.1.own_ref), channel_id=1, source_target_pairs={{0,1},{1,0},{2,3},{3,2},{4,5},{5,4},{6,7},{7,6},{8,9},{9,8},{10,11... | collective-permute-start | bytes 1179656 | tf_op jit(solution)/shard_map/ppermute | solution.py:59
  85.6 7.3 %collective-permute-start.13 = (bf16[128,768]{1,0:T(8,128)(2,1)S(1)}, bf16[128,768]{1,0:T(8,128)(2,1)S(1)}, u32[]{:S(2)}, u32[]{:S(2)}) collective-permute-start(bf16[128,768]{1,0:T(8,128)(2,1)S(1)} %pair_z.1.refs_0_), channel_id=1, source_target_pairs={{4,0},{5,1},{6,2},{7,3},{0,4},{1,5},{2,6},{3,7},{12,8},{13,9},{14,... | collective-permute-start | bytes 589832 | tf_op jit(solution)/shard_map/ppermute | solution.py:51
  86.2 8.7 %collective-permute-start.14 = (bf16[128,768]{1,0:T(8,128)(2,1)S(1)}, bf16[128,768]{1,0:T(8,128)(2,1)S(1)}, u32[]{:S(2)}, u32[]{:S(2)}) collective-permute-start(bf16[128,768]{1,0:T(8,128)(2,1)S(1)} %pair_z.1.refs_0_), channel_id=1, source_target_pairs={{6,0},{7,1},{0,2},{1,3},{2,4},{3,5},{4,6},{5,7},{14,8},{15,9},{8,1... | collective-permute-start | bytes 589832 | tf_op jit(solution)/shard_map/ppermute | solution.py:51
  98.6 8.2 %collective-permute-start.34 = (f32[256,1536]{1,0:T(8,128)S(1)}, f32[256,1536]{1,0:T(8,128)S(1)}, u32[]{:S(2)}, u32[]{:S(2)}) collective-permute-start(f32[256,1536]{1,0:T(8,128)S(1)} %get-tuple-element.81), channel_id=1, source_target_pairs={{0,8},{8,0},{16,24},{24,16},{32,40},{40,32},{48,56},{56,48},{1,9},... | collective-permute-start | bytes 4718600 | tf_op jit(solution)/shard_map/ppermute | solution.py:39
  101.7 10.2 %collective-permute-start.16 = (bf16[64,1536]{1,0:T(8,128)(2,1)S(1)}, bf16[64,1536]{1,0:T(8,128)(2,1)S(1)}, u32[]{:S(2)}, u32[]{:S(2)}) collective-permute-start(bf16[64,1536]{1,0:T(8,128)(2,1)S(1)} %get-tuple-element.61), channel_id=1, source_target_pairs={{0,16},{8,24},{16,32},{24,40},{32,48},{40,56},{48,0},{56,8},{1,17}... | collective-permute-start | bytes 589832 | tf_op jit(solution)/shard_map/ppermute | solution.py:47
  103.3 17.4 %collective-permute-start.17 = (bf16[64,1536]{1,0:T(8,128)(2,1)S(1)}, bf16[64,1536]{1,0:T(8,128)(2,1)S(1)}, u32[]{:S(2)}, u32[]{:S(2)}) collective-permute-start(bf16[64,1536]{1,0:T(8,128)(2,1)S(1)} %get-tuple-element.62), channel_id=1, source_target_pairs={{0,32},{8,40},{16,48},{24,56},{32,0},{40,8},{48,16},{56,24},{1,33}... | collective-permute-start | bytes 589832 | tf_op jit(solution)/shard_map/ppermute | solution.py:47
  106.8 13.9 %collective-permute-start.18 = (bf16[64,1536]{1,0:T(8,128)(2,1)S(1)}, bf16[64,1536]{1,0:T(8,128)(2,1)S(1)}, u32[]{:S(2)}, u32[]{:S(2)}) collective-permute-start(bf16[64,1536]{1,0:T(8,128)(2,1)S(1)} %get-tuple-element.63), channel_id=1, source_target_pairs={{0,48},{8,56},{16,0},{24,8},{32,16},{40,24},{48,32},{56,40},{1,49}... | collective-permute-start | bytes 589832 | tf_op jit(solution)/shard_map/ppermute | solution.py:47
  108.6 18.9 %collective-permute-start.35 = (bf16[64,1536]{1,0:T(8,128)(2,1)S(1)}, bf16[64,1536]{1,0:T(8,128)(2,1)S(1)}, u32[]{:S(2)}, u32[]{:S(2)}) collective-permute-start(bf16[64,1536]{1,0:T(8,128)(2,1)S(1)} %get-tuple-element.83), channel_id=1, source_target_pairs={{0,16},{8,24},{16,32},{24,40},{32,48},{40,56},{48,0},{56,8},{1,17}... | collective-permute-start | bytes 589832 | tf_op jit(solution)/shard_map/ppermute | solution.py:47
  110.7 20.0 %collective-permute-start.36 = (bf16[64,1536]{1,0:T(8,128)(2,1)S(1)}, bf16[64,1536]{1,0:T(8,128)(2,1)S(1)}, u32[]{:S(2)}, u32[]{:S(2)}) collective-permute-start(bf16[64,1536]{1,0:T(8,128)(2,1)S(1)} %get-tuple-element.84), channel_id=1, source_target_pairs={{0,32},{8,40},{16,48},{24,56},{32,0},{40,8},{48,16},{56,24},{1,33}... | collective-permute-start | bytes 589832 | tf_op jit(solution)/shard_map/ppermute | solution.py:47
  112.0 18.8 %collective-permute-start.37 = (bf16[64,1536]{1,0:T(8,128)(2,1)S(1)}, bf16[64,1536]{1,0:T(8,128)(2,1)S(1)}, u32[]{:S(2)}, u32[]{:S(2)}) collective-permute-start(bf16[64,1536]{1,0:T(8,128)(2,1)S(1)} %get-tuple-element.85), channel_id=1, source_target_pairs={{0,48},{8,56},{16,0},{24,8},{32,16},{40,24},{48,32},{56,40},{1,49}... | collective-permute-start | bytes 589832 | tf_op jit(solution)/shard_map/ppermute | solution.py:47
  120.8 12.5 %collective-permute-start.23 = (bf16[16,1536]{1,0:T(8,128)(2,1)S(1)}, bf16[16,1536]{1,0:T(8,128)(2,1)S(1)}, u32[]{:S(2)}, u32[]{:S(2)}) collective-permute-start(bf16[16,1536]{1,0:T(8,128)(2,1)S(1)} %get-tuple-element.70), channel_id=1, source_target_pairs={{0,64},{64,128},{128,192},{192,0},{1,65},{65,129},{129,193},{193,1... | collective-permute-start | bytes 147464 | tf_op jit(solution)/shard_map/ppermute | solution.py:35
  123.5 14.9 %collective-permute-start.24 = (bf16[16,1536]{1,0:T(8,128)(2,1)S(1)}, bf16[16,1536]{1,0:T(8,128)(2,1)S(1)}, u32[]{:S(2)}, u32[]{:S(2)}) collective-permute-start(bf16[16,1536]{1,0:T(8,128)(2,1)S(1)} %get-tuple-element.71), channel_id=1, source_target_pairs={{0,128},{64,192},{128,0},{192,64},{1,129},{65,193},{129,1},{193,65... | collective-permute-start | bytes 147464 | tf_op jit(solution)/shard_map/ppermute | solution.py:35
  127.5 10.8 %collective-permute-start.25 = (bf16[16,1536]{1,0:T(8,128)(2,1)S(1)}, bf16[16,1536]{1,0:T(8,128)(2,1)S(1)}, u32[]{:S(2)}, u32[]{:S(2)}) collective-permute-start(bf16[16,1536]{1,0:T(8,128)(2,1)S(1)} %get-tuple-element.72), channel_id=1, source_target_pairs={{0,192},{64,0},{128,64},{192,128},{1,193},{65,1},{129,65},{193,129... | collective-permute-start | bytes 147464 | tf_op jit(solution)/shard_map/ppermute | solution.py:35
  130.9 8.1 %collective-permute-start.38 = (bf16[16,1536]{1,0:T(8,128)(2,1)S(1)}, bf16[16,1536]{1,0:T(8,128)(2,1)S(1)}, u32[]{:S(2)}, u32[]{:S(2)}) collective-permute-start(bf16[16,1536]{1,0:T(8,128)(2,1)S(1)} %get-tuple-element.91), channel_id=1, source_target_pairs={{0,64},{64,128},{128,192},{192,0},{1,65},{65,129},{129,193},{193,1... | collective-permute-start | bytes 147464 | tf_op jit(solution)/shard_map/ppermute | solution.py:35
  130.9 8.1 %collective-permute-start.39 = (bf16[16,1536]{1,0:T(8,128)(2,1)S(1)}, bf16[16,1536]{1,0:T(8,128)(2,1)S(1)}, u32[]{:S(2)}, u32[]{:S(2)}) collective-permute-start(bf16[16,1536]{1,0:T(8,128)(2,1)S(1)} %get-tuple-element.92), channel_id=1, source_target_pairs={{0,128},{64,192},{128,0},{192,64},{1,129},{65,193},{129,1},{193,65... | collective-permute-start | bytes 147464 | tf_op jit(solution)/shard_map/ppermute | solution.py:35
  133.3 7.4 %collective-permute-start.40 = (bf16[16,1536]{1,0:T(8,128)(2,1)S(1)}, bf16[16,1536]{1,0:T(8,128)(2,1)S(1)}, u32[]{:S(2)}, u32[]{:S(2)}) collective-permute-start(bf16[16,1536]{1,0:T(8,128)(2,1)S(1)} %get-tuple-element.93), channel_id=1, source_target_pairs={{0,192},{64,0},{128,64},{192,128},{1,193},{65,1},{129,65},{193,129... | collective-permute-start | bytes 147464 | tf_op jit(solution)/shard_map/ppermute | solution.py:35
  (12 other events, 71.9 us)

commit v8 on v7

--- a/solution.py
+++ b/solution.py
@@ -85,26 +85,9 @@
     )(*args)
 
 
-def pair_kernel(inputs_ref, grads_ref, both_ref, sems):
-    copies = [
-        pltpu.make_async_copy(source, both_ref.at[pl.ds(16 * i, 16), :], sems.at[i])
-        for i, source in enumerate((inputs_ref, grads_ref))
-    ]
-    for copy in copies:
-        copy.start()
-    for copy in copies:
-        copy.wait()
-
-
-def pair(inputs, grads):
-    return pl.pallas_call(
-        pair_kernel,
-        out_shape=jax.ShapeDtypeStruct((32, inputs.shape[1]), bf16),
-        in_specs=[pl.BlockSpec(memory_space=pl.ANY)] * 2,
-        out_specs=pl.BlockSpec(memory_space=pltpu.VMEM),
-        scratch_shapes=[pltpu.SemaphoreType.DMA((2,))],
-        name="pair",
-    )(inputs, grads)
+def pair_kernel(inputs_ref, grads_ref, both_ref):
+    both_ref[:16, :] = inputs_ref[...]
+    both_ref[16:, :] = grads_ref[...]
 
 
 def columns_kernel(both_ref, first_ref, second_ref, third_ref, inputs_ref, grads_ref):
@@ -124,6 +107,16 @@
     return call(stack_kernel, name, [((4 * rows, width), bf16)], pieces, moved=2**20)[0]
 
 
+def halves_kernel(*refs):
+    for i, piece in enumerate(refs[:4]):
+        refs[4 + i // 2][64 * (i % 2) : 64 * (i % 2) + 64, :] = piece[...]
+
+
+def halves(pieces):
+    width = pieces[0].shape[1]
+    return list(call(halves_kernel, "plane", [((128, width), bf16)] * 2, pieces, moved=2**20))
+
+
 def place(index_ref):
     me = index_ref[0]
     return lax.shift_right_logical(me, 1), lax.bitwise_and(me, 1)
@@ -133,11 +126,12 @@
     return pl.ds(pl.multiple_of(lax.bitwise_and(x + step, 3) * 128 + offset, 64), size)
 
 
-def width_inputs_kernel(index_ref, near_ref, far_ref, weight_ref, *refs):
-    whole_ref, own_ref, sends, acc = refs[0], refs[1], refs[2:5], refs[5]
-    x, z = place(index_ref)
-    whole_ref[:256, :] = near_ref[...]
-    whole_ref[256:, :] = far_ref[...]
+def width_inputs_kernel(index_ref, *refs):
+    pieces, weight_ref = refs[:4], refs[4]
+    whole_ref, own_ref, sends, acc = refs[5], refs[6], refs[7:10], refs[10]
+    x, z = place(index_ref)
+    for i, piece in enumerate(pieces):
+        whole_ref[128 * i : 128 * i + 128, :] = piece[...]
 
     @pl.loop(0, own_ref.shape[1] // tile)
     def _(j):
@@ -149,11 +143,12 @@
             sends[step - 1][:, cols] = acc[block(x, step, 128), :].astype(bf16)
 
 
-def width_grad_kernel(index_ref, near_ref, far_ref, weight_ref, *refs):
-    whole_ref, own_ref, send_ref, acc = refs
-    x, z = place(index_ref)
-    whole_ref[:256, :] = near_ref[...]
-    whole_ref[256:, :] = far_ref[...]
+def width_grad_kernel(index_ref, *refs):
+    pieces, weight_ref = refs[:4], refs[4]
+    whole_ref, own_ref, send_ref, acc = refs[5:]
+    x, z = place(index_ref)
+    for i, piece in enumerate(pieces):
+        whole_ref[128 * i : 128 * i + 128, :] = piece[...]
 
     @pl.loop(0, own_ref.shape[1] // tile)
     def _(j):
@@ -328,7 +323,7 @@
     width, units = w_in.shape
     index = jnp.reshape(lax.axis_index("gz"), (1,)).astype(jnp.int32)
     steps = (1, 2, 3)
-    both = pair(inputs, grad_out)
+    (both,) = call(pair_kernel, "pair", [((32, width), bf16)], [inputs, grad_out], moved=2**18)
     columns = call(
         columns_kernel,
         "columns",
@@ -337,13 +332,13 @@
         moved=2**20,
     )
     planes = [[column] + [from_y(column, step) for step in steps] for column in columns]
-    near = stack(planes[0], "plane")
+    near = halves(planes[0])
     width_flops = 2 * 512 * width * units
     all_inputs, own, *sends = call(
         width_inputs_kernel,
         "width_inputs",
         [((512, width), bf16), ((128, units), f32)] + [((128, units), bf16)] * 3,
-        [index, near, other_core(near), w_in],
+        [index] + near + [other_core(piece) for piece in near] + [w_in],
         scratch=[((512, tile), f32)],
         flops=width_flops,
         moved=6 * 2**20,
@@ -364,12 +359,12 @@
         [mine, other_z(send)],
         moved=2**20,
     )
-    near = stack(planes[1], "plane")
+    near = halves(planes[1])
     all_grads, own, send = call(
         width_grad_kernel,
         "width_grad",
         [((512, width), bf16), ((256, units), f32), ((256, units), bf16)],
-        [index, near, other_core(near), w_out],
+        [index] + near + [other_core(piece) for piece in near] + [w_out],
         scratch=[((512, tile), f32)],
         flops=width_flops,
         moved=6 * 2**20,
@@ -382,7 +377,7 @@
         [own, other_z(send)],
         moved=2**20,
     )
-    (both_z,) = call(
+    (pair,) = call(
         pair_z_kernel,
         "pair_z",
         [((128, units), bf16)],
@@ -397,7 +392,7 @@
         [mine] + [to_x(send, step) for step, send in zip(steps, sends)] + [slope],
         moved=2**20,
     )
-    hidden_pieces = [both_z] + [from_x(both_z, step) for step in steps]
+    hidden_pieces = [pair] + [from_x(pair, step) for step in steps]
     grad_stack = stack([grad_pre] + [from_x(grad_pre, step) for step in steps], "grad_stack")
     hidden_all, far_hidden = units_far(
         far_hidden_kernel, "far_hidden", index, hidden_pieces, w_out, False

time: 142 us -> 139 us (0.979)
  Pallas kernels: 18.3 us -> 13.3 us
  local copies, waits for them, and re-layouts: 0.9 us -> 3.26 us
    pallas_call x19 -> x20, Pallas kernels: 16.8 us -> 13.3 us  [call(): pl.pallas_call(kernel, out_shape=[jax.ShapeDtypeStruct(*out) for out in o...]
    unnamed x6 -> x10, local copies, waits for them, and re-layouts: 0.9 us -> 3.26 us
    pallas_call x1 -> x0, Pallas kernels: 1.48 us -> none  [pair(): pl.pallas_call(pair_kernel, out_shape=jax.ShapeDtypeStruct((32, inputs.sh...]
  transfers between devices with their start and end apart: 41 -> 43, of which waited for: 21 -> 21; matrix products, arithmetic and copies ran while one was open for 4% -> 4% of each run, Pallas kernels for 11% -> 9%
where the time goes in v8:
time: 139 us; the launch traced here: 138 us
  starting transfers between devices  71.3 us (51%)
  waiting for transfers between devices  44.2 us (32%)
  Pallas kernels  13.3 us (10%)
  matrix products  5.65 us (4%)
  local copies, waits for them, and re-layouts  3.26 us (2%)
    ppermute x6, starting transfers between devices, to_gx(): return lax.ppermute(value, 'gx', [(i, (i + step) % 4) for i in range(4)])  14.6 us
    ppermute x6, starting transfers between devices, to_y(): lax.ppermute(value, 'gy', [(i, (i + 2 * step) % 8) for i in range(8)])  14.3 us
    ppermute x6, waiting for transfers between devices, from_x(): lax.ppermute(value, 'gz', [((i + 2 * step) % 8, i) for i in range(8)])  13.6 us
    pallas_call x20, Pallas kernels, call(): pl.pallas_call(kernel, out_shape=[jax.ShapeDtypeStruct(*out) for out in o...  13.3 us
    ppermute x6, waiting for transfers between devices, from_y(): lax.ppermute(value, 'gy', [((i + 2 * step) % 8, i) for i in range(8)])  11.1 us
    ppermute x6, starting transfers between devices, to_x(): lax.ppermute(value, 'gz', [(i, (i + 2 * step) % 8) for i in range(8)])  11.1 us
    ppermute x3, starting transfers between devices, from_gx(): return lax.ppermute(value, 'gx', [((i + step) % 4, i) for i in range(4)])  10.2 us
    ppermute x6, waiting for transfers between devices, to_x(): lax.ppermute(value, 'gz', [(i, (i + 2 * step) % 8) for i in range(8)])  8.76 us
  transfers between devices with their start and end apart: 43, of which 21 were waited for; matrix products, arithmetic and copies ran while one was open for 4% of the time, Pallas kernels for 9%

profile of v8, /device:TPU:8, one launch (start us, length us, event | category | flops | bytes accessed | tf_op | source)
XLA Modules:
  0.0 138.5 jit_solution(5568269561157224296)
XLA Ops:
  2.2 6.4 %collective-permute-start = (bf16[32,1536]{1,0:T(8,128)(2,1)S(1)}, bf16[32,1536]{1,0:T(8,128)(2,1)S(1)}, u32[]{:S(2)}, u32[]{:S(2)}) collective-permute-start(bf16[32,1536]{1,0:T(8,128)(2,1)S(1)} %pair.1.both_ref), channel_id=1, source_target_pairs={{64,0},{128,64},{192,128},{0,192},{65,1},{129,65},{193,129},{1,193... | collective-permute-start | bytes 294920 | tf_op jit(solution)/shard_map/ppermute | solution.py:31
  9.6 2.8 %collective-permute-start.2 = (bf16[32,1536]{1,0:T(8,128)(2,1)S(1)}, bf16[32,1536]{1,0:T(8,128)(2,1)S(1)}, u32[]{:S(2)}, u32[]{:S(2)}) collective-permute-start(bf16[32,1536]{1,0:T(8,128)(2,1)S(1)} %pair.1.both_ref), channel_id=1, source_target_pairs={{192,0},{0,64},{64,128},{128,192},{193,1},{1,65},{65,129},{129,193... | collective-permute-start | bytes 294920 | tf_op jit(solution)/shard_map/ppermute | solution.py:31
  12.4 4.6 %collective-permute-done.first_ref = bf16[32,1536]{1,0:T(8,128)(2,1)S(1)} collective-permute-done((bf16[32,1536]{1,0:T(8,128)(2,1)S(1)}, bf16[32,1536]{1,0:T(8,128)(2,1)S(1)}, u32[]{:S(2)}, u32[]{:S(2)}) %collective-permute-start) | collective-permute-done | bytes 98336 | tf_op jit(solution)/shard_map/ppermute | solution.py:31
  17.0 3.2 %collective-permute-done.1.second_ref = bf16[32,1536]{1,0:T(8,128)(2,1)S(1)} collective-permute-done((bf16[32,1536]{1,0:T(8,128)(2,1)S(1)}, bf16[32,1536]{1,0:T(8,128)(2,1)S(1)}, u32[]{:S(2)}, u32[]{:S(2)}) %collective-permute-start.1) | collective-permute-done | bytes 98336 | tf_op jit(solution)/shard_map/ppermute | solution.py:31
  21.0 2.4 %collective-permute-start.21 = (bf16[64,1536]{1,0:T(8,128)(2,1)S(1)}, bf16[64,1536]{1,0:T(8,128)(2,1)S(1)}, u32[]{:S(2)}, u32[]{:S(2)}) collective-permute-start(bf16[64,1536]{1,0:T(8,128)(2,1)S(1)} %get-tuple-element.70.refs_0_), channel_id=1, source_target_pairs={{32,0},{40,8},{48,16},{56,24},{0,32},{8,40},{16,48},{24,56},{33,1}... | collective-permute-start | bytes 589832 | tf_op jit(solution)/shard_map/ppermute | solution.py:43
  23.4 1.9 %collective-permute-start.22 = (bf16[64,1536]{1,0:T(8,128)(2,1)S(1)}, bf16[64,1536]{1,0:T(8,128)(2,1)S(1)}, u32[]{:S(2)}, u32[]{:S(2)}) collective-permute-start(bf16[64,1536]{1,0:T(8,128)(2,1)S(1)} %get-tuple-element.70.refs_0_), channel_id=1, source_target_pairs={{48,0},{56,8},{0,16},{8,24},{16,32},{24,40},{32,48},{40,56},{49,1}... | collective-permute-start | bytes 589832 | tf_op jit(solution)/shard_map/ppermute | solution.py:43
  26.7 2.8 %collective-permute-done.20.refs_1_ = bf16[64,1536]{1,0:T(8,128)(2,1)S(1)} collective-permute-done((bf16[64,1536]{1,0:T(8,128)(2,1)S(1)}, bf16[64,1536]{1,0:T(8,128)(2,1)S(1)}, u32[]{:S(2)}, u32[]{:S(2)}) %collective-permute-start.20) | collective-permute-done | bytes 196640 | tf_op jit(solution)/shard_map/ppermute | solution.py:43
  29.8 3.7 %collective-permute-done.21.refs_2_ = bf16[64,1536]{1,0:T(8,128)(2,1)S(1)} collective-permute-done((bf16[64,1536]{1,0:T(8,128)(2,1)S(1)}, bf16[64,1536]{1,0:T(8,128)(2,1)S(1)}, u32[]{:S(2)}, u32[]{:S(2)}) %collective-permute-start.21) | collective-permute-done | bytes 196640 | tf_op jit(solution)/shard_map/ppermute | solution.py:43
  35.7 2.1 %collective-permute-done.4.refs_2_ = bf16[64,1536]{1,0:T(8,128)(2,1)S(1)} collective-permute-done((bf16[64,1536]{1,0:T(8,128)(2,1)S(1)}, bf16[64,1536]{1,0:T(8,128)(2,1)S(1)}, u32[]{:S(2)}, u32[]{:S(2)}) %collective-permute-start.4) | collective-permute-done | bytes 196640 | tf_op jit(solution)/shard_map/ppermute | solution.py:43
  41.0 2.1 %width_grad.1 = (bf16[512,1536]{1,0:T(8,128)(2,1)S(1)}, f32[256,768]{1,0:T(8,128)S(1)}, bf16[256,768]{1,0:T(8,128)(2,1)S(1)}) custom-call(s32[1]{0:T(128)} %bitcast.index_ref, bf16[128,1536]{1,0:T(8,128)(2,1)S(1)} %get-tuple-element.71.refs_0_, bf16[128,1536]{1,0:T(8,128)(2,1)S(1)} %get-tuple-element.72.refs_1_, ...), custom_call_target="tpu_custom_call" | custom-call | flops 1207959552 | bytes 6291456 | tf_op jit(solution)/shard_map/width_grad/pallas_call | solution.py:75
  43.1 2.7 %collective-permute-start.28 = (bf16[256,768]{1,0:T(8,128)(2,1)S(1)}, bf16[256,768]{1,0:T(8,128)(2,1)S(1)}, u32[]{:S(2)}, u32[]{:S(2)}) collective-permute-start(bf16[256,768]{1,0:T(8,128)(2,1)S(1)} %get-tuple-element.82), channel_id=1, source_target_pairs={{0,1},{1,0},{2,3},{3,2},{4,5},{5,4},{6,7},{7,6},{8,9},{9,8},{10,11... | collective-permute-start | bytes 1179656 | tf_op jit(solution)/shard_map/ppermute | solution.py:59
  45.8 2.0 %width_inputs.1 = (bf16[512,1536]{1,0:T(8,128)(2,1)S(1)}, f32[128,768]{1,0:T(8,128)S(1)}, bf16[128,768]{1,0:T(8,128)(2,1)S(1)}, bf16[128,768]{1,0:T(8,128)(2,1)S(1)}, bf16[128,768]{1,0:T(8,128)(2,1)S(1)}) custom-call(s32[1]{0:T(128)} %bitcast.index_ref, bf16[128,1536]{1,0:T(8,128)(2,1)S(1)} %get-tuple-element.55.refs_0_, ...), custom_call_target="tpu_custom_call" | custom-call | flops 1207959552 | bytes 6291456 | tf_op jit(solution)/shard_map/width_inputs/pallas_call | solution.py:75
  49.4 2.7 %collective-permute-start.9 = (bf16[128,768]{1,0:T(8,128)(2,1)S(1)}, bf16[128,768]{1,0:T(8,128)(2,1)S(1)}, u32[]{:S(2)}, u32[]{:S(2)}) collective-permute-start(bf16[128,768]{1,0:T(8,128)(2,1)S(1)} %get-tuple-element.59), channel_id=1, source_target_pairs={{0,4},{1,5},{2,6},{3,7},{4,0},{5,1},{6,2},{7,3},{8,12},{9,13},{10,... | collective-permute-start | bytes 589832 | tf_op jit(solution)/shard_map/ppermute | solution.py:55
  53.6 2.4 %collective-permute-done.8.first_ref = bf16[128,768]{1,0:T(8,128)(2,1)S(1)} collective-permute-done((bf16[128,768]{1,0:T(8,128)(2,1)S(1)}, bf16[128,768]{1,0:T(8,128)(2,1)S(1)}, u32[]{:S(2)}, u32[]{:S(2)}) %collective-permute-start.8) | collective-permute-done | bytes 196640 | tf_op jit(solution)/shard_map/ppermute | solution.py:55
  56.0 5.0 %collective-permute-done.9.second_ref = bf16[128,768]{1,0:T(8,128)(2,1)S(1)} collective-permute-done((bf16[128,768]{1,0:T(8,128)(2,1)S(1)}, bf16[128,768]{1,0:T(8,128)(2,1)S(1)}, u32[]{:S(2)}, u32[]{:S(2)}) %collective-permute-start.9) | collective-permute-done | bytes 196640 | tf_op jit(solution)/shard_map/ppermute | solution.py:55
  63.1 2.4 %collective-permute-start.30 = (bf16[64,768]{1,0:T(8,128)(2,1)S(1)}, bf16[64,768]{1,0:T(8,128)(2,1)S(1)}, u32[]{:S(2)}, u32[]{:S(2)}) collective-permute-start(bf16[64,768]{1,0:T(8,128)(2,1)S(1)} %get-tuple-element.85), channel_id=1, source_target_pairs={{0,4},{1,5},{2,6},{3,7},{4,0},{5,1},{6,2},{7,3},{8,12},{9,13},{10,... | collective-permute-start | bytes 294920 | tf_op jit(solution)/shard_map/ppermute | solution.py:55
  70.5 2.7 %collective-permute-start.32 = (bf16[64,768]{1,0:T(8,128)(2,1)S(1)}, bf16[64,768]{1,0:T(8,128)(2,1)S(1)}, u32[]{:S(2)}, u32[]{:S(2)}) collective-permute-start(bf16[64,768]{1,0:T(8,128)(2,1)S(1)} %grad_pre.1.refs_0_), channel_id=1, source_target_pairs={{2,0},{3,1},{4,2},{5,3},{6,4},{7,5},{0,6},{1,7},{10,8},{11,9},{12,... | collective-permute-start | bytes 294920 | tf_op jit(solution)/shard_map/ppermute | solution.py:51
  74.2 2.2 %collective-permute-done.32.refs_1_ = bf16[64,768]{1,0:T(8,128)(2,1)S(1)} collective-permute-done((bf16[64,768]{1,0:T(8,128)(2,1)S(1)}, bf16[64,768]{1,0:T(8,128)(2,1)S(1)}, u32[]{:S(2)}, u32[]{:S(2)}) %collective-permute-start.32) | collective-permute-done | bytes 98336 | tf_op jit(solution)/shard_map/ppermute | solution.py:51
  76.4 3.0 %collective-permute-done.33.refs_2_ = bf16[64,768]{1,0:T(8,128)(2,1)S(1)} collective-permute-done((bf16[64,768]{1,0:T(8,128)(2,1)S(1)}, bf16[64,768]{1,0:T(8,128)(2,1)S(1)}, u32[]{:S(2)}, u32[]{:S(2)}) %collective-permute-start.33) | collective-permute-done | bytes 98336 | tf_op jit(solution)/shard_map/ppermute | solution.py:51
  84.4 3.3 %collective-permute-done.13.refs_1_ = bf16[128,768]{1,0:T(8,128)(2,1)S(1)} collective-permute-done((bf16[128,768]{1,0:T(8,128)(2,1)S(1)}, bf16[128,768]{1,0:T(8,128)(2,1)S(1)}, u32[]{:S(2)}, u32[]{:S(2)}) %collective-permute-start.13) | collective-permute-done | bytes 196640 | tf_op jit(solution)/shard_map/ppermute | solution.py:51
  87.7 2.2 %collective-permute-done.14.refs_2_ = bf16[128,768]{1,0:T(8,128)(2,1)S(1)} collective-permute-done((bf16[128,768]{1,0:T(8,128)(2,1)S(1)}, bf16[128,768]{1,0:T(8,128)(2,1)S(1)}, u32[]{:S(2)}, u32[]{:S(2)}) %collective-permute-start.14) | collective-permute-done | bytes 196640 | tf_op jit(solution)/shard_map/ppermute | solution.py:51
  89.9 2.0 %collective-permute-done.15.refs_3_ = bf16[128,768]{1,0:T(8,128)(2,1)S(1)} collective-permute-done((bf16[128,768]{1,0:T(8,128)(2,1)S(1)}, bf16[128,768]{1,0:T(8,128)(2,1)S(1)}, u32[]{:S(2)}, u32[]{:S(2)}) %collective-permute-start.15) | collective-permute-done | bytes 196640 | tf_op jit(solution)/shard_map/ppermute | solution.py:51
  100.2 3.5 %collective-permute-start.18 = (bf16[64,1536]{1,0:T(8,128)(2,1)S(1)}, bf16[64,1536]{1,0:T(8,128)(2,1)S(1)}, u32[]{:S(2)}, u32[]{:S(2)}) collective-permute-start(bf16[64,1536]{1,0:T(8,128)(2,1)S(1)} %get-tuple-element.68), channel_id=1, source_target_pairs={{0,32},{8,40},{16,48},{24,56},{32,0},{40,8},{48,16},{56,24},{1,33}... | collective-permute-start | bytes 589832 | tf_op jit(solution)/shard_map/ppermute | solution.py:47
  105.6 2.3 %collective-permute-start.37 = (bf16[64,1536]{1,0:T(8,128)(2,1)S(1)}, bf16[64,1536]{1,0:T(8,128)(2,1)S(1)}, u32[]{:S(2)}, u32[]{:S(2)}) collective-permute-start(bf16[64,1536]{1,0:T(8,128)(2,1)S(1)} %get-tuple-element.91), channel_id=1, source_target_pairs={{0,16},{8,24},{16,32},{24,40},{32,48},{40,56},{48,0},{56,8},{1,17}... | collective-permute-start | bytes 589832 | tf_op jit(solution)/shard_map/ppermute | solution.py:47
  109.2 5.7 %collective-permute-start.39 = (bf16[64,1536]{1,0:T(8,128)(2,1)S(1)}, bf16[64,1536]{1,0:T(8,128)(2,1)S(1)}, u32[]{:S(2)}, u32[]{:S(2)}) collective-permute-start(bf16[64,1536]{1,0:T(8,128)(2,1)S(1)} %get-tuple-element.93), channel_id=1, source_target_pairs={{0,48},{8,56},{16,0},{24,8},{32,16},{40,24},{48,32},{56,40},{1,49}... | collective-permute-start | bytes 589832 | tf_op jit(solution)/shard_map/ppermute | solution.py:47
  114.9 2.8 %convolution_convert_fusion.1 = bf16[768,1536]{1,0:T(8,128)(2,1)} fusion(bf16[512,768]{1,0:T(8,128)(2,1)S(1)} %get-tuple-element.64.whole_ref, bf16[512,1536]{1,0:T(8,128)(2,1)S(1)} %get-tuple-element.73), kind=kOutput, calls=%fused_computation.1 | convolution fusion | flops 1209139200 | bytes 4718592 | tf_op jit(solution)/shard_map/dot_general | solution.py:405
  117.8 2.7 %collective-permute-start.25 = (bf16[16,1536]{1,0:T(8,128)(2,1)S(1)}, bf16[16,1536]{1,0:T(8,128)(2,1)S(1)}, u32[]{:S(2)}, u32[]{:S(2)}) collective-permute-start(bf16[16,1536]{1,0:T(8,128)(2,1)S(1)} %get-tuple-element.78), channel_id=1, source_target_pairs={{0,64},{64,128},{128,192},{192,0},{1,65},{65,129},{129,193},{193,1... | collective-permute-start | bytes 147464 | tf_op jit(solution)/shard_map/ppermute | solution.py:35
  120.4 4.0 %collective-permute-start.26 = (bf16[16,1536]{1,0:T(8,128)(2,1)S(1)}, bf16[16,1536]{1,0:T(8,128)(2,1)S(1)}, u32[]{:S(2)}, u32[]{:S(2)}) collective-permute-start(bf16[16,1536]{1,0:T(8,128)(2,1)S(1)} %get-tuple-element.79), channel_id=1, source_target_pairs={{0,128},{64,192},{128,0},{192,64},{1,129},{65,193},{129,1},{193,65... | collective-permute-start | bytes 147464 | tf_op jit(solution)/shard_map/ppermute | solution.py:35
  124.5 3.3 %collective-permute-start.27 = (bf16[16,1536]{1,0:T(8,128)(2,1)S(1)}, bf16[16,1536]{1,0:T(8,128)(2,1)S(1)}, u32[]{:S(2)}, u32[]{:S(2)}) collective-permute-start(bf16[16,1536]{1,0:T(8,128)(2,1)S(1)} %get-tuple-element.80), channel_id=1, source_target_pairs={{0,192},{64,0},{128,64},{192,128},{1,193},{65,1},{129,65},{193,129... | collective-permute-start | bytes 147464 | tf_op jit(solution)/shard_map/ppermute | solution.py:35
  127.9 2.4 %collective-permute-start.41 = (bf16[16,1536]{1,0:T(8,128)(2,1)S(1)}, bf16[16,1536]{1,0:T(8,128)(2,1)S(1)}, u32[]{:S(2)}, u32[]{:S(2)}) collective-permute-start(bf16[16,1536]{1,0:T(8,128)(2,1)S(1)} %get-tuple-element.100), channel_id=1, source_target_pairs={{0,128},{64,192},{128,0},{192,64},{1,129},{65,193},{129,1},{193,65... | collective-permute-start | bytes 147464 | tf_op jit(solution)/shard_map/ppermute | solution.py:35
  130.3 2.2 %collective-permute-start.42 = (bf16[16,1536]{1,0:T(8,128)(2,1)S(1)}, bf16[16,1536]{1,0:T(8,128)(2,1)S(1)}, u32[]{:S(2)}, u32[]{:S(2)}) collective-permute-start(bf16[16,1536]{1,0:T(8,128)(2,1)S(1)} %get-tuple-element.101), channel_id=1, source_target_pairs={{0,192},{64,0},{128,64},{192,128},{1,193},{65,1},{129,65},{193,129... | collective-permute-start | bytes 147464 | tf_op jit(solution)/shard_map/ppermute | solution.py:35
  132.5 2.8 %convolution_convert_fusion = bf16[1536,768]{1,0:T(8,128)(2,1)} fusion(bf16[512,1536]{1,0:T(8,128)(2,1)S(1)} %get-tuple-element.102, bf16[512,768]{1,0:T(8,128)(2,1)S(1)} %get-tuple-element.88.whole_ref), kind=kOutput, calls=%fused_computation | convolution fusion | flops 1209139200 | bytes 4718592 | tf_op jit(solution)/shard_map/dot_general | solution.py:408
  (86 shorter events, 41.3 us)
Async XLA Ops:
  2.2 14.8 %collective-permute-start = (bf16[32,1536]{1,0:T(8,128)(2,1)S(1)}, bf16[32,1536]{1,0:T(8,128)(2,1)S(1)}, u32[]{:S(2)}, u32[]{:S(2)}) collective-permute-start(bf16[32,1536]{1,0:T(8,128)(2,1)S(1)} %pair.1.both_ref), channel_id=1, source_target_pairs={{64,0},{128,64},{192,128},{0,192},{65,1},{129,65},{193,129},{1,193... | collective-permute-start | bytes 294920 | tf_op jit(solution)/shard_map/ppermute | solution.py:31
  8.6 11.6 %collective-permute-start.1 = (bf16[32,1536]{1,0:T(8,128)(2,1)S(1)}, bf16[32,1536]{1,0:T(8,128)(2,1)S(1)}, u32[]{:S(2)}, u32[]{:S(2)}) collective-permute-start(bf16[32,1536]{1,0:T(8,128)(2,1)S(1)} %pair.1.both_ref), channel_id=1, source_target_pairs={{128,0},{192,64},{0,128},{64,192},{129,1},{193,65},{1,129},{65,193... | collective-permute-start | bytes 294920 | tf_op jit(solution)/shard_map/ppermute | solution.py:31
  9.6 10.6 %collective-permute-start.2 = (bf16[32,1536]{1,0:T(8,128)(2,1)S(1)}, bf16[32,1536]{1,0:T(8,128)(2,1)S(1)}, u32[]{:S(2)}, u32[]{:S(2)}) collective-permute-start(bf16[32,1536]{1,0:T(8,128)(2,1)S(1)} %pair.1.both_ref), channel_id=1, source_target_pairs={{192,0},{0,64},{64,128},{128,192},{193,1},{1,65},{65,129},{129,193... | collective-permute-start | bytes 294920 | tf_op jit(solution)/shard_map/ppermute | solution.py:31
  20.3 9.3 %collective-permute-start.20 = (bf16[64,1536]{1,0:T(8,128)(2,1)S(1)}, bf16[64,1536]{1,0:T(8,128)(2,1)S(1)}, u32[]{:S(2)}, u32[]{:S(2)}) collective-permute-start(bf16[64,1536]{1,0:T(8,128)(2,1)S(1)} %get-tuple-element.70.refs_0_), channel_id=1, source_target_pairs={{16,0},{24,8},{32,16},{40,24},{48,32},{56,40},{0,48},{8,56},{17,1}... | collective-permute-start | bytes 589832 | tf_op jit(solution)/shard_map/ppermute | solution.py:43
  21.0 12.5 %collective-permute-start.21 = (bf16[64,1536]{1,0:T(8,128)(2,1)S(1)}, bf16[64,1536]{1,0:T(8,128)(2,1)S(1)}, u32[]{:S(2)}, u32[]{:S(2)}) collective-permute-start(bf16[64,1536]{1,0:T(8,128)(2,1)S(1)} %get-tuple-element.70.refs_0_), channel_id=1, source_target_pairs={{32,0},{40,8},{48,16},{56,24},{0,32},{8,40},{16,48},{24,56},{33,1}... | collective-permute-start | bytes 589832 | tf_op jit(solution)/shard_map/ppermute | solution.py:43
  23.4 11.1 %collective-permute-start.22 = (bf16[64,1536]{1,0:T(8,128)(2,1)S(1)}, bf16[64,1536]{1,0:T(8,128)(2,1)S(1)}, u32[]{:S(2)}, u32[]{:S(2)}) collective-permute-start(bf16[64,1536]{1,0:T(8,128)(2,1)S(1)} %get-tuple-element.70.refs_0_), channel_id=1, source_target_pairs={{48,0},{56,8},{0,16},{8,24},{16,32},{24,40},{32,48},{40,56},{49,1}... | collective-permute-start | bytes 589832 | tf_op jit(solution)/shard_map/ppermute | solution.py:43
  25.3 10.5 %collective-permute-start.3 = (bf16[64,1536]{1,0:T(8,128)(2,1)S(1)}, bf16[64,1536]{1,0:T(8,128)(2,1)S(1)}, u32[]{:S(2)}, u32[]{:S(2)}) collective-permute-start(bf16[64,1536]{1,0:T(8,128)(2,1)S(1)} %get-tuple-element.54.refs_0_), channel_id=1, source_target_pairs={{16,0},{24,8},{32,16},{40,24},{48,32},{56,40},{0,48},{8,56},{17,1}... | collective-permute-start | bytes 589832 | tf_op jit(solution)/shard_map/ppermute | solution.py:43
  25.4 12.5 %collective-permute-start.4 = (bf16[64,1536]{1,0:T(8,128)(2,1)S(1)}, bf16[64,1536]{1,0:T(8,128)(2,1)S(1)}, u32[]{:S(2)}, u32[]{:S(2)}) collective-permute-start(bf16[64,1536]{1,0:T(8,128)(2,1)S(1)} %get-tuple-element.54.refs_0_), channel_id=1, source_target_pairs={{32,0},{40,8},{48,16},{56,24},{0,32},{8,40},{16,48},{24,56},{33,1}... | collective-permute-start | bytes 589832 | tf_op jit(solution)/shard_map/ppermute | solution.py:43
  29.6 9.1 %collective-permute-start.5 = (bf16[64,1536]{1,0:T(8,128)(2,1)S(1)}, bf16[64,1536]{1,0:T(8,128)(2,1)S(1)}, u32[]{:S(2)}, u32[]{:S(2)}) collective-permute-start(bf16[64,1536]{1,0:T(8,128)(2,1)S(1)} %get-tuple-element.54.refs_0_), channel_id=1, source_target_pairs={{48,0},{56,8},{0,16},{8,24},{16,32},{24,40},{32,48},{40,56},{49,1}... | collective-permute-start | bytes 589832 | tf_op jit(solution)/shard_map/ppermute | solution.py:43
  38.7 7.1 %collective-permute-start.6 = (bf16[128,1536]{1,0:T(8,128)(2,1)S(1)}, bf16[128,1536]{1,0:T(8,128)(2,1)S(1)}, u32[]{:S(2)}, u32[]{:S(2)}) collective-permute-start(bf16[128,1536]{1,0:T(8,128)(2,1)S(1)} %get-tuple-element.55.refs_0_), channel_id=1, source_target_pairs={{0,8},{8,0},{16,24},{24,16},{32,40},{40,32},{48,56},{56,48},{1,9},... | collective-permute-start | bytes 1179656 | tf_op jit(solution)/shard_map/ppermute | solution.py:39
  38.8 7.0 %collective-permute-start.7 = (bf16[128,1536]{1,0:T(8,128)(2,1)S(1)}, bf16[128,1536]{1,0:T(8,128)(2,1)S(1)}, u32[]{:S(2)}, u32[]{:S(2)}) collective-permute-start(bf16[128,1536]{1,0:T(8,128)(2,1)S(1)} %get-tuple-element.56.refs_1_), channel_id=1, source_target_pairs={{0,8},{8,0},{16,24},{24,16},{32,40},{40,32},{48,56},{56,48},{1,9},... | collective-permute-start | bytes 1179656 | tf_op jit(solution)/shard_map/ppermute | solution.py:39
  43.1 18.4 %collective-permute-start.28 = (bf16[256,768]{1,0:T(8,128)(2,1)S(1)}, bf16[256,768]{1,0:T(8,128)(2,1)S(1)}, u32[]{:S(2)}, u32[]{:S(2)}) collective-permute-start(bf16[256,768]{1,0:T(8,128)(2,1)S(1)} %get-tuple-element.82), channel_id=1, source_target_pairs={{0,1},{1,0},{2,3},{3,2},{4,5},{5,4},{6,7},{7,6},{8,9},{9,8},{10,11... | collective-permute-start | bytes 1179656 | tf_op jit(solution)/shard_map/ppermute | solution.py:59
  47.8 8.1 %collective-permute-start.8 = (bf16[128,768]{1,0:T(8,128)(2,1)S(1)}, bf16[128,768]{1,0:T(8,128)(2,1)S(1)}, u32[]{:S(2)}, u32[]{:S(2)}) collective-permute-start(bf16[128,768]{1,0:T(8,128)(2,1)S(1)} %get-tuple-element.58), channel_id=1, source_target_pairs={{0,2},{1,3},{2,4},{3,5},{4,6},{5,7},{6,0},{7,1},{8,10},{9,11},{10,... | collective-permute-start | bytes 589832 | tf_op jit(solution)/shard_map/ppermute | solution.py:55
  49.4 11.5 %collective-permute-start.9 = (bf16[128,768]{1,0:T(8,128)(2,1)S(1)}, bf16[128,768]{1,0:T(8,128)(2,1)S(1)}, u32[]{:S(2)}, u32[]{:S(2)}) collective-permute-start(bf16[128,768]{1,0:T(8,128)(2,1)S(1)} %get-tuple-element.59), channel_id=1, source_target_pairs={{0,4},{1,5},{2,6},{3,7},{4,0},{5,1},{6,2},{7,3},{8,12},{9,13},{10,... | collective-permute-start | bytes 589832 | tf_op jit(solution)/shard_map/ppermute | solution.py:55
  52.1 8.8 %collective-permute-start.10 = (bf16[128,768]{1,0:T(8,128)(2,1)S(1)}, bf16[128,768]{1,0:T(8,128)(2,1)S(1)}, u32[]{:S(2)}, u32[]{:S(2)}) collective-permute-start(bf16[128,768]{1,0:T(8,128)(2,1)S(1)} %get-tuple-element.60), channel_id=1, source_target_pairs={{0,6},{1,7},{2,0},{3,1},{4,2},{5,3},{6,4},{7,5},{8,14},{9,15},{10,... | collective-permute-start | bytes 589832 | tf_op jit(solution)/shard_map/ppermute | solution.py:55
  61.7 7.3 %collective-permute-start.29 = (bf16[64,768]{1,0:T(8,128)(2,1)S(1)}, bf16[64,768]{1,0:T(8,128)(2,1)S(1)}, u32[]{:S(2)}, u32[]{:S(2)}) collective-permute-start(bf16[64,768]{1,0:T(8,128)(2,1)S(1)} %get-tuple-element.84), channel_id=1, source_target_pairs={{0,2},{1,3},{2,4},{3,5},{4,6},{5,7},{6,0},{7,1},{8,10},{9,11},{10,... | collective-permute-start | bytes 294920 | tf_op jit(solution)/shard_map/ppermute | solution.py:55
  80.4 13.3 %collective-permute-start.35 = (bf16[256,768]{1,0:T(8,128)(2,1)S(1)}, bf16[256,768]{1,0:T(8,128)(2,1)S(1)}, u32[]{:S(2)}, u32[]{:S(2)}) collective-permute-start(bf16[256,768]{1,0:T(8,128)(2,1)S(1)} %grad_stack.1.own_ref), channel_id=1, source_target_pairs={{0,1},{1,0},{2,3},{3,2},{4,5},{5,4},{6,7},{7,6},{8,9},{9,8},{10,11... | collective-permute-start | bytes 1179656 | tf_op jit(solution)/shard_map/ppermute | solution.py:59
  82.6 7.3 %collective-permute-start.14 = (bf16[128,768]{1,0:T(8,128)(2,1)S(1)}, bf16[128,768]{1,0:T(8,128)(2,1)S(1)}, u32[]{:S(2)}, u32[]{:S(2)}) collective-permute-start(bf16[128,768]{1,0:T(8,128)(2,1)S(1)} %pair_z.1.refs_0_), channel_id=1, source_target_pairs={{4,0},{5,1},{6,2},{7,3},{0,4},{1,5},{2,6},{3,7},{12,8},{13,9},{14,... | collective-permute-start | bytes 589832 | tf_op jit(solution)/shard_map/ppermute | solution.py:51
  83.5 8.4 %collective-permute-start.15 = (bf16[128,768]{1,0:T(8,128)(2,1)S(1)}, bf16[128,768]{1,0:T(8,128)(2,1)S(1)}, u32[]{:S(2)}, u32[]{:S(2)}) collective-permute-start(bf16[128,768]{1,0:T(8,128)(2,1)S(1)} %pair_z.1.refs_0_), channel_id=1, source_target_pairs={{6,0},{7,1},{0,2},{1,3},{2,4},{3,5},{4,6},{5,7},{14,8},{15,9},{8,1... | collective-permute-start | bytes 589832 | tf_op jit(solution)/shard_map/ppermute | solution.py:51
  95.6 8.2 %collective-permute-start.36 = (f32[256,1536]{1,0:T(8,128)S(1)}, f32[256,1536]{1,0:T(8,128)S(1)}, u32[]{:S(2)}, u32[]{:S(2)}) collective-permute-start(f32[256,1536]{1,0:T(8,128)S(1)} %get-tuple-element.89), channel_id=1, source_target_pairs={{0,8},{8,0},{16,24},{24,16},{32,40},{40,32},{48,56},{56,48},{1,9},... | collective-permute-start | bytes 4718600 | tf_op jit(solution)/shard_map/ppermute | solution.py:39
  98.7 10.5 %collective-permute-start.17 = (bf16[64,1536]{1,0:T(8,128)(2,1)S(1)}, bf16[64,1536]{1,0:T(8,128)(2,1)S(1)}, u32[]{:S(2)}, u32[]{:S(2)}) collective-permute-start(bf16[64,1536]{1,0:T(8,128)(2,1)S(1)} %get-tuple-element.67), channel_id=1, source_target_pairs={{0,16},{8,24},{16,32},{24,40},{32,48},{40,56},{48,0},{56,8},{1,17}... | collective-permute-start | bytes 589832 | tf_op jit(solution)/shard_map/ppermute | solution.py:47
  100.2 17.4 %collective-permute-start.18 = (bf16[64,1536]{1,0:T(8,128)(2,1)S(1)}, bf16[64,1536]{1,0:T(8,128)(2,1)S(1)}, u32[]{:S(2)}, u32[]{:S(2)}) collective-permute-start(bf16[64,1536]{1,0:T(8,128)(2,1)S(1)} %get-tuple-element.68), channel_id=1, source_target_pairs={{0,32},{8,40},{16,48},{24,56},{32,0},{40,8},{48,16},{56,24},{1,33}... | collective-permute-start | bytes 589832 | tf_op jit(solution)/shard_map/ppermute | solution.py:47
  103.8 13.9 %collective-permute-start.19 = (bf16[64,1536]{1,0:T(8,128)(2,1)S(1)}, bf16[64,1536]{1,0:T(8,128)(2,1)S(1)}, u32[]{:S(2)}, u32[]{:S(2)}) collective-permute-start(bf16[64,1536]{1,0:T(8,128)(2,1)S(1)} %get-tuple-element.69), channel_id=1, source_target_pairs={{0,48},{8,56},{16,0},{24,8},{32,16},{40,24},{48,32},{56,40},{1,49}... | collective-permute-start | bytes 589832 | tf_op jit(solution)/shard_map/ppermute | solution.py:47
  105.6 18.9 %collective-permute-start.37 = (bf16[64,1536]{1,0:T(8,128)(2,1)S(1)}, bf16[64,1536]{1,0:T(8,128)(2,1)S(1)}, u32[]{:S(2)}, u32[]{:S(2)}) collective-permute-start(bf16[64,1536]{1,0:T(8,128)(2,1)S(1)} %get-tuple-element.91), channel_id=1, source_target_pairs={{0,16},{8,24},{16,32},{24,40},{32,48},{40,56},{48,0},{56,8},{1,17}... | collective-permute-start | bytes 589832 | tf_op jit(solution)/shard_map/ppermute | solution.py:47
  107.9 19.8 %collective-permute-start.38 = (bf16[64,1536]{1,0:T(8,128)(2,1)S(1)}, bf16[64,1536]{1,0:T(8,128)(2,1)S(1)}, u32[]{:S(2)}, u32[]{:S(2)}) collective-permute-start(bf16[64,1536]{1,0:T(8,128)(2,1)S(1)} %get-tuple-element.92), channel_id=1, source_target_pairs={{0,32},{8,40},{16,48},{24,56},{32,0},{40,8},{48,16},{56,24},{1,33}... | collective-permute-start | bytes 589832 | tf_op jit(solution)/shard_map/ppermute | solution.py:47
  109.2 18.6 %collective-permute-start.39 = (bf16[64,1536]{1,0:T(8,128)(2,1)S(1)}, bf16[64,1536]{1,0:T(8,128)(2,1)S(1)}, u32[]{:S(2)}, u32[]{:S(2)}) collective-permute-start(bf16[64,1536]{1,0:T(8,128)(2,1)S(1)} %get-tuple-element.93), channel_id=1, source_target_pairs={{0,48},{8,56},{16,0},{24,8},{32,16},{40,24},{48,32},{56,40},{1,49}... | collective-permute-start | bytes 589832 | tf_op jit(solution)/shard_map/ppermute | solution.py:47
  117.8 12.5 %collective-permute-start.25 = (bf16[16,1536]{1,0:T(8,128)(2,1)S(1)}, bf16[16,1536]{1,0:T(8,128)(2,1)S(1)}, u32[]{:S(2)}, u32[]{:S(2)}) collective-permute-start(bf16[16,1536]{1,0:T(8,128)(2,1)S(1)} %get-tuple-element.78), channel_id=1, source_target_pairs={{0,64},{64,128},{128,192},{192,0},{1,65},{65,129},{129,193},{193,1... | collective-permute-start | bytes 147464 | tf_op jit(solution)/shard_map/ppermute | solution.py:35
  120.4 14.9 %collective-permute-start.26 = (bf16[16,1536]{1,0:T(8,128)(2,1)S(1)}, bf16[16,1536]{1,0:T(8,128)(2,1)S(1)}, u32[]{:S(2)}, u32[]{:S(2)}) collective-permute-start(bf16[16,1536]{1,0:T(8,128)(2,1)S(1)} %get-tuple-element.79), channel_id=1, source_target_pairs={{0,128},{64,192},{128,0},{192,64},{1,129},{65,193},{129,1},{193,65... | collective-permute-start | bytes 147464 | tf_op jit(solution)/shard_map/ppermute | solution.py:35
  124.5 10.8 %collective-permute-start.27 = (bf16[16,1536]{1,0:T(8,128)(2,1)S(1)}, bf16[16,1536]{1,0:T(8,128)(2,1)S(1)}, u32[]{:S(2)}, u32[]{:S(2)}) collective-permute-start(bf16[16,1536]{1,0:T(8,128)(2,1)S(1)} %get-tuple-element.80), channel_id=1, source_target_pairs={{0,192},{64,0},{128,64},{192,128},{1,193},{65,1},{129,65},{193,129... | collective-permute-start | bytes 147464 | tf_op jit(solution)/shard_map/ppermute | solution.py:35
  127.8 8.1 %collective-permute-start.40 = (bf16[16,1536]{1,0:T(8,128)(2,1)S(1)}, bf16[16,1536]{1,0:T(8,128)(2,1)S(1)}, u32[]{:S(2)}, u32[]{:S(2)}) collective-permute-start(bf16[16,1536]{1,0:T(8,128)(2,1)S(1)} %get-tuple-element.99), channel_id=1, source_target_pairs={{0,64},{64,128},{128,192},{192,0},{1,65},{65,129},{129,193},{193,1... | collective-permute-start | bytes 147464 | tf_op jit(solution)/shard_map/ppermute | solution.py:35
  127.9 8.1 %collective-permute-start.41 = (bf16[16,1536]{1,0:T(8,128)(2,1)S(1)}, bf16[16,1536]{1,0:T(8,128)(2,1)S(1)}, u32[]{:S(2)}, u32[]{:S(2)}) collective-permute-start(bf16[16,1536]{1,0:T(8,128)(2,1)S(1)} %get-tuple-element.100), channel_id=1, source_target_pairs={{0,128},{64,192},{128,0},{192,64},{1,129},{65,193},{129,1},{193,65... | collective-permute-start | bytes 147464 | tf_op jit(solution)/shard_map/ppermute | solution.py:35
  130.3 7.5 %collective-permute-start.42 = (bf16[16,1536]{1,0:T(8,128)(2,1)S(1)}, bf16[16,1536]{1,0:T(8,128)(2,1)S(1)}, u32[]{:S(2)}, u32[]{:S(2)}) collective-permute-start(bf16[16,1536]{1,0:T(8,128)(2,1)S(1)} %get-tuple-element.101), channel_id=1, source_target_pairs={{0,192},{64,0},{128,64},{192,128},{1,193},{65,1},{129,65},{193,129... | collective-permute-start | bytes 147464 | tf_op jit(solution)/shard_map/ppermute | solution.py:35
  (16 other events, 100.7 us)

commit v9 on v8

--- a/solution.py
+++ b/solution.py
@@ -27,32 +27,20 @@
 barrier = lax.optimization_barrier
 
 
-def from_gx(value, step):
-    return lax.ppermute(value, "gx", [((i + step) % 4, i) for i in range(4)])
-
-
-def to_gx(value, step):
-    return lax.ppermute(value, "gx", [(i, (i + step) % 4) for i in range(4)])
+def swap_gx(value, step):
+    return lax.ppermute(value, "gx", [(i, i ^ step) for i in range(4)])
 
 
 def other_core(value):
     return lax.ppermute(value, "gy", [(i, i ^ 1) for i in range(8)])
 
 
-def from_y(value, step):
-    return lax.ppermute(value, "gy", [((i + 2 * step) % 8, i) for i in range(8)])
-
-
-def to_y(value, step):
-    return lax.ppermute(value, "gy", [(i, (i + 2 * step) % 8) for i in range(8)])
-
-
-def from_x(value, step):
-    return lax.ppermute(value, "gz", [((i + 2 * step) % 8, i) for i in range(8)])
-
-
-def to_x(value, step):
-    return lax.ppermute(value, "gz", [(i, (i + 2 * step) % 8) for i in range(8)])
+def swap_y(value, step):
+    return lax.ppermute(value, "gy", [(i, i ^ (2 * step)) for i in range(8)])
+
+
+def swap_x(value, step):
+    return lax.ppermute(value, "gz", [(i, i ^ (2 * step)) for i in range(8)])
 
 
 def other_z(value):
@@ -123,7 +111,7 @@
 
 
 def block(x, step, size, offset=0):
-    return pl.ds(pl.multiple_of(lax.bitwise_and(x + step, 3) * 128 + offset, 64), size)
+    return pl.ds(pl.multiple_of(lax.bitwise_xor(x, step) * 128 + offset, 64), size)
 
 
 def width_inputs_kernel(index_ref, *refs):
@@ -283,7 +271,7 @@
         [mine] + list(parts),
         moved=2**20,
     )
-    return mine, [to_gx(send, step) for step, send in zip((1, 2, 3), sends)]
+    return mine, [swap_gx(send, step) for step, send in zip((1, 2, 3), sends)]
 
 
 def last_sum(mine, parts):
@@ -316,7 +304,7 @@
         flops=2 * 256 * width * units,
         moved=6 * 2**20,
     )
-    return mine, [to_y(send, step) for step, send in zip((1, 2, 3), sends)]
+    return mine, [swap_y(send, step) for step, send in zip((1, 2, 3), sends)]
 
 
 def on_device(inputs, w_in, w_out, grad_out):
@@ -328,10 +316,10 @@
         columns_kernel,
         "columns",
         [((64, width), bf16)] * 2,
-        [both] + [from_gx(both, step) for step in steps],
-        moved=2**20,
-    )
-    planes = [[column] + [from_y(column, step) for step in steps] for column in columns]
+        [both] + [swap_gx(both, step) for step in steps],
+        moved=2**20,
+    )
+    planes = [[column] + [swap_y(column, step) for step in steps] for column in columns]
     near = halves(planes[0])
     width_flops = 2 * 512 * width * units
     all_inputs, own, *sends = call(
@@ -348,7 +336,7 @@
         sum_x_kernel,
         "sum_x",
         [((64, units), f32)] * 2,
-        [index, own] + [to_x(send, step) for step, send in zip(steps, sends)],
+        [index, own] + [swap_x(send, step) for step, send in zip(steps, sends)],
         moved=2**20,
         scalars=1,
     )
@@ -389,11 +377,11 @@
         grad_pre_kernel,
         "grad_pre",
         [((64, units), bf16)],
-        [mine] + [to_x(send, step) for step, send in zip(steps, sends)] + [slope],
-        moved=2**20,
-    )
-    hidden_pieces = [pair] + [from_x(pair, step) for step in steps]
-    grad_stack = stack([grad_pre] + [from_x(grad_pre, step) for step in steps], "grad_stack")
+        [mine] + [swap_x(send, step) for step, send in zip(steps, sends)] + [slope],
+        moved=2**20,
+    )
+    hidden_pieces = [pair] + [swap_x(pair, step) for step in steps]
+    grad_stack = stack([grad_pre] + [swap_x(grad_pre, step) for step in steps], "grad_stack")
     hidden_all, far_hidden = units_far(
         far_hidden_kernel, "far_hidden", index, hidden_pieces, w_out, False
     )

time: 139 us -> 139 us (level); the launches traced: 138 us -> 137 us
  starting transfers between devices: 71.3 us -> 67.5 us
  waiting for transfers between devices: 44.2 us -> 46.5 us
    ppermute x33, starting transfers between devices: 62.9 us -> 59.5 us  [the longest x9 21.9 us: swap_gx(): return lax.ppermute(value, 'gx', [(i, i ^ step) for i in range(4)])]
    ppermute x33, waiting for transfers between devices: 43.2 us -> 45 us  [the longest x12 22.6 us: swap_x(): return lax.ppermute(value, 'gz', [(i, i ^ 2 * step) for i in range(8)])]
  transfers between devices with their start and end apart: 43 -> 43, of which waited for: 21 -> 22; matrix products, arithmetic and copies ran while one was open for 4% -> 4% of each run, Pallas kernels for 9% -> 9%
where the time goes in v9:
time: 139 us; the launch traced here: 137 us
  starting transfers between devices  67.5 us (49%)
  waiting for transfers between devices  46.5 us (33%)
  Pallas kernels  13.1 us (9%)
  matrix products  5.66 us (4%)
  local copies, waits for them, and re-layouts  3.26 us (2%)
    ppermute x12, waiting for transfers between devices, swap_x(): return lax.ppermute(value, 'gz', [(i, i ^ 2 * step) for i in range(8)])  22.6 us
    ppermute x9, starting transfers between devices, swap_gx(): return lax.ppermute(value, 'gx', [(i, i ^ step) for i in range(4)])  21.9 us
    ppermute x12, starting transfers between devices, swap_x(): return lax.ppermute(value, 'gz', [(i, i ^ 2 * step) for i in range(8)])  19 us
    ppermute x12, starting transfers between devices, swap_y(): return lax.ppermute(value, 'gy', [(i, i ^ 2 * step) for i in range(8)])  18.5 us
    pallas_call x20, Pallas kernels, call(): pl.pallas_call(kernel, out_shape=[jax.ShapeDtypeStruct(*out) for out in o...  13.1 us
    ppermute x12, waiting for transfers between devices, swap_y(): return lax.ppermute(value, 'gy', [(i, i ^ 2 * step) for i in range(8)])  13 us
    ppermute x9, waiting for transfers between devices, swap_gx(): return lax.ppermute(value, 'gx', [(i, i ^ step) for i in range(4)])  9.42 us
    ppermute x4, starting transfers between devices, other_z(): return lax.ppermute(value, 'gz', [(i, i ^ 1) for i in range(8)])  6.2 us
  transfers between devices with their start and end apart: 43, of which 22 were waited for; matrix products, arithmetic and copies ran while one was open for 4% of the time, Pallas kernels for 9%

profile of v9, /device:TPU:8, one launch (start us, length us, event | category | flops | bytes accessed | tf_op | source)
XLA Modules:
  0.0 136.9 jit_solution(13039844967836535679)
XLA Ops:
  2.2 3.4 %collective-permute-start = (bf16[32,1536]{1,0:T(8,128)(2,1)S(1)}, bf16[32,1536]{1,0:T(8,128)(2,1)S(1)}, u32[]{:S(2)}, u32[]{:S(2)}) collective-permute-start(bf16[32,1536]{1,0:T(8,128)(2,1)S(1)} %pair.1.both_ref), channel_id=1, source_target_pairs={{0,64},{64,0},{128,192},{192,128},{1,65},{65,1},{129,193},{193,129... | collective-permute-start | bytes 294920 | tf_op jit(solution)/shard_map/ppermute | solution.py:31
  5.6 5.4 %collective-permute-start.1 = (bf16[32,1536]{1,0:T(8,128)(2,1)S(1)}, bf16[32,1536]{1,0:T(8,128)(2,1)S(1)}, u32[]{:S(2)}, u32[]{:S(2)}) collective-permute-start(bf16[32,1536]{1,0:T(8,128)(2,1)S(1)} %pair.1.both_ref), channel_id=1, source_target_pairs={{0,128},{64,192},{128,0},{192,64},{1,129},{65,193},{129,1},{193,65... | collective-permute-start | bytes 294920 | tf_op jit(solution)/shard_map/ppermute | solution.py:31
  11.0 6.2 %collective-permute-done.1.second_ref = bf16[32,1536]{1,0:T(8,128)(2,1)S(1)} collective-permute-done((bf16[32,1536]{1,0:T(8,128)(2,1)S(1)}, bf16[32,1536]{1,0:T(8,128)(2,1)S(1)}, u32[]{:S(2)}, u32[]{:S(2)}) %collective-permute-start.1) | collective-permute-done | bytes 98336 | tf_op jit(solution)/shard_map/ppermute | solution.py:31
  17.2 2.2 %collective-permute-done.2.third_ref = bf16[32,1536]{1,0:T(8,128)(2,1)S(1)} collective-permute-done((bf16[32,1536]{1,0:T(8,128)(2,1)S(1)}, bf16[32,1536]{1,0:T(8,128)(2,1)S(1)}, u32[]{:S(2)}, u32[]{:S(2)}) %collective-permute-start.2) | collective-permute-done | bytes 98336 | tf_op jit(solution)/shard_map/ppermute | solution.py:31
  19.9 2.6 %collective-permute-start.21 = (bf16[64,1536]{1,0:T(8,128)(2,1)S(1)}, bf16[64,1536]{1,0:T(8,128)(2,1)S(1)}, u32[]{:S(2)}, u32[]{:S(2)}) collective-permute-start(bf16[64,1536]{1,0:T(8,128)(2,1)S(1)} %get-tuple-element.70.refs_0_), channel_id=1, source_target_pairs={{0,32},{8,40},{16,48},{24,56},{32,0},{40,8},{48,16},{56,24},{1,33}... | collective-permute-start | bytes 589832 | tf_op jit(solution)/shard_map/ppermute | solution.py:39
  27.0 1.9 %collective-permute-start.5 = (bf16[64,1536]{1,0:T(8,128)(2,1)S(1)}, bf16[64,1536]{1,0:T(8,128)(2,1)S(1)}, u32[]{:S(2)}, u32[]{:S(2)}) collective-permute-start(bf16[64,1536]{1,0:T(8,128)(2,1)S(1)} %get-tuple-element.54.refs_0_), channel_id=1, source_target_pairs={{0,48},{8,56},{16,32},{24,40},{32,16},{40,24},{48,0},{56,8},{1,49}... | collective-permute-start | bytes 589832 | tf_op jit(solution)/shard_map/ppermute | solution.py:39
  28.9 3.7 %collective-permute-done.21.refs_2_ = bf16[64,1536]{1,0:T(8,128)(2,1)S(1)} collective-permute-done((bf16[64,1536]{1,0:T(8,128)(2,1)S(1)}, bf16[64,1536]{1,0:T(8,128)(2,1)S(1)}, u32[]{:S(2)}, u32[]{:S(2)}) %collective-permute-start.21) | collective-permute-done | bytes 196640 | tf_op jit(solution)/shard_map/ppermute | solution.py:39
  32.5 2.1 %collective-permute-done.22.refs_3_ = bf16[64,1536]{1,0:T(8,128)(2,1)S(1)} collective-permute-done((bf16[64,1536]{1,0:T(8,128)(2,1)S(1)}, bf16[64,1536]{1,0:T(8,128)(2,1)S(1)}, u32[]{:S(2)}, u32[]{:S(2)}) %collective-permute-start.22) | collective-permute-done | bytes 196640 | tf_op jit(solution)/shard_map/ppermute | solution.py:39
  35.4 3.7 %collective-permute-done.4.refs_2_ = bf16[64,1536]{1,0:T(8,128)(2,1)S(1)} collective-permute-done((bf16[64,1536]{1,0:T(8,128)(2,1)S(1)}, bf16[64,1536]{1,0:T(8,128)(2,1)S(1)}, u32[]{:S(2)}, u32[]{:S(2)}) %collective-permute-start.4) | collective-permute-done | bytes 196640 | tf_op jit(solution)/shard_map/ppermute | solution.py:39
  42.8 2.0 %width_grad.1 = (bf16[512,1536]{1,0:T(8,128)(2,1)S(1)}, f32[256,768]{1,0:T(8,128)S(1)}, bf16[256,768]{1,0:T(8,128)(2,1)S(1)}) custom-call(s32[1]{0:T(128)} %bitcast.index_ref, bf16[128,1536]{1,0:T(8,128)(2,1)S(1)} %get-tuple-element.71.refs_0_, bf16[128,1536]{1,0:T(8,128)(2,1)S(1)} %get-tuple-element.72.refs_1_, ...), custom_call_target="tpu_custom_call" | custom-call | flops 1207959552 | bytes 6291456 | tf_op jit(solution)/shard_map/width_grad/pallas_call | solution.py:63
  44.8 2.7 %collective-permute-start.28 = (bf16[256,768]{1,0:T(8,128)(2,1)S(1)}, bf16[256,768]{1,0:T(8,128)(2,1)S(1)}, u32[]{:S(2)}, u32[]{:S(2)}) collective-permute-start(bf16[256,768]{1,0:T(8,128)(2,1)S(1)} %get-tuple-element.82), channel_id=1, source_target_pairs={{0,1},{1,0},{2,3},{3,2},{4,5},{5,4},{6,7},{7,6},{8,9},{9,8},{10,11... | collective-permute-start | bytes 1179656 | tf_op jit(solution)/shard_map/ppermute | solution.py:47
  47.6 1.9 %width_inputs.1 = (bf16[512,1536]{1,0:T(8,128)(2,1)S(1)}, f32[128,768]{1,0:T(8,128)S(1)}, bf16[128,768]{1,0:T(8,128)(2,1)S(1)}, bf16[128,768]{1,0:T(8,128)(2,1)S(1)}, bf16[128,768]{1,0:T(8,128)(2,1)S(1)}) custom-call(s32[1]{0:T(128)} %bitcast.index_ref, bf16[128,1536]{1,0:T(8,128)(2,1)S(1)} %get-tuple-element.55.refs_0_, ...), custom_call_target="tpu_custom_call" | custom-call | flops 1207959552 | bytes 6291456 | tf_op jit(solution)/shard_map/width_inputs/pallas_call | solution.py:63
  51.1 2.7 %collective-permute-start.9 = (bf16[128,768]{1,0:T(8,128)(2,1)S(1)}, bf16[128,768]{1,0:T(8,128)(2,1)S(1)}, u32[]{:S(2)}, u32[]{:S(2)}) collective-permute-start(bf16[128,768]{1,0:T(8,128)(2,1)S(1)} %get-tuple-element.59), channel_id=1, source_target_pairs={{0,4},{1,5},{2,6},{3,7},{4,0},{5,1},{6,2},{7,3},{8,12},{9,13},{10,... | collective-permute-start | bytes 589832 | tf_op jit(solution)/shard_map/ppermute | solution.py:43
  54.3 3.1 %collective-permute-done.8.first_ref = bf16[128,768]{1,0:T(8,128)(2,1)S(1)} collective-permute-done((bf16[128,768]{1,0:T(8,128)(2,1)S(1)}, bf16[128,768]{1,0:T(8,128)(2,1)S(1)}, u32[]{:S(2)}, u32[]{:S(2)}) %collective-permute-start.8) | collective-permute-done | bytes 196640 | tf_op jit(solution)/shard_map/ppermute | solution.py:43
  57.4 5.3 %collective-permute-done.9.second_ref = bf16[128,768]{1,0:T(8,128)(2,1)S(1)} collective-permute-done((bf16[128,768]{1,0:T(8,128)(2,1)S(1)}, bf16[128,768]{1,0:T(8,128)(2,1)S(1)}, u32[]{:S(2)}, u32[]{:S(2)}) %collective-permute-start.9) | collective-permute-done | bytes 196640 | tf_op jit(solution)/shard_map/ppermute | solution.py:43
  62.7 2.6 %collective-permute-done.10.third_ref = bf16[128,768]{1,0:T(8,128)(2,1)S(1)} collective-permute-done((bf16[128,768]{1,0:T(8,128)(2,1)S(1)}, bf16[128,768]{1,0:T(8,128)(2,1)S(1)}, u32[]{:S(2)}, u32[]{:S(2)}) %collective-permute-start.10) | collective-permute-done | bytes 196640 | tf_op jit(solution)/shard_map/ppermute | solution.py:43
  66.1 1.9 %collective-permute-start.30 = (bf16[64,768]{1,0:T(8,128)(2,1)S(1)}, bf16[64,768]{1,0:T(8,128)(2,1)S(1)}, u32[]{:S(2)}, u32[]{:S(2)}) collective-permute-start(bf16[64,768]{1,0:T(8,128)(2,1)S(1)} %get-tuple-element.85), channel_id=1, source_target_pairs={{0,4},{1,5},{2,6},{3,7},{4,0},{5,1},{6,2},{7,3},{8,12},{9,13},{10,... | collective-permute-start | bytes 294920 | tf_op jit(solution)/shard_map/ppermute | solution.py:43
  68.0 2.7 %collective-permute-start.31 = (bf16[64,768]{1,0:T(8,128)(2,1)S(1)}, bf16[64,768]{1,0:T(8,128)(2,1)S(1)}, u32[]{:S(2)}, u32[]{:S(2)}) collective-permute-start(bf16[64,768]{1,0:T(8,128)(2,1)S(1)} %get-tuple-element.86), channel_id=1, source_target_pairs={{0,6},{1,7},{2,4},{3,5},{4,2},{5,3},{6,0},{7,1},{8,14},{9,15},{10,... | collective-permute-start | bytes 294920 | tf_op jit(solution)/shard_map/ppermute | solution.py:43
  74.4 3.8 %collective-permute-start.33 = (bf16[64,768]{1,0:T(8,128)(2,1)S(1)}, bf16[64,768]{1,0:T(8,128)(2,1)S(1)}, u32[]{:S(2)}, u32[]{:S(2)}) collective-permute-start(bf16[64,768]{1,0:T(8,128)(2,1)S(1)} %grad_pre.1.refs_0_), channel_id=1, source_target_pairs={{0,4},{1,5},{2,6},{3,7},{4,0},{5,1},{6,2},{7,3},{8,12},{9,13},{10,... | collective-permute-start | bytes 294920 | tf_op jit(solution)/shard_map/ppermute | solution.py:43
  78.8 3.1 %collective-permute-done.33.refs_2_ = bf16[64,768]{1,0:T(8,128)(2,1)S(1)} collective-permute-done((bf16[64,768]{1,0:T(8,128)(2,1)S(1)}, bf16[64,768]{1,0:T(8,128)(2,1)S(1)}, u32[]{:S(2)}, u32[]{:S(2)}) %collective-permute-start.33) | collective-permute-done | bytes 98336 | tf_op jit(solution)/shard_map/ppermute | solution.py:43
  81.9 2.2 %collective-permute-done.34.refs_3_ = bf16[64,768]{1,0:T(8,128)(2,1)S(1)} collective-permute-done((bf16[64,768]{1,0:T(8,128)(2,1)S(1)}, bf16[64,768]{1,0:T(8,128)(2,1)S(1)}, u32[]{:S(2)}, u32[]{:S(2)}) %collective-permute-start.34) | collective-permute-done | bytes 98336 | tf_op jit(solution)/shard_map/ppermute | solution.py:43
  85.9 2.0 %collective-permute-start.14 = (bf16[128,768]{1,0:T(8,128)(2,1)S(1)}, bf16[128,768]{1,0:T(8,128)(2,1)S(1)}, u32[]{:S(2)}, u32[]{:S(2)}) collective-permute-start(bf16[128,768]{1,0:T(8,128)(2,1)S(1)} %pair_z.1.refs_0_), channel_id=1, source_target_pairs={{0,4},{1,5},{2,6},{3,7},{4,0},{5,1},{6,2},{7,3},{8,12},{9,13},{10,... | collective-permute-start | bytes 589832 | tf_op jit(solution)/shard_map/ppermute | solution.py:43
  87.9 2.7 %collective-permute-start.15 = (bf16[128,768]{1,0:T(8,128)(2,1)S(1)}, bf16[128,768]{1,0:T(8,128)(2,1)S(1)}, u32[]{:S(2)}, u32[]{:S(2)}) collective-permute-start(bf16[128,768]{1,0:T(8,128)(2,1)S(1)} %pair_z.1.refs_0_), channel_id=1, source_target_pairs={{0,6},{1,7},{2,4},{3,5},{4,2},{5,3},{6,0},{7,1},{8,14},{9,15},{10,... | collective-permute-start | bytes 589832 | tf_op jit(solution)/shard_map/ppermute | solution.py:43
  91.6 2.2 %collective-permute-done.14.refs_2_ = bf16[128,768]{1,0:T(8,128)(2,1)S(1)} collective-permute-done((bf16[128,768]{1,0:T(8,128)(2,1)S(1)}, bf16[128,768]{1,0:T(8,128)(2,1)S(1)}, u32[]{:S(2)}, u32[]{:S(2)}) %collective-permute-start.14) | collective-permute-done | bytes 196640 | tf_op jit(solution)/shard_map/ppermute | solution.py:43
  93.8 2.0 %collective-permute-done.15.refs_3_ = bf16[128,768]{1,0:T(8,128)(2,1)S(1)} collective-permute-done((bf16[128,768]{1,0:T(8,128)(2,1)S(1)}, bf16[128,768]{1,0:T(8,128)(2,1)S(1)}, u32[]{:S(2)}, u32[]{:S(2)}) %collective-permute-start.15) | collective-permute-done | bytes 196640 | tf_op jit(solution)/shard_map/ppermute | solution.py:43
  97.6 1.9 %far_grad.1 = (bf16[512,768]{1,0:T(8,128)(2,1)S(1)}, f32[256,1536]{1,0:T(8,128)S(1)}) custom-call(s32[1]{0:T(128)} %bitcast.index_ref, bf16[256,768]{1,0:T(8,128)(2,1)S(1)} %grad_stack.1.own_ref, bf16[256,768]{1,0:T(8,128)(2,1)S(1)} %collective-permute-done.35.part_ref, bf16[1536,768]{1,0:T(8,128)(2,1)S(1)} %copy-done.2), custom_call_target="tpu_custom_call" | custom-call | flops 603979776 | bytes 6291456 | tf_op jit(solution)/shard_map/far_grad/pallas_call | solution.py:63
  102.6 3.2 %collective-permute-start.17 = (bf16[64,1536]{1,0:T(8,128)(2,1)S(1)}, bf16[64,1536]{1,0:T(8,128)(2,1)S(1)}, u32[]{:S(2)}, u32[]{:S(2)}) collective-permute-start(bf16[64,1536]{1,0:T(8,128)(2,1)S(1)} %get-tuple-element.67), channel_id=1, source_target_pairs={{0,16},{8,24},{16,0},{24,8},{32,48},{40,56},{48,32},{56,40},{1,17}... | collective-permute-start | bytes 589832 | tf_op jit(solution)/shard_map/ppermute | solution.py:39
  109.2 3.2 %collective-permute-start.37 = (bf16[64,1536]{1,0:T(8,128)(2,1)S(1)}, bf16[64,1536]{1,0:T(8,128)(2,1)S(1)}, u32[]{:S(2)}, u32[]{:S(2)}) collective-permute-start(bf16[64,1536]{1,0:T(8,128)(2,1)S(1)} %get-tuple-element.91), channel_id=1, source_target_pairs={{0,16},{8,24},{16,0},{24,8},{32,48},{40,56},{48,32},{56,40},{1,17}... | collective-permute-start | bytes 589832 | tf_op jit(solution)/shard_map/ppermute | solution.py:39
  114.0 2.8 %convolution_convert_fusion.1 = bf16[768,1536]{1,0:T(8,128)(2,1)} fusion(bf16[512,768]{1,0:T(8,128)(2,1)S(1)} %get-tuple-element.64.whole_ref, bf16[512,1536]{1,0:T(8,128)(2,1)S(1)} %get-tuple-element.73), kind=kOutput, calls=%fused_computation.1 | convolution fusion | flops 1209139200 | bytes 4718592 | tf_op jit(solution)/shard_map/dot_general | solution.py:393
  118.3 4.5 %collective-permute-start.26 = (bf16[16,1536]{1,0:T(8,128)(2,1)S(1)}, bf16[16,1536]{1,0:T(8,128)(2,1)S(1)}, u32[]{:S(2)}, u32[]{:S(2)}) collective-permute-start(bf16[16,1536]{1,0:T(8,128)(2,1)S(1)} %get-tuple-element.79), channel_id=1, source_target_pairs={{0,128},{64,192},{128,0},{192,64},{1,129},{65,193},{129,1},{193,65... | collective-permute-start | bytes 147464 | tf_op jit(solution)/shard_map/ppermute | solution.py:31
  125.6 4.5 %collective-permute-start.41 = (bf16[16,1536]{1,0:T(8,128)(2,1)S(1)}, bf16[16,1536]{1,0:T(8,128)(2,1)S(1)}, u32[]{:S(2)}, u32[]{:S(2)}) collective-permute-start(bf16[16,1536]{1,0:T(8,128)(2,1)S(1)} %get-tuple-element.100), channel_id=1, source_target_pairs={{0,128},{64,192},{128,0},{192,64},{1,129},{65,193},{129,1},{193,65... | collective-permute-start | bytes 147464 | tf_op jit(solution)/shard_map/ppermute | solution.py:31
  131.8 2.8 %convolution_convert_fusion = bf16[1536,768]{1,0:T(8,128)(2,1)} fusion(bf16[512,1536]{1,0:T(8,128)(2,1)S(1)} %get-tuple-element.102, bf16[512,768]{1,0:T(8,128)(2,1)S(1)} %get-tuple-element.88.whole_ref), kind=kOutput, calls=%fused_computation | convolution fusion | flops 1209139200 | bytes 4718592 | tf_op jit(solution)/shard_map/dot_general | solution.py:396
  (86 shorter events, 39.0 us)
Async XLA Ops:
  2.2 8.8 %collective-permute-start = (bf16[32,1536]{1,0:T(8,128)(2,1)S(1)}, bf16[32,1536]{1,0:T(8,128)(2,1)S(1)}, u32[]{:S(2)}, u32[]{:S(2)}) collective-permute-start(bf16[32,1536]{1,0:T(8,128)(2,1)S(1)} %pair.1.both_ref), channel_id=1, source_target_pairs={{0,64},{64,0},{128,192},{192,128},{1,65},{65,1},{129,193},{193,129... | collective-permute-start | bytes 294920 | tf_op jit(solution)/shard_map/ppermute | solution.py:31
  5.6 11.6 %collective-permute-start.1 = (bf16[32,1536]{1,0:T(8,128)(2,1)S(1)}, bf16[32,1536]{1,0:T(8,128)(2,1)S(1)}, u32[]{:S(2)}, u32[]{:S(2)}) collective-permute-start(bf16[32,1536]{1,0:T(8,128)(2,1)S(1)} %pair.1.both_ref), channel_id=1, source_target_pairs={{0,128},{64,192},{128,0},{192,64},{1,129},{65,193},{129,1},{193,65... | collective-permute-start | bytes 294920 | tf_op jit(solution)/shard_map/ppermute | solution.py:31
  11.0 8.4 %collective-permute-start.2 = (bf16[32,1536]{1,0:T(8,128)(2,1)S(1)}, bf16[32,1536]{1,0:T(8,128)(2,1)S(1)}, u32[]{:S(2)}, u32[]{:S(2)}) collective-permute-start(bf16[32,1536]{1,0:T(8,128)(2,1)S(1)} %pair.1.both_ref), channel_id=1, source_target_pairs={{0,192},{64,128},{128,64},{192,0},{1,193},{65,129},{129,65},{193,1... | collective-permute-start | bytes 294920 | tf_op jit(solution)/shard_map/ppermute | solution.py:31
  19.4 7.6 %collective-permute-start.20 = (bf16[64,1536]{1,0:T(8,128)(2,1)S(1)}, bf16[64,1536]{1,0:T(8,128)(2,1)S(1)}, u32[]{:S(2)}, u32[]{:S(2)}) collective-permute-start(bf16[64,1536]{1,0:T(8,128)(2,1)S(1)} %get-tuple-element.70.refs_0_), channel_id=1, source_target_pairs={{0,16},{8,24},{16,0},{24,8},{32,48},{40,56},{48,32},{56,40},{1,17}... | collective-permute-start | bytes 589832 | tf_op jit(solution)/shard_map/ppermute | solution.py:39
  19.9 12.6 %collective-permute-start.21 = (bf16[64,1536]{1,0:T(8,128)(2,1)S(1)}, bf16[64,1536]{1,0:T(8,128)(2,1)S(1)}, u32[]{:S(2)}, u32[]{:S(2)}) collective-permute-start(bf16[64,1536]{1,0:T(8,128)(2,1)S(1)} %get-tuple-element.70.refs_0_), channel_id=1, source_target_pairs={{0,32},{8,40},{16,48},{24,56},{32,0},{40,8},{48,16},{56,24},{1,33}... | collective-permute-start | bytes 589832 | tf_op jit(solution)/shard_map/ppermute | solution.py:39
  22.5 12.1 %collective-permute-start.22 = (bf16[64,1536]{1,0:T(8,128)(2,1)S(1)}, bf16[64,1536]{1,0:T(8,128)(2,1)S(1)}, u32[]{:S(2)}, u32[]{:S(2)}) collective-permute-start(bf16[64,1536]{1,0:T(8,128)(2,1)S(1)} %get-tuple-element.70.refs_0_), channel_id=1, source_target_pairs={{0,48},{8,56},{16,32},{24,40},{32,16},{40,24},{48,0},{56,8},{1,49}... | collective-permute-start | bytes 589832 | tf_op jit(solution)/shard_map/ppermute | solution.py:39
  23.0 12.4 %collective-permute-start.3 = (bf16[64,1536]{1,0:T(8,128)(2,1)S(1)}, bf16[64,1536]{1,0:T(8,128)(2,1)S(1)}, u32[]{:S(2)}, u32[]{:S(2)}) collective-permute-start(bf16[64,1536]{1,0:T(8,128)(2,1)S(1)} %get-tuple-element.54.refs_0_), channel_id=1, source_target_pairs={{0,16},{8,24},{16,0},{24,8},{32,48},{40,56},{48,32},{56,40},{1,17}... | collective-permute-start | bytes 589832 | tf_op jit(solution)/shard_map/ppermute | solution.py:39
  24.6 14.4 %collective-permute-start.4 = (bf16[64,1536]{1,0:T(8,128)(2,1)S(1)}, bf16[64,1536]{1,0:T(8,128)(2,1)S(1)}, u32[]{:S(2)}, u32[]{:S(2)}) collective-permute-start(bf16[64,1536]{1,0:T(8,128)(2,1)S(1)} %get-tuple-element.54.refs_0_), channel_id=1, source_target_pairs={{0,32},{8,40},{16,48},{24,56},{32,0},{40,8},{48,16},{56,24},{1,33}... | collective-permute-start | bytes 589832 | tf_op jit(solution)/shard_map/ppermute | solution.py:39
  27.0 13.5 %collective-permute-start.5 = (bf16[64,1536]{1,0:T(8,128)(2,1)S(1)}, bf16[64,1536]{1,0:T(8,128)(2,1)S(1)}, u32[]{:S(2)}, u32[]{:S(2)}) collective-permute-start(bf16[64,1536]{1,0:T(8,128)(2,1)S(1)} %get-tuple-element.54.refs_0_), channel_id=1, source_target_pairs={{0,48},{8,56},{16,32},{24,40},{32,16},{40,24},{48,0},{56,8},{1,49}... | collective-permute-start | bytes 589832 | tf_op jit(solution)/shard_map/ppermute | solution.py:39
  40.5 7.0 %collective-permute-start.6 = (bf16[128,1536]{1,0:T(8,128)(2,1)S(1)}, bf16[128,1536]{1,0:T(8,128)(2,1)S(1)}, u32[]{:S(2)}, u32[]{:S(2)}) collective-permute-start(bf16[128,1536]{1,0:T(8,128)(2,1)S(1)} %get-tuple-element.55.refs_0_), channel_id=1, source_target_pairs={{0,8},{8,0},{16,24},{24,16},{32,40},{40,32},{48,56},{56,48},{1,9},... | collective-permute-start | bytes 1179656 | tf_op jit(solution)/shard_map/ppermute | solution.py:35
  40.6 6.9 %collective-permute-start.7 = (bf16[128,1536]{1,0:T(8,128)(2,1)S(1)}, bf16[128,1536]{1,0:T(8,128)(2,1)S(1)}, u32[]{:S(2)}, u32[]{:S(2)}) collective-permute-start(bf16[128,1536]{1,0:T(8,128)(2,1)S(1)} %get-tuple-element.56.refs_1_), channel_id=1, source_target_pairs={{0,8},{8,0},{16,24},{24,16},{32,40},{40,32},{48,56},{56,48},{1,9},... | collective-permute-start | bytes 1179656 | tf_op jit(solution)/shard_map/ppermute | solution.py:35
  44.8 21.0 %collective-permute-start.28 = (bf16[256,768]{1,0:T(8,128)(2,1)S(1)}, bf16[256,768]{1,0:T(8,128)(2,1)S(1)}, u32[]{:S(2)}, u32[]{:S(2)}) collective-permute-start(bf16[256,768]{1,0:T(8,128)(2,1)S(1)} %get-tuple-element.82), channel_id=1, source_target_pairs={{0,1},{1,0},{2,3},{3,2},{4,5},{5,4},{6,7},{7,6},{8,9},{9,8},{10,11... | collective-permute-start | bytes 1179656 | tf_op jit(solution)/shard_map/ppermute | solution.py:47
  49.5 7.9 %collective-permute-start.8 = (bf16[128,768]{1,0:T(8,128)(2,1)S(1)}, bf16[128,768]{1,0:T(8,128)(2,1)S(1)}, u32[]{:S(2)}, u32[]{:S(2)}) collective-permute-start(bf16[128,768]{1,0:T(8,128)(2,1)S(1)} %get-tuple-element.58), channel_id=1, source_target_pairs={{0,2},{1,3},{2,0},{3,1},{4,6},{5,7},{6,4},{7,5},{8,10},{9,11},{10,... | collective-permute-start | bytes 589832 | tf_op jit(solution)/shard_map/ppermute | solution.py:43
  51.1 11.6 %collective-permute-start.9 = (bf16[128,768]{1,0:T(8,128)(2,1)S(1)}, bf16[128,768]{1,0:T(8,128)(2,1)S(1)}, u32[]{:S(2)}, u32[]{:S(2)}) collective-permute-start(bf16[128,768]{1,0:T(8,128)(2,1)S(1)} %get-tuple-element.59), channel_id=1, source_target_pairs={{0,4},{1,5},{2,6},{3,7},{4,0},{5,1},{6,2},{7,3},{8,12},{9,13},{10,... | collective-permute-start | bytes 589832 | tf_op jit(solution)/shard_map/ppermute | solution.py:43
  53.8 11.5 %collective-permute-start.10 = (bf16[128,768]{1,0:T(8,128)(2,1)S(1)}, bf16[128,768]{1,0:T(8,128)(2,1)S(1)}, u32[]{:S(2)}, u32[]{:S(2)}) collective-permute-start(bf16[128,768]{1,0:T(8,128)(2,1)S(1)} %get-tuple-element.60), channel_id=1, source_target_pairs={{0,6},{1,7},{2,4},{3,5},{4,2},{5,3},{6,0},{7,1},{8,14},{9,15},{10,... | collective-permute-start | bytes 589832 | tf_op jit(solution)/shard_map/ppermute | solution.py:43
  71.5 7.2 %collective-permute-start.12 = (bf16[64,768]{1,0:T(8,128)(2,1)S(1)}, bf16[64,768]{1,0:T(8,128)(2,1)S(1)}, u32[]{:S(2)}, u32[]{:S(2)}) collective-permute-start(bf16[64,768]{1,0:T(8,128)(2,1)S(1)} %get-tuple-element.63.own_ref), channel_id=1, source_target_pairs={{0,1},{1,0},{2,3},{3,2},{4,5},{5,4},{6,7},{7,6},{8,9},{9,8},{10,11... | collective-permute-start | bytes 294920 | tf_op jit(solution)/shard_map/ppermute | solution.py:47
  74.4 7.5 %collective-permute-start.33 = (bf16[64,768]{1,0:T(8,128)(2,1)S(1)}, bf16[64,768]{1,0:T(8,128)(2,1)S(1)}, u32[]{:S(2)}, u32[]{:S(2)}) collective-permute-start(bf16[64,768]{1,0:T(8,128)(2,1)S(1)} %grad_pre.1.refs_0_), channel_id=1, source_target_pairs={{0,4},{1,5},{2,6},{3,7},{4,0},{5,1},{6,2},{7,3},{8,12},{9,13},{10,... | collective-permute-start | bytes 294920 | tf_op jit(solution)/shard_map/ppermute | solution.py:43
  84.1 13.4 %collective-permute-start.35 = (bf16[256,768]{1,0:T(8,128)(2,1)S(1)}, bf16[256,768]{1,0:T(8,128)(2,1)S(1)}, u32[]{:S(2)}, u32[]{:S(2)}) collective-permute-start(bf16[256,768]{1,0:T(8,128)(2,1)S(1)} %grad_stack.1.own_ref), channel_id=1, source_target_pairs={{0,1},{1,0},{2,3},{3,2},{4,5},{5,4},{6,7},{7,6},{8,9},{9,8},{10,11... | collective-permute-start | bytes 1179656 | tf_op jit(solution)/shard_map/ppermute | solution.py:47
  85.9 7.8 %collective-permute-start.14 = (bf16[128,768]{1,0:T(8,128)(2,1)S(1)}, bf16[128,768]{1,0:T(8,128)(2,1)S(1)}, u32[]{:S(2)}, u32[]{:S(2)}) collective-permute-start(bf16[128,768]{1,0:T(8,128)(2,1)S(1)} %pair_z.1.refs_0_), channel_id=1, source_target_pairs={{0,4},{1,5},{2,6},{3,7},{4,0},{5,1},{6,2},{7,3},{8,12},{9,13},{10,... | collective-permute-start | bytes 589832 | tf_op jit(solution)/shard_map/ppermute | solution.py:43
  87.9 7.9 %collective-permute-start.15 = (bf16[128,768]{1,0:T(8,128)(2,1)S(1)}, bf16[128,768]{1,0:T(8,128)(2,1)S(1)}, u32[]{:S(2)}, u32[]{:S(2)}) collective-permute-start(bf16[128,768]{1,0:T(8,128)(2,1)S(1)} %pair_z.1.refs_0_), channel_id=1, source_target_pairs={{0,6},{1,7},{2,4},{3,5},{4,2},{5,3},{6,0},{7,1},{8,14},{9,15},{10,... | collective-permute-start | bytes 589832 | tf_op jit(solution)/shard_map/ppermute | solution.py:43
  99.5 7.9 %collective-permute-start.36 = (f32[256,1536]{1,0:T(8,128)S(1)}, f32[256,1536]{1,0:T(8,128)S(1)}, u32[]{:S(2)}, u32[]{:S(2)}) collective-permute-start(f32[256,1536]{1,0:T(8,128)S(1)} %get-tuple-element.89), channel_id=1, source_target_pairs={{0,8},{8,0},{16,24},{24,16},{32,40},{40,32},{48,56},{56,48},{1,9},... | collective-permute-start | bytes 4718600 | tf_op jit(solution)/shard_map/ppermute | solution.py:35
  102.6 9.8 %collective-permute-start.17 = (bf16[64,1536]{1,0:T(8,128)(2,1)S(1)}, bf16[64,1536]{1,0:T(8,128)(2,1)S(1)}, u32[]{:S(2)}, u32[]{:S(2)}) collective-permute-start(bf16[64,1536]{1,0:T(8,128)(2,1)S(1)} %get-tuple-element.67), channel_id=1, source_target_pairs={{0,16},{8,24},{16,0},{24,8},{32,48},{40,56},{48,32},{56,40},{1,17}... | collective-permute-start | bytes 589832 | tf_op jit(solution)/shard_map/ppermute | solution.py:39
  105.8 11.0 %collective-permute-start.18 = (bf16[64,1536]{1,0:T(8,128)(2,1)S(1)}, bf16[64,1536]{1,0:T(8,128)(2,1)S(1)}, u32[]{:S(2)}, u32[]{:S(2)}) collective-permute-start(bf16[64,1536]{1,0:T(8,128)(2,1)S(1)} %get-tuple-element.68), channel_id=1, source_target_pairs={{0,32},{8,40},{16,48},{24,56},{32,0},{40,8},{48,16},{56,24},{1,33}... | collective-permute-start | bytes 589832 | tf_op jit(solution)/shard_map/ppermute | solution.py:39
  105.8 12.0 %collective-permute-start.19 = (bf16[64,1536]{1,0:T(8,128)(2,1)S(1)}, bf16[64,1536]{1,0:T(8,128)(2,1)S(1)}, u32[]{:S(2)}, u32[]{:S(2)}) collective-permute-start(bf16[64,1536]{1,0:T(8,128)(2,1)S(1)} %get-tuple-element.69), channel_id=1, source_target_pairs={{0,48},{8,56},{16,32},{24,40},{32,16},{40,24},{48,0},{56,8},{1,49}... | collective-permute-start | bytes 589832 | tf_op jit(solution)/shard_map/ppermute | solution.py:39
  109.2 13.6 %collective-permute-start.37 = (bf16[64,1536]{1,0:T(8,128)(2,1)S(1)}, bf16[64,1536]{1,0:T(8,128)(2,1)S(1)}, u32[]{:S(2)}, u32[]{:S(2)}) collective-permute-start(bf16[64,1536]{1,0:T(8,128)(2,1)S(1)} %get-tuple-element.91), channel_id=1, source_target_pairs={{0,16},{8,24},{16,0},{24,8},{32,48},{40,56},{48,32},{56,40},{1,17}... | collective-permute-start | bytes 589832 | tf_op jit(solution)/shard_map/ppermute | solution.py:39
  112.4 12.1 %collective-permute-start.38 = (bf16[64,1536]{1,0:T(8,128)(2,1)S(1)}, bf16[64,1536]{1,0:T(8,128)(2,1)S(1)}, u32[]{:S(2)}, u32[]{:S(2)}) collective-permute-start(bf16[64,1536]{1,0:T(8,128)(2,1)S(1)} %get-tuple-element.92), channel_id=1, source_target_pairs={{0,32},{8,40},{16,48},{24,56},{32,0},{40,8},{48,16},{56,24},{1,33}... | collective-permute-start | bytes 589832 | tf_op jit(solution)/shard_map/ppermute | solution.py:39
  112.4 12.7 %collective-permute-start.39 = (bf16[64,1536]{1,0:T(8,128)(2,1)S(1)}, bf16[64,1536]{1,0:T(8,128)(2,1)S(1)}, u32[]{:S(2)}, u32[]{:S(2)}) collective-permute-start(bf16[64,1536]{1,0:T(8,128)(2,1)S(1)} %get-tuple-element.93), channel_id=1, source_target_pairs={{0,48},{8,56},{16,32},{24,40},{32,16},{40,24},{48,0},{56,8},{1,49}... | collective-permute-start | bytes 589832 | tf_op jit(solution)/shard_map/ppermute | solution.py:39
  117.9 12.2 %collective-permute-start.25 = (bf16[16,1536]{1,0:T(8,128)(2,1)S(1)}, bf16[16,1536]{1,0:T(8,128)(2,1)S(1)}, u32[]{:S(2)}, u32[]{:S(2)}) collective-permute-start(bf16[16,1536]{1,0:T(8,128)(2,1)S(1)} %get-tuple-element.78), channel_id=1, source_target_pairs={{0,64},{64,0},{128,192},{192,128},{1,65},{65,1},{129,193},{193,129... | collective-permute-start | bytes 147464 | tf_op jit(solution)/shard_map/ppermute | solution.py:31
  118.3 16.3 %collective-permute-start.26 = (bf16[16,1536]{1,0:T(8,128)(2,1)S(1)}, bf16[16,1536]{1,0:T(8,128)(2,1)S(1)}, u32[]{:S(2)}, u32[]{:S(2)}) collective-permute-start(bf16[16,1536]{1,0:T(8,128)(2,1)S(1)} %get-tuple-element.79), channel_id=1, source_target_pairs={{0,128},{64,192},{128,0},{192,64},{1,129},{65,193},{129,1},{193,65... | collective-permute-start | bytes 147464 | tf_op jit(solution)/shard_map/ppermute | solution.py:31
  122.8 11.8 %collective-permute-start.27 = (bf16[16,1536]{1,0:T(8,128)(2,1)S(1)}, bf16[16,1536]{1,0:T(8,128)(2,1)S(1)}, u32[]{:S(2)}, u32[]{:S(2)}) collective-permute-start(bf16[16,1536]{1,0:T(8,128)(2,1)S(1)} %get-tuple-element.80), channel_id=1, source_target_pairs={{0,192},{64,128},{128,64},{192,0},{1,193},{65,129},{129,65},{193,1... | collective-permute-start | bytes 147464 | tf_op jit(solution)/shard_map/ppermute | solution.py:31
  125.2 10.1 %collective-permute-start.40 = (bf16[16,1536]{1,0:T(8,128)(2,1)S(1)}, bf16[16,1536]{1,0:T(8,128)(2,1)S(1)}, u32[]{:S(2)}, u32[]{:S(2)}) collective-permute-start(bf16[16,1536]{1,0:T(8,128)(2,1)S(1)} %get-tuple-element.99), channel_id=1, source_target_pairs={{0,64},{64,0},{128,192},{192,128},{1,65},{65,1},{129,193},{193,129... | collective-permute-start | bytes 147464 | tf_op jit(solution)/shard_map/ppermute | solution.py:31
  125.6 9.7 %collective-permute-start.41 = (bf16[16,1536]{1,0:T(8,128)(2,1)S(1)}, bf16[16,1536]{1,0:T(8,128)(2,1)S(1)}, u32[]{:S(2)}, u32[]{:S(2)}) collective-permute-start(bf16[16,1536]{1,0:T(8,128)(2,1)S(1)} %get-tuple-element.100), channel_id=1, source_target_pairs={{0,128},{64,192},{128,0},{192,64},{1,129},{65,193},{129,1},{193,65... | collective-permute-start | bytes 147464 | tf_op jit(solution)/shard_map/ppermute | solution.py:31
  (16 other events, 101.9 us)

commit v10 on v8

--- a/solution.py
+++ b/solution.py
@@ -109,7 +109,7 @@
 
 def halves_kernel(*refs):
     for i, piece in enumerate(refs[:4]):
-        refs[4 + i // 2][64 * (i % 2) : 64 * (i % 2) + 64, :] = piece[...]
+        refs[i // 2 - 2][64 * (i % 2) : 64 * (i % 2) + 64, :] = piece[...]
 
 
 def halves(pieces):
@@ -267,11 +267,12 @@
             sends[step - 1][...] = total.astype(bf16)
 
 
-def last_kernel(mine_ref, first_ref, second_ref, third_ref, out_ref):
-    total = mine_ref[...]
-    for piece in (first_ref, second_ref, third_ref):
-        total = total + piece[...].astype(f32)
-    out_ref[...] = total.astype(bf16)
+def last_kernel(*refs):
+    for part in range(2):
+        total = refs[4 * part][...]
+        for piece in refs[4 * part + 1 : 4 * part + 4]:
+            total = total + piece[...].astype(f32)
+        refs[8 + part][...] = total.astype(bf16)
 
 
 def column_sum(mine, parts):
@@ -284,10 +285,6 @@
         moved=2**20,
     )
     return mine, [to_gx(send, step) for step, send in zip((1, 2, 3), sends)]
-
-
-def last_sum(mine, parts):
-    return call(last_kernel, "last_sum", [(mine.shape, bf16)], [mine] + list(parts), moved=2**18)[0]
 
 
 def units_far(kernel, name, index, pieces, weight, transposed):
@@ -411,9 +408,13 @@
     parts_hidden, grad_w_out = barrier((parts_hidden, grad_w_out))
     mine_hidden, ends_hidden = column_sum(mine_hidden, parts_hidden)
     mine_grad, ends_grad = column_sum(mine_grad, parts_grad)
-    ends_hidden, mine_grad = barrier((ends_hidden, mine_grad))
-    output = last_sum(mine_hidden, ends_hidden)
-    grad_inputs = last_sum(mine_grad, ends_grad)
+    output, grad_inputs = call(
+        last_kernel,
+        "last_sums",
+        [((16, width), bf16)] * 2,
+        [mine_hidden] + ends_hidden + [mine_grad] + ends_grad,
+        moved=2**19,
+    )
     return (output, grad_inputs, grad_w_in, grad_w_out)
 
 

time: 139 us -> 139 us (level)
    pallas_call x20 -> x19, Pallas kernels: 13.3 us -> 12.6 us  [call(): pl.pallas_call(kernel, out_shape=[jax.ShapeDtypeStruct(*out) for out in o...]
where the time goes in v10:
time: 139 us; the launch traced here: 138 us
  starting transfers between devices  71.3 us (51%)
  waiting for transfers between devices  44.8 us (32%)
  Pallas kernels  12.6 us (9%)
  matrix products  5.65 us (4%)
  local copies, waits for them, and re-layouts  3.26 us (2%)
    ppermute x6, starting transfers between devices, to_gx(): return lax.ppermute(value, 'gx', [(i, (i + step) % 4) for i in range(4)])  14.6 us
    ppermute x6, starting transfers between devices, to_y(): lax.ppermute(value, 'gy', [(i, (i + 2 * step) % 8) for i in range(8)])  14.3 us
    ppermute x6, waiting for transfers between devices, from_x(): lax.ppermute(value, 'gz', [((i + 2 * step) % 8, i) for i in range(8)])  13.6 us
    pallas_call x19, Pallas kernels, call(): pl.pallas_call(kernel, out_shape=[jax.ShapeDtypeStruct(*out) for out in o...  12.6 us
    ppermute x6, waiting for transfers between devices, from_y(): lax.ppermute(value, 'gy', [((i + 2 * step) % 8, i) for i in range(8)])  11.1 us
    ppermute x6, starting transfers between devices, to_x(): lax.ppermute(value, 'gz', [(i, (i + 2 * step) % 8) for i in range(8)])  11.1 us
    ppermute x3, starting transfers between devices, from_gx(): return lax.ppermute(value, 'gx', [((i + step) % 4, i) for i in range(4)])  10.2 us
    ppermute x6, waiting for transfers between devices, to_x(): lax.ppermute(value, 'gz', [(i, (i + 2 * step) % 8) for i in range(8)])  8.76 us
  transfers between devices with their start and end apart: 43, of which 21 were waited for; matrix products, arithmetic and copies ran while one was open for 4% of the time, Pallas kernels for 9%

profile of v10, /device:TPU:8, one launch (start us, length us, event | category | flops | bytes accessed | tf_op | source)
XLA Modules:
  0.0 138.5 jit_solution(7584700531742711950)
XLA Ops:
  2.2 6.4 %collective-permute-start = (bf16[32,1536]{1,0:T(8,128)(2,1)S(1)}, bf16[32,1536]{1,0:T(8,128)(2,1)S(1)}, u32[]{:S(2)}, u32[]{:S(2)}) collective-permute-start(bf16[32,1536]{1,0:T(8,128)(2,1)S(1)} %pair.1.both_ref), channel_id=1, source_target_pairs={{64,0},{128,64},{192,128},{0,192},{65,1},{129,65},{193,129},{1,193... | collective-permute-start | bytes 294920 | tf_op jit(solution)/shard_map/ppermute | solution.py:31
  9.6 2.8 %collective-permute-start.2 = (bf16[32,1536]{1,0:T(8,128)(2,1)S(1)}, bf16[32,1536]{1,0:T(8,128)(2,1)S(1)}, u32[]{:S(2)}, u32[]{:S(2)}) collective-permute-start(bf16[32,1536]{1,0:T(8,128)(2,1)S(1)} %pair.1.both_ref), channel_id=1, source_target_pairs={{192,0},{0,64},{64,128},{128,192},{193,1},{1,65},{65,129},{129,193... | collective-permute-start | bytes 294920 | tf_op jit(solution)/shard_map/ppermute | solution.py:31
  12.4 4.6 %collective-permute-done.first_ref = bf16[32,1536]{1,0:T(8,128)(2,1)S(1)} collective-permute-done((bf16[32,1536]{1,0:T(8,128)(2,1)S(1)}, bf16[32,1536]{1,0:T(8,128)(2,1)S(1)}, u32[]{:S(2)}, u32[]{:S(2)}) %collective-permute-start) | collective-permute-done | bytes 98336 | tf_op jit(solution)/shard_map/ppermute | solution.py:31
  17.0 3.2 %collective-permute-done.1.second_ref = bf16[32,1536]{1,0:T(8,128)(2,1)S(1)} collective-permute-done((bf16[32,1536]{1,0:T(8,128)(2,1)S(1)}, bf16[32,1536]{1,0:T(8,128)(2,1)S(1)}, u32[]{:S(2)}, u32[]{:S(2)}) %collective-permute-start.1) | collective-permute-done | bytes 98336 | tf_op jit(solution)/shard_map/ppermute | solution.py:31
  21.0 2.4 %collective-permute-start.21 = (bf16[64,1536]{1,0:T(8,128)(2,1)S(1)}, bf16[64,1536]{1,0:T(8,128)(2,1)S(1)}, u32[]{:S(2)}, u32[]{:S(2)}) collective-permute-start(bf16[64,1536]{1,0:T(8,128)(2,1)S(1)} %get-tuple-element.68.refs_0_), channel_id=1, source_target_pairs={{32,0},{40,8},{48,16},{56,24},{0,32},{8,40},{16,48},{24,56},{33,1}... | collective-permute-start | bytes 589832 | tf_op jit(solution)/shard_map/ppermute | solution.py:43
  23.4 1.9 %collective-permute-start.22 = (bf16[64,1536]{1,0:T(8,128)(2,1)S(1)}, bf16[64,1536]{1,0:T(8,128)(2,1)S(1)}, u32[]{:S(2)}, u32[]{:S(2)}) collective-permute-start(bf16[64,1536]{1,0:T(8,128)(2,1)S(1)} %get-tuple-element.68.refs_0_), channel_id=1, source_target_pairs={{48,0},{56,8},{0,16},{8,24},{16,32},{24,40},{32,48},{40,56},{49,1}... | collective-permute-start | bytes 589832 | tf_op jit(solution)/shard_map/ppermute | solution.py:43
  26.7 2.8 %collective-permute-done.20.refs_1_ = bf16[64,1536]{1,0:T(8,128)(2,1)S(1)} collective-permute-done((bf16[64,1536]{1,0:T(8,128)(2,1)S(1)}, bf16[64,1536]{1,0:T(8,128)(2,1)S(1)}, u32[]{:S(2)}, u32[]{:S(2)}) %collective-permute-start.20) | collective-permute-done | bytes 196640 | tf_op jit(solution)/shard_map/ppermute | solution.py:43
  29.8 3.7 %collective-permute-done.21.refs_2_ = bf16[64,1536]{1,0:T(8,128)(2,1)S(1)} collective-permute-done((bf16[64,1536]{1,0:T(8,128)(2,1)S(1)}, bf16[64,1536]{1,0:T(8,128)(2,1)S(1)}, u32[]{:S(2)}, u32[]{:S(2)}) %collective-permute-start.21) | collective-permute-done | bytes 196640 | tf_op jit(solution)/shard_map/ppermute | solution.py:43
  35.7 2.1 %collective-permute-done.4.refs_2_ = bf16[64,1536]{1,0:T(8,128)(2,1)S(1)} collective-permute-done((bf16[64,1536]{1,0:T(8,128)(2,1)S(1)}, bf16[64,1536]{1,0:T(8,128)(2,1)S(1)}, u32[]{:S(2)}, u32[]{:S(2)}) %collective-permute-start.4) | collective-permute-done | bytes 196640 | tf_op jit(solution)/shard_map/ppermute | solution.py:43
  41.0 2.1 %width_grad.1 = (bf16[512,1536]{1,0:T(8,128)(2,1)S(1)}, f32[256,768]{1,0:T(8,128)S(1)}, bf16[256,768]{1,0:T(8,128)(2,1)S(1)}) custom-call(s32[1]{0:T(128)} %bitcast.index_ref, bf16[128,1536]{1,0:T(8,128)(2,1)S(1)} %get-tuple-element.69.refs_0_, bf16[128,1536]{1,0:T(8,128)(2,1)S(1)} %get-tuple-element.70.refs_1_, ...), custom_call_target="tpu_custom_call" | custom-call | flops 1207959552 | bytes 6291456 | tf_op jit(solution)/shard_map/width_grad/pallas_call | solution.py:75
  43.1 2.7 %collective-permute-start.28 = (bf16[256,768]{1,0:T(8,128)(2,1)S(1)}, bf16[256,768]{1,0:T(8,128)(2,1)S(1)}, u32[]{:S(2)}, u32[]{:S(2)}) collective-permute-start(bf16[256,768]{1,0:T(8,128)(2,1)S(1)} %get-tuple-element.80), channel_id=1, source_target_pairs={{0,1},{1,0},{2,3},{3,2},{4,5},{5,4},{6,7},{7,6},{8,9},{9,8},{10,11... | collective-permute-start | bytes 1179656 | tf_op jit(solution)/shard_map/ppermute | solution.py:59
  45.8 2.0 %width_inputs.1 = (bf16[512,1536]{1,0:T(8,128)(2,1)S(1)}, f32[128,768]{1,0:T(8,128)S(1)}, bf16[128,768]{1,0:T(8,128)(2,1)S(1)}, bf16[128,768]{1,0:T(8,128)(2,1)S(1)}, bf16[128,768]{1,0:T(8,128)(2,1)S(1)}) custom-call(s32[1]{0:T(128)} %bitcast.index_ref, bf16[128,1536]{1,0:T(8,128)(2,1)S(1)} %get-tuple-element.53.refs_0_, ...), custom_call_target="tpu_custom_call" | custom-call | flops 1207959552 | bytes 6291456 | tf_op jit(solution)/shard_map/width_inputs/pallas_call | solution.py:75
  49.4 2.7 %collective-permute-start.9 = (bf16[128,768]{1,0:T(8,128)(2,1)S(1)}, bf16[128,768]{1,0:T(8,128)(2,1)S(1)}, u32[]{:S(2)}, u32[]{:S(2)}) collective-permute-start(bf16[128,768]{1,0:T(8,128)(2,1)S(1)} %get-tuple-element.57), channel_id=1, source_target_pairs={{0,4},{1,5},{2,6},{3,7},{4,0},{5,1},{6,2},{7,3},{8,12},{9,13},{10,... | collective-permute-start | bytes 589832 | tf_op jit(solution)/shard_map/ppermute | solution.py:55
  53.6 2.4 %collective-permute-done.8.first_ref = bf16[128,768]{1,0:T(8,128)(2,1)S(1)} collective-permute-done((bf16[128,768]{1,0:T(8,128)(2,1)S(1)}, bf16[128,768]{1,0:T(8,128)(2,1)S(1)}, u32[]{:S(2)}, u32[]{:S(2)}) %collective-permute-start.8) | collective-permute-done | bytes 196640 | tf_op jit(solution)/shard_map/ppermute | solution.py:55
  56.0 5.0 %collective-permute-done.9.second_ref = bf16[128,768]{1,0:T(8,128)(2,1)S(1)} collective-permute-done((bf16[128,768]{1,0:T(8,128)(2,1)S(1)}, bf16[128,768]{1,0:T(8,128)(2,1)S(1)}, u32[]{:S(2)}, u32[]{:S(2)}) %collective-permute-start.9) | collective-permute-done | bytes 196640 | tf_op jit(solution)/shard_map/ppermute | solution.py:55
  63.1 2.4 %collective-permute-start.30 = (bf16[64,768]{1,0:T(8,128)(2,1)S(1)}, bf16[64,768]{1,0:T(8,128)(2,1)S(1)}, u32[]{:S(2)}, u32[]{:S(2)}) collective-permute-start(bf16[64,768]{1,0:T(8,128)(2,1)S(1)} %get-tuple-element.83), channel_id=1, source_target_pairs={{0,4},{1,5},{2,6},{3,7},{4,0},{5,1},{6,2},{7,3},{8,12},{9,13},{10,... | collective-permute-start | bytes 294920 | tf_op jit(solution)/shard_map/ppermute | solution.py:55
  70.5 2.7 %collective-permute-start.32 = (bf16[64,768]{1,0:T(8,128)(2,1)S(1)}, bf16[64,768]{1,0:T(8,128)(2,1)S(1)}, u32[]{:S(2)}, u32[]{:S(2)}) collective-permute-start(bf16[64,768]{1,0:T(8,128)(2,1)S(1)} %grad_pre.1.refs_0_), channel_id=1, source_target_pairs={{2,0},{3,1},{4,2},{5,3},{6,4},{7,5},{0,6},{1,7},{10,8},{11,9},{12,... | collective-permute-start | bytes 294920 | tf_op jit(solution)/shard_map/ppermute | solution.py:51
  74.2 2.2 %collective-permute-done.32.refs_1_ = bf16[64,768]{1,0:T(8,128)(2,1)S(1)} collective-permute-done((bf16[64,768]{1,0:T(8,128)(2,1)S(1)}, bf16[64,768]{1,0:T(8,128)(2,1)S(1)}, u32[]{:S(2)}, u32[]{:S(2)}) %collective-permute-start.32) | collective-permute-done | bytes 98336 | tf_op jit(solution)/shard_map/ppermute | solution.py:51
  76.4 3.0 %collective-permute-done.33.refs_2_ = bf16[64,768]{1,0:T(8,128)(2,1)S(1)} collective-permute-done((bf16[64,768]{1,0:T(8,128)(2,1)S(1)}, bf16[64,768]{1,0:T(8,128)(2,1)S(1)}, u32[]{:S(2)}, u32[]{:S(2)}) %collective-permute-start.33) | collective-permute-done | bytes 98336 | tf_op jit(solution)/shard_map/ppermute | solution.py:51
  84.4 3.3 %collective-permute-done.13.refs_1_ = bf16[128,768]{1,0:T(8,128)(2,1)S(1)} collective-permute-done((bf16[128,768]{1,0:T(8,128)(2,1)S(1)}, bf16[128,768]{1,0:T(8,128)(2,1)S(1)}, u32[]{:S(2)}, u32[]{:S(2)}) %collective-permute-start.13) | collective-permute-done | bytes 196640 | tf_op jit(solution)/shard_map/ppermute | solution.py:51
  87.7 2.2 %collective-permute-done.14.refs_2_ = bf16[128,768]{1,0:T(8,128)(2,1)S(1)} collective-permute-done((bf16[128,768]{1,0:T(8,128)(2,1)S(1)}, bf16[128,768]{1,0:T(8,128)(2,1)S(1)}, u32[]{:S(2)}, u32[]{:S(2)}) %collective-permute-start.14) | collective-permute-done | bytes 196640 | tf_op jit(solution)/shard_map/ppermute | solution.py:51
  89.9 2.0 %collective-permute-done.15.refs_3_ = bf16[128,768]{1,0:T(8,128)(2,1)S(1)} collective-permute-done((bf16[128,768]{1,0:T(8,128)(2,1)S(1)}, bf16[128,768]{1,0:T(8,128)(2,1)S(1)}, u32[]{:S(2)}, u32[]{:S(2)}) %collective-permute-start.15) | collective-permute-done | bytes 196640 | tf_op jit(solution)/shard_map/ppermute | solution.py:51
  100.2 3.5 %collective-permute-start.18 = (bf16[64,1536]{1,0:T(8,128)(2,1)S(1)}, bf16[64,1536]{1,0:T(8,128)(2,1)S(1)}, u32[]{:S(2)}, u32[]{:S(2)}) collective-permute-start(bf16[64,1536]{1,0:T(8,128)(2,1)S(1)} %get-tuple-element.66), channel_id=1, source_target_pairs={{0,32},{8,40},{16,48},{24,56},{32,0},{40,8},{48,16},{56,24},{1,33}... | collective-permute-start | bytes 589832 | tf_op jit(solution)/shard_map/ppermute | solution.py:47
  105.6 2.3 %collective-permute-start.37 = (bf16[64,1536]{1,0:T(8,128)(2,1)S(1)}, bf16[64,1536]{1,0:T(8,128)(2,1)S(1)}, u32[]{:S(2)}, u32[]{:S(2)}) collective-permute-start(bf16[64,1536]{1,0:T(8,128)(2,1)S(1)} %get-tuple-element.89), channel_id=1, source_target_pairs={{0,16},{8,24},{16,32},{24,40},{32,48},{40,56},{48,0},{56,8},{1,17}... | collective-permute-start | bytes 589832 | tf_op jit(solution)/shard_map/ppermute | solution.py:47
  109.2 5.7 %collective-permute-start.39 = (bf16[64,1536]{1,0:T(8,128)(2,1)S(1)}, bf16[64,1536]{1,0:T(8,128)(2,1)S(1)}, u32[]{:S(2)}, u32[]{:S(2)}) collective-permute-start(bf16[64,1536]{1,0:T(8,128)(2,1)S(1)} %get-tuple-element.91), channel_id=1, source_target_pairs={{0,48},{8,56},{16,0},{24,8},{32,16},{40,24},{48,32},{56,40},{1,49}... | collective-permute-start | bytes 589832 | tf_op jit(solution)/shard_map/ppermute | solution.py:47
  114.9 2.8 %convolution_convert_fusion.1 = bf16[768,1536]{1,0:T(8,128)(2,1)} fusion(bf16[512,768]{1,0:T(8,128)(2,1)S(1)} %get-tuple-element.62.whole_ref, bf16[512,1536]{1,0:T(8,128)(2,1)S(1)} %get-tuple-element.71), kind=kOutput, calls=%fused_computation.1 | convolution fusion | flops 1209139200 | bytes 4718592 | tf_op jit(solution)/shard_map/dot_general | solution.py:402
  117.8 2.7 %collective-permute-start.25 = (bf16[16,1536]{1,0:T(8,128)(2,1)S(1)}, bf16[16,1536]{1,0:T(8,128)(2,1)S(1)}, u32[]{:S(2)}, u32[]{:S(2)}) collective-permute-start(bf16[16,1536]{1,0:T(8,128)(2,1)S(1)} %get-tuple-element.76), channel_id=1, source_target_pairs={{0,64},{64,128},{128,192},{192,0},{1,65},{65,129},{129,193},{193,1... | collective-permute-start | bytes 147464 | tf_op jit(solution)/shard_map/ppermute | solution.py:35
  120.4 4.0 %collective-permute-start.26 = (bf16[16,1536]{1,0:T(8,128)(2,1)S(1)}, bf16[16,1536]{1,0:T(8,128)(2,1)S(1)}, u32[]{:S(2)}, u32[]{:S(2)}) collective-permute-start(bf16[16,1536]{1,0:T(8,128)(2,1)S(1)} %get-tuple-element.77), channel_id=1, source_target_pairs={{0,128},{64,192},{128,0},{192,64},{1,129},{65,193},{129,1},{193,65... | collective-permute-start | bytes 147464 | tf_op jit(solution)/shard_map/ppermute | solution.py:35
  124.5 3.3 %collective-permute-start.27 = (bf16[16,1536]{1,0:T(8,128)(2,1)S(1)}, bf16[16,1536]{1,0:T(8,128)(2,1)S(1)}, u32[]{:S(2)}, u32[]{:S(2)}) collective-permute-start(bf16[16,1536]{1,0:T(8,128)(2,1)S(1)} %get-tuple-element.78), channel_id=1, source_target_pairs={{0,192},{64,0},{128,64},{192,128},{1,193},{65,1},{129,65},{193,129... | collective-permute-start | bytes 147464 | tf_op jit(solution)/shard_map/ppermute | solution.py:35
  127.9 2.4 %collective-permute-start.41 = (bf16[16,1536]{1,0:T(8,128)(2,1)S(1)}, bf16[16,1536]{1,0:T(8,128)(2,1)S(1)}, u32[]{:S(2)}, u32[]{:S(2)}) collective-permute-start(bf16[16,1536]{1,0:T(8,128)(2,1)S(1)} %get-tuple-element.94), channel_id=1, source_target_pairs={{0,128},{64,192},{128,0},{192,64},{1,129},{65,193},{129,1},{193,65... | collective-permute-start | bytes 147464 | tf_op jit(solution)/shard_map/ppermute | solution.py:35
  130.3 2.2 %collective-permute-start.42 = (bf16[16,1536]{1,0:T(8,128)(2,1)S(1)}, bf16[16,1536]{1,0:T(8,128)(2,1)S(1)}, u32[]{:S(2)}, u32[]{:S(2)}) collective-permute-start(bf16[16,1536]{1,0:T(8,128)(2,1)S(1)} %get-tuple-element.95), channel_id=1, source_target_pairs={{0,192},{64,0},{128,64},{192,128},{1,193},{65,1},{129,65},{193,129... | collective-permute-start | bytes 147464 | tf_op jit(solution)/shard_map/ppermute | solution.py:35
  132.5 2.8 %convolution_convert_fusion = bf16[1536,768]{1,0:T(8,128)(2,1)} fusion(bf16[512,1536]{1,0:T(8,128)(2,1)S(1)} %get-tuple-element.98, bf16[512,768]{1,0:T(8,128)(2,1)S(1)} %get-tuple-element.86.whole_ref), kind=kOutput, calls=%fused_computation | convolution fusion | flops 1209139200 | bytes 4718592 | tf_op jit(solution)/shard_map/dot_general | solution.py:405
  (85 shorter events, 41.3 us)
Async XLA Ops:
  2.2 14.8 %collective-permute-start = (bf16[32,1536]{1,0:T(8,128)(2,1)S(1)}, bf16[32,1536]{1,0:T(8,128)(2,1)S(1)}, u32[]{:S(2)}, u32[]{:S(2)}) collective-permute-start(bf16[32,1536]{1,0:T(8,128)(2,1)S(1)} %pair.1.both_ref), channel_id=1, source_target_pairs={{64,0},{128,64},{192,128},{0,192},{65,1},{129,65},{193,129},{1,193... | collective-permute-start | bytes 294920 | tf_op jit(solution)/shard_map/ppermute | solution.py:31
  8.6 11.6 %collective-permute-start.1 = (bf16[32,1536]{1,0:T(8,128)(2,1)S(1)}, bf16[32,1536]{1,0:T(8,128)(2,1)S(1)}, u32[]{:S(2)}, u32[]{:S(2)}) collective-permute-start(bf16[32,1536]{1,0:T(8,128)(2,1)S(1)} %pair.1.both_ref), channel_id=1, source_target_pairs={{128,0},{192,64},{0,128},{64,192},{129,1},{193,65},{1,129},{65,193... | collective-permute-start | bytes 294920 | tf_op jit(solution)/shard_map/ppermute | solution.py:31
  9.6 10.6 %collective-permute-start.2 = (bf16[32,1536]{1,0:T(8,128)(2,1)S(1)}, bf16[32,1536]{1,0:T(8,128)(2,1)S(1)}, u32[]{:S(2)}, u32[]{:S(2)}) collective-permute-start(bf16[32,1536]{1,0:T(8,128)(2,1)S(1)} %pair.1.both_ref), channel_id=1, source_target_pairs={{192,0},{0,64},{64,128},{128,192},{193,1},{1,65},{65,129},{129,193... | collective-permute-start | bytes 294920 | tf_op jit(solution)/shard_map/ppermute | solution.py:31
  20.3 9.3 %collective-permute-start.20 = (bf16[64,1536]{1,0:T(8,128)(2,1)S(1)}, bf16[64,1536]{1,0:T(8,128)(2,1)S(1)}, u32[]{:S(2)}, u32[]{:S(2)}) collective-permute-start(bf16[64,1536]{1,0:T(8,128)(2,1)S(1)} %get-tuple-element.68.refs_0_), channel_id=1, source_target_pairs={{16,0},{24,8},{32,16},{40,24},{48,32},{56,40},{0,48},{8,56},{17,1}... | collective-permute-start | bytes 589832 | tf_op jit(solution)/shard_map/ppermute | solution.py:43
  21.0 12.5 %collective-permute-start.21 = (bf16[64,1536]{1,0:T(8,128)(2,1)S(1)}, bf16[64,1536]{1,0:T(8,128)(2,1)S(1)}, u32[]{:S(2)}, u32[]{:S(2)}) collective-permute-start(bf16[64,1536]{1,0:T(8,128)(2,1)S(1)} %get-tuple-element.68.refs_0_), channel_id=1, source_target_pairs={{32,0},{40,8},{48,16},{56,24},{0,32},{8,40},{16,48},{24,56},{33,1}... | collective-permute-start | bytes 589832 | tf_op jit(solution)/shard_map/ppermute | solution.py:43
  23.4 11.1 %collective-permute-start.22 = (bf16[64,1536]{1,0:T(8,128)(2,1)S(1)}, bf16[64,1536]{1,0:T(8,128)(2,1)S(1)}, u32[]{:S(2)}, u32[]{:S(2)}) collective-permute-start(bf16[64,1536]{1,0:T(8,128)(2,1)S(1)} %get-tuple-element.68.refs_0_), channel_id=1, source_target_pairs={{48,0},{56,8},{0,16},{8,24},{16,32},{24,40},{32,48},{40,56},{49,1}... | collective-permute-start | bytes 589832 | tf_op jit(solution)/shard_map/ppermute | solution.py:43
  25.3 10.5 %collective-permute-start.3 = (bf16[64,1536]{1,0:T(8,128)(2,1)S(1)}, bf16[64,1536]{1,0:T(8,128)(2,1)S(1)}, u32[]{:S(2)}, u32[]{:S(2)}) collective-permute-start(bf16[64,1536]{1,0:T(8,128)(2,1)S(1)} %get-tuple-element.52.refs_0_), channel_id=1, source_target_pairs={{16,0},{24,8},{32,16},{40,24},{48,32},{56,40},{0,48},{8,56},{17,1}... | collective-permute-start | bytes 589832 | tf_op jit(solution)/shard_map/ppermute | solution.py:43
  25.4 12.5 %collective-permute-start.4 = (bf16[64,1536]{1,0:T(8,128)(2,1)S(1)}, bf16[64,1536]{1,0:T(8,128)(2,1)S(1)}, u32[]{:S(2)}, u32[]{:S(2)}) collective-permute-start(bf16[64,1536]{1,0:T(8,128)(2,1)S(1)} %get-tuple-element.52.refs_0_), channel_id=1, source_target_pairs={{32,0},{40,8},{48,16},{56,24},{0,32},{8,40},{16,48},{24,56},{33,1}... | collective-permute-start | bytes 589832 | tf_op jit(solution)/shard_map/ppermute | solution.py:43
  29.6 9.1 %collective-permute-start.5 = (bf16[64,1536]{1,0:T(8,128)(2,1)S(1)}, bf16[64,1536]{1,0:T(8,128)(2,1)S(1)}, u32[]{:S(2)}, u32[]{:S(2)}) collective-permute-start(bf16[64,1536]{1,0:T(8,128)(2,1)S(1)} %get-tuple-element.52.refs_0_), channel_id=1, source_target_pairs={{48,0},{56,8},{0,16},{8,24},{16,32},{24,40},{32,48},{40,56},{49,1}... | collective-permute-start | bytes 589832 | tf_op jit(solution)/shard_map/ppermute | solution.py:43
  38.7 7.1 %collective-permute-start.6 = (bf16[128,1536]{1,0:T(8,128)(2,1)S(1)}, bf16[128,1536]{1,0:T(8,128)(2,1)S(1)}, u32[]{:S(2)}, u32[]{:S(2)}) collective-permute-start(bf16[128,1536]{1,0:T(8,128)(2,1)S(1)} %get-tuple-element.53.refs_0_), channel_id=1, source_target_pairs={{0,8},{8,0},{16,24},{24,16},{32,40},{40,32},{48,56},{56,48},{1,9},... | collective-permute-start | bytes 1179656 | tf_op jit(solution)/shard_map/ppermute | solution.py:39
  38.8 7.0 %collective-permute-start.7 = (bf16[128,1536]{1,0:T(8,128)(2,1)S(1)}, bf16[128,1536]{1,0:T(8,128)(2,1)S(1)}, u32[]{:S(2)}, u32[]{:S(2)}) collective-permute-start(bf16[128,1536]{1,0:T(8,128)(2,1)S(1)} %get-tuple-element.54.refs_1_), channel_id=1, source_target_pairs={{0,8},{8,0},{16,24},{24,16},{32,40},{40,32},{48,56},{56,48},{1,9},... | collective-permute-start | bytes 1179656 | tf_op jit(solution)/shard_map/ppermute | solution.py:39
  43.1 18.4 %collective-permute-start.28 = (bf16[256,768]{1,0:T(8,128)(2,1)S(1)}, bf16[256,768]{1,0:T(8,128)(2,1)S(1)}, u32[]{:S(2)}, u32[]{:S(2)}) collective-permute-start(bf16[256,768]{1,0:T(8,128)(2,1)S(1)} %get-tuple-element.80), channel_id=1, source_target_pairs={{0,1},{1,0},{2,3},{3,2},{4,5},{5,4},{6,7},{7,6},{8,9},{9,8},{10,11... | collective-permute-start | bytes 1179656 | tf_op jit(solution)/shard_map/ppermute | solution.py:59
  47.8 8.1 %collective-permute-start.8 = (bf16[128,768]{1,0:T(8,128)(2,1)S(1)}, bf16[128,768]{1,0:T(8,128)(2,1)S(1)}, u32[]{:S(2)}, u32[]{:S(2)}) collective-permute-start(bf16[128,768]{1,0:T(8,128)(2,1)S(1)} %get-tuple-element.56), channel_id=1, source_target_pairs={{0,2},{1,3},{2,4},{3,5},{4,6},{5,7},{6,0},{7,1},{8,10},{9,11},{10,... | collective-permute-start | bytes 589832 | tf_op jit(solution)/shard_map/ppermute | solution.py:55
  49.4 11.5 %collective-permute-start.9 = (bf16[128,768]{1,0:T(8,128)(2,1)S(1)}, bf16[128,768]{1,0:T(8,128)(2,1)S(1)}, u32[]{:S(2)}, u32[]{:S(2)}) collective-permute-start(bf16[128,768]{1,0:T(8,128)(2,1)S(1)} %get-tuple-element.57), channel_id=1, source_target_pairs={{0,4},{1,5},{2,6},{3,7},{4,0},{5,1},{6,2},{7,3},{8,12},{9,13},{10,... | collective-permute-start | bytes 589832 | tf_op jit(solution)/shard_map/ppermute | solution.py:55
  52.1 8.8 %collective-permute-start.10 = (bf16[128,768]{1,0:T(8,128)(2,1)S(1)}, bf16[128,768]{1,0:T(8,128)(2,1)S(1)}, u32[]{:S(2)}, u32[]{:S(2)}) collective-permute-start(bf16[128,768]{1,0:T(8,128)(2,1)S(1)} %get-tuple-element.58), channel_id=1, source_target_pairs={{0,6},{1,7},{2,0},{3,1},{4,2},{5,3},{6,4},{7,5},{8,14},{9,15},{10,... | collective-permute-start | bytes 589832 | tf_op jit(solution)/shard_map/ppermute | solution.py:55
  61.7 7.3 %collective-permute-start.29 = (bf16[64,768]{1,0:T(8,128)(2,1)S(1)}, bf16[64,768]{1,0:T(8,128)(2,1)S(1)}, u32[]{:S(2)}, u32[]{:S(2)}) collective-permute-start(bf16[64,768]{1,0:T(8,128)(2,1)S(1)} %get-tuple-element.82), channel_id=1, source_target_pairs={{0,2},{1,3},{2,4},{3,5},{4,6},{5,7},{6,0},{7,1},{8,10},{9,11},{10,... | collective-permute-start | bytes 294920 | tf_op jit(solution)/shard_map/ppermute | solution.py:55
  80.4 13.3 %collective-permute-start.35 = (bf16[256,768]{1,0:T(8,128)(2,1)S(1)}, bf16[256,768]{1,0:T(8,128)(2,1)S(1)}, u32[]{:S(2)}, u32[]{:S(2)}) collective-permute-start(bf16[256,768]{1,0:T(8,128)(2,1)S(1)} %grad_stack.1.own_ref), channel_id=1, source_target_pairs={{0,1},{1,0},{2,3},{3,2},{4,5},{5,4},{6,7},{7,6},{8,9},{9,8},{10,11... | collective-permute-start | bytes 1179656 | tf_op jit(solution)/shard_map/ppermute | solution.py:59
  82.6 7.3 %collective-permute-start.14 = (bf16[128,768]{1,0:T(8,128)(2,1)S(1)}, bf16[128,768]{1,0:T(8,128)(2,1)S(1)}, u32[]{:S(2)}, u32[]{:S(2)}) collective-permute-start(bf16[128,768]{1,0:T(8,128)(2,1)S(1)} %pair_z.1.refs_0_), channel_id=1, source_target_pairs={{4,0},{5,1},{6,2},{7,3},{0,4},{1,5},{2,6},{3,7},{12,8},{13,9},{14,... | collective-permute-start | bytes 589832 | tf_op jit(solution)/shard_map/ppermute | solution.py:51
  83.5 8.4 %collective-permute-start.15 = (bf16[128,768]{1,0:T(8,128)(2,1)S(1)}, bf16[128,768]{1,0:T(8,128)(2,1)S(1)}, u32[]{:S(2)}, u32[]{:S(2)}) collective-permute-start(bf16[128,768]{1,0:T(8,128)(2,1)S(1)} %pair_z.1.refs_0_), channel_id=1, source_target_pairs={{6,0},{7,1},{0,2},{1,3},{2,4},{3,5},{4,6},{5,7},{14,8},{15,9},{8,1... | collective-permute-start | bytes 589832 | tf_op jit(solution)/shard_map/ppermute | solution.py:51
  95.6 8.2 %collective-permute-start.36 = (f32[256,1536]{1,0:T(8,128)S(1)}, f32[256,1536]{1,0:T(8,128)S(1)}, u32[]{:S(2)}, u32[]{:S(2)}) collective-permute-start(f32[256,1536]{1,0:T(8,128)S(1)} %get-tuple-element.87), channel_id=1, source_target_pairs={{0,8},{8,0},{16,24},{24,16},{32,40},{40,32},{48,56},{56,48},{1,9},... | collective-permute-start | bytes 4718600 | tf_op jit(solution)/shard_map/ppermute | solution.py:39
  98.7 10.5 %collective-permute-start.17 = (bf16[64,1536]{1,0:T(8,128)(2,1)S(1)}, bf16[64,1536]{1,0:T(8,128)(2,1)S(1)}, u32[]{:S(2)}, u32[]{:S(2)}) collective-permute-start(bf16[64,1536]{1,0:T(8,128)(2,1)S(1)} %get-tuple-element.65), channel_id=1, source_target_pairs={{0,16},{8,24},{16,32},{24,40},{32,48},{40,56},{48,0},{56,8},{1,17}... | collective-permute-start | bytes 589832 | tf_op jit(solution)/shard_map/ppermute | solution.py:47
  100.2 17.4 %collective-permute-start.18 = (bf16[64,1536]{1,0:T(8,128)(2,1)S(1)}, bf16[64,1536]{1,0:T(8,128)(2,1)S(1)}, u32[]{:S(2)}, u32[]{:S(2)}) collective-permute-start(bf16[64,1536]{1,0:T(8,128)(2,1)S(1)} %get-tuple-element.66), channel_id=1, source_target_pairs={{0,32},{8,40},{16,48},{24,56},{32,0},{40,8},{48,16},{56,24},{1,33}... | collective-permute-start | bytes 589832 | tf_op jit(solution)/shard_map/ppermute | solution.py:47
  103.8 13.9 %collective-permute-start.19 = (bf16[64,1536]{1,0:T(8,128)(2,1)S(1)}, bf16[64,1536]{1,0:T(8,128)(2,1)S(1)}, u32[]{:S(2)}, u32[]{:S(2)}) collective-permute-start(bf16[64,1536]{1,0:T(8,128)(2,1)S(1)} %get-tuple-element.67), channel_id=1, source_target_pairs={{0,48},{8,56},{16,0},{24,8},{32,16},{40,24},{48,32},{56,40},{1,49}... | collective-permute-start | bytes 589832 | tf_op jit(solution)/shard_map/ppermute | solution.py:47
  105.6 18.9 %collective-permute-start.37 = (bf16[64,1536]{1,0:T(8,128)(2,1)S(1)}, bf16[64,1536]{1,0:T(8,128)(2,1)S(1)}, u32[]{:S(2)}, u32[]{:S(2)}) collective-permute-start(bf16[64,1536]{1,0:T(8,128)(2,1)S(1)} %get-tuple-element.89), channel_id=1, source_target_pairs={{0,16},{8,24},{16,32},{24,40},{32,48},{40,56},{48,0},{56,8},{1,17}... | collective-permute-start | bytes 589832 | tf_op jit(solution)/shard_map/ppermute | solution.py:47
  107.9 19.8 %collective-permute-start.38 = (bf16[64,1536]{1,0:T(8,128)(2,1)S(1)}, bf16[64,1536]{1,0:T(8,128)(2,1)S(1)}, u32[]{:S(2)}, u32[]{:S(2)}) collective-permute-start(bf16[64,1536]{1,0:T(8,128)(2,1)S(1)} %get-tuple-element.90), channel_id=1, source_target_pairs={{0,32},{8,40},{16,48},{24,56},{32,0},{40,8},{48,16},{56,24},{1,33}... | collective-permute-start | bytes 589832 | tf_op jit(solution)/shard_map/ppermute | solution.py:47
  109.2 18.6 %collective-permute-start.39 = (bf16[64,1536]{1,0:T(8,128)(2,1)S(1)}, bf16[64,1536]{1,0:T(8,128)(2,1)S(1)}, u32[]{:S(2)}, u32[]{:S(2)}) collective-permute-start(bf16[64,1536]{1,0:T(8,128)(2,1)S(1)} %get-tuple-element.91), channel_id=1, source_target_pairs={{0,48},{8,56},{16,0},{24,8},{32,16},{40,24},{48,32},{56,40},{1,49}... | collective-permute-start | bytes 589832 | tf_op jit(solution)/shard_map/ppermute | solution.py:47
  117.8 12.5 %collective-permute-start.25 = (bf16[16,1536]{1,0:T(8,128)(2,1)S(1)}, bf16[16,1536]{1,0:T(8,128)(2,1)S(1)}, u32[]{:S(2)}, u32[]{:S(2)}) collective-permute-start(bf16[16,1536]{1,0:T(8,128)(2,1)S(1)} %get-tuple-element.76), channel_id=1, source_target_pairs={{0,64},{64,128},{128,192},{192,0},{1,65},{65,129},{129,193},{193,1... | collective-permute-start | bytes 147464 | tf_op jit(solution)/shard_map/ppermute | solution.py:35
  120.4 14.9 %collective-permute-start.26 = (bf16[16,1536]{1,0:T(8,128)(2,1)S(1)}, bf16[16,1536]{1,0:T(8,128)(2,1)S(1)}, u32[]{:S(2)}, u32[]{:S(2)}) collective-permute-start(bf16[16,1536]{1,0:T(8,128)(2,1)S(1)} %get-tuple-element.77), channel_id=1, source_target_pairs={{0,128},{64,192},{128,0},{192,64},{1,129},{65,193},{129,1},{193,65... | collective-permute-start | bytes 147464 | tf_op jit(solution)/shard_map/ppermute | solution.py:35
  124.5 10.8 %collective-permute-start.27 = (bf16[16,1536]{1,0:T(8,128)(2,1)S(1)}, bf16[16,1536]{1,0:T(8,128)(2,1)S(1)}, u32[]{:S(2)}, u32[]{:S(2)}) collective-permute-start(bf16[16,1536]{1,0:T(8,128)(2,1)S(1)} %get-tuple-element.78), channel_id=1, source_target_pairs={{0,192},{64,0},{128,64},{192,128},{1,193},{65,1},{129,65},{193,129... | collective-permute-start | bytes 147464 | tf_op jit(solution)/shard_map/ppermute | solution.py:35
  127.8 7.5 %collective-permute-start.40 = (bf16[16,1536]{1,0:T(8,128)(2,1)S(1)}, bf16[16,1536]{1,0:T(8,128)(2,1)S(1)}, u32[]{:S(2)}, u32[]{:S(2)}) collective-permute-start(bf16[16,1536]{1,0:T(8,128)(2,1)S(1)} %get-tuple-element.93), channel_id=1, source_target_pairs={{0,64},{64,128},{128,192},{192,0},{1,65},{65,129},{129,193},{193,1... | collective-permute-start | bytes 147464 | tf_op jit(solution)/shard_map/ppermute | solution.py:35
  127.9 8.1 %collective-permute-start.41 = (bf16[16,1536]{1,0:T(8,128)(2,1)S(1)}, bf16[16,1536]{1,0:T(8,128)(2,1)S(1)}, u32[]{:S(2)}, u32[]{:S(2)}) collective-permute-start(bf16[16,1536]{1,0:T(8,128)(2,1)S(1)} %get-tuple-element.94), channel_id=1, source_target_pairs={{0,128},{64,192},{128,0},{192,64},{1,129},{65,193},{129,1},{193,65... | collective-permute-start | bytes 147464 | tf_op jit(solution)/shard_map/ppermute | solution.py:35
  130.3 7.5 %collective-permute-start.42 = (bf16[16,1536]{1,0:T(8,128)(2,1)S(1)}, bf16[16,1536]{1,0:T(8,128)(2,1)S(1)}, u32[]{:S(2)}, u32[]{:S(2)}) collective-permute-start(bf16[16,1536]{1,0:T(8,128)(2,1)S(1)} %get-tuple-element.95), channel_id=1, source_target_pairs={{0,192},{64,0},{128,64},{192,128},{1,193},{65,1},{129,65},{193,129... | collective-permute-start | bytes 147464 | tf_op jit(solution)/shard_map/ppermute | solution.py:35
  (16 other events, 100.7 us)
